TPU v7x, 32 devices: a whole 2x2x4 slice. The times are simulated.
32 devices in a mesh: gx: 2 (over y), gy: 4 (over z), gz: 4 (over x, core).
Axes of the slice: x: 2, y: 2, z: 4, core: 2. Of those that a mesh axis runs over, the one named last changes fastest.
Arguments:
- right_side: float32 [3, 16, 32, 512], P(None, 'gx', 'gy', 'gz'), may hold values from -17 to 17
- phase_labels: int32 [8, 16, 256], P('gx', 'gy', 'gz'), may hold values from 0 to 7
- phase_moduli: float32 [8], replicated, may hold values from 0.03 to 0.3
- coarse_nodes: int32 [16, 32, 512], P('gx', 'gy', 'gz'), may hold values from 0 to 5
- coarse_inverse: float32 [1152, 1152], P(('gx', 'gy', 'gz')), as said below
Outputs:
- solution_field: float32 [3, 16, 32, 512], P(None, 'gx', 'gy', 'gz')
- residual: float32 [3, 16, 32, 512], P(None, 'gx', 'gy', 'gz')
Inputs may be any that keep to these rules, and one draw needn't show every extreme that they name: `coarse_inverse`: symmetric.
All inputs are finite; a program needn't handle non-finite values.
Results may differ from a plain program's by a relative error of at most 0.0003.
Values sent between devices are 32-bit elements; how exact they have to be, the bound alone decides.
No kernel may reach another device: no remote copies, remote signals or barrier semaphores. Data moves between devices by JAX's collectives and lax.ppermute only.
A program may use at most 64 MiB of HBM per device.

v0:
```python
import jax
import jax.numpy as jnp
from jax import lax
from jax.sharding import PartitionSpec as P

SWEEPS = 4
ITERS = 2


bond_ratio = 0.5
relax = 0.6
highest = lax.Precision.HIGHEST
neighbour_offsets = tuple(
    (
        (shift_x, shift_y, shift_z)
        for shift_x in (-1, 0, 1)
        for shift_y in (-1, 0, 1)
        for shift_z in (-1, 0, 1)
        if shift_x * shift_x + shift_y * shift_y + shift_z * shift_z > 0
    )
)


def extended(x, sides, width):
    for axis, dim in sides:
        size, length = (lax.axis_size(axis), x.shape[dim])
        up = [(i, (i + 1) % size) for i in range(size - 1)]
        down = [(j, i) for i, j in up]
        last = lax.slice_in_dim(x, length - width, length, axis=dim)
        leading = lax.slice_in_dim(x, 0, width, axis=dim)
        before = lax.ppermute(last, axis, up)
        after = lax.ppermute(leading, axis, down)
        x = jnp.concatenate([before, x, after], axis=dim)
    return x


def inner_view(array, shift_x, shift_y, shift_z):
    size_x, size_y, size_z = array.shape[-3:]
    return array[
        ...,
        1 + shift_x : size_x - 1 + shift_x,
        1 + shift_y : size_y - 1 + shift_y,
        1 + shift_z : size_z - 1 + shift_z,
    ]


def spring_force(field_pad, stiff_pad):
    centre = inner_view(field_pad, 0, 0, 0)
    stiff_centre = inner_view(stiff_pad, 0, 0, 0)
    parts = [jnp.zeros_like(centre[0]) for component in range(3)]
    for offset in neighbour_offsets:
        length = offset[0] * offset[0] + offset[1] * offset[1] + offset[2] * offset[2]
        spring = (
            0.5 * (stiff_centre + inner_view(stiff_pad, offset[0], offset[1], offset[2])) / length
        )
        partner = inner_view(field_pad, offset[0], offset[1], offset[2])
        stretch = [centre[component] - partner[component] for component in range(3)]
        projected = jnp.zeros_like(stretch[0])
        for component in range(3):
            if offset[component] != 0:
                projected = projected + offset[component] * stretch[component]
        for component in range(3):
            summand = stretch[component]
            if offset[component] != 0:
                summand = summand + bond_ratio * offset[component] / length * projected
            parts[component] = parts[component] + spring * summand
    return jnp.stack(parts)


def diagonal(stiff_pad):
    stiff_centre = inner_view(stiff_pad, 0, 0, 0)
    parts = [jnp.zeros_like(stiff_centre) for component in range(3)]
    for offset in neighbour_offsets:
        length = offset[0] * offset[0] + offset[1] * offset[1] + offset[2] * offset[2]
        spring = (
            0.5 * (stiff_centre + inner_view(stiff_pad, offset[0], offset[1], offset[2])) / length
        )
        for component in range(3):
            parts[component] = parts[component] + spring * (
                1.0 + bond_ratio * offset[component] * offset[component] / length
            )
    return jnp.stack(parts)


def local_solve(residual_ext, stiff_rim, diag_ext):
    widths = [(0, 0)] * (residual_ext.ndim - 3) + [(1, 1)] * 3
    solution = relax * residual_ext / diag_ext
    for sweep in range(SWEEPS - 1):
        solution = (
            solution
            + relax * (residual_ext - spring_force(jnp.pad(solution, widths), stiff_rim)) / diag_ext
        )
    return solution


def cross(first, second):
    return jnp.stack(
        [
            first[1] * second[2] - first[2] * second[1],
            first[2] * second[0] - first[0] * second[2],
            first[0] * second[1] - first[1] * second[0],
        ]
    )


def local_coords(size_x, size_y, size_z):
    along_x = ((2.0 * jnp.arange(size_x, dtype=jnp.float32) + 1.0) / size_x - 1.0).reshape(
        size_x, 1, 1
    )
    along_y = ((2.0 * jnp.arange(size_y, dtype=jnp.float32) + 1.0) / size_y - 1.0).reshape(
        1, size_y, 1
    )
    along_z = ((2.0 * jnp.arange(size_z, dtype=jnp.float32) + 1.0) / size_z - 1.0).reshape(
        1, 1, size_z
    )
    return (along_x, along_y, along_z)


def fold_axis(spread, axis):
    size = spread.shape[axis]
    count = size - 4
    inner = lax.slice_in_dim(spread, 2, size - 2, axis=axis)
    lower = lax.slice_in_dim(spread, 0, 1, axis=axis)
    upper = lax.slice_in_dim(spread, size - 1, size, axis=axis)
    head = lax.slice_in_dim(inner, 0, 1, axis=axis) + lower
    tail = lax.slice_in_dim(inner, count - 1, count, axis=axis) + upper
    middle = lax.slice_in_dim(inner, 1, count - 1, axis=axis)
    return jnp.concatenate([head, middle, tail], axis=axis)


def body(right_side, phase_labels, phase_moduli, coarse_nodes, coarse_inverse):
    phases = phase_moduli.shape[0]
    matches = phase_labels[None] == jnp.arange(phases, dtype=jnp.int32)[:, None, None, None]
    coarse_stiff = jnp.sum(jnp.where(matches, phase_moduli[:, None, None, None], 0.0), axis=0)
    stiffness = jnp.repeat(jnp.repeat(jnp.repeat(coarse_stiff, 2, axis=0), 2, axis=1), 2, axis=2)
    stiff_rim = extended(stiffness, (("gx", 0), ("gy", 1), ("gz", 2)), 2)
    diag_ext = diagonal(stiff_rim)
    stiff_near = stiff_rim[1:-1, 1:-1, 1:-1]
    size_x, size_y, size_z = stiffness.shape
    coords = local_coords(size_x, size_y, size_z)
    node_count = coarse_inverse.shape[0] // 6
    onehot = (
        jnp.arange(node_count, dtype=jnp.int32)[:, None] == coarse_nodes.reshape(1, -1)
    ).astype(jnp.float32)

    def accumulate(piece):
        return jnp.dot(coarse_inverse, piece, precision=highest)

    def coarse_part(residual):
        moments = jnp.concatenate([residual, cross(coords, residual)], axis=0).reshape(6, -1)
        node_sums = jnp.einsum("gc,mc->gm", onehot, moments, precision=highest).reshape(-1)
        solved = accumulate(lax.all_gather(node_sums, ("gx", "gy", "gz"), axis=0, tiled=True))
        per_cell = jnp.einsum("gm,gc->mc", solved.reshape(node_count, 6), onehot, precision=highest)
        per_cell = per_cell.reshape(6, size_x, size_y, size_z)
        return per_cell[:3] + cross(per_cell[3:], coords)

    def local_part(residual_ext):
        solution = local_solve(residual_ext, stiff_rim, diag_ext)
        spread = extended(solution, (("gx", 1), ("gy", 2), ("gz", 3)), 1)
        return fold_axis(fold_axis(fold_axis(spread, 1), 2), 3)

    def widen(vector):
        return extended(vector, (("gx", 1), ("gy", 2), ("gz", 3)), 1)

    def operate(vector):
        return spring_force(widen(vector), stiff_near)

    def precondition(residual_form):
        return local_part(widen(residual_form)) + coarse_part(residual_form)

    residual = right_side
    solution_field = jnp.zeros_like(right_side)

    def paired_sums(first, second):
        return lax.psum((first, second), ("gx", "gy", "gz"))

    search = precondition(residual)
    image = operate(search)
    norm_now, curvature = paired_sums(jnp.sum(residual * search), jnp.sum(image * search))
    step_size = norm_now / curvature
    direction = search
    along = image
    for step in range(ITERS):
        solution_field = solution_field + step_size * direction
        residual = residual - step_size * along
        if step + 1 < ITERS:
            search = precondition(residual)
            image = operate(search)
            norm_next, curvature = paired_sums(jnp.sum(residual * search), jnp.sum(image * search))
            ratio = norm_next / norm_now
            step_size = norm_next / (curvature - ratio * norm_next / step_size)
            direction = search + ratio * direction
            along = image + ratio * along
            norm_now = norm_next
    return (solution_field, residual)


def solution(mesh):
    in_specs = (
        P(None, "gx", "gy", "gz"),
        P("gx", "gy", "gz"),
        P(),
        P("gx", "gy", "gz"),
        P(("gx", "gy", "gz"), None),
    )
    out_specs = (P(None, "gx", "gy", "gz"), P(None, "gx", "gy", "gz"))
    return jax.shard_map(body, mesh=mesh, in_specs=in_specs, out_specs=out_specs, check_vma=False)
```

profile of v0, /device:TPU:0, one launch (start us, length us, event | category | flops | bytes accessed | tf_op | source)
XLA Modules:
  0.0 412.5 jit_solution(521552432372277175)
XLA Ops:
  1.7 4.9 %collective-permute-start.6 = (f32[2,8,128]{2,1,0:T(8,128)S(1)}, f32[2,8,128]{2,1,0:T(8,128)S(1)}, u32[]{:S(2)}, u32[]{:S(2)}) collective-permute-start(f32[2,8,128]{2,1,0:T(8,128)S(1)} %broadcast_in_dim.51), channel_id=1, source_target_pairs={{0,16},{1,17},{2,18},{3,19},{4,20},{5,21},{6,22},{7,23},{8,24},{9,... | collective-permute-start | bytes 24584 | tf_op jit(solution)/shard_map/ppermute | solution.py:31
  8.1 4.5 %collective-permute-start = (f32[3,1,8,128]{3,2,1,0:T(8,128)S(1)}, f32[3,1,8,128]{3,2,1,0:T(8,128)S(1)}, u32[]{:S(2)}, u32[]{:S(2)}) collective-permute-start(f32[3,1,8,128]{3,2,1,0:T(8,128)S(1)} %get-tuple-element.276), channel_id=1, source_target_pairs={{0,16},{1,17},{2,18},{3,19},{4,20},{5,21},{6,22},{7,23},{8,24},{9,... | collective-permute-start | bytes 36872 | tf_op jit(solution)/shard_map/ppermute | solution.py:31
  16.2 41.7 %all-reduce.6 = f32[1152]{0:T(1024)S(1)} all-reduce(f32[1152]{0:T(1024)S(1)} %dynamic-update-slice), channel_id=1, replica_groups=mesh['gx'=2,'gy'=4,'gz'=4] {'gx','gy','gz'}, use_global_device_ids=true, to_apply=%add.6 | all-reduce | flops 1152 | bytes 9216
  59.8 3.4 collective-permute-start.8
  64.6 4.2 %collective-permute-done.9 = f32[12,2,128]{2,1,0:T(2,128)S(1)} collective-permute-done((f32[12,2,128]{2,1,0:T(2,128)S(1)}, f32[12,2,128]{2,1,0:T(2,128)S(1)}, u32[]{:S(2)}, u32[]{:S(2)}) %collective-permute-start.9) | collective-permute-done | bytes 12320 | tf_op jit(solution)/shard_map/ppermute | solution.py:32
  71.6 3.3 collective-permute-start.2
  78.0 2.5 collective-permute-done.3
  80.7 4.1 collective-permute-start.4
  87.0 3.8 collective-permute-done.5
  91.3 1.9 fusion.1591
  93.2 1.7 fusion.1590
  94.9 1.7 fusion.1589
  96.8 1.7 fusion.1588
  100.1 1.7 fusion.1586
  102.0 2.2 fusion.1585
  106.0 1.7 fusion.1583
  108.0 2.6 collective-permute-start.12
  113.4 3.2 collective-permute-done.13
  116.7 2.3 collective-permute-start.14
  120.7 4.2 %collective-permute-done.15 = f32[3,12,1,130]{3,2,1,0:T(1,128)S(1)} collective-permute-done((f32[3,12,1,130]{3,2,1,0:T(1,128)S(1)}, f32[3,12,1,130]{3,2,1,0:T(1,128)S(1)}, u32[]{:S(2)}, u32[]{:S(2)}) %collective-permute-start.15) | collective-permute-done | bytes 18752 | tf_op jit(solution)/shard_map/ppermute | solution.py:32
  125.2 3.3 collective-permute-start.16
  130.6 3.6 collective-permute-done.17
  140.3 4.2 %collective-permute-done.19 = f32[3,1,8,128]{3,2,1,0:T(8,128)S(1)} collective-permute-done((f32[3,1,8,128]{3,2,1,0:T(8,128)S(1)}, f32[3,1,8,128]{3,2,1,0:T(8,128)S(1)}, u32[]{:S(2)}, u32[]{:S(2)}) %collective-permute-start.19) | collective-permute-done | bytes 12320 | tf_op jit(solution)/shard_map/ppermute | solution.py:32
  144.6 2.0 collective-permute-start.20
  148.1 4.1 %collective-permute-done.21 = f32[3,10,1,128]{3,2,1,0:T(1,128)S(1)} collective-permute-done((f32[3,10,1,128]{3,2,1,0:T(1,128)S(1)}, f32[3,10,1,128]{3,2,1,0:T(1,128)S(1)}, u32[]{:S(2)}, u32[]{:S(2)}) %collective-permute-start.21) | collective-permute-done | bytes 15392 | tf_op jit(solution)/shard_map/ppermute | solution.py:32
  152.5 4.1 collective-permute-start.22
  158.1 4.0 collective-permute-done.23
  170.6 40.3 %all-reduce.9 = (f32[]{:T(128)}, f32[]{:T(128)}) all-reduce(f32[]{:T(128)} %get-tuple-element.31, f32[]{:T(128)} %fusion.1595), channel_id=1, replica_groups=mesh['gx'=2,'gy'=4,'gz'=4] {'gx','gy','gz'}, use_global_device_ids=true, to_apply=%region_2.3 | all-reduce | flops 2 | bytes 16 | tf_op jit(solution)/shard_map/psum | solution.py:175
  214.7 5.0 %collective-permute-start.24 = (f32[3,1,8,128]{3,2,1,0:T(8,128)}, f32[3,1,8,128]{3,2,1,0:T(8,128)}, u32[]{:S(2)}, u32[]{:S(2)}) collective-permute-start(f32[3,1,8,128]{3,2,1,0:T(8,128)} %get-tuple-element.269), channel_id=1, source_target_pairs={{0,16},{1,17},{2,18},{3,19},{4,20},{5,21},{6,22},{7,23},{8,24},{9,... | collective-permute-start | bytes 36872 | tf_op jit(solution)/shard_map/ppermute | solution.py:31
  223.2 42.9 %all-reduce.7 = f32[1152]{0:T(1024)} all-reduce(f32[1152]{0:T(1024)S(1)} %dynamic-update-slice.1), channel_id=1, replica_groups=mesh['gx'=2,'gy'=4,'gz'=4] {'gx','gy','gz'}, use_global_device_ids=true, to_apply=%add.7 | all-reduce | flops 1152 | bytes 9216
  269.0 2.5 collective-permute-start.26
  274.9 2.8 collective-permute-done.27
  281.1 4.0 collective-permute-done.29
  286.8 1.7 fusion.1582
  292.0 1.7 fusion.1579
  297.2 2.1 fusion.1576
  303.0 2.3 collective-permute-start.30
  307.0 4.3 %collective-permute-done.31 = f32[3,1,10,130]{3,2,1,0:T(8,128)S(1)} collective-permute-done((f32[3,1,10,130]{3,2,1,0:T(8,128)S(1)}, f32[3,1,10,130]{3,2,1,0:T(8,128)S(1)}, u32[]{:S(2)}, u32[]{:S(2)}) %collective-permute-start.31) | collective-permute-done | bytes 15632 | tf_op jit(solution)/shard_map/ppermute | solution.py:32
  311.4 2.0 collective-permute-start.32
  315.0 4.2 %collective-permute-done.33 = f32[3,12,1,130]{3,2,1,0:T(1,128)S(1)} collective-permute-done((f32[3,12,1,130]{3,2,1,0:T(1,128)S(1)}, f32[3,12,1,130]{3,2,1,0:T(1,128)S(1)}, u32[]{:S(2)}, u32[]{:S(2)}) %collective-permute-start.33) | collective-permute-done | bytes 18752 | tf_op jit(solution)/shard_map/ppermute | solution.py:32
  319.5 3.5 collective-permute-start.34
  325.1 3.3 collective-permute-done.35
  334.6 4.2 %collective-permute-done.37 = f32[3,1,8,128]{3,2,1,0:T(8,128)S(1)} collective-permute-done((f32[3,1,8,128]{3,2,1,0:T(8,128)S(1)}, f32[3,1,8,128]{3,2,1,0:T(8,128)S(1)}, u32[]{:S(2)}, u32[]{:S(2)}) %collective-permute-start.37) | collective-permute-done | bytes 12320 | tf_op jit(solution)/shard_map/ppermute | solution.py:32
  338.8 3.9 collective-permute-start.38
  344.2 4.1 collective-permute-done.39
  348.6 4.1 collective-permute-start.40
  354.2 4.0 collective-permute-done.41
  366.9 40.3 %all-reduce.8 = (f32[]{:T(128)}, f32[]{:T(128)}) all-reduce(f32[]{:T(128)} %get-tuple-element.20, f32[]{:T(128)} %fusion.1593), channel_id=1, replica_groups=mesh['gx'=2,'gy'=4,'gz'=4] {'gx','gy','gz'}, use_global_device_ids=true, to_apply=%region_6.7 | all-reduce | flops 2 | bytes 16 | tf_op jit(solution)/shard_map/psum | solution.py:175
  (407 shorter events, 97.6 us)
Async XLA Ops:
  0.6 57.3 %copy-start = (f32[36,1152]{1,0:T(8,128)S(1)}, f32[36,1152]{1,0:T(8,128)}, u32[]{:S(2)}) copy-start(f32[36,1152]{1,0:T(8,128)} %param.9) | copy-start | bytes 497668
  1.7 58.1 %collective-permute-start.6 = (f32[2,8,128]{2,1,0:T(8,128)S(1)}, f32[2,8,128]{2,1,0:T(8,128)S(1)}, u32[]{:S(2)}, u32[]{:S(2)}) collective-permute-start(f32[2,8,128]{2,1,0:T(8,128)S(1)} %broadcast_in_dim.51), channel_id=1, source_target_pairs={{0,16},{1,17},{2,18},{3,19},{4,20},{5,21},{6,22},{7,23},{8,24},{9,... | collective-permute-start | bytes 24584 | tf_op jit(solution)/shard_map/ppermute | solution.py:31
  6.8 53.0 %collective-permute-start.7 = (f32[2,8,128]{2,1,0:T(8,128)S(1)}, f32[2,8,128]{2,1,0:T(8,128)S(1)}, u32[]{:S(2)}, u32[]{:S(2)}) collective-permute-start(f32[2,8,128]{2,1,0:T(8,128)S(1)} %broadcast_in_dim.59), channel_id=1, source_target_pairs={{16,0},{17,1},{18,2},{19,3},{20,4},{21,5},{22,6},{23,7},{24,8},{25... | collective-permute-start | bytes 24584 | tf_op jit(solution)/shard_map/ppermute | solution.py:32
  8.1 56.4 %collective-permute-start = (f32[3,1,8,128]{3,2,1,0:T(8,128)S(1)}, f32[3,1,8,128]{3,2,1,0:T(8,128)S(1)}, u32[]{:S(2)}, u32[]{:S(2)}) collective-permute-start(f32[3,1,8,128]{3,2,1,0:T(8,128)S(1)} %get-tuple-element.276), channel_id=1, source_target_pairs={{0,16},{1,17},{2,18},{3,19},{4,20},{5,21},{6,22},{7,23},{8,24},{9,... | collective-permute-start | bytes 36872 | tf_op jit(solution)/shard_map/ppermute | solution.py:31
  12.6 51.9 %collective-permute-start.1 = (f32[3,1,8,128]{3,2,1,0:T(8,128)S(1)}, f32[3,1,8,128]{3,2,1,0:T(8,128)S(1)}, u32[]{:S(2)}, u32[]{:S(2)}) collective-permute-start(f32[3,1,8,128]{3,2,1,0:T(8,128)S(1)} %get-tuple-element.275), channel_id=1, source_target_pairs={{16,0},{17,1},{18,2},{19,3},{20,4},{21,5},{22,6},{23,7},{24,8},{25... | collective-permute-start | bytes 36872 | tf_op jit(solution)/shard_map/ppermute | solution.py:32
  59.8 4.8 %collective-permute-start.8 = (f32[12,2,128]{2,1,0:T(2,128)S(1)}, f32[12,2,128]{2,1,0:T(2,128)S(1)}, u32[]{:S(2)}, u32[]{:S(2)}) collective-permute-start(f32[12,2,128]{2,1,0:T(2,128)S(1)} %get-tuple-element.281), channel_id=1, source_target_pairs={{0,4},{4,8},{8,12},{1,5},{5,9},{9,13},{2,6},{6,10},{10,14},{3,7},{... | collective-permute-start | bytes 36872 | tf_op jit(solution)/shard_map/ppermute | solution.py:31
  63.2 5.6 %collective-permute-start.9 = (f32[12,2,128]{2,1,0:T(2,128)S(1)}, f32[12,2,128]{2,1,0:T(2,128)S(1)}, u32[]{:S(2)}, u32[]{:S(2)}) collective-permute-start(f32[12,2,128]{2,1,0:T(2,128)S(1)} %get-tuple-element.282), channel_id=1, source_target_pairs={{4,0},{8,4},{12,8},{5,1},{9,5},{13,9},{6,2},{10,6},{14,10},{7,3},{... | collective-permute-start | bytes 36872 | tf_op jit(solution)/shard_map/ppermute | solution.py:32
  68.9 7.2 %collective-permute-start.10 = (f32[12,12,2]{2,1,0:T(8,128)S(1)}, f32[12,12,2]{2,1,0:T(8,128)S(1)}, u32[]{:S(2)}, u32[]{:S(2)}) collective-permute-start(f32[12,12,2]{2,1,0:T(8,128)S(1)} %get-tuple-element.273), channel_id=1, source_target_pairs={{0,1},{1,2},{2,3},{4,5},{5,6},{6,7},{8,9},{9,10},{10,11},{12,13},{... | collective-permute-start | bytes 3464 | tf_op jit(solution)/shard_map/ppermute | solution.py:31
  70.2 5.9 %collective-permute-start.11 = (f32[12,12,2]{2,1,0:T(8,128)S(1)}, f32[12,12,2]{2,1,0:T(8,128)S(1)}, u32[]{:S(2)}, u32[]{:S(2)}) collective-permute-start(f32[12,12,2]{2,1,0:T(8,128)S(1)} %get-tuple-element.274), channel_id=1, source_target_pairs={{1,0},{2,1},{3,2},{5,4},{6,5},{7,6},{9,8},{10,9},{11,10},{13,12},{... | collective-permute-start | bytes 3464 | tf_op jit(solution)/shard_map/ppermute | solution.py:32
  71.6 6.3 %collective-permute-start.2 = (f32[3,10,1,128]{3,2,1,0:T(1,128)S(1)}, f32[3,10,1,128]{3,2,1,0:T(1,128)S(1)}, u32[]{:S(2)}, u32[]{:S(2)}) collective-permute-start(f32[3,10,1,128]{3,2,1,0:T(1,128)S(1)} %get-tuple-element.260), channel_id=1, source_target_pairs={{0,4},{4,8},{8,12},{1,5},{5,9},{9,13},{2,6},{6,10},{10,14},{3,7},{... | collective-permute-start | bytes 46088 | tf_op jit(solution)/shard_map/ppermute | solution.py:31
  74.9 5.6 %collective-permute-start.3 = (f32[3,10,1,128]{3,2,1,0:T(1,128)S(1)}, f32[3,10,1,128]{3,2,1,0:T(1,128)S(1)}, u32[]{:S(2)}, u32[]{:S(2)}) collective-permute-start(f32[3,10,1,128]{3,2,1,0:T(1,128)S(1)} %get-tuple-element.259), channel_id=1, source_target_pairs={{4,0},{8,4},{12,8},{5,1},{9,5},{13,9},{6,2},{10,6},{14,10},{7,3},{... | collective-permute-start | bytes 46088 | tf_op jit(solution)/shard_map/ppermute | solution.py:32
  77.2 28.7 %copy-start.1 = (f32[10,10,130]{2,1,0:T(8,128)}, f32[10,10,130]{2,1,0:T(8,128)S(1)}, u32[]{:S(2)}) copy-start(f32[10,10,130]{2,1,0:T(8,128)S(1)} %get-tuple-element.74) | copy-start | bytes 156004
  77.2 30.4 %copy-start.17 = (f32[1,10,10,130]{3,2,1,0:T(8,128)}, f32[1,10,10,130]{3,2,1,0:T(8,128)S(1)}, u32[]{:S(2)}) copy-start(f32[1,10,10,130]{3,2,1,0:T(8,128)S(1)} %get-tuple-element.72) | copy-start | bytes 156004
  77.8 29.8 %copy-start.13 = (f32[1,10,10,130]{3,2,1,0:T(8,128)}, f32[1,10,10,130]{3,2,1,0:T(8,128)S(1)}, u32[]{:S(2)}) copy-start(f32[1,10,10,130]{3,2,1,0:T(8,128)S(1)} %get-tuple-element.94) | copy-start | bytes 156004
  80.7 6.3 %collective-permute-start.4 = (f32[3,10,10,1]{3,0,2,1:T(4,128)S(1)}, f32[3,10,10,1]{3,0,2,1:T(4,128)S(1)}, u32[]{:S(2)}, u32[]{:S(2)}) collective-permute-start(f32[3,10,10,1]{3,0,2,1:T(4,128)S(1)} %get-tuple-element.243), channel_id=1, source_target_pairs={{0,1},{1,2},{2,3},{4,5},{5,6},{6,7},{8,9},{9,10},{10,11},{12,13},{... | collective-permute-start | bytes 3608 | tf_op jit(solution)/shard_map/ppermute | solution.py:31
  84.8 6.0 %collective-permute-start.5 = (f32[3,10,10,1]{3,0,2,1:T(4,128)S(1)}, f32[3,10,10,1]{3,0,2,1:T(4,128)S(1)}, u32[]{:S(2)}, u32[]{:S(2)}) collective-permute-start(f32[3,10,10,1]{3,0,2,1:T(4,128)S(1)} %get-tuple-element.244), channel_id=1, source_target_pairs={{1,0},{2,1},{3,2},{5,4},{6,5},{7,6},{9,8},{10,9},{11,10},{13,12},{... | collective-permute-start | bytes 3608 | tf_op jit(solution)/shard_map/ppermute | solution.py:32
  108.0 5.4 %collective-permute-start.12 = (f32[3,1,10,130]{3,2,1,0:T(8,128)S(1)}, f32[3,1,10,130]{3,2,1,0:T(8,128)S(1)}, u32[]{:S(2)}, u32[]{:S(2)}) collective-permute-start(f32[3,1,10,130]{3,2,1,0:T(8,128)S(1)} %get-tuple-element.109), channel_id=1, source_target_pairs={{0,16},{1,17},{2,18},{3,19},{4,20},{5,21},{6,22},{7,23},{8,24},{9,... | collective-permute-start | bytes 46808 | tf_op jit(solution)/shard_map/ppermute | solution.py:31
  110.6 6.0 %collective-permute-start.13 = (f32[3,1,10,130]{3,2,1,0:T(8,128)S(1)}, f32[3,1,10,130]{3,2,1,0:T(8,128)S(1)}, u32[]{:S(2)}, u32[]{:S(2)}) collective-permute-start(f32[3,1,10,130]{3,2,1,0:T(8,128)S(1)} %get-tuple-element.110), channel_id=1, source_target_pairs={{16,0},{17,1},{18,2},{19,3},{20,4},{21,5},{22,6},{23,7},{24,8},{25... | collective-permute-start | bytes 46808 | tf_op jit(solution)/shard_map/ppermute | solution.py:32
  116.7 4.0 collective-permute-start.14
  119.1 5.9 %collective-permute-start.15 = (f32[3,12,1,130]{3,2,1,0:T(1,128)S(1)}, f32[3,12,1,130]{3,2,1,0:T(1,128)S(1)}, u32[]{:S(2)}, u32[]{:S(2)}) collective-permute-start(f32[3,12,1,130]{3,2,1,0:T(1,128)S(1)} %get-tuple-element.106), channel_id=1, source_target_pairs={{4,0},{8,4},{12,8},{5,1},{9,5},{13,9},{6,2},{10,6},{14,10},{7,3},{... | collective-permute-start | bytes 56168 | tf_op jit(solution)/shard_map/ppermute | solution.py:32
  125.2 5.4 %collective-permute-start.16 = (f32[3,12,12,1]{3,2,1,0:T(8,128)S(1)}, f32[3,12,12,1]{3,2,1,0:T(8,128)S(1)}, u32[]{:S(2)}, u32[]{:S(2)}) collective-permute-start(f32[3,12,12,1]{3,2,1,0:T(8,128)S(1)} %get-tuple-element.103), channel_id=1, source_target_pairs={{0,1},{1,2},{2,3},{4,5},{5,6},{6,7},{8,9},{9,10},{10,11},{12,13},{... | collective-permute-start | bytes 5192 | tf_op jit(solution)/shard_map/ppermute | solution.py:31
  128.5 5.7 %collective-permute-start.17 = (f32[3,12,12,1]{3,2,1,0:T(8,128)S(1)}, f32[3,12,12,1]{3,2,1,0:T(8,128)S(1)}, u32[]{:S(2)}, u32[]{:S(2)}) collective-permute-start(f32[3,12,12,1]{3,2,1,0:T(8,128)S(1)} %get-tuple-element.104), channel_id=1, source_target_pairs={{1,0},{2,1},{3,2},{5,4},{6,5},{7,6},{9,8},{10,9},{11,10},{13,12},{... | collective-permute-start | bytes 5192 | tf_op jit(solution)/shard_map/ppermute | solution.py:32
  137.3 31.7 %copy-start.19 = (f32[3,8,8,128]{3,2,1,0:T(8,128)}, f32[3,8,8,128]{3,2,1,0:T(8,128)S(1)}, u32[]{:S(2)}) copy-start(f32[3,8,8,128]{3,2,1,0:T(8,128)S(1)} %get-tuple-element.32) | copy-start | bytes 294916
  137.3 3.0 collective-permute-start.18
  138.9 5.6 %collective-permute-start.19 = (f32[3,1,8,128]{3,2,1,0:T(8,128)S(1)}, f32[3,1,8,128]{3,2,1,0:T(8,128)S(1)}, u32[]{:S(2)}, u32[]{:S(2)}) collective-permute-start(f32[3,1,8,128]{3,2,1,0:T(8,128)S(1)} %get-tuple-element.272), channel_id=1, source_target_pairs={{16,0},{17,1},{18,2},{19,3},{20,4},{21,5},{22,6},{23,7},{24,8},{25... | collective-permute-start | bytes 36872 | tf_op jit(solution)/shard_map/ppermute | solution.py:32
  144.6 3.5 collective-permute-start.20
  146.6 5.6 %collective-permute-start.21 = (f32[3,10,1,128]{3,2,1,0:T(1,128)S(1)}, f32[3,10,1,128]{3,2,1,0:T(1,128)S(1)}, u32[]{:S(2)}, u32[]{:S(2)}) collective-permute-start(f32[3,10,1,128]{3,2,1,0:T(1,128)S(1)} %get-tuple-element.258), channel_id=1, source_target_pairs={{4,0},{8,4},{12,8},{5,1},{9,5},{13,9},{6,2},{10,6},{14,10},{7,3},{... | collective-permute-start | bytes 46088 | tf_op jit(solution)/shard_map/ppermute | solution.py:32
  152.5 12.2 %collective-permute-start.22 = (f32[3,10,10,1]{3,0,2,1:T(4,128)S(1)}, f32[3,10,10,1]{3,0,2,1:T(4,128)S(1)}, u32[]{:S(2)}, u32[]{:S(2)}) collective-permute-start(f32[3,10,10,1]{3,0,2,1:T(4,128)S(1)} %get-tuple-element.241), channel_id=1, source_target_pairs={{0,1},{1,2},{2,3},{4,5},{5,6},{6,7},{8,9},{9,10},{10,11},{12,13},{... | collective-permute-start | bytes 3608 | tf_op jit(solution)/shard_map/ppermute | solution.py:31
  156.6 5.5 %collective-permute-start.23 = (f32[3,10,10,1]{3,0,2,1:T(4,128)S(1)}, f32[3,10,10,1]{3,0,2,1:T(4,128)S(1)}, u32[]{:S(2)}, u32[]{:S(2)}) collective-permute-start(f32[3,10,10,1]{3,0,2,1:T(4,128)S(1)} %get-tuple-element.242), channel_id=1, source_target_pairs={{1,0},{2,1},{3,2},{5,4},{6,5},{7,6},{9,8},{10,9},{11,10},{13,12},{... | collective-permute-start | bytes 3608 | tf_op jit(solution)/shard_map/ppermute | solution.py:32
  214.7 52.1 %collective-permute-start.24 = (f32[3,1,8,128]{3,2,1,0:T(8,128)}, f32[3,1,8,128]{3,2,1,0:T(8,128)}, u32[]{:S(2)}, u32[]{:S(2)}) collective-permute-start(f32[3,1,8,128]{3,2,1,0:T(8,128)} %get-tuple-element.269), channel_id=1, source_target_pairs={{0,16},{1,17},{2,18},{3,19},{4,20},{5,21},{6,22},{7,23},{8,24},{9,... | collective-permute-start | bytes 36872 | tf_op jit(solution)/shard_map/ppermute | solution.py:31
  219.7 47.1 %collective-permute-start.25 = (f32[3,1,8,128]{3,2,1,0:T(8,128)}, f32[3,1,8,128]{3,2,1,0:T(8,128)}, u32[]{:S(2)}, u32[]{:S(2)}) collective-permute-start(f32[3,1,8,128]{3,2,1,0:T(8,128)} %get-tuple-element.270), channel_id=1, source_target_pairs={{16,0},{17,1},{18,2},{19,3},{20,4},{21,5},{22,6},{23,7},{24,8},{25... | collective-permute-start | bytes 36872 | tf_op jit(solution)/shard_map/ppermute | solution.py:32
  269.0 4.2 %collective-permute-start.26 = (f32[3,10,1,128]{3,2,1,0:T(1,128)}, f32[3,10,1,128]{3,2,1,0:T(1,128)}, u32[]{:S(2)}, u32[]{:S(2)}) collective-permute-start(f32[3,10,1,128]{3,2,1,0:T(1,128)} %get-tuple-element.254), channel_id=1, source_target_pairs={{0,4},{4,8},{8,12},{1,5},{5,9},{9,13},{2,6},{6,10},{10,14},{3,7},{... | collective-permute-start | bytes 46088 | tf_op jit(solution)/shard_map/ppermute | solution.py:31
  271.8 5.9 %collective-permute-start.27 = (f32[3,10,1,128]{3,2,1,0:T(1,128)}, f32[3,10,1,128]{3,2,1,0:T(1,128)S(1)}, u32[]{:S(2)}, u32[]{:S(2)}) collective-permute-start(f32[3,10,1,128]{3,2,1,0:T(1,128)} %get-tuple-element.253), channel_id=1, source_target_pairs={{4,0},{8,4},{12,8},{5,1},{9,5},{13,9},{6,2},{10,6},{14,10},{7,3},{... | collective-permute-start | bytes 46088 | tf_op jit(solution)/shard_map/ppermute | solution.py:32
  277.9 3.2 collective-permute-start.28
  279.2 5.8 %collective-permute-start.29 = (f32[3,10,10,1]{3,0,2,1:T(4,128)S(1)}, f32[3,10,10,1]{3,0,2,1:T(4,128)S(1)}, u32[]{:S(2)}, u32[]{:S(2)}) collective-permute-start(f32[3,10,10,1]{3,0,2,1:T(4,128)S(1)} %get-tuple-element.240), channel_id=1, source_target_pairs={{1,0},{2,1},{3,2},{5,4},{6,5},{7,6},{9,8},{10,9},{11,10},{13,12},{... | collective-permute-start | bytes 3608 | tf_op jit(solution)/shard_map/ppermute | solution.py:32
  303.0 4.1 collective-permute-start.30
  305.3 6.0 %collective-permute-start.31 = (f32[3,1,10,130]{3,2,1,0:T(8,128)S(1)}, f32[3,1,10,130]{3,2,1,0:T(8,128)S(1)}, u32[]{:S(2)}, u32[]{:S(2)}) collective-permute-start(f32[3,1,10,130]{3,2,1,0:T(8,128)S(1)} %get-tuple-element.108), channel_id=1, source_target_pairs={{16,0},{17,1},{18,2},{19,3},{20,4},{21,5},{22,6},{23,7},{24,8},{25... | collective-permute-start | bytes 46808 | tf_op jit(solution)/shard_map/ppermute | solution.py:32
  311.4 3.6 collective-permute-start.32
  313.3 5.9 %collective-permute-start.33 = (f32[3,12,1,130]{3,2,1,0:T(1,128)S(1)}, f32[3,12,1,130]{3,2,1,0:T(1,128)S(1)}, u32[]{:S(2)}, u32[]{:S(2)}) collective-permute-start(f32[3,12,1,130]{3,2,1,0:T(1,128)S(1)} %get-tuple-element.102), channel_id=1, source_target_pairs={{4,0},{8,4},{12,8},{5,1},{9,5},{13,9},{6,2},{10,6},{14,10},{7,3},{... | collective-permute-start | bytes 56168 | tf_op jit(solution)/shard_map/ppermute | solution.py:32
  319.5 5.6 %collective-permute-start.34 = (f32[3,12,12,1]{3,2,1,0:T(8,128)S(1)}, f32[3,12,12,1]{3,2,1,0:T(8,128)S(1)}, u32[]{:S(2)}, u32[]{:S(2)}) collective-permute-start(f32[3,12,12,1]{3,2,1,0:T(8,128)S(1)} %get-tuple-element.99), channel_id=1, source_target_pairs={{0,1},{1,2},{2,3},{4,5},{5,6},{6,7},{8,9},{9,10},{10,11},{12,13},{... | collective-permute-start | bytes 5192 | tf_op jit(solution)/shard_map/ppermute | solution.py:31
  323.0 5.4 %collective-permute-start.35 = (f32[3,12,12,1]{3,2,1,0:T(8,128)S(1)}, f32[3,12,12,1]{3,2,1,0:T(8,128)S(1)}, u32[]{:S(2)}, u32[]{:S(2)}) collective-permute-start(f32[3,12,12,1]{3,2,1,0:T(8,128)S(1)} %get-tuple-element.100), channel_id=1, source_target_pairs={{1,0},{2,1},{3,2},{5,4},{6,5},{7,6},{9,8},{10,9},{11,10},{13,12},{... | collective-permute-start | bytes 5192 | tf_op jit(solution)/shard_map/ppermute | solution.py:32
  331.6 3.0 collective-permute-start.36
  333.2 5.6 %collective-permute-start.37 = (f32[3,1,8,128]{3,2,1,0:T(8,128)S(1)}, f32[3,1,8,128]{3,2,1,0:T(8,128)S(1)}, u32[]{:S(2)}, u32[]{:S(2)}) collective-permute-start(f32[3,1,8,128]{3,2,1,0:T(8,128)S(1)} %get-tuple-element.268), channel_id=1, source_target_pairs={{16,0},{17,1},{18,2},{19,3},{20,4},{21,5},{22,6},{23,7},{24,8},{25... | collective-permute-start | bytes 36872 | tf_op jit(solution)/shard_map/ppermute | solution.py:32
  338.8 5.3 %collective-permute-start.38 = (f32[3,10,1,128]{3,2,1,0:T(1,128)S(1)}, f32[3,10,1,128]{3,2,1,0:T(1,128)S(1)}, u32[]{:S(2)}, u32[]{:S(2)}) collective-permute-start(f32[3,10,1,128]{3,2,1,0:T(1,128)S(1)} %get-tuple-element.251), channel_id=1, source_target_pairs={{0,4},{4,8},{8,12},{1,5},{5,9},{9,13},{2,6},{6,10},{10,14},{3,7},{... | collective-permute-start | bytes 46088 | tf_op jit(solution)/shard_map/ppermute | solution.py:31
  342.7 5.6 %collective-permute-start.39 = (f32[3,10,1,128]{3,2,1,0:T(1,128)S(1)}, f32[3,10,1,128]{3,2,1,0:T(1,128)S(1)}, u32[]{:S(2)}, u32[]{:S(2)}) collective-permute-start(f32[3,10,1,128]{3,2,1,0:T(1,128)S(1)} %get-tuple-element.252), channel_id=1, source_target_pairs={{4,0},{8,4},{12,8},{5,1},{9,5},{13,9},{6,2},{10,6},{14,10},{7,3},{... | collective-permute-start | bytes 46088 | tf_op jit(solution)/shard_map/ppermute | solution.py:32
  348.6 12.2 %collective-permute-start.40 = (f32[3,10,10,1]{3,0,2,1:T(4,128)S(1)}, f32[3,10,10,1]{3,0,2,1:T(4,128)S(1)}, u32[]{:S(2)}, u32[]{:S(2)}) collective-permute-start(f32[3,10,10,1]{3,0,2,1:T(4,128)S(1)} %get-tuple-element.237), channel_id=1, source_target_pairs={{0,1},{1,2},{2,3},{4,5},{5,6},{6,7},{8,9},{9,10},{10,11},{12,13},{... | collective-permute-start | bytes 3608 | tf_op jit(solution)/shard_map/ppermute | solution.py:31
  352.7 5.5 %collective-permute-start.41 = (f32[3,10,10,1]{3,0,2,1:T(4,128)S(1)}, f32[3,10,10,1]{3,0,2,1:T(4,128)S(1)}, u32[]{:S(2)}, u32[]{:S(2)}) collective-permute-start(f32[3,10,10,1]{3,0,2,1:T(4,128)S(1)} %get-tuple-element.238), channel_id=1, source_target_pairs={{1,0},{2,1},{3,2},{5,4},{6,5},{7,6},{9,8},{10,9},{11,10},{13,12},{... | collective-permute-start | bytes 3608 | tf_op jit(solution)/shard_map/ppermute | solution.py:32
  366.0 45.5 %copy-start.20 = (f32[3,8,8,128]{3,2,1,0:T(8,128)S(1)}, f32[3,8,8,128]{3,2,1,0:T(8,128)}, u32[]{:S(2)}) copy-start(f32[3,8,8,128]{3,2,1,0:T(8,128)} %copy-done.19) | copy-start | bytes 294916
  (86 other events, 241.2 us)
where the time goes:
time: 419 us; the launch traced here: 412 us
  blocking collectives  165 us (39%)
  starting transfers between devices  91.9 us (22%)
  waiting for transfers between devices  66.1 us (16%)
  other arithmetic  62.9 us (15%)
  local copies, waits for them, and re-layouts  14.8 us (4%)
  between operations  8.8 us (2%)
    unnamed x2, blocking collectives  84.6 us
    psum x2, blocking collectives, paired_sums(): return lax.psum((first, second), ('gx', 'gy', 'gz'))  80.6 us
    ppermute x21, waiting for transfers between devices, extended(): after = lax.ppermute(leading, axis, down)  64.9 us
    ppermute x21, starting transfers between devices, extended(): before = lax.ppermute(last, axis, up)  63.8 us
    another operation x18, other arithmetic, spring_force(): return jnp.stack(parts)  31 us
    ppermute x21, starting transfers between devices, extended(): after = lax.ppermute(leading, axis, down)  28.2 us
    concatenate x27, other arithmetic, extended(): x = jnp.concatenate([before, x, after], axis=dim)  15.2 us
    unnamed x204, local copies, waits for them, and re-layouts  8.91 us
  transfers between devices with their start and end apart: 42, of which 24 were waited for; matrix products, arithmetic and copies ran while one was open for 5% of the time, Pallas kernels for 0%

commit v1 on v0

v1 whole, which is shorter than its diff:
```python
import jax
import jax.numpy as jnp
from jax import lax
from jax.experimental import pallas as pl
from jax.experimental.pallas import tpu as pltpu
from jax.sharding import PartitionSpec as P

AXES = ("gx", "gy", "gz")
SWEEPS = 4
relax = 0.6
highest = lax.Precision.HIGHEST
f32 = jnp.float32
LANES = 128
EDGE = 8
BLOCK = 16

ALONG1, ACROSS1 = 0.75, 0.5
ALONG2, ACROSS2, MIXED2 = 0.3125, 0.25, 0.0625
SAME3, MIXED3 = 7.0 / 36.0, 1.0 / 36.0
TOTAL = 2 * ALONG1 + 4 * ACROSS1 + 8 * ALONG2 + 4 * ACROSS2 + 8 * SAME3


class Exchange:
    def __init__(self, fields, layers, up, down):
        self.fields, self.layers, self.up, self.down = fields, layers, up, down


SPREAD = Exchange(4, 2, -2, 0)
DEEP = Exchange(3, 3, -2, -1)
NEAR = Exchange(3, 2, -1, -1)


class Shape:
    def __init__(self, size_x, size_y, size_z, phases, mesh_sizes):
        self.x, self.y, self.z = size_x, size_y, size_z
        self.pitch = size_y + 4
        self.used = (size_x + 2) * self.pitch
        assert self.used <= LANES and size_z % BLOCK == 0
        self.rows = size_z + 2 * EDGE
        self.tall = self.rows + 2 * EDGE
        self.phases = phases
        self.sizes = mesh_sizes
        self.devices = mesh_sizes[0] * mesh_sizes[1] * mesh_sizes[2]
        self.cells = size_x * size_y
        self.links = [1 if n <= 2 else 2 for n in mesh_sizes]
        self.x_links, self.y_links, self.z_links = self.links

    def lane_grid(self, rows):
        lane = lax.broadcasted_iota(jnp.int32, (rows, LANES), 1)
        column = jnp.zeros_like(lane)
        for j in range(1, self.x + 2):
            column = column + (lane >= j * self.pitch).astype(jnp.int32)
        offset = lane - column * self.pitch
        return lane, column - 1, offset - 2

    def here(self, axis):
        return lax.axis_index(AXES[axis])


def shift(value, amount):
    amount = amount % LANES
    return value if amount == 0 else pltpu.roll(value, amount, 1)


def pick(mask, value):
    return jnp.where(mask, value, 0.0)


def scale(flag, value):
    return value * flag.astype(f32)


def pair(links, even, upward, downward):
    first = jnp.where(even, upward, downward)
    return (first,) if links == 1 else (first, jnp.where(even, downward, upward))


def sides(sh, axis, received):
    index, size = sh.here(axis), sh.sizes[axis]
    even = index % 2 == 0
    first = received[0]
    second = received[1] if len(received) > 1 else jnp.zeros_like(first)
    below = jnp.where(even, second, first)
    above = jnp.where(even, first, second)
    return scale(index > 0, below), scale(index < size - 1, above)


def lane_range(lane, start, count):
    return (lane >= start) & (lane < start + count)


def pack_z(sh, ex, source, out_refs):
    even = sh.here(2) % 2 == 0
    zero = jnp.zeros((8 - ex.layers, LANES), f32)
    for f in range(ex.fields):
        upward = source(f, EDGE + sh.z + ex.up, ex.layers)
        downward = source(f, EDGE + ex.down, ex.layers)
        for ref, message in zip(out_refs, pair(sh.z_links, even, upward, downward)):
            ref[8 * f : 8 * f + ex.layers, :] = message
            ref[8 * f + ex.layers : 8 * f + 8, :] = zero


def merge_z(sh, ex, field_ref, received_refs, scratch, guard):
    below, above = sides(sh, 2, [ref[...] for ref in received_refs])
    for f in range(ex.fields):
        scratch[f, guard : guard + sh.rows, :] = field_ref[f]
        low = guard + EDGE + ex.up
        high = guard + EDGE + sh.z + ex.down
        scratch[f, low : low + ex.layers, :] += below[8 * f : 8 * f + ex.layers]
        scratch[f, high : high + ex.layers, :] += above[8 * f : 8 * f + ex.layers]


def pack_xy(sh, ex, scratch, x_refs, y_refs):
    rows = sh.rows
    lane, _, across = sh.lane_grid(1)
    even_x, even_y = sh.here(0) % 2 == 0, sh.here(1) % 2 == 0
    span = ex.layers * sh.pitch
    x_up = x_down = y_up = y_down = jnp.zeros((rows, LANES), f32)
    for f in range(ex.fields):
        value = scratch[f]
        start = (sh.x + ex.up + 1) * sh.pitch
        x_up = x_up + shift(pick(lane_range(lane, start, span), value), f * span - start)
        start = (ex.down + 1) * sh.pitch
        x_down = x_down + shift(pick(lane_range(lane, start, span), value), f * span - start)
        inside = lane < sh.used
        start = sh.y + ex.up
        y_up = y_up + shift(
            pick(inside & lane_range(across, start, ex.layers), value), f * ex.layers - start - 2
        )
        start = ex.down
        y_down = y_down + shift(
            pick(inside & lane_range(across, start, ex.layers), value), f * ex.layers - start - 2
        )
    for ref, message in zip(x_refs, pair(sh.x_links, even_x, x_up, x_down)):
        ref[...] = message
    for ref, message in zip(y_refs, pair(sh.y_links, even_y, y_up, y_down)):
        ref[...] = message


def merge_xy(sh, ex, scratch, rim, guard, y_refs, x_refs):
    lane, _, across = sh.lane_grid(1)
    inside = lane < sh.used
    low_mask = inside & lane_range(across, ex.up, ex.layers)
    high_mask = inside & lane_range(across, sh.y + ex.down, ex.layers)
    span = ex.layers * sh.pitch
    below_y, above_y = sides(sh, 1, [ref[...] for ref in y_refs])
    per_link = 1 + sh.y_links
    sums = []
    for link in range(sh.x_links):
        straight, diagonal = x_refs[link * per_link], x_refs[link * per_link + 1 : (link + 1) * per_link]
        below, above = sides(sh, 1, [ref[...] for ref in diagonal])
        sums.append(
            straight[...]
            + pick(low_mask, shift(below, -sh.y))
            + pick(high_mask, shift(above, sh.y))
        )
    below_x, above_x = sides(sh, 0, sums)
    first = 1 if ex.up == -2 else 0
    last = ex.layers - 1 if ex.down + ex.layers == 2 else ex.layers
    for f in range(ex.fields):
        addend = pick(low_mask, shift(below_y, ex.up + 2 - ex.layers * f))
        addend = addend + pick(high_mask, shift(above_y, sh.y + ex.down + 2 - ex.layers * f))
        start = (ex.up + first + 1) * sh.pitch
        count = (ex.layers - first) * sh.pitch
        moved = shift(below_x, start - f * span - first * sh.pitch)
        addend = addend + pick(lane_range(lane, start, count), moved)
        start = (sh.x + ex.down + 1) * sh.pitch
        moved = shift(above_x, start - f * span)
        addend = addend + pick(lane_range(lane, start, last * sh.pitch), moved)
        scratch[f, guard : guard + sh.rows, :] += addend
        if rim is not None:
            low = pick(lane_range(lane, 0, sh.pitch), shift(below_x, -f * span))
            start = (sh.x + 1) * sh.pitch
            moved = shift(above_x, start - f * span - last * sh.pitch)
            high = pick(lane_range(lane, start, sh.pitch), moved)
            rim[f, guard : guard + sh.rows, :] = low + high


def clear_guards(sh, refs):
    for ref in refs:
        for f in range(ref.shape[0]):
            ref[f, :EDGE, :] = jnp.zeros((EDGE, LANES), f32)
            ref[f, sh.tall - EDGE :, :] = jnp.zeros((EDGE, LANES), f32)


def z_stage(ref, f, base):
    centre = ref[f, pl.ds(base, BLOCK), :]
    after = ref[f, pl.ds(base + 1, BLOCK), :]
    before = ref[f, pl.ds(base - 1, BLOCK), :]
    return centre, before + after, after - before


def y_stage(value):
    after, before = shift(value, -1), shift(value, 1)
    return before + after, after - before


def yz_parts(ref, base):
    a, a_sum, a_dif = z_stage(ref, 0, base)
    b, b_sum, b_dif = z_stage(ref, 1, base)
    c, c_sum, c_dif = z_stage(ref, 2, base)
    pa, ma = y_stage(a)
    pas, mas = y_stage(a_sum)
    pad, _ = y_stage(a_dif)
    pb, mb = y_stage(b)
    pbs, mbs = y_stage(b_sum)
    _, mbd = y_stage(b_dif)
    pc, _ = y_stage(c)
    pcs, _ = y_stage(c_sum)
    pcd, mcd = y_stage(c_dif)
    own_x = ACROSS1 * (pa + a_sum) + ACROSS2 * pas
    even_x = ALONG1 * a + ALONG2 * (pa + a_sum) + SAME3 * pas
    odd_x = MIXED2 * (mb + c_dif) + MIXED3 * (mbs + pcd)
    own_y = ALONG1 * pb + ACROSS1 * b_sum + ALONG2 * pbs + MIXED2 * mcd
    even_y = ACROSS1 * b + ALONG2 * pb + ACROSS2 * b_sum + SAME3 * pbs + MIXED3 * mcd
    odd_y = MIXED2 * ma + MIXED3 * mas
    own_z = ALONG1 * c_sum + ACROSS1 * pc + ALONG2 * pcs + MIXED2 * mbd
    even_z = ACROSS1 * c + ACROSS2 * pc + ALONG2 * c_sum + SAME3 * pcs + MIXED3 * mbd
    odd_z = MIXED2 * a_dif + MIXED3 * pad
    return (own_x, even_x, odd_x), (own_y, even_y, odd_y), (own_z, even_z, odd_z)


def x_stage(sh, lane, own, plus, minus, rim_plus, rim_minus):
    after, before = shift(plus, -sh.pitch), shift(minus, sh.pitch)
    last = (sh.x + 1) * sh.pitch
    if rim_plus is None:
        return own + pick(lane < last, after) + pick(lane >= sh.pitch, before)
    return own + jnp.where(lane < last, after, rim_plus) + jnp.where(lane >= sh.pitch, before, rim_minus)


def stencil(sh, lane, ref, rim, base):
    parts = yz_parts(ref, base)
    rims = yz_parts(rim, base) if rim is not None else [None] * 3
    out = []
    for (own, even, odd), rim_part in zip(parts, rims):
        if rim_part is None:
            out.append(x_stage(sh, lane, own, even + odd, even - odd, None, None))
        else:
            _, rim_even, rim_odd = rim_part
            out.append(
                x_stage(sh, lane, own, even + odd, even - odd, rim_even + rim_odd, rim_even - rim_odd)
            )
    return out


def spring_parts(ref, base):
    k, k_sum, k_dif = z_stage(ref, 0, base)
    pk, mk = y_stage(k)
    pks, mks = y_stage(k_sum)
    pkd, mkd = y_stage(k_dif)
    zero = jnp.zeros_like(k)
    xx = (ACROSS1 * (pk + k_sum) + ACROSS2 * pks, ALONG1 * k + ALONG2 * (pk + k_sum) + SAME3 * pks, zero)
    yy = (
        ALONG1 * pk + ACROSS1 * k_sum + ALONG2 * pks,
        ACROSS1 * k + ALONG2 * pk + ACROSS2 * k_sum + SAME3 * pks,
        zero,
    )
    zz = (
        ALONG1 * k_sum + ACROSS1 * pk + ALONG2 * pks,
        ACROSS1 * k + ACROSS2 * pk + ALONG2 * k_sum + SAME3 * pks,
        zero,
    )
    xy = (zero, zero, MIXED2 * mk + MIXED3 * mks)
    xz = (zero, zero, MIXED2 * k_dif + MIXED3 * pkd)
    yz = (MIXED2 * mkd, MIXED3 * mkd, zero)
    return xx, yy, zz, xy, xz, yz


def own_block(sh, lane, springs, base):
    main, rim = springs
    k = main[0, pl.ds(base, BLOCK), :]
    out = []
    for index, ((own, even, odd), (_, rim_even, rim_odd)) in enumerate(
        zip(spring_parts(main, base), spring_parts(rim, base))
    ):
        total = x_stage(sh, lane, own, even + odd, even - odd, rim_even + rim_odd, rim_even - rim_odd)
        out.append(total + TOTAL * k if index < 3 else total)
    return out


def apply_block(d, v):
    return (
        d[0] * v[0] + d[3] * v[1] + d[4] * v[2],
        d[3] * v[0] + d[1] * v[1] + d[5] * v[2],
        d[4] * v[0] + d[5] * v[1] + d[2] * v[2],
    )


def image_at(sh, lane, v, kv, rims, k, d, base):
    outer = stencil(sh, lane, v, rims and rims[0], base)
    inner = stencil(sh, lane, kv, rims and rims[1], base)
    own = apply_block(d, [v[m, pl.ds(base, BLOCK), :] for m in range(3)])
    return [own[m] - (k * outer[m] + inner[m]) for m in range(3)]


def blocks(sh, step):
    def body(i, carry):
        step(pl.multiple_of(i * BLOCK, BLOCK))
        return carry

    lax.fori_loop(0, sh.rows // BLOCK, body, 0)


def extended_mask(sh, base):
    lane, _, across = sh.lane_grid(BLOCK)
    z = base - EDGE + lax.broadcasted_iota(jnp.int32, (BLOCK, LANES), 0)
    return (lane < sh.used) & (across >= -1) & (across <= sh.y) & (z >= -1) & (z <= sh.z)


def grid_mask(sh, rows, first):
    lane, along, across = sh.lane_grid(rows)
    z = first - EDGE + lax.broadcasted_iota(jnp.int32, (rows, LANES), 0)
    mask = lane < sh.used
    for axis, place, size in ((0, along, sh.x), (1, across, sh.y), (2, z, sh.z)):
        index = sh.here(axis)
        low = jnp.where(index > 0, -EDGE, 0)
        high = jnp.where(index < sh.sizes[axis] - 1, size + EDGE, size)
        mask = mask & (place >= low) & (place < high)
    return mask


def rim_mask(sh, rows, first):
    lane, _, across = sh.lane_grid(rows)
    z = first - EDGE + lax.broadcasted_iota(jnp.int32, (rows, LANES), 0)
    mask = lane < sh.used
    for axis, place, size in ((1, across, sh.y), (2, z, sh.z)):
        index = sh.here(axis)
        low = jnp.where(index > 0, -EDGE, 0)
        high = jnp.where(index < sh.sizes[axis] - 1, size + EDGE, size)
        mask = mask & (place >= low) & (place < high)
    return mask


def local_solve(sh, residual, k_ref, d_ref, v, kv):
    lane, _, _ = sh.lane_grid(1)
    at = lambda ref, f, base: ref[f, pl.ds(base, BLOCK), :]

    def inverse(base, mask):
        return [jnp.where(mask, relax / jnp.where(mask, at(d_ref, m, base), 1.0), 0.0) for m in range(3)]

    def start(base):
        inv = inverse(base, extended_mask(sh, base))
        k = k_ref[pl.ds(base, BLOCK), :]
        for m in range(3):
            z = residual(m, base) * inv[m]
            v[0][m, pl.ds(base + EDGE, BLOCK), :] = z
            kv[0][m, pl.ds(base + EDGE, BLOCK), :] = k * z

    blocks(sh, start)
    for sweep in range(SWEEPS - 1):
        old, new = sweep % 2, (sweep + 1) % 2

        def step(base, old=old, new=new):
            k = k_ref[pl.ds(base, BLOCK), :]
            d = [at(d_ref, f, base) for f in range(6)]
            inv = inverse(base, extended_mask(sh, base))
            image = image_at(sh, lane, v[old], kv[old], None, k, d, base + EDGE)
            for m in range(3):
                z = v[old][m, pl.ds(base + EDGE, BLOCK), :] + inv[m] * (residual(m, base) - image[m])
                v[new][m, pl.ds(base + EDGE, BLOCK), :] = z
                kv[new][m, pl.ds(base + EDGE, BLOCK), :] = k * z

        blocks(sh, step)
    return (SWEEPS - 1) % 2


def coords(sh):
    lane, along, across = sh.lane_grid(sh.z)
    z = lax.broadcasted_iota(jnp.int32, (sh.z, LANES), 0)
    place = lambda index, size: (2 * index + 1).astype(f32) / size - 1.0
    return place(along, sh.x), place(across, sh.y), place(z, sh.z)


def cross(a, b):
    return (a[1] * b[2] - a[2] * b[1], a[2] * b[0] - a[0] * b[2], a[0] * b[1] - a[1] * b[0])


def fold_rows(value):
    total = value[0:8]
    for i in range(8, value.shape[0], 8):
        total = total + value[i : i + 8]
    return jnp.sum(total, axis=0, keepdims=True)


def lane_sums(rows_ref):
    ones = jnp.ones((8, LANES), f32)
    return lax.dot_general(
        ones, rows_ref[...], (((1,), (1,)), ((), ())), precision=highest, preferred_element_type=f32
    )


def coarse_sums(sh, nodes, field, count, sums, slots_ref):
    moments = tuple(field) + cross(coords(sh), field)
    for node in range(count):
        mask = nodes == float(node)
        for m in range(6):
            sums[node * 6 + m : node * 6 + m + 1, :] = fold_rows(pick(mask, moments[m]))
    line = lane_sums(sums)[0:1]
    slots_ref[...] = jnp.broadcast_to(line, slots_ref.shape)


def coarse_values(sh, nodes, received, inverse_ref, values):
    unknowns, total = inverse_ref.shape
    column = lax.broadcasted_iota(jnp.int32, (1, total), 1)
    owner = column // unknowns
    place = column - owner * unknowns
    spread = (lax.broadcasted_iota(jnp.int32, (LANES, total), 0) == place).astype(f32)
    lines = jnp.dot(received, spread, precision=highest, preferred_element_type=f32)
    mine = lax.broadcasted_iota(jnp.int32, lines.shape, 0) == owner
    vector = jnp.sum(pick(mine, lines), axis=0, keepdims=True)
    product = inverse_ref[...] * vector
    part = product[:, 0:LANES]
    for i in range(LANES, total, LANES):
        part = part + product[:, i : i + LANES]
    values[0:unknowns, :] = jnp.dot(
        part, jnp.ones((LANES, LANES), f32), precision=highest, preferred_element_type=f32
    )
    cells = []
    for m in range(6):
        cell = jnp.zeros((sh.z, LANES), f32)
        for node in range(unknowns // 6):
            cell = jnp.where(nodes == float(node), values[node * 6 + m : node * 6 + m + 1, :], cell)
        cells.append(cell)
    turned = cross(cells[3:], coords(sh))
    return [cells[m] + turned[m] for m in range(3)]


def selection(sh):
    lane, along, across = sh.lane_grid(sh.cells)
    inside = (along >= 0) & (along < sh.x) & (across >= 0) & (across < sh.y)
    row = lax.broadcasted_iota(jnp.int32, (sh.cells, LANES), 0)
    return (inside & (row == along * sh.y + across)).astype(f32)


def to_lanes(value, select):
    return lax.dot_general(
        value, select, (((0,), (0,)), ((), ())), precision=highest, preferred_element_type=f32
    )


def to_cells(value, select):
    return lax.dot_general(
        select, value, (((1,), (1,)), ((), ())), precision=highest, preferred_element_type=f32
    )


def call(kernel, name, outs, ins, scratch=(), smem=()):
    return pl.pallas_call(
        kernel,
        out_shape=[jax.ShapeDtypeStruct(shape, f32) for shape in outs],
        in_specs=[
            pl.BlockSpec(memory_space=pltpu.SMEM if i in smem else pltpu.VMEM) for i in range(len(ins))
        ],
        out_specs=[pl.BlockSpec(memory_space=pltpu.VMEM) for _ in outs],
        scratch_shapes=[pltpu.VMEM(shape, f32) for shape in scratch],
        compiler_params=pltpu.CompilerParams(vmem_limit_bytes=48 * 1024 * 1024),
        name=name,
    )(*ins)


def permutation(sizes, moves):
    def partner(axis, link, index):
        size = sizes[axis]
        other = index ^ 1 if link == 0 else index + (1 if index % 2 else -1)
        if 0 <= other < size:
            return other
        return size - 1 - index if axis == 2 and size % 2 == 0 else index

    pairs = []
    for x in range(sizes[0]):
        for y in range(sizes[1]):
            for z in range(sizes[2]):
                place = [x, y, z]
                goal = [partner(a, moves[a], place[a]) if a in moves else place[a] for a in range(3)]
                if goal == place and 0 not in moves and sizes[0] % 2 == 0:
                    goal[0] = partner(0, 0, x)
                flat = [(p[0] * sizes[1] + p[1]) * sizes[2] + p[2] for p in (place, goal)]
                pairs.append(tuple(flat))
    return pairs


def send(sh, value, moves):
    return lax.ppermute(value, AXES, permutation(sh.sizes, moves))


def send_z(sh, messages):
    return [send(sh, message, {2: link}) for link, message in enumerate(messages)]


def send_xy(sh, x_messages, y_messages):
    from_y = [send(sh, message, {1: link}) for link, message in enumerate(y_messages)]
    from_x = []
    for link, message in enumerate(x_messages):
        from_x.append(send(sh, message, {0: link}))
        from_x.extend(send(sh, message, {0: link, 1: other}) for other in range(sh.y_links))
    return from_y, from_x


def to_all(slots):
    return lax.all_to_all(slots, AXES, 0, 0, tiled=True)


def exchange(sh, ex, name, field, z_messages):
    from_z = send_z(sh, z_messages)

    def packer(*refs):
        field_ref, z_refs = refs[0], refs[1 : 1 + sh.z_links]
        x_refs = refs[1 + sh.z_links : 1 + sh.z_links + sh.x_links]
        y_refs = refs[1 + sh.z_links + sh.x_links : -1]
        scratch = refs[-1]
        merge_z(sh, ex, field_ref, z_refs, scratch, 0)
        pack_xy(sh, ex, scratch, x_refs, y_refs)

    plane = (sh.rows, LANES)
    messages = call(
        packer,
        name,
        [plane] * (sh.x_links + sh.y_links),
        [field] + from_z,
        [(ex.fields,) + plane],
    )
    from_y, from_x = send_xy(sh, messages[: sh.x_links], messages[sh.x_links :])
    return from_z, from_y, from_x


class Taker:
    def __init__(self, refs):
        self.refs, self.at = refs, 0

    def __call__(self, count):
        self.at += count
        return self.refs[self.at - count : self.at]

    def one(self):
        return self(1)[0]


def merge_all(sh, ex, take, scratch, rim, guard):
    field = take.one()
    from_z, from_y = take(sh.z_links), take(sh.y_links)
    from_x = take(sh.x_links * (1 + sh.y_links))
    merge_z(sh, ex, field, from_z, scratch, guard)
    merge_xy(sh, ex, scratch, rim, guard, from_y, from_x)


def body(right_side, phase_labels, phase_moduli, coarse_nodes, coarse_inverse):
    sizes = tuple(lax.axis_size(axis) for axis in AXES)
    _, size_x, size_y, size_z = right_side.shape
    sh = Shape(size_x, size_y, size_z, phase_moduli.shape[0], sizes)
    unknowns = coarse_inverse.shape[0]
    node_count = unknowns // 6
    sum_rows = -(-unknowns // 8) * 8
    own = slice(EDGE, EDGE + sh.z)
    plane = (sh.rows, LANES)
    fields = (3,) + plane
    tall = (3, sh.tall, LANES)
    slots = (sh.devices, LANES)
    z_shape = lambda ex: [(8 * ex.fields, LANES)] * sh.z_links
    natural = right_side.reshape(3, sh.cells, sh.z)
    nodes_natural = coarse_nodes.reshape(sh.cells, sh.z)
    label_x, label_y, label_z = phase_labels.shape

    def begin(natural_ref, labels_ref, moduli_ref, nodes_ref, field_ref, lanes_ref, slots_ref, *rest):
        z_refs, (sums, stiff) = rest[: sh.z_links], rest[sh.z_links :]
        select = selection(sh)
        field_ref[...] = jnp.zeros(field_ref.shape, f32)
        residual = []
        for m in range(3):
            residual.append(to_lanes(natural_ref[m], select))
            field_ref[m, own, :] = residual[m]
        for i in range(label_x):
            labels = labels_ref[i]
            moduli = jnp.zeros(labels.shape, f32)
            for phase in range(sh.phases):
                moduli = jnp.where(labels == phase, moduli_ref[phase], moduli)
            stiff[i * label_y : (i + 1) * label_y, :] = moduli
        row = lax.broadcasted_iota(jnp.int32, (sh.z, label_z), 0)
        column = lax.broadcasted_iota(jnp.int32, (sh.z, label_z), 1)
        wide = ((row >= 2 * column) & (row < 2 * column + 2)).astype(f32)
        by_z = lax.dot_general(
            wide, stiff[...], (((1,), (1,)), ((), ())), precision=highest, preferred_element_type=f32
        )
        lane, along, across = sh.lane_grid(label_x * label_y)
        inside = (along >= 0) & (along < sh.x) & (across >= 0) & (across < sh.y)
        block = lax.broadcasted_iota(jnp.int32, along.shape, 0)
        to_block = (inside & (block == (along >> 1) * label_y + (across >> 1))).astype(f32)
        field_ref[3, own, :] = jnp.dot(by_z, to_block, precision=highest, preferred_element_type=f32)
        nodes = to_lanes(nodes_ref[...].astype(f32) + 1.0, select) - 1.0
        lanes_ref[...] = nodes
        sums[...] = jnp.zeros(sums.shape, f32)
        coarse_sums(sh, nodes, residual, node_count, sums, slots_ref)
        pack_z(sh, SPREAD, lambda f, start, count: field_ref[f, start : start + count, :], z_refs)

    start_field, nodes, sums, *z_messages = call(
        begin,
        "begin",
        [(4,) + plane, (sh.z, LANES), slots] + z_shape(SPREAD),
        [natural, phase_labels, phase_moduli, nodes_natural],
        [(LANES, LANES), (label_x * label_y, label_z)],
        smem=(2,),
    )
    from_z, from_y, from_x = exchange(sh, SPREAD, "spread", start_field, z_messages)
    coarse = to_all(sums)

    def finish_solve(index, v, nodes_ref, coarse_ref, inverse_ref, values, solution_ref, z_refs, ex):
        for m in range(3):
            solution_ref[m] = v[index][m, EDGE : EDGE + sh.rows, :]
        added = coarse_values(sh, nodes_ref[...], coarse_ref[...], inverse_ref, values)
        valid = nodes_ref[...] >= 0.0
        for m in range(3):
            solution_ref[m, own, :] += pick(valid, added[m])
        pack_z(sh, ex, lambda f, start, count: solution_ref[f, start : start + count, :], z_refs)

    def first_solve(*refs):
        take = Taker(refs)
        merging = take(1 + sh.z_links + sh.y_links + sh.x_links * (1 + sh.y_links))
        nodes_ref, coarse_ref, inverse_ref = take(3)
        solution_ref, springs_ref = take(2)
        z_refs = take(sh.z_links)
        all_fields, rims, stiff, stiff_rim, v0, v1, kv0, kv1, values = take(9)
        clear_guards(sh, (stiff, stiff_rim, v0, v1, kv0, kv1))
        merge_all(sh, SPREAD, Taker(merging), all_fields, rims, 0)
        stiff[0, EDGE : EDGE + sh.rows, :] = all_fields[3]
        stiff_rim[0, EDGE : EDGE + sh.rows, :] = rims[3]
        springs_ref[6] = all_fields[3]
        springs_ref[7] = rims[3]
        lane, _, _ = sh.lane_grid(1)

        def springs(base):
            for f, entry in enumerate(own_block(sh, lane, (stiff, stiff_rim), base + EDGE)):
                springs_ref[f, pl.ds(base, BLOCK), :] = entry

        blocks(sh, springs)
        residual = lambda m, base: all_fields[m, pl.ds(base, BLOCK), :]
        index = local_solve(sh, residual, springs_ref.at[6], springs_ref, (v0, v1), (kv0, kv1))
        finish_solve(index, (v0, v1), nodes_ref, coarse_ref, inverse_ref, values, solution_ref, z_refs, DEEP)

    solved, springs, *z_messages = call(
        first_solve,
        "first_solve",
        [fields, (8,) + plane] + z_shape(DEEP),
        [start_field, *from_z, *from_y, *from_x, nodes, coarse, coarse_inverse],
        [(4,) + plane, (4,) + plane, (1, sh.tall, LANES), (1, sh.tall, LANES)] + [tall] * 4 + [(LANES, LANES)],
    )
    from_z, from_y, from_x = exchange(sh, DEEP, "deep", solved, z_messages)

    def first_image(*refs):
        take = Taker(refs)
        merging = take(1 + sh.z_links + sh.y_links + sh.x_links * (1 + sh.y_links))
        nodes_ref, springs_ref = take(2)
        search_ref, image_ref, slots_ref = take(3)
        v, rim, kv, k_rim, sums = take(5)
        clear_guards(sh, (v, rim, kv, k_rim))
        merge_all(sh, DEEP, Taker(merging), v, rim, EDGE)
        lane, _, _ = sh.lane_grid(1)

        def mask(base):
            rows, tall_rows = pl.ds(base, BLOCK), pl.ds(base + EDGE, BLOCK)
            in_grid, in_rim = grid_mask(sh, BLOCK, base), rim_mask(sh, BLOCK, base)
            k, k_edge = springs_ref[6, rows, :], springs_ref[7, rows, :]
            for m in range(3):
                value = pick(in_grid, v[m, tall_rows, :])
                v[m, tall_rows, :] = value
                search_ref[m, rows, :] = value
                kv[m, tall_rows, :] = k * value
                value = pick(in_rim, rim[m, tall_rows, :])
                rim[m, tall_rows, :] = value
                k_rim[m, tall_rows, :] = k_edge * value

        blocks(sh, mask)

        def step(base):
            rows = pl.ds(base, BLOCK)
            d = [springs_ref[f, rows, :] for f in range(6)]
            image = image_at(sh, lane, v, kv, (rim, k_rim), springs_ref[6, rows, :], d, base + EDGE)
            keep = grid_mask(sh, BLOCK, base) & extended_mask(sh, base)
            for m in range(3):
                image_ref[m, rows, :] = pick(keep, image[m])

        blocks(sh, step)
        sums[...] = jnp.zeros(sums.shape, f32)
        coarse_sums(sh, nodes_ref[...], [image_ref[m, own, :] for m in range(3)], node_count, sums, slots_ref)

    search, image, sums = call(
        first_image,
        "first_image",
        [fields, fields, slots],
        [solved, *from_z, *from_y, *from_x, nodes, springs],
        [tall] * 4 + [(LANES, LANES)],
    )
    coarse = to_all(sums)

    def second_solve(*refs):
        take = Taker(refs)
        image_ref, springs_ref, nodes_ref, coarse_ref, inverse_ref = take(5)
        solution_ref = take.one()
        z_refs = take(sh.z_links)
        v0, v1, kv0, kv1, values = take(5)
        clear_guards(sh, (v0, v1, kv0, kv1))
        residual = lambda m, base: image_ref[m, pl.ds(base, BLOCK), :]
        index = local_solve(sh, residual, springs_ref.at[6], springs_ref, (v0, v1), (kv0, kv1))
        finish_solve(index, (v0, v1), nodes_ref, coarse_ref, inverse_ref, values, solution_ref, z_refs, NEAR)

    solved, *z_messages = call(
        second_solve,
        "second_solve",
        [fields] + z_shape(NEAR),
        [image, springs, nodes, coarse, coarse_inverse],
        [tall] * 4 + [(LANES, LANES)],
    )
    from_z, from_y, from_x = exchange(sh, NEAR, "near", solved, z_messages)

    def second_image(*refs):
        take = Taker(refs)
        merging = take(1 + sh.z_links + sh.y_links + sh.x_links * (1 + sh.y_links))
        nodes_ref, springs_ref, start_ref, search_ref, first_ref = take(5)
        second_ref, image_ref, slots_ref = take(3)
        v, kv, sums = take(3)
        clear_guards(sh, (v, kv))
        merge_all(sh, NEAR, Taker(merging), v, None, EDGE)
        lane, _, _ = sh.lane_grid(1)

        def mask(base):
            rows, tall_rows = pl.ds(base, BLOCK), pl.ds(base + EDGE, BLOCK)
            in_grid = grid_mask(sh, BLOCK, base)
            k = springs_ref[6, rows, :]
            for m in range(3):
                value = pick(in_grid, v[m, tall_rows, :])
                v[m, tall_rows, :] = value
                kv[m, tall_rows, :] = k * value

        blocks(sh, mask)

        def step(base):
            rows = pl.ds(base, BLOCK)
            d = [springs_ref[f, rows, :] for f in range(6)]
            image = image_at(sh, lane, v, kv, None, springs_ref[6, rows, :], d, base + EDGE)
            for m in range(3):
                image_ref[m, rows, :] = image[m]
                second_ref[m, rows, :] = v[m, pl.ds(base + EDGE, BLOCK), :]

        blocks(sh, step)
        valid = nodes_ref[...] >= 0.0
        names = ("r", "z", "w", "q", "v")
        sources = (start_ref, search_ref, first_ref, second_ref, image_ref)
        get = {name: [source[m, own, :] for m in range(3)] for name, source in zip(names, sources)}
        sums[...] = jnp.zeros(sums.shape, f32)
        for i, (a, b) in enumerate(("rz", "zw", "rq", "wq", "zv", "qv")):
            product = sum(get[a][m] * get[b][m] for m in range(3))
            sums[i : i + 1, :] = fold_rows(pick(valid, product))
        slots_ref[...] = jnp.broadcast_to(lane_sums(sums)[0:1], slots_ref.shape)

    second, second_image_field, sums = call(
        second_image,
        "second_image",
        [fields, fields, slots],
        [solved, *from_z, *from_y, *from_x, nodes, springs, start_field, search, image],
        [tall] * 2 + [(LANES, LANES)],
    )
    totals = to_all(sums)

    def finish(totals_ref, natural_ref, search_ref, first_ref, second_ref, image_ref, field_ref, residual_ref):
        total = jnp.sum(totals_ref[...], axis=0, keepdims=True)
        rz, zw, rq, wq, zv, qv = [total[:, i : i + 1] for i in range(6)]
        step0 = rz / zw
        rho = rz - step0 * zw - step0 * rq + step0 * step0 * wq
        grow = 1.0 + rho / rz
        curvature = grow * grow * zw - grow * step0 * (zv + wq) + step0 * step0 * qv
        step1 = rho / curvature
        first = step0 + step1 * grow
        second = step0 * step1
        select = selection(sh)
        for m in range(3):
            update = first * search_ref[m, own, :] - second * second_ref[m, own, :]
            field_ref[m] = to_cells(update, select)
            update = first * first_ref[m, own, :] - second * image_ref[m, own, :]
            residual_ref[m] = natural_ref[m] - to_cells(update, select)

    solution_field, residual = call(
        finish,
        "finish",
        [natural.shape, natural.shape],
        [totals, natural, search, image, second, second_image_field],
    )
    return solution_field.reshape(right_side.shape), residual.reshape(right_side.shape)


def solution(mesh):
    in_specs = (
        P(None, "gx", "gy", "gz"),
        P("gx", "gy", "gz"),
        P(),
        P("gx", "gy", "gz"),
        P(("gx", "gy", "gz"), None),
    )
    out_specs = (P(None, "gx", "gy", "gz"), P(None, "gx", "gy", "gz"))
    return jax.shard_map(body, mesh=mesh, in_specs=in_specs, out_specs=out_specs, check_vma=False)
```

time: 419 us -> 99.3 us (0.24); the launches traced: 412 us -> 98.9 us
  blocking collectives: 165 us -> 30.1 us
  starting transfers between devices: 91.9 us -> 23.1 us
  other arithmetic: 62.9 us -> 0 us
  waiting for transfers between devices: 66.1 us -> 14.6 us
  Pallas kernels: 0 us -> 27.4 us
  local copies, waits for them, and re-layouts: 14.8 us -> 3 us
  between operations: 8.8 us -> 0.73 us
    unnamed x2 -> x0, blocking collectives: 84.6 us -> none
    psum x2 -> x0, blocking collectives: 80.6 us -> none  [paired_sums(): return lax.psum((first, second), ('gx', 'gy', 'gz'))]
    ppermute x42 -> x21, starting transfers between devices: 91.9 us -> 23.1 us  [send(): return lax.ppermute(value, AXES, permutation(sh.sizes, moves))]
    ppermute x42 -> x21, waiting for transfers between devices: 66.1 us -> 14.6 us  [send(): return lax.ppermute(value, AXES, permutation(sh.sizes, moves))]
    another operation x21 -> x0, other arithmetic: 32.8 us -> none  [the longest x18 31 us: spring_force(): return jnp.stack(parts)]
    all_to_all x0 -> x3, blocking collectives: none -> 30.1 us  [to_all(): return lax.all_to_all(slots, AXES, 0, 0, tiled=True)]
    pallas_call x0 -> x9, Pallas kernels: none -> 27.4 us  [call(): pl.pallas_call(kernel, out_shape=[jax.ShapeDtypeStruct(shape, f32) for sh...]
    concatenate x31 -> x0, other arithmetic: 15.6 us -> none  [the longest x27 15.2 us: extended(): x = jnp.concatenate([before, x, after], axis=dim)]
  transfers between devices with their start and end apart: 42 -> 21, of which waited for: 24 -> 11; matrix products, arithmetic and copies ran while one was open for 5% -> 0% of each run, Pallas kernels for 0% -> 0%
where the time goes in v1:
time: 99.3 us; the launch traced here: 98.9 us
  blocking collectives  30.1 us (30%)
  Pallas kernels  27.4 us (28%)
  starting transfers between devices  23.1 us (23%)
  waiting for transfers between devices  14.6 us (15%)
  local copies, waits for them, and re-layouts  3 us (3%)
    all_to_all x3, blocking collectives, to_all(): return lax.all_to_all(slots, AXES, 0, 0, tiled=True)  30.1 us
    pallas_call x9, Pallas kernels, call(): pl.pallas_call(kernel, out_shape=[jax.ShapeDtypeStruct(shape, f32) for sh...  27.4 us
    ppermute x21, starting transfers between devices, send(): return lax.ppermute(value, AXES, permutation(sh.sizes, moves))  23.1 us
    ppermute x21, waiting for transfers between devices, send(): return lax.ppermute(value, AXES, permutation(sh.sizes, moves))  14.6 us
    unnamed x10, local copies, waits for them, and re-layouts  3 us
  transfers between devices with their start and end apart: 21, of which 11 were waited for; matrix products, arithmetic and copies ran while one was open for 0% of the time, Pallas kernels for 0%

profile of v1, /device:TPU:0, one launch (start us, length us, event | category | flops | bytes accessed | tf_op | source)
XLA Modules:
  0.0 98.9 jit_solution(14590197053354242481)
XLA Ops:
  0.6 0.6 copy-done.4
  1.3 0.9 copy-done.1
  2.2 0.8 copy-done.2
  2.9 0.7 copy-done.3
  3.6 1.4 %begin.1 = (f32[4,144,128]{2,1,0:T(8,128)S(1)}, f32[128,128]{1,0:T(8,128)S(1)}, f32[32,128]{1,0:T(8,128)S(1)}, f32[32,128]{1,0:T(8,128)S(1)}, f32[32,128]{1,0:T(8,128)S(1)}) custom-call(f32[3,64,128]{2,1,0:T(8,128)S(1)} %bitcast.16, s32[4,4,64]{2,1,0:T(4,128)S(1)} %copy-done.3, f32[8]{0:T(128)S(1)} %copy-done.4, s32[64,128]{1,0:T(8,128)S(1)} %bitcast.21), custom_call_target="tpu_custom_call" | custom-call | tf_op jit(solution)/shard_map/begin/pallas_call | solution.py:448
  5.1 0.5 collective-permute-start
  5.6 2.6 %collective-permute-start.1 = (f32[32,128]{1,0:T(8,128)S(1)}, f32[32,128]{1,0:T(8,128)S(1)}, u32[]{:S(2)}, u32[]{:S(2)}) collective-permute-start(f32[32,128]{1,0:T(8,128)S(1)} %get-tuple-element.33), channel_id=1, source_target_pairs={{0,3},{1,2},{2,1},{3,0},{4,7},{5,6},{6,5},{7,4},{8,11},{9,10},{10,... | collective-permute-start | bytes 49160 | tf_op jit(solution)/shard_map/ppermute | solution.py:483
  8.2 1.4 %collective-permute-done.1.refs_2_ = f32[32,128]{1,0:T(8,128)S(1)} collective-permute-done((f32[32,128]{1,0:T(8,128)S(1)}, f32[32,128]{1,0:T(8,128)S(1)}, u32[]{:S(2)}, u32[]{:S(2)}) %collective-permute-start.1) | collective-permute-done | bytes 16416 | tf_op jit(solution)/shard_map/ppermute | solution.py:483
  9.6 0.4 spread.1
  10.0 1.8 %collective-permute-start.2 = (f32[144,128]{1,0:T(8,128)S(1)}, f32[144,128]{1,0:T(8,128)S(1)}, u32[]{:S(2)}, u32[]{:S(2)}) collective-permute-start(f32[144,128]{1,0:T(8,128)S(1)} %get-tuple-element.34), channel_id=1, source_target_pairs={{0,4},{1,5},{2,6},{3,7},{4,0},{5,1},{6,2},{7,3},{8,12},{9,13},{10,... | collective-permute-start | bytes 221192 | tf_op jit(solution)/shard_map/ppermute | solution.py:483
  11.7 1.5 %collective-permute-start.3 = (f32[144,128]{1,0:T(8,128)S(1)}, f32[144,128]{1,0:T(8,128)S(1)}, u32[]{:S(2)}, u32[]{:S(2)}) collective-permute-start(f32[144,128]{1,0:T(8,128)S(1)} %get-tuple-element.35), channel_id=1, source_target_pairs={{0,16},{1,17},{2,18},{3,19},{4,8},{5,9},{6,10},{7,11},{8,4},{9,5},... | collective-permute-start | bytes 221192 | tf_op jit(solution)/shard_map/ppermute | solution.py:483
  13.3 0.5 collective-permute-start.6
  13.8 2.1 %collective-permute-start.5 = (f32[144,128]{1,0:T(8,128)S(1)}, f32[144,128]{1,0:T(8,128)S(1)}, u32[]{:S(2)}, u32[]{:S(2)}) collective-permute-start(f32[144,128]{1,0:T(8,128)S(1)} %get-tuple-element.36), channel_id=1, source_target_pairs={{0,20},{1,21},{2,22},{3,23},{4,16},{5,17},{6,18},{7,19},{8,28},{9,... | collective-permute-start | bytes 221192 | tf_op jit(solution)/shard_map/ppermute | solution.py:483
  15.9 1.5 %collective-permute-start.4 = (f32[144,128]{1,0:T(8,128)S(1)}, f32[144,128]{1,0:T(8,128)S(1)}, u32[]{:S(2)}, u32[]{:S(2)}) collective-permute-start(f32[144,128]{1,0:T(8,128)S(1)} %get-tuple-element.36), channel_id=1, source_target_pairs={{0,16},{1,17},{2,18},{3,19},{4,20},{5,21},{6,22},{7,23},{8,24},{9,... | collective-permute-start | bytes 221192 | tf_op jit(solution)/shard_map/ppermute | solution.py:483
  17.3 11.2 %all_to_all.33 = f32[32,1,128]{2,1,0:T(1,128)S(1)} all-to-all(f32[32,1,128]{2,1,0:T(1,128)S(1)} %bitcast.22), channel_id=1, replica_groups=mesh['gx'=2,'gy'=4,'gz'=4] {'gx','gy','gz'}, dimensions={0} | all-to-all | bytes 32768 | tf_op jit(solution)/shard_map/all_to_all | solution.py:500
  28.5 9.3 %first_solve.1 = (f32[3,144,128]{2,1,0:T(8,128)S(1)}, f32[8,144,128]{2,1,0:T(8,128)S(1)}, f32[24,128]{1,0:T(8,128)S(1)}, f32[24,128]{1,0:T(8,128)S(1)}) custom-call(f32[4,144,128]{2,1,0:T(8,128)S(1)} %get-tuple-element.31.refs_0_.refs_10_, f32[32,128]{1,0:T(8,128)S(1)} %collective-permute-done.refs_1_, f32[32,128]{1,0:T(8,128)S(1)} %collective-permute-done.1.refs_2_, ...), custom_call_target="tpu_custom_call" | custom-call | tf_op jit(solution)/shard_map/first_solve/pallas_call | solution.py:448
  37.8 0.1 collective-permute-start.7
  37.9 0.7 collective-permute-start.8
  38.6 0.5 collective-permute-done.7.refs_1_
  39.1 2.0 %collective-permute-done.8.refs_2_ = f32[24,128]{1,0:T(8,128)S(1)} collective-permute-done((f32[24,128]{1,0:T(8,128)S(1)}, f32[24,128]{1,0:T(8,128)S(1)}, u32[]{:S(2)}, u32[]{:S(2)}) %collective-permute-start.8) | collective-permute-done | bytes 12320 | tf_op jit(solution)/shard_map/ppermute | solution.py:483
  41.1 0.3 deep.1
  41.4 0.6 collective-permute-start.9
  42.0 0.6 collective-permute-start.10
  42.6 1.4 %collective-permute-start.13 = (f32[144,128]{1,0:T(8,128)S(1)}, f32[144,128]{1,0:T(8,128)S(1)}, u32[]{:S(2)}, u32[]{:S(2)}) collective-permute-start(f32[144,128]{1,0:T(8,128)S(1)} %get-tuple-element.44), channel_id=1, source_target_pairs={{0,16},{1,17},{2,18},{3,19},{4,24},{5,25},{6,26},{7,27},{8,20},{9,... | collective-permute-start | bytes 221192 | tf_op jit(solution)/shard_map/ppermute | solution.py:483
  44.0 2.4 %collective-permute-start.12 = (f32[144,128]{1,0:T(8,128)S(1)}, f32[144,128]{1,0:T(8,128)S(1)}, u32[]{:S(2)}, u32[]{:S(2)}) collective-permute-start(f32[144,128]{1,0:T(8,128)S(1)} %get-tuple-element.44), channel_id=1, source_target_pairs={{0,20},{1,21},{2,22},{3,23},{4,16},{5,17},{6,18},{7,19},{8,28},{9,... | collective-permute-start | bytes 221192 | tf_op jit(solution)/shard_map/ppermute | solution.py:483
  46.4 0.6 collective-permute-start.11
  47.0 0.1 collective-permute-done.10.refs_4_
  47.1 2.7 %collective-permute-done.13.refs_7_ = f32[144,128]{1,0:T(8,128)S(1)} collective-permute-done((f32[144,128]{1,0:T(8,128)S(1)}, f32[144,128]{1,0:T(8,128)S(1)}, u32[]{:S(2)}, u32[]{:S(2)}) %collective-permute-start.13) | collective-permute-done | bytes 73760 | tf_op jit(solution)/shard_map/ppermute | solution.py:483
  49.8 1.3 %collective-permute-done.11.refs_5_ = f32[144,128]{1,0:T(8,128)S(1)} collective-permute-done((f32[144,128]{1,0:T(8,128)S(1)}, f32[144,128]{1,0:T(8,128)S(1)}, u32[]{:S(2)}, u32[]{:S(2)}) %collective-permute-start.11) | collective-permute-done | bytes 73760 | tf_op jit(solution)/shard_map/ppermute | solution.py:483
  51.0 3.8 %first_image.1 = (f32[3,144,128]{2,1,0:T(8,128)S(1)}, f32[3,144,128]{2,1,0:T(8,128)S(1)}, f32[32,128]{1,0:T(8,128)S(1)}) custom-call(f32[3,144,128]{2,1,0:T(8,128)S(1)} %get-tuple-element.39.refs_0_, f32[24,128]{1,0:T(8,128)S(1)} %collective-permute-done.7.refs_1_, f32[24,128]{1,0:T(8,128)S(1)} %collective-permute-done.8.refs_2_, ...), custom_call_target="tpu_custom_call" | custom-call | tf_op jit(solution)/shard_map/first_image/pallas_call | solution.py:448
  54.9 9.5 %all_to_all.34 = f32[32,1,128]{2,1,0:T(1,128)S(1)} all-to-all(f32[32,1,128]{2,1,0:T(1,128)S(1)} %bitcast.24), channel_id=1, replica_groups=mesh['gx'=2,'gy'=4,'gz'=4] {'gx','gy','gz'}, dimensions={0} | all-to-all | bytes 32768 | tf_op jit(solution)/shard_map/all_to_all | solution.py:500
  64.4 7.4 %second_solve.1 = (f32[3,144,128]{2,1,0:T(8,128)S(1)}, f32[24,128]{1,0:T(8,128)S(1)}, f32[24,128]{1,0:T(8,128)S(1)}) custom-call(f32[3,144,128]{2,1,0:T(8,128)S(1)} %get-tuple-element.46.refs_0_.refs_12_.first_ref, f32[8,144,128]{2,1,0:T(8,128)S(1)} %get-tuple-element.45.refs_9_.refs_1_, f32[128,128]{1,0:T(8,128)S(1)} %get-tuple-element.37.refs_8_.refs_2_, ...), custom_call_target="tpu_custom_call" | custom-call | tf_op jit(solution)/shard_map/second_solve/pallas_call | solution.py:448
  71.7 0.1 collective-permute-start.14
  71.8 0.7 collective-permute-start.15
  72.5 0.5 collective-permute-done.14.refs_1_
  73.0 2.0 %collective-permute-done.15.refs_2_ = f32[24,128]{1,0:T(8,128)S(1)} collective-permute-done((f32[24,128]{1,0:T(8,128)S(1)}, f32[24,128]{1,0:T(8,128)S(1)}, u32[]{:S(2)}, u32[]{:S(2)}) %collective-permute-start.15) | collective-permute-done | bytes 12320 | tf_op jit(solution)/shard_map/ppermute | solution.py:483
  75.0 0.3 near.1
  75.3 0.6 collective-permute-start.16
  75.9 0.6 collective-permute-start.17
  76.4 1.4 %collective-permute-start.20 = (f32[144,128]{1,0:T(8,128)S(1)}, f32[144,128]{1,0:T(8,128)S(1)}, u32[]{:S(2)}, u32[]{:S(2)}) collective-permute-start(f32[144,128]{1,0:T(8,128)S(1)} %get-tuple-element.53), channel_id=1, source_target_pairs={{0,16},{1,17},{2,18},{3,19},{4,24},{5,25},{6,26},{7,27},{8,20},{9,... | collective-permute-start | bytes 221192 | tf_op jit(solution)/shard_map/ppermute | solution.py:483
  77.9 2.4 %collective-permute-start.19 = (f32[144,128]{1,0:T(8,128)S(1)}, f32[144,128]{1,0:T(8,128)S(1)}, u32[]{:S(2)}, u32[]{:S(2)}) collective-permute-start(f32[144,128]{1,0:T(8,128)S(1)} %get-tuple-element.53), channel_id=1, source_target_pairs={{0,20},{1,21},{2,22},{3,23},{4,16},{5,17},{6,18},{7,19},{8,28},{9,... | collective-permute-start | bytes 221192 | tf_op jit(solution)/shard_map/ppermute | solution.py:483
  80.3 0.6 collective-permute-start.18
  80.9 0.1 collective-permute-done.17.refs_4_
  81.0 2.7 %collective-permute-done.20.refs_7_ = f32[144,128]{1,0:T(8,128)S(1)} collective-permute-done((f32[144,128]{1,0:T(8,128)S(1)}, f32[144,128]{1,0:T(8,128)S(1)}, u32[]{:S(2)}, u32[]{:S(2)}) %collective-permute-start.20) | collective-permute-done | bytes 73760 | tf_op jit(solution)/shard_map/ppermute | solution.py:483
  83.6 1.3 %collective-permute-done.18.refs_5_ = f32[144,128]{1,0:T(8,128)S(1)} collective-permute-done((f32[144,128]{1,0:T(8,128)S(1)}, f32[144,128]{1,0:T(8,128)S(1)}, u32[]{:S(2)}, u32[]{:S(2)}) %collective-permute-start.18) | collective-permute-done | bytes 73760 | tf_op jit(solution)/shard_map/ppermute | solution.py:483
  84.9 2.8 %second_image.1 = (f32[3,144,128]{2,1,0:T(8,128)S(1)}, f32[3,144,128]{2,1,0:T(8,128)S(1)}, f32[32,128]{1,0:T(8,128)S(1)}) custom-call(f32[3,144,128]{2,1,0:T(8,128)S(1)} %get-tuple-element.48.refs_0_, f32[24,128]{1,0:T(8,128)S(1)} %collective-permute-done.14.refs_1_, f32[24,128]{1,0:T(8,128)S(1)} %collective-permute-done.15.refs_2_, ...), custom_call_target="tpu_custom_call" | custom-call | tf_op jit(solution)/shard_map/second_image/pallas_call | solution.py:448
  87.7 9.5 %all_to_all.35 = f32[32,1,128]{2,1,0:T(1,128)S(1)} all-to-all(f32[32,1,128]{2,1,0:T(1,128)S(1)} %bitcast.23), channel_id=1, replica_groups=mesh['gx'=2,'gy'=4,'gz'=4] {'gx','gy','gz'}, dimensions={0} | all-to-all | bytes 32768 | tf_op jit(solution)/shard_map/all_to_all | solution.py:500
  97.2 1.7 %finish.1 = (f32[3,64,128]{2,1,0:T(8,128)}, f32[3,64,128]{2,1,0:T(8,128)}) custom-call(f32[32,128]{1,0:T(8,128)S(1)} %bitcast.19, f32[3,64,128]{2,1,0:T(8,128)S(1)} %bitcast.17, f32[3,144,128]{2,1,0:T(8,128)S(1)} %get-tuple-element.54.refs_11_.search_ref, f32[3,144,128]{2,1,0:T(8,128)S(1)} %get-tuple-element.46.refs_0_.refs_12_.first_ref, ...), custom_call_target="tpu_custom_call" | custom-call | tf_op jit(solution)/shard_map/finish/pallas_call | solution.py:448
  (16 shorter events, 0.0 us)
Async XLA Ops:
  0.6 0.7 copy-start.4
  1.3 0.9 copy-start.1
  2.2 0.8 copy-start.2
  2.9 0.7 copy-start.3
  5.1 3.1 %collective-permute-start = (f32[32,128]{1,0:T(8,128)S(1)}, f32[32,128]{1,0:T(8,128)S(1)}, u32[]{:S(2)}, u32[]{:S(2)}) collective-permute-start(f32[32,128]{1,0:T(8,128)S(1)} %get-tuple-element.32), channel_id=1, source_target_pairs={{0,1},{1,0},{2,3},{3,2},{4,5},{5,4},{6,7},{7,6},{8,9},{9,8},{10,11... | collective-permute-start | bytes 49160 | tf_op jit(solution)/shard_map/ppermute | solution.py:483
  5.6 4.0 %collective-permute-start.1 = (f32[32,128]{1,0:T(8,128)S(1)}, f32[32,128]{1,0:T(8,128)S(1)}, u32[]{:S(2)}, u32[]{:S(2)}) collective-permute-start(f32[32,128]{1,0:T(8,128)S(1)} %get-tuple-element.33), channel_id=1, source_target_pairs={{0,3},{1,2},{2,1},{3,0},{4,7},{5,6},{6,5},{7,4},{8,11},{9,10},{10,... | collective-permute-start | bytes 49160 | tf_op jit(solution)/shard_map/ppermute | solution.py:483
  9.6 18.9 %copy-start = (f32[36,1152]{1,0:T(8,128)S(1)}, f32[36,1152]{1,0:T(8,128)}, u32[]{:S(2)}) copy-start(f32[36,1152]{1,0:T(8,128)} %refs_4_.1) | copy-start | bytes 497668
  10.0 18.5 %collective-permute-start.2 = (f32[144,128]{1,0:T(8,128)S(1)}, f32[144,128]{1,0:T(8,128)S(1)}, u32[]{:S(2)}, u32[]{:S(2)}) collective-permute-start(f32[144,128]{1,0:T(8,128)S(1)} %get-tuple-element.34), channel_id=1, source_target_pairs={{0,4},{1,5},{2,6},{3,7},{4,0},{5,1},{6,2},{7,3},{8,12},{9,13},{10,... | collective-permute-start | bytes 221192 | tf_op jit(solution)/shard_map/ppermute | solution.py:483
  11.7 16.7 %collective-permute-start.3 = (f32[144,128]{1,0:T(8,128)S(1)}, f32[144,128]{1,0:T(8,128)S(1)}, u32[]{:S(2)}, u32[]{:S(2)}) collective-permute-start(f32[144,128]{1,0:T(8,128)S(1)} %get-tuple-element.35), channel_id=1, source_target_pairs={{0,16},{1,17},{2,18},{3,19},{4,8},{5,9},{6,10},{7,11},{8,4},{9,5},... | collective-permute-start | bytes 221192 | tf_op jit(solution)/shard_map/ppermute | solution.py:483
  13.3 15.2 %collective-permute-start.6 = (f32[144,128]{1,0:T(8,128)S(1)}, f32[144,128]{1,0:T(8,128)S(1)}, u32[]{:S(2)}, u32[]{:S(2)}) collective-permute-start(f32[144,128]{1,0:T(8,128)S(1)} %get-tuple-element.36), channel_id=1, source_target_pairs={{0,16},{1,17},{2,18},{3,19},{4,24},{5,25},{6,26},{7,27},{8,20},{9,... | collective-permute-start | bytes 221192 | tf_op jit(solution)/shard_map/ppermute | solution.py:483
  13.8 14.7 %collective-permute-start.5 = (f32[144,128]{1,0:T(8,128)S(1)}, f32[144,128]{1,0:T(8,128)S(1)}, u32[]{:S(2)}, u32[]{:S(2)}) collective-permute-start(f32[144,128]{1,0:T(8,128)S(1)} %get-tuple-element.36), channel_id=1, source_target_pairs={{0,20},{1,21},{2,22},{3,23},{4,16},{5,17},{6,18},{7,19},{8,28},{9,... | collective-permute-start | bytes 221192 | tf_op jit(solution)/shard_map/ppermute | solution.py:483
  15.9 12.6 %collective-permute-start.4 = (f32[144,128]{1,0:T(8,128)S(1)}, f32[144,128]{1,0:T(8,128)S(1)}, u32[]{:S(2)}, u32[]{:S(2)}) collective-permute-start(f32[144,128]{1,0:T(8,128)S(1)} %get-tuple-element.36), channel_id=1, source_target_pairs={{0,16},{1,17},{2,18},{3,19},{4,20},{5,21},{6,22},{7,23},{8,24},{9,... | collective-permute-start | bytes 221192 | tf_op jit(solution)/shard_map/ppermute | solution.py:483
  37.8 1.2 %collective-permute-start.7 = (f32[24,128]{1,0:T(8,128)S(1)}, f32[24,128]{1,0:T(8,128)S(1)}, u32[]{:S(2)}, u32[]{:S(2)}) collective-permute-start(f32[24,128]{1,0:T(8,128)S(1)} %get-tuple-element.40), channel_id=1, source_target_pairs={{0,1},{1,0},{2,3},{3,2},{4,5},{5,4},{6,7},{7,6},{8,9},{9,8},{10,11... | collective-permute-start | bytes 36872 | tf_op jit(solution)/shard_map/ppermute | solution.py:483
  37.9 3.2 %collective-permute-start.8 = (f32[24,128]{1,0:T(8,128)S(1)}, f32[24,128]{1,0:T(8,128)S(1)}, u32[]{:S(2)}, u32[]{:S(2)}) collective-permute-start(f32[24,128]{1,0:T(8,128)S(1)} %get-tuple-element.41), channel_id=1, source_target_pairs={{0,3},{1,2},{2,1},{3,0},{4,7},{5,6},{6,5},{7,4},{8,11},{9,10},{10,... | collective-permute-start | bytes 36872 | tf_op jit(solution)/shard_map/ppermute | solution.py:483
  41.4 5.6 %collective-permute-start.9 = (f32[144,128]{1,0:T(8,128)S(1)}, f32[144,128]{1,0:T(8,128)S(1)}, u32[]{:S(2)}, u32[]{:S(2)}) collective-permute-start(f32[144,128]{1,0:T(8,128)S(1)} %get-tuple-element.42), channel_id=1, source_target_pairs={{0,4},{1,5},{2,6},{3,7},{4,0},{5,1},{6,2},{7,3},{8,12},{9,13},{10,... | collective-permute-start | bytes 221192 | tf_op jit(solution)/shard_map/ppermute | solution.py:483
  42.0 5.1 %collective-permute-start.10 = (f32[144,128]{1,0:T(8,128)S(1)}, f32[144,128]{1,0:T(8,128)S(1)}, u32[]{:S(2)}, u32[]{:S(2)}) collective-permute-start(f32[144,128]{1,0:T(8,128)S(1)} %get-tuple-element.43), channel_id=1, source_target_pairs={{0,16},{1,17},{2,18},{3,19},{4,8},{5,9},{6,10},{7,11},{8,4},{9,5},... | collective-permute-start | bytes 221192 | tf_op jit(solution)/shard_map/ppermute | solution.py:483
  42.6 7.2 %collective-permute-start.13 = (f32[144,128]{1,0:T(8,128)S(1)}, f32[144,128]{1,0:T(8,128)S(1)}, u32[]{:S(2)}, u32[]{:S(2)}) collective-permute-start(f32[144,128]{1,0:T(8,128)S(1)} %get-tuple-element.44), channel_id=1, source_target_pairs={{0,16},{1,17},{2,18},{3,19},{4,24},{5,25},{6,26},{7,27},{8,20},{9,... | collective-permute-start | bytes 221192 | tf_op jit(solution)/shard_map/ppermute | solution.py:483
  44.0 5.8 %collective-permute-start.12 = (f32[144,128]{1,0:T(8,128)S(1)}, f32[144,128]{1,0:T(8,128)S(1)}, u32[]{:S(2)}, u32[]{:S(2)}) collective-permute-start(f32[144,128]{1,0:T(8,128)S(1)} %get-tuple-element.44), channel_id=1, source_target_pairs={{0,20},{1,21},{2,22},{3,23},{4,16},{5,17},{6,18},{7,19},{8,28},{9,... | collective-permute-start | bytes 221192 | tf_op jit(solution)/shard_map/ppermute | solution.py:483
  46.4 4.6 %collective-permute-start.11 = (f32[144,128]{1,0:T(8,128)S(1)}, f32[144,128]{1,0:T(8,128)S(1)}, u32[]{:S(2)}, u32[]{:S(2)}) collective-permute-start(f32[144,128]{1,0:T(8,128)S(1)} %get-tuple-element.44), channel_id=1, source_target_pairs={{0,16},{1,17},{2,18},{3,19},{4,20},{5,21},{6,22},{7,23},{8,24},{9,... | collective-permute-start | bytes 221192 | tf_op jit(solution)/shard_map/ppermute | solution.py:483
  71.7 1.2 %collective-permute-start.14 = (f32[24,128]{1,0:T(8,128)S(1)}, f32[24,128]{1,0:T(8,128)S(1)}, u32[]{:S(2)}, u32[]{:S(2)}) collective-permute-start(f32[24,128]{1,0:T(8,128)S(1)} %get-tuple-element.49), channel_id=1, source_target_pairs={{0,1},{1,0},{2,3},{3,2},{4,5},{5,4},{6,7},{7,6},{8,9},{9,8},{10,11... | collective-permute-start | bytes 36872 | tf_op jit(solution)/shard_map/ppermute | solution.py:483
  71.8 3.2 %collective-permute-start.15 = (f32[24,128]{1,0:T(8,128)S(1)}, f32[24,128]{1,0:T(8,128)S(1)}, u32[]{:S(2)}, u32[]{:S(2)}) collective-permute-start(f32[24,128]{1,0:T(8,128)S(1)} %get-tuple-element.50), channel_id=1, source_target_pairs={{0,3},{1,2},{2,1},{3,0},{4,7},{5,6},{6,5},{7,4},{8,11},{9,10},{10,... | collective-permute-start | bytes 36872 | tf_op jit(solution)/shard_map/ppermute | solution.py:483
  75.3 5.6 %collective-permute-start.16 = (f32[144,128]{1,0:T(8,128)S(1)}, f32[144,128]{1,0:T(8,128)S(1)}, u32[]{:S(2)}, u32[]{:S(2)}) collective-permute-start(f32[144,128]{1,0:T(8,128)S(1)} %get-tuple-element.51), channel_id=1, source_target_pairs={{0,4},{1,5},{2,6},{3,7},{4,0},{5,1},{6,2},{7,3},{8,12},{9,13},{10,... | collective-permute-start | bytes 221192 | tf_op jit(solution)/shard_map/ppermute | solution.py:483
  75.9 5.1 %collective-permute-start.17 = (f32[144,128]{1,0:T(8,128)S(1)}, f32[144,128]{1,0:T(8,128)S(1)}, u32[]{:S(2)}, u32[]{:S(2)}) collective-permute-start(f32[144,128]{1,0:T(8,128)S(1)} %get-tuple-element.52), channel_id=1, source_target_pairs={{0,16},{1,17},{2,18},{3,19},{4,8},{5,9},{6,10},{7,11},{8,4},{9,5},... | collective-permute-start | bytes 221192 | tf_op jit(solution)/shard_map/ppermute | solution.py:483
  76.4 7.2 %collective-permute-start.20 = (f32[144,128]{1,0:T(8,128)S(1)}, f32[144,128]{1,0:T(8,128)S(1)}, u32[]{:S(2)}, u32[]{:S(2)}) collective-permute-start(f32[144,128]{1,0:T(8,128)S(1)} %get-tuple-element.53), channel_id=1, source_target_pairs={{0,16},{1,17},{2,18},{3,19},{4,24},{5,25},{6,26},{7,27},{8,20},{9,... | collective-permute-start | bytes 221192 | tf_op jit(solution)/shard_map/ppermute | solution.py:483
  77.9 5.8 %collective-permute-start.19 = (f32[144,128]{1,0:T(8,128)S(1)}, f32[144,128]{1,0:T(8,128)S(1)}, u32[]{:S(2)}, u32[]{:S(2)}) collective-permute-start(f32[144,128]{1,0:T(8,128)S(1)} %get-tuple-element.53), channel_id=1, source_target_pairs={{0,20},{1,21},{2,22},{3,23},{4,16},{5,17},{6,18},{7,19},{8,28},{9,... | collective-permute-start | bytes 221192 | tf_op jit(solution)/shard_map/ppermute | solution.py:483
  80.3 4.6 %collective-permute-start.18 = (f32[144,128]{1,0:T(8,128)S(1)}, f32[144,128]{1,0:T(8,128)S(1)}, u32[]{:S(2)}, u32[]{:S(2)}) collective-permute-start(f32[144,128]{1,0:T(8,128)S(1)} %get-tuple-element.53), channel_id=1, source_target_pairs={{0,16},{1,17},{2,18},{3,19},{4,20},{5,21},{6,22},{7,23},{8,24},{9,... | collective-permute-start | bytes 221192 | tf_op jit(solution)/shard_map/ppermute | solution.py:483

commit v2 on v1

--- a/solution.py
+++ b/solution.py
@@ -12,7 +12,6 @@
 f32 = jnp.float32
 LANES = 128
 EDGE = 8
-BLOCK = 16
 
 ALONG1, ACROSS1 = 0.75, 0.5
 ALONG2, ACROSS2, MIXED2 = 0.3125, 0.25, 0.0625
@@ -35,7 +34,7 @@
         self.x, self.y, self.z = size_x, size_y, size_z
         self.pitch = size_y + 4
         self.used = (size_x + 2) * self.pitch
-        assert self.used <= LANES and size_z % BLOCK == 0
+        assert self.used <= LANES
         self.rows = size_z + 2 * EDGE
         self.tall = self.rows + 2 * EDGE
         self.phases = phases
@@ -183,11 +182,15 @@
             ref[f, sh.tall - EDGE :, :] = jnp.zeros((EDGE, LANES), f32)
 
 
-def z_stage(ref, f, base):
-    centre = ref[f, pl.ds(base, BLOCK), :]
-    after = ref[f, pl.ds(base + 1, BLOCK), :]
-    before = ref[f, pl.ds(base - 1, BLOCK), :]
-    return centre, before + after, after - before
+def inner(ref, f):
+    return ref[f, EDGE : ref.shape[1] - EDGE, :]
+
+
+def z_stage(ref, f):
+    end = ref.shape[1] - EDGE
+    after = ref[f, EDGE + 1 : end + 1, :]
+    before = ref[f, EDGE - 1 : end - 1, :]
+    return inner(ref, f), before + after, after - before
 
 
 def y_stage(value):
@@ -195,10 +198,10 @@
     return before + after, after - before
 
 
-def yz_parts(ref, base):
-    a, a_sum, a_dif = z_stage(ref, 0, base)
-    b, b_sum, b_dif = z_stage(ref, 1, base)
-    c, c_sum, c_dif = z_stage(ref, 2, base)
+def yz_parts(ref):
+    a, a_sum, a_dif = z_stage(ref, 0)
+    b, b_sum, b_dif = z_stage(ref, 1)
+    c, c_sum, c_dif = z_stage(ref, 2)
     pa, ma = y_stage(a)
     pas, mas = y_stage(a_sum)
     pad, _ = y_stage(a_dif)
@@ -228,9 +231,9 @@
     return own + jnp.where(lane < last, after, rim_plus) + jnp.where(lane >= sh.pitch, before, rim_minus)
 
 
-def stencil(sh, lane, ref, rim, base):
-    parts = yz_parts(ref, base)
-    rims = yz_parts(rim, base) if rim is not None else [None] * 3
+def stencil(sh, lane, ref, rim):
+    parts = yz_parts(ref)
+    rims = yz_parts(rim) if rim is not None else [None] * 3
     out = []
     for (own, even, odd), rim_part in zip(parts, rims):
         if rim_part is None:
@@ -243,8 +246,8 @@
     return out
 
 
-def spring_parts(ref, base):
-    k, k_sum, k_dif = z_stage(ref, 0, base)
+def spring_parts(ref):
+    k, k_sum, k_dif = z_stage(ref, 0)
     pk, mk = y_stage(k)
     pks, mks = y_stage(k_sum)
     pkd, mkd = y_stage(k_dif)
@@ -266,12 +269,12 @@
     return xx, yy, zz, xy, xz, yz
 
 
-def own_block(sh, lane, springs, base):
+def own_block(sh, lane, springs):
     main, rim = springs
-    k = main[0, pl.ds(base, BLOCK), :]
+    k = inner(main, 0)
     out = []
     for index, ((own, even, odd), (_, rim_even, rim_odd)) in enumerate(
-        zip(spring_parts(main, base), spring_parts(rim, base))
+        zip(spring_parts(main), spring_parts(rim))
     ):
         total = x_stage(sh, lane, own, even + odd, even - odd, rim_even + rim_odd, rim_even - rim_odd)
         out.append(total + TOTAL * k if index < 3 else total)
@@ -286,81 +289,56 @@
     )
 
 
-def image_at(sh, lane, v, kv, rims, k, d, base):
-    outer = stencil(sh, lane, v, rims and rims[0], base)
-    inner = stencil(sh, lane, kv, rims and rims[1], base)
-    own = apply_block(d, [v[m, pl.ds(base, BLOCK), :] for m in range(3)])
-    return [own[m] - (k * outer[m] + inner[m]) for m in range(3)]
-
-
-def blocks(sh, step):
-    def body(i, carry):
-        step(pl.multiple_of(i * BLOCK, BLOCK))
-        return carry
-
-    lax.fori_loop(0, sh.rows // BLOCK, body, 0)
-
-
-def extended_mask(sh, base):
-    lane, _, across = sh.lane_grid(BLOCK)
-    z = base - EDGE + lax.broadcasted_iota(jnp.int32, (BLOCK, LANES), 0)
-    return (lane < sh.used) & (across >= -1) & (across <= sh.y) & (z >= -1) & (z <= sh.z)
-
-
-def grid_mask(sh, rows, first):
-    lane, along, across = sh.lane_grid(rows)
-    z = first - EDGE + lax.broadcasted_iota(jnp.int32, (rows, LANES), 0)
-    mask = lane < sh.used
-    for axis, place, size in ((0, along, sh.x), (1, across, sh.y), (2, z, sh.z)):
-        index = sh.here(axis)
-        low = jnp.where(index > 0, -EDGE, 0)
-        high = jnp.where(index < sh.sizes[axis] - 1, size + EDGE, size)
-        mask = mask & (place >= low) & (place < high)
-    return mask
-
-
-def rim_mask(sh, rows, first):
-    lane, _, across = sh.lane_grid(rows)
-    z = first - EDGE + lax.broadcasted_iota(jnp.int32, (rows, LANES), 0)
-    mask = lane < sh.used
-    for axis, place, size in ((1, across, sh.y), (2, z, sh.z)):
-        index = sh.here(axis)
-        low = jnp.where(index > 0, -EDGE, 0)
-        high = jnp.where(index < sh.sizes[axis] - 1, size + EDGE, size)
-        mask = mask & (place >= low) & (place < high)
-    return mask
-
-
-def local_solve(sh, residual, k_ref, d_ref, v, kv):
+def image_of(sh, lane, v, kv, rims, springs_ref):
+    outer = stencil(sh, lane, v, rims and rims[0])
+    scaled = stencil(sh, lane, kv, rims and rims[1])
+    own = apply_block([springs_ref[f] for f in range(6)], [inner(v, m) for m in range(3)])
+    return [own[m] - (springs_ref[6] * outer[m] + scaled[m]) for m in range(3)]
+
+
+def level(sh):
+    return lax.broadcasted_iota(jnp.int32, (sh.rows, LANES), 0) - EDGE
+
+
+def extended_mask(sh):
+    lane, _, across = sh.lane_grid(1)
+    z = level(sh)
+    return ((lane < sh.used) & (across >= -1) & (across <= sh.y)) & ((z >= -1) & (z <= sh.z))
+
+
+def within(sh, axis, place, size):
+    index = sh.here(axis)
+    low = jnp.where(index > 0, -EDGE, 0)
+    high = jnp.where(index < sh.sizes[axis] - 1, size + EDGE, size)
+    return (place >= low) & (place < high)
+
+
+def grid_masks(sh):
+    lane, along, across = sh.lane_grid(1)
+    lanes = (lane < sh.used) & within(sh, 1, across, sh.y)
+    rows = within(sh, 2, level(sh), sh.z)
+    return (lanes & within(sh, 0, along, sh.x)) & rows, lanes & rows
+
+
+def put(ref, f, value):
+    ref[f, EDGE : ref.shape[1] - EDGE, :] = value
+
+
+def local_solve(sh, residual_ref, springs_ref, v, kv, factor):
     lane, _, _ = sh.lane_grid(1)
-    at = lambda ref, f, base: ref[f, pl.ds(base, BLOCK), :]
-
-    def inverse(base, mask):
-        return [jnp.where(mask, relax / jnp.where(mask, at(d_ref, m, base), 1.0), 0.0) for m in range(3)]
-
-    def start(base):
-        inv = inverse(base, extended_mask(sh, base))
-        k = k_ref[pl.ds(base, BLOCK), :]
-        for m in range(3):
-            z = residual(m, base) * inv[m]
-            v[0][m, pl.ds(base + EDGE, BLOCK), :] = z
-            kv[0][m, pl.ds(base + EDGE, BLOCK), :] = k * z
-
-    blocks(sh, start)
+    mask = extended_mask(sh)
+    for m in range(3):
+        factor[m] = pick(mask, relax / jnp.where(mask, springs_ref[m], 1.0))
+        z = residual_ref[m] * factor[m]
+        put(v[0], m, z)
+        put(kv[0], m, springs_ref[6] * z)
     for sweep in range(SWEEPS - 1):
         old, new = sweep % 2, (sweep + 1) % 2
-
-        def step(base, old=old, new=new):
-            k = k_ref[pl.ds(base, BLOCK), :]
-            d = [at(d_ref, f, base) for f in range(6)]
-            inv = inverse(base, extended_mask(sh, base))
-            image = image_at(sh, lane, v[old], kv[old], None, k, d, base + EDGE)
-            for m in range(3):
-                z = v[old][m, pl.ds(base + EDGE, BLOCK), :] + inv[m] * (residual(m, base) - image[m])
-                v[new][m, pl.ds(base + EDGE, BLOCK), :] = z
-                kv[new][m, pl.ds(base + EDGE, BLOCK), :] = k * z
-
-        blocks(sh, step)
+        image = image_of(sh, lane, v[old], kv[old], None, springs_ref)
+        for m in range(3):
+            z = inner(v[old], m) + factor[m] * (residual_ref[m] - image[m])
+            put(v[new], m, z)
+            put(kv[new], m, springs_ref[6] * z)
     return (SWEEPS - 1) % 2
 
 
@@ -617,22 +595,18 @@
         nodes_ref, coarse_ref, inverse_ref = take(3)
         solution_ref, springs_ref = take(2)
         z_refs = take(sh.z_links)
-        all_fields, rims, stiff, stiff_rim, v0, v1, kv0, kv1, values = take(9)
+        all_fields, rims, stiff, stiff_rim, v0, v1, kv0, kv1, factor, values = take(10)
         clear_guards(sh, (stiff, stiff_rim, v0, v1, kv0, kv1))
         merge_all(sh, SPREAD, Taker(merging), all_fields, rims, 0)
-        stiff[0, EDGE : EDGE + sh.rows, :] = all_fields[3]
-        stiff_rim[0, EDGE : EDGE + sh.rows, :] = rims[3]
+        put(stiff, 0, all_fields[3])
+        put(stiff_rim, 0, rims[3])
         springs_ref[6] = all_fields[3]
         springs_ref[7] = rims[3]
         lane, _, _ = sh.lane_grid(1)
 
-        def springs(base):
-            for f, entry in enumerate(own_block(sh, lane, (stiff, stiff_rim), base + EDGE)):
-                springs_ref[f, pl.ds(base, BLOCK), :] = entry
-
-        blocks(sh, springs)
-        residual = lambda m, base: all_fields[m, pl.ds(base, BLOCK), :]
-        index = local_solve(sh, residual, springs_ref.at[6], springs_ref, (v0, v1), (kv0, kv1))
+        for f, entry in enumerate(own_block(sh, lane, (stiff, stiff_rim))):
+            springs_ref[f] = entry
+        index = local_solve(sh, all_fields, springs_ref, (v0, v1), (kv0, kv1), factor)
         finish_solve(index, (v0, v1), nodes_ref, coarse_ref, inverse_ref, values, solution_ref, z_refs, DEEP)
 
     solved, springs, *z_messages = call(
@@ -640,7 +614,7 @@
         "first_solve",
         [fields, (8,) + plane] + z_shape(DEEP),
         [start_field, *from_z, *from_y, *from_x, nodes, coarse, coarse_inverse],
-        [(4,) + plane, (4,) + plane, (1, sh.tall, LANES), (1, sh.tall, LANES)] + [tall] * 4 + [(LANES, LANES)],
+        [(4,) + plane, (4,) + plane, (1, sh.tall, LANES), (1, sh.tall, LANES)] + [tall] * 4 + [fields, (LANES, LANES)],
     )
     from_z, from_y, from_x = exchange(sh, DEEP, "deep", solved, z_messages)
 
@@ -654,30 +628,19 @@
         merge_all(sh, DEEP, Taker(merging), v, rim, EDGE)
         lane, _, _ = sh.lane_grid(1)
 
-        def mask(base):
-            rows, tall_rows = pl.ds(base, BLOCK), pl.ds(base + EDGE, BLOCK)
-            in_grid, in_rim = grid_mask(sh, BLOCK, base), rim_mask(sh, BLOCK, base)
-            k, k_edge = springs_ref[6, rows, :], springs_ref[7, rows, :]
-            for m in range(3):
-                value = pick(in_grid, v[m, tall_rows, :])
-                v[m, tall_rows, :] = value
-                search_ref[m, rows, :] = value
-                kv[m, tall_rows, :] = k * value
-                value = pick(in_rim, rim[m, tall_rows, :])
-                rim[m, tall_rows, :] = value
-                k_rim[m, tall_rows, :] = k_edge * value
-
-        blocks(sh, mask)
-
-        def step(base):
-            rows = pl.ds(base, BLOCK)
-            d = [springs_ref[f, rows, :] for f in range(6)]
-            image = image_at(sh, lane, v, kv, (rim, k_rim), springs_ref[6, rows, :], d, base + EDGE)
-            keep = grid_mask(sh, BLOCK, base) & extended_mask(sh, base)
-            for m in range(3):
-                image_ref[m, rows, :] = pick(keep, image[m])
-
-        blocks(sh, step)
+        in_grid, in_rim = grid_masks(sh)
+        for m in range(3):
+            value = pick(in_grid, inner(v, m))
+            put(v, m, value)
+            search_ref[m] = value
+            put(kv, m, springs_ref[6] * value)
+            value = pick(in_rim, inner(rim, m))
+            put(rim, m, value)
+            put(k_rim, m, springs_ref[7] * value)
+        image = image_of(sh, lane, v, kv, (rim, k_rim), springs_ref)
+        keep = in_grid & extended_mask(sh)
+        for m in range(3):
+            image_ref[m] = pick(keep, image[m])
         sums[...] = jnp.zeros(sums.shape, f32)
         coarse_sums(sh, nodes_ref[...], [image_ref[m, own, :] for m in range(3)], node_count, sums, slots_ref)
 
@@ -695,10 +658,9 @@
         image_ref, springs_ref, nodes_ref, coarse_ref, inverse_ref = take(5)
         solution_ref = take.one()
         z_refs = take(sh.z_links)
-        v0, v1, kv0, kv1, values = take(5)
+        v0, v1, kv0, kv1, factor, values = take(6)
         clear_guards(sh, (v0, v1, kv0, kv1))
-        residual = lambda m, base: image_ref[m, pl.ds(base, BLOCK), :]
-        index = local_solve(sh, residual, springs_ref.at[6], springs_ref, (v0, v1), (kv0, kv1))
+        index = local_solve(sh, image_ref, springs_ref, (v0, v1), (kv0, kv1), factor)
         finish_solve(index, (v0, v1), nodes_ref, coarse_ref, inverse_ref, values, solution_ref, z_refs, NEAR)
 
     solved, *z_messages = call(
@@ -706,7 +668,7 @@
         "second_solve",
         [fields] + z_shape(NEAR),
         [image, springs, nodes, coarse, coarse_inverse],
-        [tall] * 4 + [(LANES, LANES)],
+        [tall] * 4 + [fields, (LANES, LANES)],
     )
     from_z, from_y, from_x = exchange(sh, NEAR, "near", solved, z_messages)
 
@@ -720,26 +682,15 @@
         merge_all(sh, NEAR, Taker(merging), v, None, EDGE)
         lane, _, _ = sh.lane_grid(1)
 
-        def mask(base):
-            rows, tall_rows = pl.ds(base, BLOCK), pl.ds(base + EDGE, BLOCK)
-            in_grid = grid_mask(sh, BLOCK, base)
-            k = springs_ref[6, rows, :]
-            for m in range(3):
-                value = pick(in_grid, v[m, tall_rows, :])
-                v[m, tall_rows, :] = value
-                kv[m, tall_rows, :] = k * value
-
-        blocks(sh, mask)
-
-        def step(base):
-            rows = pl.ds(base, BLOCK)
-            d = [springs_ref[f, rows, :] for f in range(6)]
-            image = image_at(sh, lane, v, kv, None, springs_ref[6, rows, :], d, base + EDGE)
-            for m in range(3):
-                image_ref[m, rows, :] = image[m]
-                second_ref[m, rows, :] = v[m, pl.ds(base + EDGE, BLOCK), :]
-
-        blocks(sh, step)
+        in_grid, _ = grid_masks(sh)
+        for m in range(3):
+            value = pick(in_grid, inner(v, m))
+            put(v, m, value)
+            second_ref[m] = value
+            put(kv, m, springs_ref[6] * value)
+        image = image_of(sh, lane, v, kv, None, springs_ref)
+        for m in range(3):
+            image_ref[m] = image[m]
         valid = nodes_ref[...] >= 0.0
         names = ("r", "z", "w", "q", "v")
         sources = (start_ref, search_ref, first_ref, second_ref, image_ref)

time: 99.3 us -> 89.1 us (0.90)
  Pallas kernels: 27.4 us -> 17.2 us
    pallas_call x9, Pallas kernels: 27.4 us -> 17.2 us  [call(): pl.pallas_call(kernel, out_shape=[jax.ShapeDtypeStruct(shape, f32) for sh...]
where the time goes in v2:
time: 89.1 us; the launch traced here: 88.8 us
  blocking collectives  30.1 us (34%)
  starting transfers between devices  23.1 us (26%)
  Pallas kernels  17.2 us (19%)
  waiting for transfers between devices  14.6 us (16%)
  local copies, waits for them, and re-layouts  3 us (3%)
    all_to_all x3, blocking collectives, to_all(): return lax.all_to_all(slots, AXES, 0, 0, tiled=True)  30.1 us
    ppermute x21, starting transfers between devices, send(): return lax.ppermute(value, AXES, permutation(sh.sizes, moves))  23.1 us
    pallas_call x9, Pallas kernels, call(): pl.pallas_call(kernel, out_shape=[jax.ShapeDtypeStruct(shape, f32) for sh...  17.2 us
    ppermute x21, waiting for transfers between devices, send(): return lax.ppermute(value, AXES, permutation(sh.sizes, moves))  14.6 us
    unnamed x10, local copies, waits for them, and re-layouts  3 us
  transfers between devices with their start and end apart: 21, of which 11 were waited for; matrix products, arithmetic and copies ran while one was open for 0% of the time, Pallas kernels for 0%

profile of v2, /device:TPU:0, one launch (start us, length us, event | category | flops | bytes accessed | tf_op | source)
XLA Modules:
  0.0 88.8 jit_solution(2447035003556451949)
XLA Ops:
  0.6 0.6 copy-done.4
  1.3 0.9 %copy-done.1 = f32[3,8,8,128]{3,2,1,0:T(8,128)S(1)} copy-done((f32[3,8,8,128]{3,2,1,0:T(8,128)S(1)}, f32[3,8,8,128]{3,2,1,0:T(8,128)}, u32[]{:S(2)}) %copy-start.1) | copy-done | bytes 98328
  2.2 0.8 copy-done.2
  2.9 0.7 copy-done.3
  3.6 1.4 %begin.1 = (f32[4,144,128]{2,1,0:T(8,128)S(1)}, f32[128,128]{1,0:T(8,128)S(1)}, f32[32,128]{1,0:T(8,128)S(1)}, f32[32,128]{1,0:T(8,128)S(1)}, f32[32,128]{1,0:T(8,128)S(1)}) custom-call(f32[3,64,128]{2,1,0:T(8,128)S(1)} %bitcast.16, s32[4,4,64]{2,1,0:T(4,128)S(1)} %copy-done.3, f32[8]{0:T(128)S(1)} %copy-done.4, s32[64,128]{1,0:T(8,128)S(1)} %bitcast.21), custom_call_target="tpu_custom_call" | custom-call | tf_op jit(solution)/shard_map/begin/pallas_call | solution.py:426
  5.1 0.5 collective-permute-start
  5.6 2.6 %collective-permute-start.1 = (f32[32,128]{1,0:T(8,128)S(1)}, f32[32,128]{1,0:T(8,128)S(1)}, u32[]{:S(2)}, u32[]{:S(2)}) collective-permute-start(f32[32,128]{1,0:T(8,128)S(1)} %get-tuple-element.33), channel_id=1, source_target_pairs={{0,3},{1,2},{2,1},{3,0},{4,7},{5,6},{6,5},{7,4},{8,11},{9,10},{10,... | collective-permute-start | bytes 49160 | tf_op jit(solution)/shard_map/ppermute | solution.py:461
  8.2 1.4 %collective-permute-done.1.refs_2_ = f32[32,128]{1,0:T(8,128)S(1)} collective-permute-done((f32[32,128]{1,0:T(8,128)S(1)}, f32[32,128]{1,0:T(8,128)S(1)}, u32[]{:S(2)}, u32[]{:S(2)}) %collective-permute-start.1) | collective-permute-done | bytes 16416 | tf_op jit(solution)/shard_map/ppermute | solution.py:461
  9.6 0.4 spread.1
  10.0 1.8 %collective-permute-start.2 = (f32[144,128]{1,0:T(8,128)S(1)}, f32[144,128]{1,0:T(8,128)S(1)}, u32[]{:S(2)}, u32[]{:S(2)}) collective-permute-start(f32[144,128]{1,0:T(8,128)S(1)} %get-tuple-element.34), channel_id=1, source_target_pairs={{0,4},{1,5},{2,6},{3,7},{4,0},{5,1},{6,2},{7,3},{8,12},{9,13},{10,... | collective-permute-start | bytes 221192 | tf_op jit(solution)/shard_map/ppermute | solution.py:461
  11.7 1.5 %collective-permute-start.3 = (f32[144,128]{1,0:T(8,128)S(1)}, f32[144,128]{1,0:T(8,128)S(1)}, u32[]{:S(2)}, u32[]{:S(2)}) collective-permute-start(f32[144,128]{1,0:T(8,128)S(1)} %get-tuple-element.35), channel_id=1, source_target_pairs={{0,16},{1,17},{2,18},{3,19},{4,8},{5,9},{6,10},{7,11},{8,4},{9,5},... | collective-permute-start | bytes 221192 | tf_op jit(solution)/shard_map/ppermute | solution.py:461
  13.3 0.5 collective-permute-start.6
  13.8 2.1 %collective-permute-start.5 = (f32[144,128]{1,0:T(8,128)S(1)}, f32[144,128]{1,0:T(8,128)S(1)}, u32[]{:S(2)}, u32[]{:S(2)}) collective-permute-start(f32[144,128]{1,0:T(8,128)S(1)} %get-tuple-element.36), channel_id=1, source_target_pairs={{0,20},{1,21},{2,22},{3,23},{4,16},{5,17},{6,18},{7,19},{8,28},{9,... | collective-permute-start | bytes 221192 | tf_op jit(solution)/shard_map/ppermute | solution.py:461
  15.9 1.5 %collective-permute-start.4 = (f32[144,128]{1,0:T(8,128)S(1)}, f32[144,128]{1,0:T(8,128)S(1)}, u32[]{:S(2)}, u32[]{:S(2)}) collective-permute-start(f32[144,128]{1,0:T(8,128)S(1)} %get-tuple-element.36), channel_id=1, source_target_pairs={{0,16},{1,17},{2,18},{3,19},{4,20},{5,21},{6,22},{7,23},{8,24},{9,... | collective-permute-start | bytes 221192 | tf_op jit(solution)/shard_map/ppermute | solution.py:461
  17.3 11.2 %all_to_all.33 = f32[32,1,128]{2,1,0:T(1,128)S(1)} all-to-all(f32[32,1,128]{2,1,0:T(1,128)S(1)} %bitcast.22), channel_id=1, replica_groups=mesh['gx'=2,'gy'=4,'gz'=4] {'gx','gy','gz'}, dimensions={0} | all-to-all | bytes 32768 | tf_op jit(solution)/shard_map/all_to_all | solution.py:478
  28.5 4.8 %first_solve.1 = (f32[3,144,128]{2,1,0:T(8,128)S(1)}, f32[8,144,128]{2,1,0:T(8,128)S(1)}, f32[24,128]{1,0:T(8,128)S(1)}, f32[24,128]{1,0:T(8,128)S(1)}) custom-call(f32[4,144,128]{2,1,0:T(8,128)S(1)} %get-tuple-element.31.refs_0_.refs_10_, f32[32,128]{1,0:T(8,128)S(1)} %collective-permute-done.refs_1_, f32[32,128]{1,0:T(8,128)S(1)} %collective-permute-done.1.refs_2_, ...), custom_call_target="tpu_custom_call" | custom-call | tf_op jit(solution)/shard_map/first_solve/pallas_call | solution.py:426
  33.3 0.1 collective-permute-start.7
  33.4 0.7 collective-permute-start.8
  34.1 0.5 collective-permute-done.7.refs_1_
  34.6 2.0 %collective-permute-done.8.refs_2_ = f32[24,128]{1,0:T(8,128)S(1)} collective-permute-done((f32[24,128]{1,0:T(8,128)S(1)}, f32[24,128]{1,0:T(8,128)S(1)}, u32[]{:S(2)}, u32[]{:S(2)}) %collective-permute-start.8) | collective-permute-done | bytes 12320 | tf_op jit(solution)/shard_map/ppermute | solution.py:461
  36.6 0.3 deep.1
  36.9 0.6 collective-permute-start.9
  37.5 0.6 collective-permute-start.10
  38.1 1.4 %collective-permute-start.13 = (f32[144,128]{1,0:T(8,128)S(1)}, f32[144,128]{1,0:T(8,128)S(1)}, u32[]{:S(2)}, u32[]{:S(2)}) collective-permute-start(f32[144,128]{1,0:T(8,128)S(1)} %get-tuple-element.44), channel_id=1, source_target_pairs={{0,16},{1,17},{2,18},{3,19},{4,24},{5,25},{6,26},{7,27},{8,20},{9,... | collective-permute-start | bytes 221192 | tf_op jit(solution)/shard_map/ppermute | solution.py:461
  39.5 2.4 %collective-permute-start.12 = (f32[144,128]{1,0:T(8,128)S(1)}, f32[144,128]{1,0:T(8,128)S(1)}, u32[]{:S(2)}, u32[]{:S(2)}) collective-permute-start(f32[144,128]{1,0:T(8,128)S(1)} %get-tuple-element.44), channel_id=1, source_target_pairs={{0,20},{1,21},{2,22},{3,23},{4,16},{5,17},{6,18},{7,19},{8,28},{9,... | collective-permute-start | bytes 221192 | tf_op jit(solution)/shard_map/ppermute | solution.py:461
  41.9 0.6 collective-permute-start.11
  42.5 0.1 collective-permute-done.10.refs_4_
  42.6 2.7 %collective-permute-done.13.refs_7_ = f32[144,128]{1,0:T(8,128)S(1)} collective-permute-done((f32[144,128]{1,0:T(8,128)S(1)}, f32[144,128]{1,0:T(8,128)S(1)}, u32[]{:S(2)}, u32[]{:S(2)}) %collective-permute-start.13) | collective-permute-done | bytes 73760 | tf_op jit(solution)/shard_map/ppermute | solution.py:461
  45.3 1.3 %collective-permute-done.11.refs_5_ = f32[144,128]{1,0:T(8,128)S(1)} collective-permute-done((f32[144,128]{1,0:T(8,128)S(1)}, f32[144,128]{1,0:T(8,128)S(1)}, u32[]{:S(2)}, u32[]{:S(2)}) %collective-permute-start.11) | collective-permute-done | bytes 73760 | tf_op jit(solution)/shard_map/ppermute | solution.py:461
  46.5 2.7 %first_image.1 = (f32[3,144,128]{2,1,0:T(8,128)S(1)}, f32[3,144,128]{2,1,0:T(8,128)S(1)}, f32[32,128]{1,0:T(8,128)S(1)}) custom-call(f32[3,144,128]{2,1,0:T(8,128)S(1)} %get-tuple-element.39.refs_0_, f32[24,128]{1,0:T(8,128)S(1)} %collective-permute-done.7.refs_1_, f32[24,128]{1,0:T(8,128)S(1)} %collective-permute-done.8.refs_2_, ...), custom_call_target="tpu_custom_call" | custom-call | tf_op jit(solution)/shard_map/first_image/pallas_call | solution.py:426
  49.3 9.5 %all_to_all.34 = f32[32,1,128]{2,1,0:T(1,128)S(1)} all-to-all(f32[32,1,128]{2,1,0:T(1,128)S(1)} %bitcast.24), channel_id=1, replica_groups=mesh['gx'=2,'gy'=4,'gz'=4] {'gx','gy','gz'}, dimensions={0} | all-to-all | bytes 32768 | tf_op jit(solution)/shard_map/all_to_all | solution.py:478
  58.8 3.9 %second_solve.1 = (f32[3,144,128]{2,1,0:T(8,128)S(1)}, f32[24,128]{1,0:T(8,128)S(1)}, f32[24,128]{1,0:T(8,128)S(1)}) custom-call(f32[3,144,128]{2,1,0:T(8,128)S(1)} %get-tuple-element.46.refs_0_.refs_12_.first_ref, f32[8,144,128]{2,1,0:T(8,128)S(1)} %get-tuple-element.45.refs_9_.refs_1_, f32[128,128]{1,0:T(8,128)S(1)} %get-tuple-element.37.refs_8_.refs_2_, ...), custom_call_target="tpu_custom_call" | custom-call | tf_op jit(solution)/shard_map/second_solve/pallas_call | solution.py:426
  62.7 0.1 collective-permute-start.14
  62.8 0.7 collective-permute-start.15
  63.4 0.5 collective-permute-done.14.refs_1_
  63.9 2.0 %collective-permute-done.15.refs_2_ = f32[24,128]{1,0:T(8,128)S(1)} collective-permute-done((f32[24,128]{1,0:T(8,128)S(1)}, f32[24,128]{1,0:T(8,128)S(1)}, u32[]{:S(2)}, u32[]{:S(2)}) %collective-permute-start.15) | collective-permute-done | bytes 12320 | tf_op jit(solution)/shard_map/ppermute | solution.py:461
  65.9 0.3 near.1
  66.2 0.6 collective-permute-start.16
  66.8 0.6 collective-permute-start.17
  67.4 1.4 %collective-permute-start.20 = (f32[144,128]{1,0:T(8,128)S(1)}, f32[144,128]{1,0:T(8,128)S(1)}, u32[]{:S(2)}, u32[]{:S(2)}) collective-permute-start(f32[144,128]{1,0:T(8,128)S(1)} %get-tuple-element.53), channel_id=1, source_target_pairs={{0,16},{1,17},{2,18},{3,19},{4,24},{5,25},{6,26},{7,27},{8,20},{9,... | collective-permute-start | bytes 221192 | tf_op jit(solution)/shard_map/ppermute | solution.py:461
  68.8 2.4 %collective-permute-start.19 = (f32[144,128]{1,0:T(8,128)S(1)}, f32[144,128]{1,0:T(8,128)S(1)}, u32[]{:S(2)}, u32[]{:S(2)}) collective-permute-start(f32[144,128]{1,0:T(8,128)S(1)} %get-tuple-element.53), channel_id=1, source_target_pairs={{0,20},{1,21},{2,22},{3,23},{4,16},{5,17},{6,18},{7,19},{8,28},{9,... | collective-permute-start | bytes 221192 | tf_op jit(solution)/shard_map/ppermute | solution.py:461
  71.3 0.6 collective-permute-start.18
  71.8 0.1 collective-permute-done.17.refs_4_
  71.9 2.7 %collective-permute-done.20.refs_7_ = f32[144,128]{1,0:T(8,128)S(1)} collective-permute-done((f32[144,128]{1,0:T(8,128)S(1)}, f32[144,128]{1,0:T(8,128)S(1)}, u32[]{:S(2)}, u32[]{:S(2)}) %collective-permute-start.20) | collective-permute-done | bytes 73760 | tf_op jit(solution)/shard_map/ppermute | solution.py:461
  74.6 1.3 %collective-permute-done.18.refs_5_ = f32[144,128]{1,0:T(8,128)S(1)} collective-permute-done((f32[144,128]{1,0:T(8,128)S(1)}, f32[144,128]{1,0:T(8,128)S(1)}, u32[]{:S(2)}, u32[]{:S(2)}) %collective-permute-start.18) | collective-permute-done | bytes 73760 | tf_op jit(solution)/shard_map/ppermute | solution.py:461
  75.9 1.7 %second_image.1 = (f32[3,144,128]{2,1,0:T(8,128)S(1)}, f32[3,144,128]{2,1,0:T(8,128)S(1)}, f32[32,128]{1,0:T(8,128)S(1)}) custom-call(f32[3,144,128]{2,1,0:T(8,128)S(1)} %get-tuple-element.48.refs_0_, f32[24,128]{1,0:T(8,128)S(1)} %collective-permute-done.14.refs_1_, f32[24,128]{1,0:T(8,128)S(1)} %collective-permute-done.15.refs_2_, ...), custom_call_target="tpu_custom_call" | custom-call | tf_op jit(solution)/shard_map/second_image/pallas_call | solution.py:426
  77.6 9.5 %all_to_all.35 = f32[32,1,128]{2,1,0:T(1,128)S(1)} all-to-all(f32[32,1,128]{2,1,0:T(1,128)S(1)} %bitcast.23), channel_id=1, replica_groups=mesh['gx'=2,'gy'=4,'gz'=4] {'gx','gy','gz'}, dimensions={0} | all-to-all | bytes 32768 | tf_op jit(solution)/shard_map/all_to_all | solution.py:478
  87.0 1.7 %finish.1 = (f32[3,64,128]{2,1,0:T(8,128)}, f32[3,64,128]{2,1,0:T(8,128)}) custom-call(f32[32,128]{1,0:T(8,128)S(1)} %bitcast.19, f32[3,64,128]{2,1,0:T(8,128)S(1)} %bitcast.17, f32[3,144,128]{2,1,0:T(8,128)S(1)} %get-tuple-element.54.refs_11_.search_ref, f32[3,144,128]{2,1,0:T(8,128)S(1)} %get-tuple-element.46.refs_0_.refs_12_.first_ref, ...), custom_call_target="tpu_custom_call" | custom-call | tf_op jit(solution)/shard_map/finish/pallas_call | solution.py:426
  (16 shorter events, 0.0 us)
Async XLA Ops:
  0.6 0.7 copy-start.4
  1.3 0.9 %copy-start.1 = (f32[3,8,8,128]{3,2,1,0:T(8,128)S(1)}, f32[3,8,8,128]{3,2,1,0:T(8,128)}, u32[]{:S(2)}) copy-start(f32[3,8,8,128]{3,2,1,0:T(8,128)} %param.5) | copy-start | bytes 294916
  2.2 0.8 copy-start.2
  2.9 0.7 copy-start.3
  5.1 3.1 %collective-permute-start = (f32[32,128]{1,0:T(8,128)S(1)}, f32[32,128]{1,0:T(8,128)S(1)}, u32[]{:S(2)}, u32[]{:S(2)}) collective-permute-start(f32[32,128]{1,0:T(8,128)S(1)} %get-tuple-element.32), channel_id=1, source_target_pairs={{0,1},{1,0},{2,3},{3,2},{4,5},{5,4},{6,7},{7,6},{8,9},{9,8},{10,11... | collective-permute-start | bytes 49160 | tf_op jit(solution)/shard_map/ppermute | solution.py:461
  5.6 4.0 %collective-permute-start.1 = (f32[32,128]{1,0:T(8,128)S(1)}, f32[32,128]{1,0:T(8,128)S(1)}, u32[]{:S(2)}, u32[]{:S(2)}) collective-permute-start(f32[32,128]{1,0:T(8,128)S(1)} %get-tuple-element.33), channel_id=1, source_target_pairs={{0,3},{1,2},{2,1},{3,0},{4,7},{5,6},{6,5},{7,4},{8,11},{9,10},{10,... | collective-permute-start | bytes 49160 | tf_op jit(solution)/shard_map/ppermute | solution.py:461
  9.6 18.9 %copy-start = (f32[36,1152]{1,0:T(8,128)S(1)}, f32[36,1152]{1,0:T(8,128)}, u32[]{:S(2)}) copy-start(f32[36,1152]{1,0:T(8,128)} %refs_4_.1) | copy-start | bytes 497668
  10.0 18.5 %collective-permute-start.2 = (f32[144,128]{1,0:T(8,128)S(1)}, f32[144,128]{1,0:T(8,128)S(1)}, u32[]{:S(2)}, u32[]{:S(2)}) collective-permute-start(f32[144,128]{1,0:T(8,128)S(1)} %get-tuple-element.34), channel_id=1, source_target_pairs={{0,4},{1,5},{2,6},{3,7},{4,0},{5,1},{6,2},{7,3},{8,12},{9,13},{10,... | collective-permute-start | bytes 221192 | tf_op jit(solution)/shard_map/ppermute | solution.py:461
  11.7 16.7 %collective-permute-start.3 = (f32[144,128]{1,0:T(8,128)S(1)}, f32[144,128]{1,0:T(8,128)S(1)}, u32[]{:S(2)}, u32[]{:S(2)}) collective-permute-start(f32[144,128]{1,0:T(8,128)S(1)} %get-tuple-element.35), channel_id=1, source_target_pairs={{0,16},{1,17},{2,18},{3,19},{4,8},{5,9},{6,10},{7,11},{8,4},{9,5},... | collective-permute-start | bytes 221192 | tf_op jit(solution)/shard_map/ppermute | solution.py:461
  13.3 15.2 %collective-permute-start.6 = (f32[144,128]{1,0:T(8,128)S(1)}, f32[144,128]{1,0:T(8,128)S(1)}, u32[]{:S(2)}, u32[]{:S(2)}) collective-permute-start(f32[144,128]{1,0:T(8,128)S(1)} %get-tuple-element.36), channel_id=1, source_target_pairs={{0,16},{1,17},{2,18},{3,19},{4,24},{5,25},{6,26},{7,27},{8,20},{9,... | collective-permute-start | bytes 221192 | tf_op jit(solution)/shard_map/ppermute | solution.py:461
  13.8 14.7 %collective-permute-start.5 = (f32[144,128]{1,0:T(8,128)S(1)}, f32[144,128]{1,0:T(8,128)S(1)}, u32[]{:S(2)}, u32[]{:S(2)}) collective-permute-start(f32[144,128]{1,0:T(8,128)S(1)} %get-tuple-element.36), channel_id=1, source_target_pairs={{0,20},{1,21},{2,22},{3,23},{4,16},{5,17},{6,18},{7,19},{8,28},{9,... | collective-permute-start | bytes 221192 | tf_op jit(solution)/shard_map/ppermute | solution.py:461
  15.9 12.7 %collective-permute-start.4 = (f32[144,128]{1,0:T(8,128)S(1)}, f32[144,128]{1,0:T(8,128)S(1)}, u32[]{:S(2)}, u32[]{:S(2)}) collective-permute-start(f32[144,128]{1,0:T(8,128)S(1)} %get-tuple-element.36), channel_id=1, source_target_pairs={{0,16},{1,17},{2,18},{3,19},{4,20},{5,21},{6,22},{7,23},{8,24},{9,... | collective-permute-start | bytes 221192 | tf_op jit(solution)/shard_map/ppermute | solution.py:461
  33.3 1.2 %collective-permute-start.7 = (f32[24,128]{1,0:T(8,128)S(1)}, f32[24,128]{1,0:T(8,128)S(1)}, u32[]{:S(2)}, u32[]{:S(2)}) collective-permute-start(f32[24,128]{1,0:T(8,128)S(1)} %get-tuple-element.40), channel_id=1, source_target_pairs={{0,1},{1,0},{2,3},{3,2},{4,5},{5,4},{6,7},{7,6},{8,9},{9,8},{10,11... | collective-permute-start | bytes 36872 | tf_op jit(solution)/shard_map/ppermute | solution.py:461
  33.4 3.2 %collective-permute-start.8 = (f32[24,128]{1,0:T(8,128)S(1)}, f32[24,128]{1,0:T(8,128)S(1)}, u32[]{:S(2)}, u32[]{:S(2)}) collective-permute-start(f32[24,128]{1,0:T(8,128)S(1)} %get-tuple-element.41), channel_id=1, source_target_pairs={{0,3},{1,2},{2,1},{3,0},{4,7},{5,6},{6,5},{7,4},{8,11},{9,10},{10,... | collective-permute-start | bytes 36872 | tf_op jit(solution)/shard_map/ppermute | solution.py:461
  36.9 5.6 %collective-permute-start.9 = (f32[144,128]{1,0:T(8,128)S(1)}, f32[144,128]{1,0:T(8,128)S(1)}, u32[]{:S(2)}, u32[]{:S(2)}) collective-permute-start(f32[144,128]{1,0:T(8,128)S(1)} %get-tuple-element.42), channel_id=1, source_target_pairs={{0,4},{1,5},{2,6},{3,7},{4,0},{5,1},{6,2},{7,3},{8,12},{9,13},{10,... | collective-permute-start | bytes 221192 | tf_op jit(solution)/shard_map/ppermute | solution.py:461
  37.5 5.1 %collective-permute-start.10 = (f32[144,128]{1,0:T(8,128)S(1)}, f32[144,128]{1,0:T(8,128)S(1)}, u32[]{:S(2)}, u32[]{:S(2)}) collective-permute-start(f32[144,128]{1,0:T(8,128)S(1)} %get-tuple-element.43), channel_id=1, source_target_pairs={{0,16},{1,17},{2,18},{3,19},{4,8},{5,9},{6,10},{7,11},{8,4},{9,5},... | collective-permute-start | bytes 221192 | tf_op jit(solution)/shard_map/ppermute | solution.py:461
  38.1 7.2 %collective-permute-start.13 = (f32[144,128]{1,0:T(8,128)S(1)}, f32[144,128]{1,0:T(8,128)S(1)}, u32[]{:S(2)}, u32[]{:S(2)}) collective-permute-start(f32[144,128]{1,0:T(8,128)S(1)} %get-tuple-element.44), channel_id=1, source_target_pairs={{0,16},{1,17},{2,18},{3,19},{4,24},{5,25},{6,26},{7,27},{8,20},{9,... | collective-permute-start | bytes 221192 | tf_op jit(solution)/shard_map/ppermute | solution.py:461
  39.5 5.8 %collective-permute-start.12 = (f32[144,128]{1,0:T(8,128)S(1)}, f32[144,128]{1,0:T(8,128)S(1)}, u32[]{:S(2)}, u32[]{:S(2)}) collective-permute-start(f32[144,128]{1,0:T(8,128)S(1)} %get-tuple-element.44), channel_id=1, source_target_pairs={{0,20},{1,21},{2,22},{3,23},{4,16},{5,17},{6,18},{7,19},{8,28},{9,... | collective-permute-start | bytes 221192 | tf_op jit(solution)/shard_map/ppermute | solution.py:461
  41.9 4.6 %collective-permute-start.11 = (f32[144,128]{1,0:T(8,128)S(1)}, f32[144,128]{1,0:T(8,128)S(1)}, u32[]{:S(2)}, u32[]{:S(2)}) collective-permute-start(f32[144,128]{1,0:T(8,128)S(1)} %get-tuple-element.44), channel_id=1, source_target_pairs={{0,16},{1,17},{2,18},{3,19},{4,20},{5,21},{6,22},{7,23},{8,24},{9,... | collective-permute-start | bytes 221192 | tf_op jit(solution)/shard_map/ppermute | solution.py:461
  62.7 1.2 %collective-permute-start.14 = (f32[24,128]{1,0:T(8,128)S(1)}, f32[24,128]{1,0:T(8,128)S(1)}, u32[]{:S(2)}, u32[]{:S(2)}) collective-permute-start(f32[24,128]{1,0:T(8,128)S(1)} %get-tuple-element.49), channel_id=1, source_target_pairs={{0,1},{1,0},{2,3},{3,2},{4,5},{5,4},{6,7},{7,6},{8,9},{9,8},{10,11... | collective-permute-start | bytes 36872 | tf_op jit(solution)/shard_map/ppermute | solution.py:461
  62.8 3.2 %collective-permute-start.15 = (f32[24,128]{1,0:T(8,128)S(1)}, f32[24,128]{1,0:T(8,128)S(1)}, u32[]{:S(2)}, u32[]{:S(2)}) collective-permute-start(f32[24,128]{1,0:T(8,128)S(1)} %get-tuple-element.50), channel_id=1, source_target_pairs={{0,3},{1,2},{2,1},{3,0},{4,7},{5,6},{6,5},{7,4},{8,11},{9,10},{10,... | collective-permute-start | bytes 36872 | tf_op jit(solution)/shard_map/ppermute | solution.py:461
  66.2 5.6 %collective-permute-start.16 = (f32[144,128]{1,0:T(8,128)S(1)}, f32[144,128]{1,0:T(8,128)S(1)}, u32[]{:S(2)}, u32[]{:S(2)}) collective-permute-start(f32[144,128]{1,0:T(8,128)S(1)} %get-tuple-element.51), channel_id=1, source_target_pairs={{0,4},{1,5},{2,6},{3,7},{4,0},{5,1},{6,2},{7,3},{8,12},{9,13},{10,... | collective-permute-start | bytes 221192 | tf_op jit(solution)/shard_map/ppermute | solution.py:461
  66.8 5.1 %collective-permute-start.17 = (f32[144,128]{1,0:T(8,128)S(1)}, f32[144,128]{1,0:T(8,128)S(1)}, u32[]{:S(2)}, u32[]{:S(2)}) collective-permute-start(f32[144,128]{1,0:T(8,128)S(1)} %get-tuple-element.52), channel_id=1, source_target_pairs={{0,16},{1,17},{2,18},{3,19},{4,8},{5,9},{6,10},{7,11},{8,4},{9,5},... | collective-permute-start | bytes 221192 | tf_op jit(solution)/shard_map/ppermute | solution.py:461
  67.4 7.2 %collective-permute-start.20 = (f32[144,128]{1,0:T(8,128)S(1)}, f32[144,128]{1,0:T(8,128)S(1)}, u32[]{:S(2)}, u32[]{:S(2)}) collective-permute-start(f32[144,128]{1,0:T(8,128)S(1)} %get-tuple-element.53), channel_id=1, source_target_pairs={{0,16},{1,17},{2,18},{3,19},{4,24},{5,25},{6,26},{7,27},{8,20},{9,... | collective-permute-start | bytes 221192 | tf_op jit(solution)/shard_map/ppermute | solution.py:461
  68.8 5.8 %collective-permute-start.19 = (f32[144,128]{1,0:T(8,128)S(1)}, f32[144,128]{1,0:T(8,128)S(1)}, u32[]{:S(2)}, u32[]{:S(2)}) collective-permute-start(f32[144,128]{1,0:T(8,128)S(1)} %get-tuple-element.53), channel_id=1, source_target_pairs={{0,20},{1,21},{2,22},{3,23},{4,16},{5,17},{6,18},{7,19},{8,28},{9,... | collective-permute-start | bytes 221192 | tf_op jit(solution)/shard_map/ppermute | solution.py:461
  71.3 4.6 %collective-permute-start.18 = (f32[144,128]{1,0:T(8,128)S(1)}, f32[144,128]{1,0:T(8,128)S(1)}, u32[]{:S(2)}, u32[]{:S(2)}) collective-permute-start(f32[144,128]{1,0:T(8,128)S(1)} %get-tuple-element.53), channel_id=1, source_target_pairs={{0,16},{1,17},{2,18},{3,19},{4,20},{5,21},{6,22},{7,23},{8,24},{9,... | collective-permute-start | bytes 221192 | tf_op jit(solution)/shard_map/ppermute | solution.py:461

commit v3 on v2

--- a/solution.py
+++ b/solution.py
@@ -143,16 +143,15 @@
     high_mask = inside & lane_range(across, sh.y + ex.down, ex.layers)
     span = ex.layers * sh.pitch
     below_y, above_y = sides(sh, 1, [ref[...] for ref in y_refs])
-    per_link = 1 + sh.y_links
+    per_link = len(x_refs) // sh.x_links
     sums = []
     for link in range(sh.x_links):
         straight, diagonal = x_refs[link * per_link], x_refs[link * per_link + 1 : (link + 1) * per_link]
-        below, above = sides(sh, 1, [ref[...] for ref in diagonal])
-        sums.append(
-            straight[...]
-            + pick(low_mask, shift(below, -sh.y))
-            + pick(high_mask, shift(above, sh.y))
-        )
+        total = straight[...]
+        if diagonal:
+            below, above = sides(sh, 1, [ref[...] for ref in diagonal])
+            total = total + pick(low_mask, shift(below, -sh.y)) + pick(high_mask, shift(above, sh.y))
+        sums.append(total)
     below_x, above_x = sides(sh, 0, sums)
     first = 1 if ex.up == -2 else 0
     last = ex.layers - 1 if ex.down + ex.layers == 2 else ex.layers
@@ -367,29 +366,24 @@
     )
 
 
-def coarse_sums(sh, nodes, field, count, sums, slots_ref):
+def coarse_sums(sh, nodes, field, count, sums):
     moments = tuple(field) + cross(coords(sh), field)
     for node in range(count):
         mask = nodes == float(node)
         for m in range(6):
             sums[node * 6 + m : node * 6 + m + 1, :] = fold_rows(pick(mask, moments[m]))
-    line = lane_sums(sums)[0:1]
-    slots_ref[...] = jnp.broadcast_to(line, slots_ref.shape)
+    flat = (sh.here(0) * sh.sizes[1] + sh.here(1)) * sh.sizes[2] + sh.here(2)
+    return pltpu.roll(lane_sums(sums), lax.rem(flat * (6 * count), LANES), 1)[0:1]
 
 
 def coarse_values(sh, nodes, received, inverse_ref, values):
     unknowns, total = inverse_ref.shape
-    column = lax.broadcasted_iota(jnp.int32, (1, total), 1)
-    owner = column // unknowns
-    place = column - owner * unknowns
-    spread = (lax.broadcasted_iota(jnp.int32, (LANES, total), 0) == place).astype(f32)
-    lines = jnp.dot(received, spread, precision=highest, preferred_element_type=f32)
-    mine = lax.broadcasted_iota(jnp.int32, lines.shape, 0) == owner
-    vector = jnp.sum(pick(mine, lines), axis=0, keepdims=True)
-    product = inverse_ref[...] * vector
-    part = product[:, 0:LANES]
-    for i in range(LANES, total, LANES):
-        part = part + product[:, i : i + LANES]
+    row = lax.broadcasted_iota(jnp.int32, received.shape, 0)
+    part = jnp.zeros((unknowns, LANES), f32)
+    for i in range(0, total, LANES):
+        owner = (i + lax.broadcasted_iota(jnp.int32, (1, LANES), 1)) // unknowns
+        vector = jnp.sum(pick(row == owner, received), axis=0, keepdims=True)
+        part = part + inverse_ref[:, i : i + LANES] * vector
     values[0:unknowns, :] = jnp.dot(
         part, jnp.ones((LANES, LANES), f32), precision=highest, preferred_element_type=f32
     )
@@ -422,15 +416,93 @@
     )
 
 
-def call(kernel, name, outs, ins, scratch=(), smem=()):
+def send_lines(sh, lines, slots_ref):
+    here = [sh.here(axis) for axis in range(3)]
+    corner = [lines[8 * i : 8 * i + 8, :] for i in range(4)]
+    top, bottom = lines[32:40, :], lines[40:48, :]
+    for x in range(sh.sizes[0]):
+        low_high = [jnp.where(x > here[0], corner[2 + high], corner[high]) for high in range(2)]
+        for y in range(sh.sizes[1]):
+            column = jnp.where(y > here[1], low_high[1], low_high[0])
+            for z in range(sh.sizes[2]):
+                slot = jnp.where(z == here[2] + 1, top, jnp.where(z == here[2] - 1, bottom, column))
+                place = 8 * ((x * sh.sizes[1] + y) * sh.sizes[2] + z)
+                slots_ref[place : place + 8, :] = slot
+
+
+def slot_from(sh, received_ref, step):
+    place, exists = 0, None
+    for axis in range(3):
+        index = sh.here(axis) + step[axis]
+        inside = (index >= 0) & (index < sh.sizes[axis])
+        exists = inside if exists is None else exists & inside
+        place = place * sh.sizes[axis] + jnp.clip(index, 0, sh.sizes[axis] - 1)
+    return scale(exists, received_ref[pl.ds(pl.multiple_of(place * 8, 8), 8), :])
+
+
+def repeat_twice(count):
+    row = lax.broadcasted_iota(jnp.int32, (2 * count, count), 0)
+    column = lax.broadcasted_iota(jnp.int32, (2 * count, count), 1)
+    return ((row >= 2 * column) & (row < 2 * column + 2)).astype(f32)
+
+
+def merge_lines(sh, received_ref, all_fields, rims, corners, label_z):
+    lane, along, across = sh.lane_grid(1)
+    inside = lane < sh.used
+    last = (sh.x + 1) * sh.pitch
+    x_mask = {-1: lane < sh.pitch, 0: (lane >= sh.pitch) & (lane < last), 1: (lane >= last) & inside}
+    y_mask = {-1: across < 0, 0: (across >= 0) & (across < sh.y), 1: across >= sh.y}
+    for dz in (-1, 1):
+        main = edge = jnp.zeros((8, LANES), f32)
+        for dx in (-1, 0, 1):
+            for dy in (-1, 0, 1):
+                slot = slot_from(sh, received_ref, (dx, dy, dz))
+                mask = x_mask[dx] & y_mask[dy]
+                main = main + pick(mask, shift(slot, dx * sh.x * sh.pitch + dy * sh.y))
+                if dx:
+                    edge = edge + pick(mask, shift(slot, dx * (sh.x - 1) * sh.pitch + dy * sh.y))
+        near = EDGE + sh.z if dz > 0 else EDGE - 1
+        for f in range(4):
+            all_fields[f, near : near + 1, :] += main[f : f + 1]
+        rims[3, near : near + 1, :] += edge[3:4]
+        all_fields[3, near + dz : near + dz + 1, :] += main[3:4]
+        rims[3, near + dz : near + dz + 1, :] += edge[3:4]
+    corners[...] = jnp.zeros(corners.shape, f32)
+    number = lax.broadcasted_iota(jnp.int32, (8, LANES), 0)
+    lanes, lanes_along, lanes_across = sh.lane_grid(8)
+    same = thick = lanes < 0
+    for i, (dx, dy) in enumerate(((-1, -1), (-1, 1), (1, -1), (1, 1))):
+        slot = slot_from(sh, received_ref, (dx, dy, 0))
+        for f in range(4):
+            corners[8 * f + i : 8 * f + i + 1, :] = slot[f : f + 1]
+        here = (number == i) & (lanes < sh.used)
+        at_x = lanes_along == (sh.x if dx > 0 else -1)
+        beyond = lanes_across >= sh.y if dy > 0 else lanes_across < 0
+        same = same | (here & at_x & (lanes_across == (sh.y if dy > 0 else -1)))
+        thick = thick | (here & at_x & beyond)
+    own = slice(EDGE, EDGE + sh.z)
+    for m in range(3):
+        all_fields[m, own, :] += to_lanes(corners[8 * m : 8 * m + 8, :], same.astype(f32))
+    by_z = lax.dot_general(
+        repeat_twice(label_z),
+        corners[24:32, 0:label_z],
+        (((1,), (1,)), ((), ())),
+        precision=highest,
+        preferred_element_type=f32,
+    )
+    columns = jnp.dot(by_z, thick.astype(f32), precision=highest, preferred_element_type=f32)
+    all_fields[3, own, :] += columns
+    rims[3, own, :] += columns
+
+
+def call(kernel, name, outs, ins, scratch=(), remote_ins=False):
+    space = pltpu.HBM if remote_ins else pltpu.VMEM
     return pl.pallas_call(
         kernel,
         out_shape=[jax.ShapeDtypeStruct(shape, f32) for shape in outs],
-        in_specs=[
-            pl.BlockSpec(memory_space=pltpu.SMEM if i in smem else pltpu.VMEM) for i in range(len(ins))
-        ],
+        in_specs=[pl.BlockSpec(memory_space=space) for _ in ins],
         out_specs=[pl.BlockSpec(memory_space=pltpu.VMEM) for _ in outs],
-        scratch_shapes=[pltpu.VMEM(shape, f32) for shape in scratch],
+        scratch_shapes=[pltpu.VMEM(shape, f32) if isinstance(shape, tuple) else shape for shape in scratch],
         compiler_params=pltpu.CompilerParams(vmem_limit_bytes=48 * 1024 * 1024),
         name=name,
     )(*ins)
@@ -465,12 +537,13 @@
     return [send(sh, message, {2: link}) for link, message in enumerate(messages)]
 
 
-def send_xy(sh, x_messages, y_messages):
+def send_xy(sh, x_messages, y_messages, diagonal=True):
     from_y = [send(sh, message, {1: link}) for link, message in enumerate(y_messages)]
     from_x = []
     for link, message in enumerate(x_messages):
         from_x.append(send(sh, message, {0: link}))
-        from_x.extend(send(sh, message, {0: link, 1: other}) for other in range(sh.y_links))
+        if diagonal:
+            from_x.extend(send(sh, message, {0: link, 1: other}) for other in range(sh.y_links))
     return from_y, from_x
 
 
@@ -538,10 +611,19 @@
     nodes_natural = coarse_nodes.reshape(sh.cells, sh.z)
     label_x, label_y, label_z = phase_labels.shape
 
-    def begin(natural_ref, labels_ref, moduli_ref, nodes_ref, field_ref, lanes_ref, slots_ref, *rest):
-        z_refs, (sums, stiff) = rest[: sh.z_links], rest[sh.z_links :]
+    def begin(natural_in, labels_in, moduli_in, nodes_in, field_ref, lanes_ref, slots_ref, *rest):
+        x_refs, y_refs = rest[: sh.x_links], rest[sh.x_links : sh.x_links + sh.y_links]
+        natural_ref, labels_ref, moduli_ref, nodes_ref, sems, sums, stiff, lines = rest[sh.x_links + sh.y_links :]
+        pairs = ((natural_in, natural_ref), (labels_in, labels_ref), (moduli_in, moduli_ref), (nodes_in, nodes_ref))
+        copies = [pltpu.make_async_copy(a, b, sems.at[i]) for i, (a, b) in enumerate(pairs)]
+        for copy in copies:
+            copy.start()
         select = selection(sh)
         field_ref[...] = jnp.zeros(field_ref.shape, f32)
+        sums[...] = jnp.zeros(sums.shape, f32)
+        lines[...] = jnp.zeros(lines.shape, f32)
+        for copy in copies:
+            copy.wait()
         residual = []
         for m in range(3):
             residual.append(to_lanes(natural_ref[m], select))
@@ -552,11 +634,8 @@
             for phase in range(sh.phases):
                 moduli = jnp.where(labels == phase, moduli_ref[phase], moduli)
             stiff[i * label_y : (i + 1) * label_y, :] = moduli
-        row = lax.broadcasted_iota(jnp.int32, (sh.z, label_z), 0)
-        column = lax.broadcasted_iota(jnp.int32, (sh.z, label_z), 1)
-        wide = ((row >= 2 * column) & (row < 2 * column + 2)).astype(f32)
         by_z = lax.dot_general(
-            wide, stiff[...], (((1,), (1,)), ((), ())), precision=highest, preferred_element_type=f32
+            repeat_twice(label_z), stiff[...], (((1,), (1,)), ((), ())), precision=highest, preferred_element_type=f32
         )
         lane, along, across = sh.lane_grid(label_x * label_y)
         inside = (along >= 0) & (along < sh.x) & (across >= 0) & (across < sh.y)
@@ -565,25 +644,50 @@
         field_ref[3, own, :] = jnp.dot(by_z, to_block, precision=highest, preferred_element_type=f32)
         nodes = to_lanes(nodes_ref[...].astype(f32) + 1.0, select) - 1.0
         lanes_ref[...] = nodes
-        sums[...] = jnp.zeros(sums.shape, f32)
-        coarse_sums(sh, nodes, residual, node_count, sums, slots_ref)
-        pack_z(sh, SPREAD, lambda f, start, count: field_ref[f, start : start + count, :], z_refs)
-
-    start_field, nodes, sums, *z_messages = call(
+        line = coarse_sums(sh, nodes, residual, node_count, sums)
+        for i, (cell, block) in enumerate(
+            (
+                (0, 0),
+                (sh.y - 1, label_y - 1),
+                ((sh.x - 1) * sh.y, (label_x - 1) * label_y),
+                (sh.cells - 1, label_x * label_y - 1),
+            )
+        ):
+            for m in range(3):
+                lines[8 * i + m : 8 * i + m + 1, :] = natural_ref[m, cell : cell + 1, :]
+            lines[8 * i + 3 : 8 * i + 4, 0:label_z] = stiff[block : block + 1, :]
+        for i, layer in ((4, EDGE + sh.z - 1), (5, EDGE)):
+            for f in range(4):
+                lines[8 * i + f : 8 * i + f + 1, :] = field_ref[f, layer : layer + 1, :]
+        for i in range(6):
+            lines[8 * i + 4 : 8 * i + 5, :] = line
+        send_lines(sh, lines, slots_ref)
+        pack_xy(sh, SPREAD, field_ref, x_refs, y_refs)
+
+    start_field, nodes, lines, *messages = call(
         begin,
         "begin",
-        [(4,) + plane, (sh.z, LANES), slots] + z_shape(SPREAD),
+        [(4,) + plane, (sh.z, LANES), (8 * sh.devices, LANES)] + [plane] * (sh.x_links + sh.y_links),
         [natural, phase_labels, phase_moduli, nodes_natural],
-        [(LANES, LANES), (label_x * label_y, label_z)],
-        smem=(2,),
-    )
-    from_z, from_y, from_x = exchange(sh, SPREAD, "spread", start_field, z_messages)
-    coarse = to_all(sums)
-
-    def finish_solve(index, v, nodes_ref, coarse_ref, inverse_ref, values, solution_ref, z_refs, ex):
+        [
+            natural.shape,
+            pltpu.VMEM(phase_labels.shape, jnp.int32),
+            pltpu.SMEM(phase_moduli.shape, f32),
+            pltpu.VMEM(nodes_natural.shape, jnp.int32),
+            pltpu.SemaphoreType.DMA((4,)),
+            (LANES, LANES),
+            (label_x * label_y, label_z),
+            (48, LANES),
+        ],
+        remote_ins=True,
+    )
+    from_y, from_x = send_xy(sh, messages[: sh.x_links], messages[sh.x_links :], diagonal=False)
+    lines = to_all(lines)
+
+    def finish_solve(index, v, nodes_ref, coarse, inverse_ref, values, solution_ref, z_refs, ex):
         for m in range(3):
             solution_ref[m] = v[index][m, EDGE : EDGE + sh.rows, :]
-        added = coarse_values(sh, nodes_ref[...], coarse_ref[...], inverse_ref, values)
+        added = coarse_values(sh, nodes_ref[...], coarse, inverse_ref, values)
         valid = nodes_ref[...] >= 0.0
         for m in range(3):
             solution_ref[m, own, :] += pick(valid, added[m])
@@ -591,13 +695,16 @@
 
     def first_solve(*refs):
         take = Taker(refs)
-        merging = take(1 + sh.z_links + sh.y_links + sh.x_links * (1 + sh.y_links))
-        nodes_ref, coarse_ref, inverse_ref = take(3)
+        field_ref = take.one()
+        y_refs, x_refs = take(sh.y_links), take(sh.x_links)
+        nodes_ref, lines_ref, inverse_ref = take(3)
         solution_ref, springs_ref = take(2)
         z_refs = take(sh.z_links)
-        all_fields, rims, stiff, stiff_rim, v0, v1, kv0, kv1, factor, values = take(10)
+        all_fields, rims, stiff, stiff_rim, v0, v1, kv0, kv1, factor, values, corners = take(11)
         clear_guards(sh, (stiff, stiff_rim, v0, v1, kv0, kv1))
-        merge_all(sh, SPREAD, Taker(merging), all_fields, rims, 0)
+        all_fields[...] = field_ref[...]
+        merge_xy(sh, SPREAD, all_fields, rims, 0, y_refs, x_refs)
+        merge_lines(sh, lines_ref, all_fields, rims, corners, label_z)
         put(stiff, 0, all_fields[3])
         put(stiff_rim, 0, rims[3])
         springs_ref[6] = all_fields[3]
@@ -607,14 +714,17 @@
         for f, entry in enumerate(own_block(sh, lane, (stiff, stiff_rim))):
             springs_ref[f] = entry
         index = local_solve(sh, all_fields, springs_ref, (v0, v1), (kv0, kv1), factor)
-        finish_solve(index, (v0, v1), nodes_ref, coarse_ref, inverse_ref, values, solution_ref, z_refs, DEEP)
+        coarse = lines_ref[pl.ds(4, sh.devices, stride=8), :]
+        finish_solve(index, (v0, v1), nodes_ref, coarse, inverse_ref, values, solution_ref, z_refs, DEEP)
 
     solved, springs, *z_messages = call(
         first_solve,
         "first_solve",
         [fields, (8,) + plane] + z_shape(DEEP),
-        [start_field, *from_z, *from_y, *from_x, nodes, coarse, coarse_inverse],
-        [(4,) + plane, (4,) + plane, (1, sh.tall, LANES), (1, sh.tall, LANES)] + [tall] * 4 + [fields, (LANES, LANES)],
+        [start_field, *from_y, *from_x, nodes, lines, coarse_inverse],
+        [(4,) + plane, (4,) + plane, (1, sh.tall, LANES), (1, sh.tall, LANES)]
+        + [tall] * 4
+        + [fields, (LANES, LANES), (32, LANES)],
     )
     from_z, from_y, from_x = exchange(sh, DEEP, "deep", solved, z_messages)
 
@@ -642,7 +752,8 @@
         for m in range(3):
             image_ref[m] = pick(keep, image[m])
         sums[...] = jnp.zeros(sums.shape, f32)
-        coarse_sums(sh, nodes_ref[...], [image_ref[m, own, :] for m in range(3)], node_count, sums, slots_ref)
+        line = coarse_sums(sh, nodes_ref[...], [image_ref[m, own, :] for m in range(3)], node_count, sums)
+        slots_ref[...] = jnp.broadcast_to(line, slots_ref.shape)
 
     search, image, sums = call(
         first_image,
@@ -661,7 +772,7 @@
         v0, v1, kv0, kv1, factor, values = take(6)
         clear_guards(sh, (v0, v1, kv0, kv1))
         index = local_solve(sh, image_ref, springs_ref, (v0, v1), (kv0, kv1), factor)
-        finish_solve(index, (v0, v1), nodes_ref, coarse_ref, inverse_ref, values, solution_ref, z_refs, NEAR)
+        finish_solve(index, (v0, v1), nodes_ref, coarse_ref[...], inverse_ref, values, solution_ref, z_refs, NEAR)
 
     solved, *z_messages = call(
         second_solve,

time: 89.1 us -> 83.9 us (0.942)
  blocking collectives: 30.1 us -> 20.3 us
  waiting for transfers between devices: 14.6 us -> 17.1 us
  starting transfers between devices: 23.1 us -> 24.8 us
    all_to_all x3 -> x2, blocking collectives: 30.1 us -> 20.3 us  [to_all(): return lax.all_to_all(slots, AXES, 0, 0, tiled=True)]
    all_to_all x0 -> x1, starting transfers between devices: none -> 7.3 us  [to_all(): return lax.all_to_all(slots, AXES, 0, 0, tiled=True)]
    ppermute x21 -> x17, starting transfers between devices: 23.1 us -> 17.5 us  [send(): return lax.ppermute(value, AXES, permutation(sh.sizes, moves))]
    ppermute x21 -> x17, waiting for transfers between devices: 14.6 us -> 17.1 us  [send(): return lax.ppermute(value, AXES, permutation(sh.sizes, moves))]
    pallas_call x9 -> x8, Pallas kernels: 17.2 us -> 17.7 us  [call(): pl.pallas_call(kernel, out_shape=[jax.ShapeDtypeStruct(shape, f32) for sh...]
    unnamed x10 -> x12, local copies, waits for them, and re-layouts: 3 us -> 3 us
  transfers between devices with their start and end apart: 21 -> 18, of which waited for: 11 -> 11; matrix products, arithmetic and copies ran while one was open for 0% -> 0% of each run, Pallas kernels for 0% -> 0%
where the time goes in v3:
time: 83.9 us; the launch traced here: 83.5 us
  starting transfers between devices  24.8 us (30%)
  blocking collectives  20.3 us (24%)
  Pallas kernels  17.7 us (21%)
  waiting for transfers between devices  17.1 us (20%)
  local copies, waits for them, and re-layouts  3 us (4%)
    all_to_all x2, blocking collectives, to_all(): return lax.all_to_all(slots, AXES, 0, 0, tiled=True)  20.3 us
    pallas_call x8, Pallas kernels, call(): pl.pallas_call(kernel, out_shape=[jax.ShapeDtypeStruct(shape, f32) for sh...  17.7 us
    ppermute x17, starting transfers between devices, send(): return lax.ppermute(value, AXES, permutation(sh.sizes, moves))  17.5 us
    ppermute x17, waiting for transfers between devices, send(): return lax.ppermute(value, AXES, permutation(sh.sizes, moves))  17.1 us
    all_to_all x1, starting transfers between devices, to_all(): return lax.all_to_all(slots, AXES, 0, 0, tiled=True)  7.3 us
    unnamed x12, local copies, waits for them, and re-layouts  3 us
  transfers between devices with their start and end apart: 18, of which 11 were waited for; matrix products, arithmetic and copies ran while one was open for 0% of the time, Pallas kernels for 0%

profile of v3, /device:TPU:0, one launch (start us, length us, event | category | flops | bytes accessed | tf_op | source)
XLA Modules:
  0.0 83.5 jit_solution(16532396086904242067)
XLA Ops:
  0.6 0.6 copy-done.5
  1.3 0.9 %copy-done.1 = f32[3,8,8,128]{3,2,1,0:T(8,128)S(1)} copy-done((f32[3,8,8,128]{3,2,1,0:T(8,128)S(1)}, f32[3,8,8,128]{3,2,1,0:T(8,128)}, u32[]{:S(2)}) %copy-start.1) | copy-done | bytes 98328
  2.2 0.8 copy-done.3
  2.9 0.7 copy-done.4
  3.6 2.4 %begin.1 = (f32[4,144,128]{2,1,0:T(8,128)S(1)}, f32[128,128]{1,0:T(8,128)S(1)}, f32[256,128]{1,0:T(8,128)}, f32[144,128]{1,0:T(8,128)S(1)}, f32[144,128]{1,0:T(8,128)S(1)}, /*index=5*/f32[144,128]{1,0:T(8,128)S(1)}) custom-call(f32[3,64,128]{2,1,0:T(8,128)S(1)} %bitcast.15, s32[4,4,64]{2,1,0:T(4,128)S(1)} %copy-done.4, f32[8]{0:T(128)S(1)} %copy-done.5, ...), custom_call_target="tpu_custom_call" | custom-call | tf_op jit(solution)/shard_map/begin/pallas_call | solution.py:500
  6.0 7.3 %all-to-all-start = ((f32[32,8,128]{2,1,0:T(8,128)}), f32[32,8,128]{2,1,0:T(8,128)S(1)}, u32[]{:S(2)}, u32[]{:S(2)}) async-start(f32[32,8,128]{2,1,0:T(8,128)} %bitcast.2), calls=%async_computation | async-start | bytes 262144 | tf_op jit(solution)/shard_map/all_to_all | solution.py:551
  13.3 1.8 %collective-permute-start = (f32[144,128]{1,0:T(8,128)S(1)}, f32[144,128]{1,0:T(8,128)S(1)}, u32[]{:S(2)}, u32[]{:S(2)}) collective-permute-start(f32[144,128]{1,0:T(8,128)S(1)} %get-tuple-element.30), channel_id=1, source_target_pairs={{0,4},{1,5},{2,6},{3,7},{4,0},{5,1},{6,2},{7,3},{8,12},{9,13},{10,... | collective-permute-start | bytes 221192 | tf_op jit(solution)/shard_map/ppermute | solution.py:533
  15.2 1.5 %collective-permute-start.1 = (f32[144,128]{1,0:T(8,128)S(1)}, f32[144,128]{1,0:T(8,128)S(1)}, u32[]{:S(2)}, u32[]{:S(2)}) collective-permute-start(f32[144,128]{1,0:T(8,128)S(1)} %get-tuple-element.31), channel_id=1, source_target_pairs={{0,16},{1,17},{2,18},{3,19},{4,8},{5,9},{6,10},{7,11},{8,4},{9,5},... | collective-permute-start | bytes 221192 | tf_op jit(solution)/shard_map/ppermute | solution.py:533
  16.6 0.6 collective-permute-start.2
  17.2 2.3 %collective-permute-done.refs_1_ = f32[144,128]{1,0:T(8,128)S(1)} collective-permute-done((f32[144,128]{1,0:T(8,128)S(1)}, f32[144,128]{1,0:T(8,128)S(1)}, u32[]{:S(2)}, u32[]{:S(2)}) %collective-permute-start) | collective-permute-done | bytes 73760 | tf_op jit(solution)/shard_map/ppermute | solution.py:533
  19.5 1.4 %collective-permute-done.1.refs_2_ = f32[144,128]{1,0:T(8,128)S(1)} collective-permute-done((f32[144,128]{1,0:T(8,128)S(1)}, f32[144,128]{1,0:T(8,128)S(1)}, u32[]{:S(2)}, u32[]{:S(2)}) %collective-permute-start.1) | collective-permute-done | bytes 73760 | tf_op jit(solution)/shard_map/ppermute | solution.py:533
  20.9 0.9 %collective-permute-done.2.refs_3_ = f32[144,128]{1,0:T(8,128)S(1)} collective-permute-done((f32[144,128]{1,0:T(8,128)S(1)}, f32[144,128]{1,0:T(8,128)S(1)}, u32[]{:S(2)}, u32[]{:S(2)}) %collective-permute-start.2) | collective-permute-done | bytes 73760 | tf_op jit(solution)/shard_map/ppermute | solution.py:533
  21.8 0.0 all-to-all-done
  21.8 4.8 %first_solve.1 = (f32[3,144,128]{2,1,0:T(8,128)S(1)}, f32[8,144,128]{2,1,0:T(8,128)S(1)}, f32[24,128]{1,0:T(8,128)S(1)}, f32[24,128]{1,0:T(8,128)S(1)}) custom-call(f32[4,144,128]{2,1,0:T(8,128)S(1)} %get-tuple-element.29.refs_0_.refs_10_, f32[144,128]{1,0:T(8,128)S(1)} %collective-permute-done.refs_1_, f32[144,128]{1,0:T(8,128)S(1)} %collective-permute-done.1.refs_2_, ...), custom_call_target="tpu_custom_call" | custom-call | tf_op jit(solution)/shard_map/first_solve/pallas_call | solution.py:500
  26.6 0.6 collective-permute-start.3
  27.1 1.0 %collective-permute-start.4 = (f32[24,128]{1,0:T(8,128)S(1)}, f32[24,128]{1,0:T(8,128)S(1)}, u32[]{:S(2)}, u32[]{:S(2)}) collective-permute-start(f32[24,128]{1,0:T(8,128)S(1)} %get-tuple-element.37), channel_id=1, source_target_pairs={{0,3},{1,2},{2,1},{3,0},{4,7},{5,6},{6,5},{7,4},{8,11},{9,10},{10,... | collective-permute-start | bytes 36872 | tf_op jit(solution)/shard_map/ppermute | solution.py:533
  28.1 0.0 collective-permute-done.3.refs_1_
  28.1 2.1 %collective-permute-done.4.refs_2_ = f32[24,128]{1,0:T(8,128)S(1)} collective-permute-done((f32[24,128]{1,0:T(8,128)S(1)}, f32[24,128]{1,0:T(8,128)S(1)}, u32[]{:S(2)}, u32[]{:S(2)}) %collective-permute-start.4) | collective-permute-done | bytes 12320 | tf_op jit(solution)/shard_map/ppermute | solution.py:533
  30.2 0.3 deep.1
  30.5 0.4 collective-permute-start.5
  31.0 1.4 %collective-permute-start.6 = (f32[144,128]{1,0:T(8,128)S(1)}, f32[144,128]{1,0:T(8,128)S(1)}, u32[]{:S(2)}, u32[]{:S(2)}) collective-permute-start(f32[144,128]{1,0:T(8,128)S(1)} %get-tuple-element.39), channel_id=1, source_target_pairs={{0,16},{1,17},{2,18},{3,19},{4,8},{5,9},{6,10},{7,11},{8,4},{9,5},... | collective-permute-start | bytes 221192 | tf_op jit(solution)/shard_map/ppermute | solution.py:533
  32.4 0.6 collective-permute-start.9
  33.0 2.6 %collective-permute-start.8 = (f32[144,128]{1,0:T(8,128)S(1)}, f32[144,128]{1,0:T(8,128)S(1)}, u32[]{:S(2)}, u32[]{:S(2)}) collective-permute-start(f32[144,128]{1,0:T(8,128)S(1)} %get-tuple-element.40), channel_id=1, source_target_pairs={{0,20},{1,21},{2,22},{3,23},{4,16},{5,17},{6,18},{7,19},{8,28},{9,... | collective-permute-start | bytes 221192 | tf_op jit(solution)/shard_map/ppermute | solution.py:533
  35.5 0.8 collective-permute-start.7
  36.3 0.0 collective-permute-done.6.refs_4_
  36.3 2.7 %collective-permute-done.9.refs_7_ = f32[144,128]{1,0:T(8,128)S(1)} collective-permute-done((f32[144,128]{1,0:T(8,128)S(1)}, f32[144,128]{1,0:T(8,128)S(1)}, u32[]{:S(2)}, u32[]{:S(2)}) %collective-permute-start.9) | collective-permute-done | bytes 73760 | tf_op jit(solution)/shard_map/ppermute | solution.py:533
  39.0 0.0 collective-permute-done.8.refs_6_
  39.0 1.0 %collective-permute-done.7.refs_5_ = f32[144,128]{1,0:T(8,128)S(1)} collective-permute-done((f32[144,128]{1,0:T(8,128)S(1)}, f32[144,128]{1,0:T(8,128)S(1)}, u32[]{:S(2)}, u32[]{:S(2)}) %collective-permute-start.7) | collective-permute-done | bytes 73760 | tf_op jit(solution)/shard_map/ppermute | solution.py:533
  40.1 2.8 %first_image.1 = (f32[3,144,128]{2,1,0:T(8,128)S(1)}, f32[3,144,128]{2,1,0:T(8,128)S(1)}, f32[32,128]{1,0:T(8,128)S(1)}) custom-call(f32[3,144,128]{2,1,0:T(8,128)S(1)} %get-tuple-element.35.refs_0_, f32[24,128]{1,0:T(8,128)S(1)} %collective-permute-done.3.refs_1_, f32[24,128]{1,0:T(8,128)S(1)} %collective-permute-done.4.refs_2_, ...), custom_call_target="tpu_custom_call" | custom-call | tf_op jit(solution)/shard_map/first_image/pallas_call | solution.py:500
  42.8 10.8 %all_to_all.33 = f32[32,1,128]{2,1,0:T(1,128)S(1)} all-to-all(f32[32,1,128]{2,1,0:T(1,128)S(1)} %bitcast.21), channel_id=1, replica_groups=mesh['gx'=2,'gy'=4,'gz'=4] {'gx','gy','gz'}, dimensions={0} | all-to-all | bytes 32768 | tf_op jit(solution)/shard_map/all_to_all | solution.py:551
  53.6 3.8 %second_solve.1 = (f32[3,144,128]{2,1,0:T(8,128)S(1)}, f32[24,128]{1,0:T(8,128)S(1)}, f32[24,128]{1,0:T(8,128)S(1)}) custom-call(f32[3,144,128]{2,1,0:T(8,128)S(1)} %get-tuple-element.42.refs_0_.refs_12_.first_ref, f32[8,144,128]{2,1,0:T(8,128)S(1)} %get-tuple-element.41.refs_9_.refs_1_, f32[128,128]{1,0:T(8,128)S(1)} %get-tuple-element.33.refs_4_.refs_8_.refs_2_, ...), custom_call_target="tpu_custom_call" | custom-call | tf_op jit(solution)/shard_map/second_solve/pallas_call | solution.py:500
  57.4 0.1 collective-permute-start.10
  57.5 0.7 collective-permute-start.11
  58.2 0.5 collective-permute-done.10.refs_1_
  58.7 2.0 %collective-permute-done.11.refs_2_ = f32[24,128]{1,0:T(8,128)S(1)} collective-permute-done((f32[24,128]{1,0:T(8,128)S(1)}, f32[24,128]{1,0:T(8,128)S(1)}, u32[]{:S(2)}, u32[]{:S(2)}) %collective-permute-start.11) | collective-permute-done | bytes 12320 | tf_op jit(solution)/shard_map/ppermute | solution.py:533
  60.7 0.3 near.1
  61.0 0.6 collective-permute-start.12
  61.6 0.6 collective-permute-start.13
  62.2 1.4 %collective-permute-start.16 = (f32[144,128]{1,0:T(8,128)S(1)}, f32[144,128]{1,0:T(8,128)S(1)}, u32[]{:S(2)}, u32[]{:S(2)}) collective-permute-start(f32[144,128]{1,0:T(8,128)S(1)} %get-tuple-element.49), channel_id=1, source_target_pairs={{0,16},{1,17},{2,18},{3,19},{4,24},{5,25},{6,26},{7,27},{8,20},{9,... | collective-permute-start | bytes 221192 | tf_op jit(solution)/shard_map/ppermute | solution.py:533
  63.6 2.4 %collective-permute-start.15 = (f32[144,128]{1,0:T(8,128)S(1)}, f32[144,128]{1,0:T(8,128)S(1)}, u32[]{:S(2)}, u32[]{:S(2)}) collective-permute-start(f32[144,128]{1,0:T(8,128)S(1)} %get-tuple-element.49), channel_id=1, source_target_pairs={{0,20},{1,21},{2,22},{3,23},{4,16},{5,17},{6,18},{7,19},{8,28},{9,... | collective-permute-start | bytes 221192 | tf_op jit(solution)/shard_map/ppermute | solution.py:533
  66.0 0.6 collective-permute-start.14
  66.6 0.1 collective-permute-done.13.refs_4_
  66.7 2.7 %collective-permute-done.16.refs_7_ = f32[144,128]{1,0:T(8,128)S(1)} collective-permute-done((f32[144,128]{1,0:T(8,128)S(1)}, f32[144,128]{1,0:T(8,128)S(1)}, u32[]{:S(2)}, u32[]{:S(2)}) %collective-permute-start.16) | collective-permute-done | bytes 73760 | tf_op jit(solution)/shard_map/ppermute | solution.py:533
  69.3 0.0 collective-permute-done.15.refs_6_
  69.3 1.3 %collective-permute-done.14.refs_5_ = f32[144,128]{1,0:T(8,128)S(1)} collective-permute-done((f32[144,128]{1,0:T(8,128)S(1)}, f32[144,128]{1,0:T(8,128)S(1)}, u32[]{:S(2)}, u32[]{:S(2)}) %collective-permute-start.14) | collective-permute-done | bytes 73760 | tf_op jit(solution)/shard_map/ppermute | solution.py:533
  70.6 1.7 %second_image.1 = (f32[3,144,128]{2,1,0:T(8,128)S(1)}, f32[3,144,128]{2,1,0:T(8,128)S(1)}, f32[32,128]{1,0:T(8,128)S(1)}) custom-call(f32[3,144,128]{2,1,0:T(8,128)S(1)} %get-tuple-element.44.refs_0_, f32[24,128]{1,0:T(8,128)S(1)} %collective-permute-done.10.refs_1_, f32[24,128]{1,0:T(8,128)S(1)} %collective-permute-done.11.refs_2_, ...), custom_call_target="tpu_custom_call" | custom-call | tf_op jit(solution)/shard_map/second_image/pallas_call | solution.py:500
  72.3 9.5 %all_to_all.34 = f32[32,1,128]{2,1,0:T(1,128)S(1)} all-to-all(f32[32,1,128]{2,1,0:T(1,128)S(1)} %bitcast.20), channel_id=1, replica_groups=mesh['gx'=2,'gy'=4,'gz'=4] {'gx','gy','gz'}, dimensions={0} | all-to-all | bytes 32768 | tf_op jit(solution)/shard_map/all_to_all | solution.py:551
  81.8 1.7 %finish.1 = (f32[3,64,128]{2,1,0:T(8,128)}, f32[3,64,128]{2,1,0:T(8,128)}) custom-call(f32[32,128]{1,0:T(8,128)S(1)} %bitcast.17, f32[3,64,128]{2,1,0:T(8,128)S(1)} %bitcast.16, f32[3,144,128]{2,1,0:T(8,128)S(1)} %get-tuple-element.50.refs_11_.search_ref, f32[3,144,128]{2,1,0:T(8,128)S(1)} %get-tuple-element.42.refs_0_.refs_12_.first_ref, ...), custom_call_target="tpu_custom_call" | custom-call | tf_op jit(solution)/shard_map/finish/pallas_call | solution.py:500
  (10 shorter events, 0.0 us)
Async XLA Ops:
  0.6 0.7 copy-start.5
  1.3 0.9 %copy-start.1 = (f32[3,8,8,128]{3,2,1,0:T(8,128)S(1)}, f32[3,8,8,128]{3,2,1,0:T(8,128)}, u32[]{:S(2)}) copy-start(f32[3,8,8,128]{3,2,1,0:T(8,128)} %param.5) | copy-start | bytes 294916
  2.2 0.8 copy-start.3
  2.9 0.7 copy-start.4
  3.6 18.2 %copy-start = (f32[36,1152]{1,0:T(8,128)S(1)}, f32[36,1152]{1,0:T(8,128)}, u32[]{:S(2)}) copy-start(f32[36,1152]{1,0:T(8,128)} %refs_4_.1) | copy-start | bytes 497668
  6.0 15.8 %all-to-all-start = ((f32[32,8,128]{2,1,0:T(8,128)}), f32[32,8,128]{2,1,0:T(8,128)S(1)}, u32[]{:S(2)}, u32[]{:S(2)}) async-start(f32[32,8,128]{2,1,0:T(8,128)} %bitcast.2), calls=%async_computation | async-start | bytes 262144 | tf_op jit(solution)/shard_map/all_to_all | solution.py:551
  13.3 6.2 %collective-permute-start = (f32[144,128]{1,0:T(8,128)S(1)}, f32[144,128]{1,0:T(8,128)S(1)}, u32[]{:S(2)}, u32[]{:S(2)}) collective-permute-start(f32[144,128]{1,0:T(8,128)S(1)} %get-tuple-element.30), channel_id=1, source_target_pairs={{0,4},{1,5},{2,6},{3,7},{4,0},{5,1},{6,2},{7,3},{8,12},{9,13},{10,... | collective-permute-start | bytes 221192 | tf_op jit(solution)/shard_map/ppermute | solution.py:533
  15.2 5.7 %collective-permute-start.1 = (f32[144,128]{1,0:T(8,128)S(1)}, f32[144,128]{1,0:T(8,128)S(1)}, u32[]{:S(2)}, u32[]{:S(2)}) collective-permute-start(f32[144,128]{1,0:T(8,128)S(1)} %get-tuple-element.31), channel_id=1, source_target_pairs={{0,16},{1,17},{2,18},{3,19},{4,8},{5,9},{6,10},{7,11},{8,4},{9,5},... | collective-permute-start | bytes 221192 | tf_op jit(solution)/shard_map/ppermute | solution.py:533
  16.6 5.2 %collective-permute-start.2 = (f32[144,128]{1,0:T(8,128)S(1)}, f32[144,128]{1,0:T(8,128)S(1)}, u32[]{:S(2)}, u32[]{:S(2)}) collective-permute-start(f32[144,128]{1,0:T(8,128)S(1)} %get-tuple-element.32), channel_id=1, source_target_pairs={{0,16},{1,17},{2,18},{3,19},{4,20},{5,21},{6,22},{7,23},{8,24},{9,... | collective-permute-start | bytes 221192 | tf_op jit(solution)/shard_map/ppermute | solution.py:533
  26.6 1.5 %collective-permute-start.3 = (f32[24,128]{1,0:T(8,128)S(1)}, f32[24,128]{1,0:T(8,128)S(1)}, u32[]{:S(2)}, u32[]{:S(2)}) collective-permute-start(f32[24,128]{1,0:T(8,128)S(1)} %get-tuple-element.36), channel_id=1, source_target_pairs={{0,1},{1,0},{2,3},{3,2},{4,5},{5,4},{6,7},{7,6},{8,9},{9,8},{10,11... | collective-permute-start | bytes 36872 | tf_op jit(solution)/shard_map/ppermute | solution.py:533
  27.1 3.1 %collective-permute-start.4 = (f32[24,128]{1,0:T(8,128)S(1)}, f32[24,128]{1,0:T(8,128)S(1)}, u32[]{:S(2)}, u32[]{:S(2)}) collective-permute-start(f32[24,128]{1,0:T(8,128)S(1)} %get-tuple-element.37), channel_id=1, source_target_pairs={{0,3},{1,2},{2,1},{3,0},{4,7},{5,6},{6,5},{7,4},{8,11},{9,10},{10,... | collective-permute-start | bytes 36872 | tf_op jit(solution)/shard_map/ppermute | solution.py:533
  30.5 5.8 %collective-permute-start.5 = (f32[144,128]{1,0:T(8,128)S(1)}, f32[144,128]{1,0:T(8,128)S(1)}, u32[]{:S(2)}, u32[]{:S(2)}) collective-permute-start(f32[144,128]{1,0:T(8,128)S(1)} %get-tuple-element.38), channel_id=1, source_target_pairs={{0,4},{1,5},{2,6},{3,7},{4,0},{5,1},{6,2},{7,3},{8,12},{9,13},{10,... | collective-permute-start | bytes 221192 | tf_op jit(solution)/shard_map/ppermute | solution.py:533
  31.0 5.4 %collective-permute-start.6 = (f32[144,128]{1,0:T(8,128)S(1)}, f32[144,128]{1,0:T(8,128)S(1)}, u32[]{:S(2)}, u32[]{:S(2)}) collective-permute-start(f32[144,128]{1,0:T(8,128)S(1)} %get-tuple-element.39), channel_id=1, source_target_pairs={{0,16},{1,17},{2,18},{3,19},{4,8},{5,9},{6,10},{7,11},{8,4},{9,5},... | collective-permute-start | bytes 221192 | tf_op jit(solution)/shard_map/ppermute | solution.py:533
  32.4 6.7 %collective-permute-start.9 = (f32[144,128]{1,0:T(8,128)S(1)}, f32[144,128]{1,0:T(8,128)S(1)}, u32[]{:S(2)}, u32[]{:S(2)}) collective-permute-start(f32[144,128]{1,0:T(8,128)S(1)} %get-tuple-element.40), channel_id=1, source_target_pairs={{0,16},{1,17},{2,18},{3,19},{4,24},{5,25},{6,26},{7,27},{8,20},{9,... | collective-permute-start | bytes 221192 | tf_op jit(solution)/shard_map/ppermute | solution.py:533
  33.0 6.0 %collective-permute-start.8 = (f32[144,128]{1,0:T(8,128)S(1)}, f32[144,128]{1,0:T(8,128)S(1)}, u32[]{:S(2)}, u32[]{:S(2)}) collective-permute-start(f32[144,128]{1,0:T(8,128)S(1)} %get-tuple-element.40), channel_id=1, source_target_pairs={{0,20},{1,21},{2,22},{3,23},{4,16},{5,17},{6,18},{7,19},{8,28},{9,... | collective-permute-start | bytes 221192 | tf_op jit(solution)/shard_map/ppermute | solution.py:533
  35.5 4.5 %collective-permute-start.7 = (f32[144,128]{1,0:T(8,128)S(1)}, f32[144,128]{1,0:T(8,128)S(1)}, u32[]{:S(2)}, u32[]{:S(2)}) collective-permute-start(f32[144,128]{1,0:T(8,128)S(1)} %get-tuple-element.40), channel_id=1, source_target_pairs={{0,16},{1,17},{2,18},{3,19},{4,20},{5,21},{6,22},{7,23},{8,24},{9,... | collective-permute-start | bytes 221192 | tf_op jit(solution)/shard_map/ppermute | solution.py:533
  57.4 1.2 %collective-permute-start.10 = (f32[24,128]{1,0:T(8,128)S(1)}, f32[24,128]{1,0:T(8,128)S(1)}, u32[]{:S(2)}, u32[]{:S(2)}) collective-permute-start(f32[24,128]{1,0:T(8,128)S(1)} %get-tuple-element.45), channel_id=1, source_target_pairs={{0,1},{1,0},{2,3},{3,2},{4,5},{5,4},{6,7},{7,6},{8,9},{9,8},{10,11... | collective-permute-start | bytes 36872 | tf_op jit(solution)/shard_map/ppermute | solution.py:533
  57.5 3.2 %collective-permute-start.11 = (f32[24,128]{1,0:T(8,128)S(1)}, f32[24,128]{1,0:T(8,128)S(1)}, u32[]{:S(2)}, u32[]{:S(2)}) collective-permute-start(f32[24,128]{1,0:T(8,128)S(1)} %get-tuple-element.46), channel_id=1, source_target_pairs={{0,3},{1,2},{2,1},{3,0},{4,7},{5,6},{6,5},{7,4},{8,11},{9,10},{10,... | collective-permute-start | bytes 36872 | tf_op jit(solution)/shard_map/ppermute | solution.py:533
  61.0 5.6 %collective-permute-start.12 = (f32[144,128]{1,0:T(8,128)S(1)}, f32[144,128]{1,0:T(8,128)S(1)}, u32[]{:S(2)}, u32[]{:S(2)}) collective-permute-start(f32[144,128]{1,0:T(8,128)S(1)} %get-tuple-element.47), channel_id=1, source_target_pairs={{0,4},{1,5},{2,6},{3,7},{4,0},{5,1},{6,2},{7,3},{8,12},{9,13},{10,... | collective-permute-start | bytes 221192 | tf_op jit(solution)/shard_map/ppermute | solution.py:533
  61.6 5.1 %collective-permute-start.13 = (f32[144,128]{1,0:T(8,128)S(1)}, f32[144,128]{1,0:T(8,128)S(1)}, u32[]{:S(2)}, u32[]{:S(2)}) collective-permute-start(f32[144,128]{1,0:T(8,128)S(1)} %get-tuple-element.48), channel_id=1, source_target_pairs={{0,16},{1,17},{2,18},{3,19},{4,8},{5,9},{6,10},{7,11},{8,4},{9,5},... | collective-permute-start | bytes 221192 | tf_op jit(solution)/shard_map/ppermute | solution.py:533
  62.2 7.2 %collective-permute-start.16 = (f32[144,128]{1,0:T(8,128)S(1)}, f32[144,128]{1,0:T(8,128)S(1)}, u32[]{:S(2)}, u32[]{:S(2)}) collective-permute-start(f32[144,128]{1,0:T(8,128)S(1)} %get-tuple-element.49), channel_id=1, source_target_pairs={{0,16},{1,17},{2,18},{3,19},{4,24},{5,25},{6,26},{7,27},{8,20},{9,... | collective-permute-start | bytes 221192 | tf_op jit(solution)/shard_map/ppermute | solution.py:533
  63.6 5.8 %collective-permute-start.15 = (f32[144,128]{1,0:T(8,128)S(1)}, f32[144,128]{1,0:T(8,128)S(1)}, u32[]{:S(2)}, u32[]{:S(2)}) collective-permute-start(f32[144,128]{1,0:T(8,128)S(1)} %get-tuple-element.49), channel_id=1, source_target_pairs={{0,20},{1,21},{2,22},{3,23},{4,16},{5,17},{6,18},{7,19},{8,28},{9,... | collective-permute-start | bytes 221192 | tf_op jit(solution)/shard_map/ppermute | solution.py:533
  66.0 4.6 %collective-permute-start.14 = (f32[144,128]{1,0:T(8,128)S(1)}, f32[144,128]{1,0:T(8,128)S(1)}, u32[]{:S(2)}, u32[]{:S(2)}) collective-permute-start(f32[144,128]{1,0:T(8,128)S(1)} %get-tuple-element.49), channel_id=1, source_target_pairs={{0,16},{1,17},{2,18},{3,19},{4,20},{5,21},{6,22},{7,23},{8,24},{9,... | collective-permute-start | bytes 221192 | tf_op jit(solution)/shard_map/ppermute | solution.py:533
  70.6 11.2 %copy-start.2 = (f32[3,8,8,128]{3,2,1,0:T(8,128)S(1)}, f32[3,8,8,128]{3,2,1,0:T(8,128)}, u32[]{:S(2)}) copy-start(f32[3,8,8,128]{3,2,1,0:T(8,128)} %param.5) | copy-start | bytes 294916

commit v4 on v3

--- a/solution.py
+++ b/solution.py
@@ -24,7 +24,6 @@
         self.fields, self.layers, self.up, self.down = fields, layers, up, down
 
 
-SPREAD = Exchange(4, 2, -2, 0)
 DEEP = Exchange(3, 3, -2, -1)
 NEAR = Exchange(3, 2, -1, -1)
 
@@ -109,31 +108,64 @@
         scratch[f, high : high + ex.layers, :] += above[8 * f : 8 * f + ex.layers]
 
 
-def pack_xy(sh, ex, scratch, x_refs, y_refs):
+def fold(sh, value, layers, start=None):
+    folds = sh.pitch // layers
+    height = -(-sh.rows // (8 * folds)) * 8
+    lane, _, across = sh.lane_grid(1)
+    total = jnp.zeros((height, LANES), f32)
+    for i, first in enumerate(range(0, sh.rows, height)):
+        part = value[first : first + height]
+        if start is not None:
+            part = pick((lane < sh.used) & lane_range(across, start, layers), part)
+        part = shift(part, i * layers - (0 if start is None else start + 2))
+        if part.shape[0] < height:
+            part = jnp.concatenate([part, jnp.zeros((height - part.shape[0], LANES), f32)], axis=0)
+        total = total + part
+    return total
+
+
+def folded_shape(sh, layers):
+    return (-(-sh.rows // (8 * (sh.pitch // layers))) * 8, LANES)
+
+
+def unfold(sh, message, layers, start):
+    height = message.shape[0]
+    lane, _, across = sh.lane_grid(1)
+    mask = (lane < sh.used) & lane_range(across, start, layers)
+    parts = []
+    for i, first in enumerate(range(0, sh.rows, height)):
+        part = message[0 : min(height, sh.rows - first)]
+        parts.append(pick(mask, shift(part, start + 2 - i * layers)))
+    return jnp.concatenate(parts, axis=0) if len(parts) > 1 else parts[0]
+
+
+def pack_xy(sh, ex, scratch, x_refs, y_refs, corner_refs):
     rows = sh.rows
     lane, _, across = sh.lane_grid(1)
     even_x, even_y = sh.here(0) % 2 == 0, sh.here(1) % 2 == 0
     span = ex.layers * sh.pitch
     x_up = x_down = y_up = y_down = jnp.zeros((rows, LANES), f32)
+    inside = lane < sh.used
+    y_above, y_below = sh.y + ex.up, ex.down
     for f in range(ex.fields):
         value = scratch[f]
         start = (sh.x + ex.up + 1) * sh.pitch
         x_up = x_up + shift(pick(lane_range(lane, start, span), value), f * span - start)
         start = (ex.down + 1) * sh.pitch
         x_down = x_down + shift(pick(lane_range(lane, start, span), value), f * span - start)
-        inside = lane < sh.used
-        start = sh.y + ex.up
-        y_up = y_up + shift(
-            pick(inside & lane_range(across, start, ex.layers), value), f * ex.layers - start - 2
-        )
-        start = ex.down
-        y_down = y_down + shift(
-            pick(inside & lane_range(across, start, ex.layers), value), f * ex.layers - start - 2
-        )
-    for ref, message in zip(x_refs, pair(sh.x_links, even_x, x_up, x_down)):
-        ref[...] = message
+        mask = inside & lane_range(across, y_above, ex.layers)
+        y_up = y_up + shift(pick(mask, value), f * ex.layers - y_above - 2)
+        mask = inside & lane_range(across, y_below, ex.layers)
+        y_down = y_down + shift(pick(mask, value), f * ex.layers - y_below - 2)
+    packed = ex.fields * ex.layers
+    y_up, y_down = fold(sh, y_up, packed), fold(sh, y_down, packed)
     for ref, message in zip(y_refs, pair(sh.y_links, even_y, y_up, y_down)):
         ref[...] = message
+    for i, message in enumerate(pair(sh.x_links, even_x, x_up, x_down)):
+        x_refs[i][...] = message
+        upward, downward = fold(sh, message, ex.layers, y_above), fold(sh, message, ex.layers, y_below)
+        for j, corner in enumerate(pair(sh.y_links, even_y, upward, downward)):
+            corner_refs[i * sh.y_links + j][...] = corner
 
 
 def merge_xy(sh, ex, scratch, rim, guard, y_refs, x_refs):
@@ -142,16 +174,16 @@
     low_mask = inside & lane_range(across, ex.up, ex.layers)
     high_mask = inside & lane_range(across, sh.y + ex.down, ex.layers)
     span = ex.layers * sh.pitch
-    below_y, above_y = sides(sh, 1, [ref[...] for ref in y_refs])
-    per_link = len(x_refs) // sh.x_links
+    packed = ex.fields * ex.layers
+    below_y, above_y = [unfold(sh, value, packed, -2) for value in sides(sh, 1, [ref[...] for ref in y_refs])]
+    per_link = 1 + sh.y_links
     sums = []
     for link in range(sh.x_links):
         straight, diagonal = x_refs[link * per_link], x_refs[link * per_link + 1 : (link + 1) * per_link]
         total = straight[...]
-        if diagonal:
-            below, above = sides(sh, 1, [ref[...] for ref in diagonal])
-            total = total + pick(low_mask, shift(below, -sh.y)) + pick(high_mask, shift(above, sh.y))
-        sums.append(total)
+        below, above = sides(sh, 1, [ref[...] for ref in diagonal])
+        total = total + unfold(sh, below, ex.layers, ex.up)
+        sums.append(total + unfold(sh, above, ex.layers, sh.y + ex.down))
     below_x, above_x = sides(sh, 0, sums)
     first = 1 if ex.up == -2 else 0
     last = ex.layers - 1 if ex.down + ex.layers == 2 else ex.layers
@@ -446,12 +478,91 @@
     return ((row >= 2 * column) & (row < 2 * column + 2)).astype(f32)
 
 
-def merge_lines(sh, received_ref, all_fields, rims, corners, label_z):
+def ring(size_x, size_y, rows):
+    row = lax.broadcasted_iota(jnp.int32, (rows, LANES), 0)
+    sides_x, both = 2 * size_y, 2 * size_y + 2 * size_x
+    corner = row - both
+    x = jnp.where(row < size_y, -1, size_x)
+    x = jnp.where(row < sides_x, x, jnp.where(row < sides_x + size_x, row - sides_x, row - sides_x - size_x))
+    x = jnp.where(row < both, x, jnp.where(corner < 2, -1, size_x))
+    y = jnp.where(row < size_y, row, row - size_y)
+    y = jnp.where(row < sides_x, y, jnp.where(row < sides_x + size_x, -1, size_y))
+    y = jnp.where(row < both, y, jnp.where((corner == 0) | (corner == 2), -1, size_y))
+    return x, y, (row < sides_x) | (row >= both), row < both + 4
+
+
+def face_shape(sh, label_x, label_y):
+    rows = max(3 * sh.x + label_x, 3 * sh.y + label_y)
+    return (-(-rows // 8) * 8, LANES)
+
+
+def pack_faces(sh, natural_ref, stiff, label_x, label_y, x_refs, y_refs):
+    even_x, even_y = sh.here(0) % 2 == 0, sh.here(1) % 2 == 0
+
+    def face(at, count, stride, label_at, label_count, label_stride):
+        rows = [natural_ref[m, pl.ds(at, count, stride=stride), :] for m in range(3)]
+        return rows, stiff[pl.ds(label_at, label_count, stride=label_stride), :]
+
+    above = face(sh.cells - sh.y, sh.y, 1, (label_x - 1) * label_y, label_y, 1)
+    below = face(0, sh.y, 1, 0, label_y, 1)
+    for refs, links, even, above, below in (
+        (x_refs, sh.x_links, even_x, above, below),
+        (
+            y_refs,
+            sh.y_links,
+            even_y,
+            face(sh.y - 1, sh.x, sh.y, label_y - 1, label_x, label_y),
+            face(0, sh.x, sh.y, 0, label_x, label_y),
+        ),
+    ):
+        for i, ref in enumerate(refs):
+            ref[...] = jnp.zeros(ref.shape, f32)
+            count = above[0][0].shape[0]
+            for m in range(3):
+                ref[m * count : (m + 1) * count, :] = pair(links, even, above[0][m], below[0][m])[i]
+            labels, length = above[1].shape
+            ref[3 * count : 3 * count + labels, 0:length] = pair(links, even, above[1], below[1])[i]
+
+
+def merge_start(sh, refs, x_refs, y_refs, received_ref, sizes, cells, labels):
+    residual, stiff, stiff_rim = refs
+    label_x, label_y, label_z = sizes
     lane, along, across = sh.lane_grid(1)
     inside = lane < sh.used
     last = (sh.x + 1) * sh.pitch
     x_mask = {-1: lane < sh.pitch, 0: (lane >= sh.pitch) & (lane < last), 1: (lane >= last) & inside}
     y_mask = {-1: across < 0, 0: (across >= 0) & (across < sh.y), 1: across >= sh.y}
+    cells[...] = jnp.zeros(cells.shape, f32)
+    labels[...] = jnp.zeros(labels.shape, f32)
+    count, label_count = cells.shape[1], labels.shape[0]
+    at = label_at = 0
+    for axis, face_refs, size, label_size in ((0, x_refs, sh.y, label_y), (1, y_refs, sh.x, label_x)):
+        for message in sides(sh, axis, [ref[...] for ref in face_refs]):
+            for m in range(3):
+                cells[m, at : at + size, :] = message[m * size : (m + 1) * size]
+            labels[label_at : label_at + label_size, :] = message[3 * size : 3 * size + label_size, 0:label_z]
+            at, label_at = at + size, label_at + label_size
+    for dx, dy in ((-1, -1), (-1, 1), (1, -1), (1, 1)):
+        slot = slot_from(sh, received_ref, (dx, dy, 0))
+        for m in range(3):
+            cells[m, at : at + 1, :] = slot[m : m + 1]
+        labels[label_at : label_at + 1, :] = slot[3:4, 0:label_z]
+        at, label_at = at + 1, label_at + 1
+    x, y, _, valid = ring(sh.x, sh.y, count)
+    place = (valid & inside & (along == x) & (across == y)).astype(f32)
+    own = slice(EDGE, EDGE + sh.z)
+    tall_own = slice(2 * EDGE, 2 * EDGE + sh.z)
+    for m in range(3):
+        residual[m, own, :] += to_lanes(cells[m], place)
+    by_z = lax.dot_general(
+        repeat_twice(label_z), labels[...], (((1,), (1,)), ((), ())), precision=highest, preferred_element_type=f32
+    )
+    x, y, at_x, valid = ring(label_x, label_y, label_count)
+    match = valid & inside & ((along >> 1) == x) & ((across >> 1) == y)
+    columns = jnp.dot(by_z, (match & at_x).astype(f32), precision=highest, preferred_element_type=f32)
+    stiff_rim[0, tall_own, :] = columns
+    columns = columns + jnp.dot(by_z, (match & ~at_x).astype(f32), precision=highest, preferred_element_type=f32)
+    stiff[0, tall_own, :] += columns
     for dz in (-1, 1):
         main = edge = jnp.zeros((8, LANES), f32)
         for dx in (-1, 0, 1):
@@ -462,37 +573,11 @@
                 if dx:
                     edge = edge + pick(mask, shift(slot, dx * (sh.x - 1) * sh.pitch + dy * sh.y))
         near = EDGE + sh.z if dz > 0 else EDGE - 1
-        for f in range(4):
-            all_fields[f, near : near + 1, :] += main[f : f + 1]
-        rims[3, near : near + 1, :] += edge[3:4]
-        all_fields[3, near + dz : near + dz + 1, :] += main[3:4]
-        rims[3, near + dz : near + dz + 1, :] += edge[3:4]
-    corners[...] = jnp.zeros(corners.shape, f32)
-    number = lax.broadcasted_iota(jnp.int32, (8, LANES), 0)
-    lanes, lanes_along, lanes_across = sh.lane_grid(8)
-    same = thick = lanes < 0
-    for i, (dx, dy) in enumerate(((-1, -1), (-1, 1), (1, -1), (1, 1))):
-        slot = slot_from(sh, received_ref, (dx, dy, 0))
-        for f in range(4):
-            corners[8 * f + i : 8 * f + i + 1, :] = slot[f : f + 1]
-        here = (number == i) & (lanes < sh.used)
-        at_x = lanes_along == (sh.x if dx > 0 else -1)
-        beyond = lanes_across >= sh.y if dy > 0 else lanes_across < 0
-        same = same | (here & at_x & (lanes_across == (sh.y if dy > 0 else -1)))
-        thick = thick | (here & at_x & beyond)
-    own = slice(EDGE, EDGE + sh.z)
-    for m in range(3):
-        all_fields[m, own, :] += to_lanes(corners[8 * m : 8 * m + 8, :], same.astype(f32))
-    by_z = lax.dot_general(
-        repeat_twice(label_z),
-        corners[24:32, 0:label_z],
-        (((1,), (1,)), ((), ())),
-        precision=highest,
-        preferred_element_type=f32,
-    )
-    columns = jnp.dot(by_z, thick.astype(f32), precision=highest, preferred_element_type=f32)
-    all_fields[3, own, :] += columns
-    rims[3, own, :] += columns
+        for m in range(3):
+            residual[m, near : near + 1, :] = main[m : m + 1]
+        for row in (EDGE + near, EDGE + near + dz):
+            stiff[0, row : row + 1, :] = main[3:4]
+            stiff_rim[0, row : row + 1, :] = edge[3:4]
 
 
 def call(kernel, name, outs, ins, scratch=(), remote_ins=False):
@@ -537,13 +622,9 @@
     return [send(sh, message, {2: link}) for link, message in enumerate(messages)]
 
 
-def send_xy(sh, x_messages, y_messages, diagonal=True):
+def send_faces(sh, x_messages, y_messages):
     from_y = [send(sh, message, {1: link}) for link, message in enumerate(y_messages)]
-    from_x = []
-    for link, message in enumerate(x_messages):
-        from_x.append(send(sh, message, {0: link}))
-        if diagonal:
-            from_x.extend(send(sh, message, {0: link, 1: other}) for other in range(sh.y_links))
+    from_x = [send(sh, message, {0: link}) for link, message in enumerate(x_messages)]
     return from_y, from_x
 
 
@@ -554,23 +635,32 @@
 def exchange(sh, ex, name, field, z_messages):
     from_z = send_z(sh, z_messages)
 
+    corners = sh.x_links * sh.y_links
+
     def packer(*refs):
-        field_ref, z_refs = refs[0], refs[1 : 1 + sh.z_links]
-        x_refs = refs[1 + sh.z_links : 1 + sh.z_links + sh.x_links]
-        y_refs = refs[1 + sh.z_links + sh.x_links : -1]
-        scratch = refs[-1]
+        take = Taker(refs)
+        field_ref, z_refs = take.one(), take(sh.z_links)
+        x_refs, y_refs, corner_refs, scratch = take(sh.x_links), take(sh.y_links), take(corners), take.one()
         merge_z(sh, ex, field_ref, z_refs, scratch, 0)
-        pack_xy(sh, ex, scratch, x_refs, y_refs)
+        pack_xy(sh, ex, scratch, x_refs, y_refs, corner_refs)
 
     plane = (sh.rows, LANES)
     messages = call(
         packer,
         name,
-        [plane] * (sh.x_links + sh.y_links),
+        [plane] * sh.x_links
+        + [folded_shape(sh, ex.fields * ex.layers)] * sh.y_links
+        + [folded_shape(sh, ex.layers)] * corners,
         [field] + from_z,
         [(ex.fields,) + plane],
     )
-    from_y, from_x = send_xy(sh, messages[: sh.x_links], messages[sh.x_links :])
+    take = Taker(messages)
+    x_messages, y_messages = take(sh.x_links), take(sh.y_links)
+    from_y, straight = send_faces(sh, x_messages, y_messages)
+    from_x = []
+    for link in range(sh.x_links):
+        from_x.append(straight[link])
+        from_x.extend(send(sh, take.one(), {0: link, 1: other}) for other in range(sh.y_links))
     return from_z, from_y, from_x
 
 
@@ -662,12 +752,13 @@
         for i in range(6):
             lines[8 * i + 4 : 8 * i + 5, :] = line
         send_lines(sh, lines, slots_ref)
-        pack_xy(sh, SPREAD, field_ref, x_refs, y_refs)
+        pack_faces(sh, natural_ref, stiff, label_x, label_y, x_refs, y_refs)
 
     start_field, nodes, lines, *messages = call(
         begin,
         "begin",
-        [(4,) + plane, (sh.z, LANES), (8 * sh.devices, LANES)] + [plane] * (sh.x_links + sh.y_links),
+        [(4,) + plane, (sh.z, LANES), (8 * sh.devices, LANES)]
+        + [face_shape(sh, label_x, label_y)] * (sh.x_links + sh.y_links),
         [natural, phase_labels, phase_moduli, nodes_natural],
         [
             natural.shape,
@@ -681,12 +772,10 @@
         ],
         remote_ins=True,
     )
-    from_y, from_x = send_xy(sh, messages[: sh.x_links], messages[sh.x_links :], diagonal=False)
+    from_y, from_x = send_faces(sh, messages[: sh.x_links], messages[sh.x_links :])
     lines = to_all(lines)
 
-    def finish_solve(index, v, nodes_ref, coarse, inverse_ref, values, solution_ref, z_refs, ex):
-        for m in range(3):
-            solution_ref[m] = v[index][m, EDGE : EDGE + sh.rows, :]
+    def add_coarse(nodes_ref, coarse, inverse_ref, values, solution_ref, z_refs, ex):
         added = coarse_values(sh, nodes_ref[...], coarse, inverse_ref, values)
         valid = nodes_ref[...] >= 0.0
         for m in range(3):
@@ -700,31 +789,36 @@
         nodes_ref, lines_ref, inverse_ref = take(3)
         solution_ref, springs_ref = take(2)
         z_refs = take(sh.z_links)
-        all_fields, rims, stiff, stiff_rim, v0, v1, kv0, kv1, factor, values, corners = take(11)
+        residual, stiff, stiff_rim, v0, v1, kv0, kv1, factor, values, cells, labels = take(11)
         clear_guards(sh, (stiff, stiff_rim, v0, v1, kv0, kv1))
-        all_fields[...] = field_ref[...]
-        merge_xy(sh, SPREAD, all_fields, rims, 0, y_refs, x_refs)
-        merge_lines(sh, lines_ref, all_fields, rims, corners, label_z)
-        put(stiff, 0, all_fields[3])
-        put(stiff_rim, 0, rims[3])
-        springs_ref[6] = all_fields[3]
-        springs_ref[7] = rims[3]
+        residual[...] = field_ref[0:3]
+        put(stiff, 0, field_ref[3])
+        put(stiff_rim, 0, jnp.zeros(plane, f32))
+        sizes = phase_labels.shape
+        merge_start(sh, (residual, stiff, stiff_rim), x_refs, y_refs, lines_ref, sizes, cells, labels)
+        springs_ref[6] = inner(stiff, 0)
+        springs_ref[7] = inner(stiff_rim, 0)
         lane, _, _ = sh.lane_grid(1)
-
         for f, entry in enumerate(own_block(sh, lane, (stiff, stiff_rim))):
             springs_ref[f] = entry
-        index = local_solve(sh, all_fields, springs_ref, (v0, v1), (kv0, kv1), factor)
+        index = local_solve(sh, residual, springs_ref, (v0, v1), (kv0, kv1), factor)
         coarse = lines_ref[pl.ds(4, sh.devices, stride=8), :]
-        finish_solve(index, (v0, v1), nodes_ref, coarse, inverse_ref, values, solution_ref, z_refs, DEEP)
+        for m in range(3):
+            solution_ref[m] = inner((v0, v1)[index], m)
+        add_coarse(nodes_ref, coarse, inverse_ref, values, solution_ref, z_refs, DEEP)
 
     solved, springs, *z_messages = call(
         first_solve,
         "first_solve",
         [fields, (8,) + plane] + z_shape(DEEP),
         [start_field, *from_y, *from_x, nodes, lines, coarse_inverse],
-        [(4,) + plane, (4,) + plane, (1, sh.tall, LANES), (1, sh.tall, LANES)]
+        [fields, (1, sh.tall, LANES), (1, sh.tall, LANES)]
         + [tall] * 4
-        + [fields, (LANES, LANES), (32, LANES)],
+        + [fields, (LANES, LANES)]
+        + [
+            (3, 8 * -(-(2 * sh.x + 2 * sh.y + 4) // 8), LANES),
+            (8 * -(-(2 * label_x + 2 * label_y + 4) // 8), label_z),
+        ],
     )
     from_z, from_y, from_x = exchange(sh, DEEP, "deep", solved, z_messages)
 
@@ -764,22 +858,25 @@
     )
     coarse = to_all(sums)
 
-    def second_solve(*refs):
-        take = Taker(refs)
-        image_ref, springs_ref, nodes_ref, coarse_ref, inverse_ref = take(5)
-        solution_ref = take.one()
-        z_refs = take(sh.z_links)
-        v0, v1, kv0, kv1, factor, values = take(6)
+    def second_solve(image_ref, springs_ref, local_ref, v0, v1, kv0, kv1, factor):
         clear_guards(sh, (v0, v1, kv0, kv1))
         index = local_solve(sh, image_ref, springs_ref, (v0, v1), (kv0, kv1), factor)
-        finish_solve(index, (v0, v1), nodes_ref, coarse_ref[...], inverse_ref, values, solution_ref, z_refs, NEAR)
+        for m in range(3):
+            local_ref[m] = inner((v0, v1)[index], m)
+
+    (local,) = call(second_solve, "second_solve", [fields], [image, springs], [tall] * 4 + [fields])
+
+    def second_add(local_ref, nodes_ref, coarse_ref, inverse_ref, *rest):
+        solution_ref, z_refs, values = rest[0], rest[1:-1], rest[-1]
+        solution_ref[...] = local_ref[...]
+        add_coarse(nodes_ref, coarse_ref[...], inverse_ref, values, solution_ref, z_refs, NEAR)
 
     solved, *z_messages = call(
-        second_solve,
-        "second_solve",
+        second_add,
+        "second_add",
         [fields] + z_shape(NEAR),
-        [image, springs, nodes, coarse, coarse_inverse],
-        [tall] * 4 + [fields, (LANES, LANES)],
+        [local, nodes, coarse, coarse_inverse],
+        [(LANES, LANES)],
     )
     from_z, from_y, from_x = exchange(sh, NEAR, "near", solved, z_messages)
 
@@ -821,7 +918,15 @@
     )
     totals = to_all(sums)
 
-    def finish(totals_ref, natural_ref, search_ref, first_ref, second_ref, image_ref, field_ref, residual_ref):
+    def turn(search_ref, first_ref, second_ref, image_ref, out_ref):
+        select = selection(sh)
+        for i, ref in enumerate((search_ref, first_ref, second_ref, image_ref)):
+            for m in range(3):
+                out_ref[i, m] = to_cells(ref[m, own, :], select)
+
+    (turned,) = call(turn, "turn", [(4,) + natural.shape], [search, image, second, second_image_field])
+
+    def finish(totals_ref, natural_ref, turned_ref, field_ref, residual_ref):
         total = jnp.sum(totals_ref[...], axis=0, keepdims=True)
         rz, zw, rq, wq, zv, qv = [total[:, i : i + 1] for i in range(6)]
         step0 = rz / zw
@@ -831,18 +936,12 @@
         step1 = rho / curvature
         first = step0 + step1 * grow
         second = step0 * step1
-        select = selection(sh)
-        for m in range(3):
-            update = first * search_ref[m, own, :] - second * second_ref[m, own, :]
-            field_ref[m] = to_cells(update, select)
-            update = first * first_ref[m, own, :] - second * image_ref[m, own, :]
-            residual_ref[m] = natural_ref[m] - to_cells(update, select)
+        for m in range(3):
+            field_ref[m] = first * turned_ref[0, m] - second * turned_ref[2, m]
+            residual_ref[m] = natural_ref[m] - (first * turned_ref[1, m] - second * turned_ref[3, m])
 
     solution_field, residual = call(
-        finish,
-        "finish",
-        [natural.shape, natural.shape],
-        [totals, natural, search, image, second, second_image_field],
+        finish, "finish", [natural.shape, natural.shape], [totals, natural, turned]
     )
     return solution_field.reshape(right_side.shape), residual.reshape(right_side.shape)
 

time: 83.9 us -> 77 us (0.918)
  blocking collectives: 20.3 us -> 0 us
  waiting for transfers between devices: 17.1 us -> 24.8 us
  starting transfers between devices: 24.8 us -> 28.2 us
  Pallas kernels: 17.7 us -> 19.9 us
    all_to_all x2 -> x0, blocking collectives: 20.3 us -> none  [to_all(): return lax.all_to_all(slots, AXES, 0, 0, tiled=True)]
    all_to_all x1 -> x3, waiting for transfers between devices: 0.01 us -> 10 us  [to_all(): return lax.all_to_all(slots, AXES, 0, 0, tiled=True)]
    all_to_all x1 -> x3, starting transfers between devices: 7.3 us -> 14.3 us  [to_all(): return lax.all_to_all(slots, AXES, 0, 0, tiled=True)]
    ppermute x17, starting transfers between devices: 17.5 us -> 13.9 us  [send(): return lax.ppermute(value, AXES, permutation(sh.sizes, moves))]
    ppermute x17, waiting for transfers between devices: 17.1 us -> 14.8 us  [send(): return lax.ppermute(value, AXES, permutation(sh.sizes, moves))]
    pallas_call x8 -> x10, Pallas kernels: 17.7 us -> 19.9 us  [call(): pl.pallas_call(kernel, out_shape=[jax.ShapeDtypeStruct(shape, f32) for sh...]
  transfers between devices with their start and end apart: 18 -> 20, of which waited for: 11 -> 14; matrix products, arithmetic and copies ran while one was open for 0% -> 0% of each run, Pallas kernels for 0% -> 7%
where the time goes in v4:
time: 77 us; the launch traced here: 76.6 us
  starting transfers between devices  28.2 us (37%)
  waiting for transfers between devices  24.8 us (32%)
  Pallas kernels  19.9 us (26%)
  local copies, waits for them, and re-layouts  3 us (4%)
    pallas_call x10, Pallas kernels, call(): pl.pallas_call(kernel, out_shape=[jax.ShapeDtypeStruct(shape, f32) for sh...  19.9 us
    ppermute x17, waiting for transfers between devices, send(): return lax.ppermute(value, AXES, permutation(sh.sizes, moves))  14.8 us
    all_to_all x3, starting transfers between devices, to_all(): return lax.all_to_all(slots, AXES, 0, 0, tiled=True)  14.3 us
    ppermute x17, starting transfers between devices, send(): return lax.ppermute(value, AXES, permutation(sh.sizes, moves))  13.9 us
    all_to_all x3, waiting for transfers between devices, to_all(): return lax.all_to_all(slots, AXES, 0, 0, tiled=True)  10 us
    unnamed x12, local copies, waits for them, and re-layouts  3 us
  transfers between devices with their start and end apart: 20, of which 14 were waited for; matrix products, arithmetic and copies ran while one was open for 0% of the time, Pallas kernels for 7%

profile of v4, /device:TPU:0, one launch (start us, length us, event | category | flops | bytes accessed | tf_op | source)
XLA Modules:
  0.0 76.6 jit_solution(13743514310050196892)
XLA Ops:
  0.6 0.6 copy-done.5
  1.3 0.9 %copy-done.1 = f32[3,8,8,128]{3,2,1,0:T(8,128)S(1)} copy-done((f32[3,8,8,128]{3,2,1,0:T(8,128)S(1)}, f32[3,8,8,128]{3,2,1,0:T(8,128)}, u32[]{:S(2)}) %copy-start.1) | copy-done | bytes 98328
  2.2 0.8 copy-done.3
  2.9 0.7 copy-done.4
  3.6 2.4 %begin.1 = (f32[4,144,128]{2,1,0:T(8,128)S(1)}, f32[128,128]{1,0:T(8,128)S(1)}, f32[256,128]{1,0:T(8,128)}, f32[32,128]{1,0:T(8,128)S(1)}, f32[32,128]{1,0:T(8,128)S(1)}, /*index=5*/f32[32,128]{1,0:T(8,128)S(1)}) custom-call(f32[3,64,128]{2,1,0:T(8,128)S(1)} %bitcast.15, s32[4,4,64]{2,1,0:T(4,128)S(1)} %copy-done.4, f32[8]{0:T(128)S(1)} %copy-done.5, ...), custom_call_target="tpu_custom_call" | custom-call | tf_op jit(solution)/shard_map/begin/pallas_call | solution.py:585
  6.0 7.3 %all-to-all-start = ((f32[32,8,128]{2,1,0:T(8,128)}), f32[32,8,128]{2,1,0:T(8,128)S(1)}, u32[]{:S(2)}, u32[]{:S(2)}) async-start(f32[32,8,128]{2,1,0:T(8,128)} %bitcast.2), calls=%async_computation | async-start | bytes 262144 | tf_op jit(solution)/shard_map/all_to_all | solution.py:632
  13.3 1.8 %collective-permute-start = (f32[32,128]{1,0:T(8,128)S(1)}, f32[32,128]{1,0:T(8,128)S(1)}, u32[]{:S(2)}, u32[]{:S(2)}) collective-permute-start(f32[32,128]{1,0:T(8,128)S(1)} %get-tuple-element.34), channel_id=1, source_target_pairs={{0,4},{1,5},{2,6},{3,7},{4,0},{5,1},{6,2},{7,3},{8,12},{9,13},{10,... | collective-permute-start | bytes 49160 | tf_op jit(solution)/shard_map/ppermute | solution.py:618
  15.2 1.5 %collective-permute-start.1 = (f32[32,128]{1,0:T(8,128)S(1)}, f32[32,128]{1,0:T(8,128)S(1)}, u32[]{:S(2)}, u32[]{:S(2)}) collective-permute-start(f32[32,128]{1,0:T(8,128)S(1)} %get-tuple-element.35), channel_id=1, source_target_pairs={{0,16},{1,17},{2,18},{3,19},{4,8},{5,9},{6,10},{7,11},{8,4},{9,5},... | collective-permute-start | bytes 49160 | tf_op jit(solution)/shard_map/ppermute | solution.py:618
  16.6 0.6 collective-permute-start.2
  17.2 0.1 collective-permute-done.refs_1_
  17.3 1.9 %collective-permute-done.1.refs_2_ = f32[32,128]{1,0:T(8,128)S(1)} collective-permute-done((f32[32,128]{1,0:T(8,128)S(1)}, f32[32,128]{1,0:T(8,128)S(1)}, u32[]{:S(2)}, u32[]{:S(2)}) %collective-permute-start.1) | collective-permute-done | bytes 16416 | tf_op jit(solution)/shard_map/ppermute | solution.py:618
  19.2 1.2 %collective-permute-done.2.refs_3_ = f32[32,128]{1,0:T(8,128)S(1)} collective-permute-done((f32[32,128]{1,0:T(8,128)S(1)}, f32[32,128]{1,0:T(8,128)S(1)}, u32[]{:S(2)}, u32[]{:S(2)}) %collective-permute-start.2) | collective-permute-done | bytes 16416 | tf_op jit(solution)/shard_map/ppermute | solution.py:618
  20.4 1.2 %all-to-all-done = f32[32,8,128]{2,1,0:T(8,128)S(1)} async-done(((f32[32,8,128]{2,1,0:T(8,128)}), f32[32,8,128]{2,1,0:T(8,128)S(1)}, u32[]{:S(2)}, u32[]{:S(2)}) %all-to-all-start) | async-done | bytes 131104 | tf_op jit(solution)/shard_map/all_to_all | solution.py:632
  21.6 4.7 %first_solve.1 = (f32[3,144,128]{2,1,0:T(8,128)S(1)}, f32[8,144,128]{2,1,0:T(8,128)S(1)}, f32[24,128]{1,0:T(8,128)S(1)}, f32[24,128]{1,0:T(8,128)S(1)}) custom-call(f32[4,144,128]{2,1,0:T(8,128)S(1)} %get-tuple-element.33.refs_0_.refs_10_, f32[32,128]{1,0:T(8,128)S(1)} %collective-permute-done.refs_1_, f32[32,128]{1,0:T(8,128)S(1)} %collective-permute-done.1.refs_2_, ...), custom_call_target="tpu_custom_call" | custom-call | tf_op jit(solution)/shard_map/first_solve/pallas_call | solution.py:585
  26.3 0.5 collective-permute-start.3
  26.8 0.3 collective-permute-start.4
  27.1 0.5 collective-permute-done.3.refs_1_
  27.6 2.3 %collective-permute-done.4.refs_2_ = f32[24,128]{1,0:T(8,128)S(1)} collective-permute-done((f32[24,128]{1,0:T(8,128)S(1)}, f32[24,128]{1,0:T(8,128)S(1)}, u32[]{:S(2)}, u32[]{:S(2)}) %collective-permute-start.4) | collective-permute-done | bytes 12320 | tf_op jit(solution)/shard_map/ppermute | solution.py:618
  29.9 0.3 deep.1
  30.2 0.1 collective-permute-start.5
  30.3 1.4 %collective-permute-start.6 = (f32[144,128]{1,0:T(8,128)S(1)}, f32[144,128]{1,0:T(8,128)S(1)}, u32[]{:S(2)}, u32[]{:S(2)}) collective-permute-start(f32[144,128]{1,0:T(8,128)S(1)} %get-tuple-element.43), channel_id=1, source_target_pairs={{0,16},{1,17},{2,18},{3,19},{4,8},{5,9},{6,10},{7,11},{8,4},{9,5},... | collective-permute-start | bytes 221192 | tf_op jit(solution)/shard_map/ppermute | solution.py:618
  31.8 0.6 collective-permute-start.7
  32.4 1.5 %collective-permute-start.8 = (f32[40,128]{1,0:T(8,128)S(1)}, f32[40,128]{1,0:T(8,128)S(1)}, u32[]{:S(2)}, u32[]{:S(2)}) collective-permute-start(f32[40,128]{1,0:T(8,128)S(1)} %get-tuple-element.45), channel_id=1, source_target_pairs={{0,20},{1,21},{2,22},{3,23},{4,16},{5,17},{6,18},{7,19},{8,28},{9,... | collective-permute-start | bytes 61448 | tf_op jit(solution)/shard_map/ppermute | solution.py:618
  33.9 0.6 collective-permute-start.9
  34.5 2.6 %collective-permute-done.8.refs_6_ = f32[40,128]{1,0:T(8,128)S(1)} collective-permute-done((f32[40,128]{1,0:T(8,128)S(1)}, f32[40,128]{1,0:T(8,128)S(1)}, u32[]{:S(2)}, u32[]{:S(2)}) %collective-permute-start.8) | collective-permute-done | bytes 20512 | tf_op jit(solution)/shard_map/ppermute | solution.py:618
  37.1 0.6 collective-permute-done.9.refs_7_
  37.7 3.4 %first_image.1 = (f32[3,144,128]{2,1,0:T(8,128)S(1)}, f32[3,144,128]{2,1,0:T(8,128)S(1)}, f32[32,128]{1,0:T(8,128)}) custom-call(f32[3,144,128]{2,1,0:T(8,128)S(1)} %get-tuple-element.39.refs_0_, f32[24,128]{1,0:T(8,128)S(1)} %collective-permute-done.3.refs_1_, f32[24,128]{1,0:T(8,128)S(1)} %collective-permute-done.4.refs_2_, ...), custom_call_target="tpu_custom_call" | custom-call | tf_op jit(solution)/shard_map/first_image/pallas_call | solution.py:585
  41.1 3.7 %all-to-all-start.1 = ((f32[32,1,128]{2,1,0:T(1,128)}), f32[32,1,128]{2,1,0:T(1,128)S(1)}, u32[]{:S(2)}, u32[]{:S(2)}) async-start(f32[32,1,128]{2,1,0:T(1,128)} %bitcast.5), calls=%async_computation.1 | async-start | bytes 32768 | tf_op jit(solution)/shard_map/all_to_all | solution.py:632
  44.8 3.5 %second_solve.1.local_ref = f32[3,144,128]{2,1,0:T(8,128)S(1)} custom-call(f32[3,144,128]{2,1,0:T(8,128)S(1)} %get-tuple-element.48.image_ref.refs_12_.first_ref, f32[8,144,128]{2,1,0:T(8,128)S(1)} %get-tuple-element.47.refs_9_.springs_ref), custom_call_target="tpu_custom_call" | custom-call | tf_op jit(solution)/shard_map/second_solve/pallas_call | solution.py:585
  48.3 3.4 %all-to-all-done.1 = f32[32,1,128]{2,1,0:T(1,128)S(1)} async-done(((f32[32,1,128]{2,1,0:T(1,128)}), f32[32,1,128]{2,1,0:T(1,128)S(1)}, u32[]{:S(2)}, u32[]{:S(2)}) %all-to-all-start.1) | async-done | bytes 16416 | tf_op jit(solution)/shard_map/all_to_all | solution.py:632
  51.7 0.4 second_add.1
  52.1 0.1 collective-permute-start.10
  52.2 0.7 collective-permute-start.11
  52.8 0.5 collective-permute-done.10.refs_1_
  53.4 2.0 %collective-permute-done.11.refs_2_ = f32[24,128]{1,0:T(8,128)S(1)} collective-permute-done((f32[24,128]{1,0:T(8,128)S(1)}, f32[24,128]{1,0:T(8,128)S(1)}, u32[]{:S(2)}, u32[]{:S(2)}) %collective-permute-start.11) | collective-permute-done | bytes 12320 | tf_op jit(solution)/shard_map/ppermute | solution.py:618
  55.4 0.4 near.1
  55.8 0.7 collective-permute-start.14
  56.4 0.5 collective-permute-start.12
  56.9 1.4 %collective-permute-start.13 = (f32[72,128]{1,0:T(8,128)S(1)}, f32[72,128]{1,0:T(8,128)S(1)}, u32[]{:S(2)}, u32[]{:S(2)}) collective-permute-start(f32[72,128]{1,0:T(8,128)S(1)} %get-tuple-element.54), channel_id=1, source_target_pairs={{0,16},{1,17},{2,18},{3,19},{4,8},{5,9},{6,10},{7,11},{8,4},{9,5},... | collective-permute-start | bytes 110600 | tf_op jit(solution)/shard_map/ppermute | solution.py:618
  58.4 1.0 %collective-permute-start.15 = (f32[24,128]{1,0:T(8,128)S(1)}, f32[24,128]{1,0:T(8,128)S(1)}, u32[]{:S(2)}, u32[]{:S(2)}) collective-permute-start(f32[24,128]{1,0:T(8,128)S(1)} %get-tuple-element.56), channel_id=1, source_target_pairs={{0,20},{1,21},{2,22},{3,23},{4,16},{5,17},{6,18},{7,19},{8,28},{9,... | collective-permute-start | bytes 36872 | tf_op jit(solution)/shard_map/ppermute | solution.py:618
  59.3 0.7 collective-permute-start.16
  60.1 2.9 %collective-permute-done.15.refs_6_ = f32[24,128]{1,0:T(8,128)S(1)} collective-permute-done((f32[24,128]{1,0:T(8,128)S(1)}, f32[24,128]{1,0:T(8,128)S(1)}, u32[]{:S(2)}, u32[]{:S(2)}) %collective-permute-start.15) | collective-permute-done | bytes 12320 | tf_op jit(solution)/shard_map/ppermute | solution.py:618
  63.0 0.1 collective-permute-done.16.refs_7_
  63.1 2.3 %second_image.1 = (f32[3,144,128]{2,1,0:T(8,128)S(1)}, f32[3,144,128]{2,1,0:T(8,128)S(1)}, f32[32,128]{1,0:T(8,128)}) custom-call(f32[3,144,128]{2,1,0:T(8,128)S(1)} %get-tuple-element.50.refs_0_, f32[24,128]{1,0:T(8,128)S(1)} %collective-permute-done.10.refs_1_, f32[24,128]{1,0:T(8,128)S(1)} %collective-permute-done.11.refs_2_, ...), custom_call_target="tpu_custom_call" | custom-call | tf_op jit(solution)/shard_map/second_image/pallas_call | solution.py:585
  65.4 3.3 %all-to-all-start.2 = ((f32[32,1,128]{2,1,0:T(1,128)}), f32[32,1,128]{2,1,0:T(1,128)S(1)}, u32[]{:S(2)}, u32[]{:S(2)}) async-start(f32[32,1,128]{2,1,0:T(1,128)} %bitcast.8), calls=%async_computation.2 | async-start | bytes 32768 | tf_op jit(solution)/shard_map/all_to_all | solution.py:632
  68.7 1.6 %turn.1.turned_ref = f32[4,3,64,128]{3,2,1,0:T(8,128)S(1)} custom-call(f32[3,144,128]{2,1,0:T(8,128)S(1)} %get-tuple-element.58.refs_11_.search_ref, f32[3,144,128]{2,1,0:T(8,128)S(1)} %get-tuple-element.48.image_ref.refs_12_.first_ref, f32[3,144,128]{2,1,0:T(8,128)S(1)} %get-tuple-element.60.second_ref, f32[3,144,128]{2,1,0:T(8,128)S(1)} %get-tuple-element.61.image_ref), custom_call_target="tpu_custom_call" | custom-call | tf_op jit(solution)/shard_map/turn/pallas_call | solution.py:585
  70.3 5.5 %all-to-all-done.2 = f32[32,1,128]{2,1,0:T(1,128)S(1)} async-done(((f32[32,1,128]{2,1,0:T(1,128)}), f32[32,1,128]{2,1,0:T(1,128)S(1)}, u32[]{:S(2)}, u32[]{:S(2)}) %all-to-all-start.2) | async-done | bytes 16416 | tf_op jit(solution)/shard_map/all_to_all | solution.py:632
  75.8 0.9 %finish.1 = (f32[3,64,128]{2,1,0:T(8,128)}, f32[3,64,128]{2,1,0:T(8,128)}) custom-call(f32[32,128]{1,0:T(8,128)S(1)} %bitcast.17, f32[3,64,128]{2,1,0:T(8,128)S(1)} %bitcast.16, f32[4,3,64,128]{3,2,1,0:T(8,128)S(1)} %turn.1.turned_ref), custom_call_target="tpu_custom_call" | custom-call | tf_op jit(solution)/shard_map/finish/pallas_call | solution.py:585
  (14 shorter events, 0.0 us)
Async XLA Ops:
  0.6 0.7 copy-start.5
  1.3 0.9 %copy-start.1 = (f32[3,8,8,128]{3,2,1,0:T(8,128)S(1)}, f32[3,8,8,128]{3,2,1,0:T(8,128)}, u32[]{:S(2)}) copy-start(f32[3,8,8,128]{3,2,1,0:T(8,128)} %param.5) | copy-start | bytes 294916
  2.2 0.8 copy-start.3
  2.9 0.7 copy-start.4
  3.6 18.0 %copy-start = (f32[36,1152]{1,0:T(8,128)S(1)}, f32[36,1152]{1,0:T(8,128)}, u32[]{:S(2)}) copy-start(f32[36,1152]{1,0:T(8,128)} %inverse_ref.1) | copy-start | bytes 497668
  6.0 15.6 %all-to-all-start = ((f32[32,8,128]{2,1,0:T(8,128)}), f32[32,8,128]{2,1,0:T(8,128)S(1)}, u32[]{:S(2)}, u32[]{:S(2)}) async-start(f32[32,8,128]{2,1,0:T(8,128)} %bitcast.2), calls=%async_computation | async-start | bytes 262144 | tf_op jit(solution)/shard_map/all_to_all | solution.py:632
  13.3 3.9 %collective-permute-start = (f32[32,128]{1,0:T(8,128)S(1)}, f32[32,128]{1,0:T(8,128)S(1)}, u32[]{:S(2)}, u32[]{:S(2)}) collective-permute-start(f32[32,128]{1,0:T(8,128)S(1)} %get-tuple-element.34), channel_id=1, source_target_pairs={{0,4},{1,5},{2,6},{3,7},{4,0},{5,1},{6,2},{7,3},{8,12},{9,13},{10,... | collective-permute-start | bytes 49160 | tf_op jit(solution)/shard_map/ppermute | solution.py:618
  15.2 4.0 %collective-permute-start.1 = (f32[32,128]{1,0:T(8,128)S(1)}, f32[32,128]{1,0:T(8,128)S(1)}, u32[]{:S(2)}, u32[]{:S(2)}) collective-permute-start(f32[32,128]{1,0:T(8,128)S(1)} %get-tuple-element.35), channel_id=1, source_target_pairs={{0,16},{1,17},{2,18},{3,19},{4,8},{5,9},{6,10},{7,11},{8,4},{9,5},... | collective-permute-start | bytes 49160 | tf_op jit(solution)/shard_map/ppermute | solution.py:618
  16.6 3.8 %collective-permute-start.2 = (f32[32,128]{1,0:T(8,128)S(1)}, f32[32,128]{1,0:T(8,128)S(1)}, u32[]{:S(2)}, u32[]{:S(2)}) collective-permute-start(f32[32,128]{1,0:T(8,128)S(1)} %get-tuple-element.36), channel_id=1, source_target_pairs={{0,16},{1,17},{2,18},{3,19},{4,20},{5,21},{6,22},{7,23},{8,24},{9,... | collective-permute-start | bytes 49160 | tf_op jit(solution)/shard_map/ppermute | solution.py:618
  26.3 1.3 %collective-permute-start.3 = (f32[24,128]{1,0:T(8,128)S(1)}, f32[24,128]{1,0:T(8,128)S(1)}, u32[]{:S(2)}, u32[]{:S(2)}) collective-permute-start(f32[24,128]{1,0:T(8,128)S(1)} %get-tuple-element.40), channel_id=1, source_target_pairs={{0,1},{1,0},{2,3},{3,2},{4,5},{5,4},{6,7},{7,6},{8,9},{9,8},{10,11... | collective-permute-start | bytes 36872 | tf_op jit(solution)/shard_map/ppermute | solution.py:618
  26.8 3.1 %collective-permute-start.4 = (f32[24,128]{1,0:T(8,128)S(1)}, f32[24,128]{1,0:T(8,128)S(1)}, u32[]{:S(2)}, u32[]{:S(2)}) collective-permute-start(f32[24,128]{1,0:T(8,128)S(1)} %get-tuple-element.41), channel_id=1, source_target_pairs={{0,3},{1,2},{2,1},{3,0},{4,7},{5,6},{6,5},{7,4},{8,11},{9,10},{10,... | collective-permute-start | bytes 36872 | tf_op jit(solution)/shard_map/ppermute | solution.py:618
  30.2 7.5 %collective-permute-start.5 = (f32[144,128]{1,0:T(8,128)S(1)}, f32[144,128]{1,0:T(8,128)S(1)}, u32[]{:S(2)}, u32[]{:S(2)}) collective-permute-start(f32[144,128]{1,0:T(8,128)S(1)} %get-tuple-element.42), channel_id=1, source_target_pairs={{0,4},{1,5},{2,6},{3,7},{4,0},{5,1},{6,2},{7,3},{8,12},{9,13},{10,... | collective-permute-start | bytes 221192 | tf_op jit(solution)/shard_map/ppermute | solution.py:618
  30.3 7.4 %collective-permute-start.6 = (f32[144,128]{1,0:T(8,128)S(1)}, f32[144,128]{1,0:T(8,128)S(1)}, u32[]{:S(2)}, u32[]{:S(2)}) collective-permute-start(f32[144,128]{1,0:T(8,128)S(1)} %get-tuple-element.43), channel_id=1, source_target_pairs={{0,16},{1,17},{2,18},{3,19},{4,8},{5,9},{6,10},{7,11},{8,4},{9,5},... | collective-permute-start | bytes 221192 | tf_op jit(solution)/shard_map/ppermute | solution.py:618
  31.8 5.9 %collective-permute-start.7 = (f32[144,128]{1,0:T(8,128)S(1)}, f32[144,128]{1,0:T(8,128)S(1)}, u32[]{:S(2)}, u32[]{:S(2)}) collective-permute-start(f32[144,128]{1,0:T(8,128)S(1)} %get-tuple-element.44), channel_id=1, source_target_pairs={{0,16},{1,17},{2,18},{3,19},{4,20},{5,21},{6,22},{7,23},{8,24},{9,... | collective-permute-start | bytes 221192 | tf_op jit(solution)/shard_map/ppermute | solution.py:618
  32.4 4.7 %collective-permute-start.8 = (f32[40,128]{1,0:T(8,128)S(1)}, f32[40,128]{1,0:T(8,128)S(1)}, u32[]{:S(2)}, u32[]{:S(2)}) collective-permute-start(f32[40,128]{1,0:T(8,128)S(1)} %get-tuple-element.45), channel_id=1, source_target_pairs={{0,20},{1,21},{2,22},{3,23},{4,16},{5,17},{6,18},{7,19},{8,28},{9,... | collective-permute-start | bytes 61448 | tf_op jit(solution)/shard_map/ppermute | solution.py:618
  33.9 3.8 %collective-permute-start.9 = (f32[40,128]{1,0:T(8,128)S(1)}, f32[40,128]{1,0:T(8,128)S(1)}, u32[]{:S(2)}, u32[]{:S(2)}) collective-permute-start(f32[40,128]{1,0:T(8,128)S(1)} %get-tuple-element.46), channel_id=1, source_target_pairs={{0,16},{1,17},{2,18},{3,19},{4,24},{5,25},{6,26},{7,27},{8,20},{9,... | collective-permute-start | bytes 61448 | tf_op jit(solution)/shard_map/ppermute | solution.py:618
  41.1 10.6 %all-to-all-start.1 = ((f32[32,1,128]{2,1,0:T(1,128)}), f32[32,1,128]{2,1,0:T(1,128)S(1)}, u32[]{:S(2)}, u32[]{:S(2)}) async-start(f32[32,1,128]{2,1,0:T(1,128)} %bitcast.5), calls=%async_computation.1 | async-start | bytes 32768 | tf_op jit(solution)/shard_map/all_to_all | solution.py:632
  52.1 1.2 %collective-permute-start.10 = (f32[24,128]{1,0:T(8,128)S(1)}, f32[24,128]{1,0:T(8,128)S(1)}, u32[]{:S(2)}, u32[]{:S(2)}) collective-permute-start(f32[24,128]{1,0:T(8,128)S(1)} %get-tuple-element.51), channel_id=1, source_target_pairs={{0,1},{1,0},{2,3},{3,2},{4,5},{5,4},{6,7},{7,6},{8,9},{9,8},{10,11... | collective-permute-start | bytes 36872 | tf_op jit(solution)/shard_map/ppermute | solution.py:618
  52.2 3.2 %collective-permute-start.11 = (f32[24,128]{1,0:T(8,128)S(1)}, f32[24,128]{1,0:T(8,128)S(1)}, u32[]{:S(2)}, u32[]{:S(2)}) collective-permute-start(f32[24,128]{1,0:T(8,128)S(1)} %get-tuple-element.52), channel_id=1, source_target_pairs={{0,3},{1,2},{2,1},{3,0},{4,7},{5,6},{6,5},{7,4},{8,11},{9,10},{10,... | collective-permute-start | bytes 36872 | tf_op jit(solution)/shard_map/ppermute | solution.py:618
  55.8 7.3 %collective-permute-start.14 = (f32[144,128]{1,0:T(8,128)S(1)}, f32[144,128]{1,0:T(8,128)S(1)}, u32[]{:S(2)}, u32[]{:S(2)}) collective-permute-start(f32[144,128]{1,0:T(8,128)S(1)} %get-tuple-element.55), channel_id=1, source_target_pairs={{0,16},{1,17},{2,18},{3,19},{4,20},{5,21},{6,22},{7,23},{8,24},{9,... | collective-permute-start | bytes 221192 | tf_op jit(solution)/shard_map/ppermute | solution.py:618
  56.4 6.7 %collective-permute-start.12 = (f32[72,128]{1,0:T(8,128)S(1)}, f32[72,128]{1,0:T(8,128)S(1)}, u32[]{:S(2)}, u32[]{:S(2)}) collective-permute-start(f32[72,128]{1,0:T(8,128)S(1)} %get-tuple-element.53), channel_id=1, source_target_pairs={{0,4},{1,5},{2,6},{3,7},{4,0},{5,1},{6,2},{7,3},{8,12},{9,13},{10,... | collective-permute-start | bytes 110600 | tf_op jit(solution)/shard_map/ppermute | solution.py:618
  56.9 6.2 %collective-permute-start.13 = (f32[72,128]{1,0:T(8,128)S(1)}, f32[72,128]{1,0:T(8,128)S(1)}, u32[]{:S(2)}, u32[]{:S(2)}) collective-permute-start(f32[72,128]{1,0:T(8,128)S(1)} %get-tuple-element.54), channel_id=1, source_target_pairs={{0,16},{1,17},{2,18},{3,19},{4,8},{5,9},{6,10},{7,11},{8,4},{9,5},... | collective-permute-start | bytes 110600 | tf_op jit(solution)/shard_map/ppermute | solution.py:618
  58.4 4.6 %collective-permute-start.15 = (f32[24,128]{1,0:T(8,128)S(1)}, f32[24,128]{1,0:T(8,128)S(1)}, u32[]{:S(2)}, u32[]{:S(2)}) collective-permute-start(f32[24,128]{1,0:T(8,128)S(1)} %get-tuple-element.56), channel_id=1, source_target_pairs={{0,20},{1,21},{2,22},{3,23},{4,16},{5,17},{6,18},{7,19},{8,28},{9,... | collective-permute-start | bytes 36872 | tf_op jit(solution)/shard_map/ppermute | solution.py:618
  59.3 3.8 %collective-permute-start.16 = (f32[24,128]{1,0:T(8,128)S(1)}, f32[24,128]{1,0:T(8,128)S(1)}, u32[]{:S(2)}, u32[]{:S(2)}) collective-permute-start(f32[24,128]{1,0:T(8,128)S(1)} %get-tuple-element.57), channel_id=1, source_target_pairs={{0,16},{1,17},{2,18},{3,19},{4,24},{5,25},{6,26},{7,27},{8,20},{9,... | collective-permute-start | bytes 36872 | tf_op jit(solution)/shard_map/ppermute | solution.py:618
  65.4 10.3 %all-to-all-start.2 = ((f32[32,1,128]{2,1,0:T(1,128)}), f32[32,1,128]{2,1,0:T(1,128)S(1)}, u32[]{:S(2)}, u32[]{:S(2)}) async-start(f32[32,1,128]{2,1,0:T(1,128)} %bitcast.8), calls=%async_computation.2 | async-start | bytes 32768 | tf_op jit(solution)/shard_map/all_to_all | solution.py:632
  68.7 7.1 %copy-start.2 = (f32[3,8,8,128]{3,2,1,0:T(8,128)S(1)}, f32[3,8,8,128]{3,2,1,0:T(8,128)}, u32[]{:S(2)}) copy-start(f32[3,8,8,128]{3,2,1,0:T(8,128)} %param.5) | copy-start | bytes 294916

commit v5 on v4

--- a/solution.py
+++ b/solution.py
@@ -321,10 +321,25 @@
 
 
 def image_of(sh, lane, v, kv, rims, springs_ref):
-    outer = stencil(sh, lane, v, rims and rims[0])
-    scaled = stencil(sh, lane, kv, rims and rims[1])
+    k = springs_ref[6]
+    k_before, k_after = shift(k, sh.pitch), shift(k, -sh.pitch)
+    last = (sh.x + 1) * sh.pitch
     own = apply_block([springs_ref[f] for f in range(6)], [inner(v, m) for m in range(3)])
-    return [own[m] - (springs_ref[6] * outer[m] + scaled[m]) for m in range(3)]
+    rim_parts = [yz_parts(rims[0]), yz_parts(rims[1])] if rims else None
+    out = []
+    for m, (plain, scaled) in enumerate(zip(yz_parts(v), yz_parts(kv))):
+        after = shift(k_before * (plain[1] + plain[2]) + (scaled[1] + scaled[2]), -sh.pitch)
+        before = shift(k_after * (plain[1] - plain[2]) + (scaled[1] - scaled[2]), sh.pitch)
+        if rims is None:
+            after, before = pick(lane < last, after), pick(lane >= sh.pitch, before)
+        else:
+            plain_rim, scaled_rim = rim_parts[0][m], rim_parts[1][m]
+            edge = k * (plain_rim[1] + plain_rim[2]) + (scaled_rim[1] + scaled_rim[2])
+            after = jnp.where(lane < last, after, edge)
+            edge = k * (plain_rim[1] - plain_rim[2]) + (scaled_rim[1] - scaled_rim[2])
+            before = jnp.where(lane >= sh.pitch, before, edge)
+        out.append(own[m] - (k * plain[0] + scaled[0] + after + before))
+    return out
 
 
 def level(sh):
@@ -380,6 +395,14 @@
     return place(along, sh.x), place(across, sh.y), place(z, sh.z)
 
 
+def cell_coords(sh):
+    cell = lax.broadcasted_iota(jnp.int32, (sh.cells, sh.z), 0)
+    z = lax.broadcasted_iota(jnp.int32, (sh.cells, sh.z), 1)
+    x = cell // sh.y
+    place = lambda index, size: (2 * index + 1).astype(f32) / size - 1.0
+    return place(x, sh.x), place(cell - x * sh.y, sh.y), place(z, sh.z)
+
+
 def cross(a, b):
     return (a[1] * b[2] - a[2] * b[1], a[2] * b[0] - a[0] * b[2], a[0] * b[1] - a[1] * b[0])
 
@@ -398,10 +421,10 @@
     )
 
 
-def coarse_sums(sh, nodes, field, count, sums):
-    moments = tuple(field) + cross(coords(sh), field)
+def coarse_sums(sh, nodes, field, places, count, sums):
+    moments = tuple(field) + cross(places, field)
     for node in range(count):
-        mask = nodes == float(node)
+        mask = nodes == node
         for m in range(6):
             sums[node * 6 + m : node * 6 + m + 1, :] = fold_rows(pick(mask, moments[m]))
     flat = (sh.here(0) * sh.sizes[1] + sh.here(1)) * sh.sizes[2] + sh.here(2)
@@ -588,7 +611,7 @@
         in_specs=[pl.BlockSpec(memory_space=space) for _ in ins],
         out_specs=[pl.BlockSpec(memory_space=pltpu.VMEM) for _ in outs],
         scratch_shapes=[pltpu.VMEM(shape, f32) if isinstance(shape, tuple) else shape for shape in scratch],
-        compiler_params=pltpu.CompilerParams(vmem_limit_bytes=48 * 1024 * 1024),
+        compiler_params=pltpu.CompilerParams(vmem_limit_bytes=(62 if remote_ins else 48) * 1024 * 1024),
         name=name,
     )(*ins)
 
@@ -701,40 +724,38 @@
     nodes_natural = coarse_nodes.reshape(sh.cells, sh.z)
     label_x, label_y, label_z = phase_labels.shape
 
-    def begin(natural_in, labels_in, moduli_in, nodes_in, field_ref, lanes_ref, slots_ref, *rest):
+    def block_places():
+        lane, along, across = sh.lane_grid(label_x * label_y)
+        inside = (along >= 0) & (along < sh.x) & (across >= 0) & (across < sh.y)
+        block = lax.broadcasted_iota(jnp.int32, along.shape, 0)
+        return (inside & (block == (along >> 1) * label_y + (across >> 1))).astype(f32)
+
+    def end_layers(values, places):
+        length = values.shape[1]
+        row = lax.broadcasted_iota(jnp.int32, (8, length), 0)
+        at = lax.broadcasted_iota(jnp.int32, (8, length), 1)
+        ends = ((row == 0) & (at == length - 1)) | ((row == 1) & (at == 0))
+        return jnp.dot(to_cells(values, ends.astype(f32)), places, precision=highest, preferred_element_type=f32)
+
+    def begin(natural_in, labels_in, moduli_in, nodes_in, stiff, slots_ref, *rest):
         x_refs, y_refs = rest[: sh.x_links], rest[sh.x_links : sh.x_links + sh.y_links]
-        natural_ref, labels_ref, moduli_ref, nodes_ref, sems, sums, stiff, lines = rest[sh.x_links + sh.y_links :]
+        natural_ref, labels_ref, moduli_ref, nodes_ref, sems, sums, lines = rest[sh.x_links + sh.y_links :]
         pairs = ((natural_in, natural_ref), (labels_in, labels_ref), (moduli_in, moduli_ref), (nodes_in, nodes_ref))
         copies = [pltpu.make_async_copy(a, b, sems.at[i]) for i, (a, b) in enumerate(pairs)]
         for copy in copies:
             copy.start()
-        select = selection(sh)
-        field_ref[...] = jnp.zeros(field_ref.shape, f32)
         sums[...] = jnp.zeros(sums.shape, f32)
         lines[...] = jnp.zeros(lines.shape, f32)
         for copy in copies:
             copy.wait()
-        residual = []
-        for m in range(3):
-            residual.append(to_lanes(natural_ref[m], select))
-            field_ref[m, own, :] = residual[m]
         for i in range(label_x):
             labels = labels_ref[i]
             moduli = jnp.zeros(labels.shape, f32)
             for phase in range(sh.phases):
                 moduli = jnp.where(labels == phase, moduli_ref[phase], moduli)
             stiff[i * label_y : (i + 1) * label_y, :] = moduli
-        by_z = lax.dot_general(
-            repeat_twice(label_z), stiff[...], (((1,), (1,)), ((), ())), precision=highest, preferred_element_type=f32
-        )
-        lane, along, across = sh.lane_grid(label_x * label_y)
-        inside = (along >= 0) & (along < sh.x) & (across >= 0) & (across < sh.y)
-        block = lax.broadcasted_iota(jnp.int32, along.shape, 0)
-        to_block = (inside & (block == (along >> 1) * label_y + (across >> 1))).astype(f32)
-        field_ref[3, own, :] = jnp.dot(by_z, to_block, precision=highest, preferred_element_type=f32)
-        nodes = to_lanes(nodes_ref[...].astype(f32) + 1.0, select) - 1.0
-        lanes_ref[...] = nodes
-        line = coarse_sums(sh, nodes, residual, node_count, sums)
+        cells = [natural_ref[m] for m in range(3)]
+        line = coarse_sums(sh, nodes_ref[...], cells, cell_coords(sh), node_count, sums)
         for i, (cell, block) in enumerate(
             (
                 (0, 0),
@@ -746,18 +767,20 @@
             for m in range(3):
                 lines[8 * i + m : 8 * i + m + 1, :] = natural_ref[m, cell : cell + 1, :]
             lines[8 * i + 3 : 8 * i + 4, 0:label_z] = stiff[block : block + 1, :]
-        for i, layer in ((4, EDGE + sh.z - 1), (5, EDGE)):
+        select = selection(sh)
+        layers = [end_layers(cells[m], select) for m in range(3)] + [end_layers(stiff[...], block_places())]
+        for i in range(2):
             for f in range(4):
-                lines[8 * i + f : 8 * i + f + 1, :] = field_ref[f, layer : layer + 1, :]
+                lines[8 * (4 + i) + f : 8 * (4 + i) + f + 1, :] = layers[f][i : i + 1]
         for i in range(6):
             lines[8 * i + 4 : 8 * i + 5, :] = line
         send_lines(sh, lines, slots_ref)
         pack_faces(sh, natural_ref, stiff, label_x, label_y, x_refs, y_refs)
 
-    start_field, nodes, lines, *messages = call(
+    stiff_blocks, lines, *messages = call(
         begin,
         "begin",
-        [(4,) + plane, (sh.z, LANES), (8 * sh.devices, LANES)]
+        [(label_x * label_y, label_z), (8 * sh.devices, LANES)]
         + [face_shape(sh, label_x, label_y)] * (sh.x_links + sh.y_links),
         [natural, phase_labels, phase_moduli, nodes_natural],
         [
@@ -767,10 +790,24 @@
             pltpu.VMEM(nodes_natural.shape, jnp.int32),
             pltpu.SemaphoreType.DMA((4,)),
             (LANES, LANES),
-            (label_x * label_y, label_z),
             (48, LANES),
         ],
         remote_ins=True,
+    )
+
+    def spread(natural_ref, nodes_ref, stiff, field_ref, lanes_ref):
+        select = selection(sh)
+        field_ref[...] = jnp.zeros(field_ref.shape, f32)
+        for m in range(3):
+            field_ref[m, own, :] = to_lanes(natural_ref[m], select)
+        by_z = lax.dot_general(
+            repeat_twice(label_z), stiff[...], (((1,), (1,)), ((), ())), precision=highest, preferred_element_type=f32
+        )
+        field_ref[3, own, :] = jnp.dot(by_z, block_places(), precision=highest, preferred_element_type=f32)
+        lanes_ref[...] = to_lanes(nodes_ref[...].astype(f32) + 1.0, select) - 1.0
+
+    start_field, nodes = call(
+        spread, "spread", [(4,) + plane, (sh.z, LANES)], [natural, nodes_natural, stiff_blocks]
     )
     from_y, from_x = send_faces(sh, messages[: sh.x_links], messages[sh.x_links :])
     lines = to_all(lines)
@@ -846,7 +883,7 @@
         for m in range(3):
             image_ref[m] = pick(keep, image[m])
         sums[...] = jnp.zeros(sums.shape, f32)
-        line = coarse_sums(sh, nodes_ref[...], [image_ref[m, own, :] for m in range(3)], node_count, sums)
+        line = coarse_sums(sh, nodes_ref[...], [image_ref[m, own, :] for m in range(3)], coords(sh), node_count, sums)
         slots_ref[...] = jnp.broadcast_to(line, slots_ref.shape)
 
     search, image, sums = call(

time: 77 us -> 74 us (0.961)
  local copies, waits for them, and re-layouts: 3 us -> 0.04 us
    unnamed x12 -> x14, local copies, waits for them, and re-layouts: 3 us -> 0.04 us
    pallas_call x10 -> x11, Pallas kernels: 19.9 us -> 20.3 us  [call(): pl.pallas_call(kernel, out_shape=[jax.ShapeDtypeStruct(shape, f32) for sh...]
  transfers between devices with their start and end apart: 20 -> 20, of which waited for: 14 -> 13; matrix products, arithmetic and copies ran while one was open for 0% -> 0% of each run, Pallas kernels for 7% -> 7%
where the time goes in v5:
time: 74 us; the launch traced here: 73.8 us
  starting transfers between devices  28.1 us (38%)
  waiting for transfers between devices  24.6 us (33%)
  Pallas kernels  20.3 us (27%)
  between operations  0.81 us (1%)
    pallas_call x11, Pallas kernels, call(): pl.pallas_call(kernel, out_shape=[jax.ShapeDtypeStruct(shape, f32) for sh...  20.3 us
    ppermute x17, waiting for transfers between devices, send(): return lax.ppermute(value, AXES, permutation(sh.sizes, moves))  14.3 us
    all_to_all x3, starting transfers between devices, to_all(): return lax.all_to_all(slots, AXES, 0, 0, tiled=True)  14.3 us
    ppermute x17, starting transfers between devices, send(): return lax.ppermute(value, AXES, permutation(sh.sizes, moves))  13.8 us
    all_to_all x3, waiting for transfers between devices, to_all(): return lax.all_to_all(slots, AXES, 0, 0, tiled=True)  10.2 us
  transfers between devices with their start and end apart: 20, of which 13 were waited for; matrix products, arithmetic and copies ran while one was open for 0% of the time, Pallas kernels for 7%

profile of v5, /device:TPU:0, one launch (start us, length us, event | category | flops | bytes accessed | tf_op | source)
XLA Modules:
  0.0 73.8 jit_solution(8961828021693029647)
XLA Ops:
  0.6 2.7 %begin.1 = (f32[16,64]{1,0:T(8,128)}, f32[256,128]{1,0:T(8,128)}, f32[32,128]{1,0:T(8,128)}, f32[32,128]{1,0:T(8,128)}, f32[32,128]{1,0:T(8,128)}) custom-call(f32[3,64,128]{2,1,0:T(8,128)} %bitcast.14, s32[4,4,64]{2,1,0:T(4,128)} %labels_in.1, f32[8]{0:T(128)} %moduli_in.1, s32[64,128]{1,0:T(8,128)} %bitcast.18), custom_call_target="tpu_custom_call" | custom-call | tf_op jit(solution)/shard_map/begin/pallas_call | solution.py:608
  3.3 0.0 copy-start.6
  3.4 0.0 copy-start.4
  3.4 0.0 copy-start
  3.4 0.0 copy-start.1
  3.4 7.3 %all-to-all-start = ((f32[32,8,128]{2,1,0:T(8,128)}), f32[32,8,128]{2,1,0:T(8,128)S(1)}, u32[]{:S(2)}, u32[]{:S(2)}) async-start(f32[32,8,128]{2,1,0:T(8,128)} %bitcast.22), calls=%async_computation | async-start | bytes 262144 | tf_op jit(solution)/shard_map/all_to_all | solution.py:655
  10.7 1.8 %collective-permute-start = (f32[32,128]{1,0:T(8,128)S(1)}, f32[32,128]{1,0:T(8,128)S(1)}, u32[]{:S(2)}, u32[]{:S(2)}) collective-permute-start(f32[32,128]{1,0:T(8,128)S(1)} %copy-done.6), channel_id=1, source_target_pairs={{0,4},{1,5},{2,6},{3,7},{4,0},{5,1},{6,2},{7,3},{8,12},{9,13},{10,... | collective-permute-start | bytes 49160 | tf_op jit(solution)/shard_map/ppermute | solution.py:641
  12.6 1.5 %collective-permute-start.1 = (f32[32,128]{1,0:T(8,128)S(1)}, f32[32,128]{1,0:T(8,128)S(1)}, u32[]{:S(2)}, u32[]{:S(2)}) collective-permute-start(f32[32,128]{1,0:T(8,128)S(1)} %copy-done.5), channel_id=1, source_target_pairs={{0,16},{1,17},{2,18},{3,19},{4,8},{5,9},{6,10},{7,11},{8,4},{9,5},... | collective-permute-start | bytes 49160 | tf_op jit(solution)/shard_map/ppermute | solution.py:641
  14.0 0.6 collective-permute-start.2
  14.6 0.6 spread.1
  15.2 1.4 %collective-permute-done.1.refs_2_ = f32[32,128]{1,0:T(8,128)S(1)} collective-permute-done((f32[32,128]{1,0:T(8,128)S(1)}, f32[32,128]{1,0:T(8,128)S(1)}, u32[]{:S(2)}, u32[]{:S(2)}) %collective-permute-start.1) | collective-permute-done | bytes 16416 | tf_op jit(solution)/shard_map/ppermute | solution.py:641
  16.6 1.2 %collective-permute-done.2.refs_3_ = f32[32,128]{1,0:T(8,128)S(1)} collective-permute-done((f32[32,128]{1,0:T(8,128)S(1)}, f32[32,128]{1,0:T(8,128)S(1)}, u32[]{:S(2)}, u32[]{:S(2)}) %collective-permute-start.2) | collective-permute-done | bytes 16416 | tf_op jit(solution)/shard_map/ppermute | solution.py:641
  17.8 1.2 %all-to-all-done = f32[32,8,128]{2,1,0:T(8,128)S(1)} async-done(((f32[32,8,128]{2,1,0:T(8,128)}), f32[32,8,128]{2,1,0:T(8,128)S(1)}, u32[]{:S(2)}, u32[]{:S(2)}) %all-to-all-start) | async-done | bytes 131104 | tf_op jit(solution)/shard_map/all_to_all | solution.py:655
  19.0 4.5 %first_solve.1 = (f32[3,144,128]{2,1,0:T(8,128)S(1)}, f32[8,144,128]{2,1,0:T(8,128)S(1)}, f32[24,128]{1,0:T(8,128)S(1)}, f32[24,128]{1,0:T(8,128)S(1)}) custom-call(f32[4,144,128]{2,1,0:T(8,128)S(1)} %get-tuple-element.35.refs_0_.refs_10_, f32[32,128]{1,0:T(8,128)S(1)} %collective-permute-done.refs_1_, f32[32,128]{1,0:T(8,128)S(1)} %collective-permute-done.1.refs_2_, ...), custom_call_target="tpu_custom_call" | custom-call | tf_op jit(solution)/shard_map/first_solve/pallas_call | solution.py:608
  23.5 0.5 collective-permute-start.3
  23.9 0.3 collective-permute-start.4
  24.3 0.5 collective-permute-done.3.refs_1_
  24.8 2.3 %collective-permute-done.4.refs_2_ = f32[24,128]{1,0:T(8,128)S(1)} collective-permute-done((f32[24,128]{1,0:T(8,128)S(1)}, f32[24,128]{1,0:T(8,128)S(1)}, u32[]{:S(2)}, u32[]{:S(2)}) %collective-permute-start.4) | collective-permute-done | bytes 12320 | tf_op jit(solution)/shard_map/ppermute | solution.py:641
  27.1 0.3 deep.1
  27.4 0.1 collective-permute-start.5
  27.5 1.4 %collective-permute-start.6 = (f32[144,128]{1,0:T(8,128)S(1)}, f32[144,128]{1,0:T(8,128)S(1)}, u32[]{:S(2)}, u32[]{:S(2)}) collective-permute-start(f32[144,128]{1,0:T(8,128)S(1)} %get-tuple-element.45), channel_id=1, source_target_pairs={{0,16},{1,17},{2,18},{3,19},{4,8},{5,9},{6,10},{7,11},{8,4},{9,5},... | collective-permute-start | bytes 221192 | tf_op jit(solution)/shard_map/ppermute | solution.py:641
  29.0 0.6 collective-permute-start.7
  29.6 1.5 %collective-permute-start.8 = (f32[40,128]{1,0:T(8,128)S(1)}, f32[40,128]{1,0:T(8,128)S(1)}, u32[]{:S(2)}, u32[]{:S(2)}) collective-permute-start(f32[40,128]{1,0:T(8,128)S(1)} %get-tuple-element.47), channel_id=1, source_target_pairs={{0,20},{1,21},{2,22},{3,23},{4,16},{5,17},{6,18},{7,19},{8,28},{9,... | collective-permute-start | bytes 61448 | tf_op jit(solution)/shard_map/ppermute | solution.py:641
  31.1 0.6 collective-permute-start.9
  31.6 2.6 %collective-permute-done.8.refs_6_ = f32[40,128]{1,0:T(8,128)S(1)} collective-permute-done((f32[40,128]{1,0:T(8,128)S(1)}, f32[40,128]{1,0:T(8,128)S(1)}, u32[]{:S(2)}, u32[]{:S(2)}) %collective-permute-start.8) | collective-permute-done | bytes 20512 | tf_op jit(solution)/shard_map/ppermute | solution.py:641
  34.3 0.6 collective-permute-done.9.refs_7_
  34.9 3.4 %first_image.1 = (f32[3,144,128]{2,1,0:T(8,128)S(1)}, f32[3,144,128]{2,1,0:T(8,128)S(1)}, f32[32,128]{1,0:T(8,128)}) custom-call(f32[3,144,128]{2,1,0:T(8,128)S(1)} %get-tuple-element.41.refs_0_, f32[24,128]{1,0:T(8,128)S(1)} %collective-permute-done.3.refs_1_, f32[24,128]{1,0:T(8,128)S(1)} %collective-permute-done.4.refs_2_, ...), custom_call_target="tpu_custom_call" | custom-call | tf_op jit(solution)/shard_map/first_image/pallas_call | solution.py:608
  38.2 3.7 %all-to-all-start.1 = ((f32[32,1,128]{2,1,0:T(1,128)}), f32[32,1,128]{2,1,0:T(1,128)S(1)}, u32[]{:S(2)}, u32[]{:S(2)}) async-start(f32[32,1,128]{2,1,0:T(1,128)} %bitcast.5), calls=%async_computation.1 | async-start | bytes 32768 | tf_op jit(solution)/shard_map/all_to_all | solution.py:655
  42.0 3.3 %second_solve.1.local_ref = f32[3,144,128]{2,1,0:T(8,128)S(1)} custom-call(f32[3,144,128]{2,1,0:T(8,128)S(1)} %get-tuple-element.50.image_ref.refs_12_.first_ref, f32[8,144,128]{2,1,0:T(8,128)S(1)} %get-tuple-element.49.refs_9_.springs_ref), custom_call_target="tpu_custom_call" | custom-call | tf_op jit(solution)/shard_map/second_solve/pallas_call | solution.py:608
  45.3 3.6 %all-to-all-done.1 = f32[32,1,128]{2,1,0:T(1,128)S(1)} async-done(((f32[32,1,128]{2,1,0:T(1,128)}), f32[32,1,128]{2,1,0:T(1,128)S(1)}, u32[]{:S(2)}, u32[]{:S(2)}) %all-to-all-start.1) | async-done | bytes 16416 | tf_op jit(solution)/shard_map/all_to_all | solution.py:655
  48.9 0.4 second_add.1
  49.3 0.1 collective-permute-start.10
  49.4 0.7 collective-permute-start.11
  50.0 0.5 collective-permute-done.10.refs_1_
  50.5 2.0 %collective-permute-done.11.refs_2_ = f32[24,128]{1,0:T(8,128)S(1)} collective-permute-done((f32[24,128]{1,0:T(8,128)S(1)}, f32[24,128]{1,0:T(8,128)S(1)}, u32[]{:S(2)}, u32[]{:S(2)}) %collective-permute-start.11) | collective-permute-done | bytes 12320 | tf_op jit(solution)/shard_map/ppermute | solution.py:641
  52.6 0.4 near.1
  53.0 0.7 collective-permute-start.14
  53.6 0.5 collective-permute-start.12
  54.1 1.4 %collective-permute-start.13 = (f32[72,128]{1,0:T(8,128)S(1)}, f32[72,128]{1,0:T(8,128)S(1)}, u32[]{:S(2)}, u32[]{:S(2)}) collective-permute-start(f32[72,128]{1,0:T(8,128)S(1)} %get-tuple-element.56), channel_id=1, source_target_pairs={{0,16},{1,17},{2,18},{3,19},{4,8},{5,9},{6,10},{7,11},{8,4},{9,5},... | collective-permute-start | bytes 110600 | tf_op jit(solution)/shard_map/ppermute | solution.py:641
  55.6 1.0 %collective-permute-start.15 = (f32[24,128]{1,0:T(8,128)S(1)}, f32[24,128]{1,0:T(8,128)S(1)}, u32[]{:S(2)}, u32[]{:S(2)}) collective-permute-start(f32[24,128]{1,0:T(8,128)S(1)} %get-tuple-element.58), channel_id=1, source_target_pairs={{0,20},{1,21},{2,22},{3,23},{4,16},{5,17},{6,18},{7,19},{8,28},{9,... | collective-permute-start | bytes 36872 | tf_op jit(solution)/shard_map/ppermute | solution.py:641
  56.5 0.6 collective-permute-start.16
  57.1 3.1 %collective-permute-done.15.refs_6_ = f32[24,128]{1,0:T(8,128)S(1)} collective-permute-done((f32[24,128]{1,0:T(8,128)S(1)}, f32[24,128]{1,0:T(8,128)S(1)}, u32[]{:S(2)}, u32[]{:S(2)}) %collective-permute-start.15) | collective-permute-done | bytes 12320 | tf_op jit(solution)/shard_map/ppermute | solution.py:641
  60.2 0.1 collective-permute-done.16.refs_7_
  60.3 2.2 %second_image.1 = (f32[3,144,128]{2,1,0:T(8,128)S(1)}, f32[3,144,128]{2,1,0:T(8,128)S(1)}, f32[32,128]{1,0:T(8,128)}) custom-call(f32[3,144,128]{2,1,0:T(8,128)S(1)} %get-tuple-element.52.refs_0_, f32[24,128]{1,0:T(8,128)S(1)} %collective-permute-done.10.refs_1_, f32[24,128]{1,0:T(8,128)S(1)} %collective-permute-done.11.refs_2_, ...), custom_call_target="tpu_custom_call" | custom-call | tf_op jit(solution)/shard_map/second_image/pallas_call | solution.py:608
  62.5 3.3 %all-to-all-start.2 = ((f32[32,1,128]{2,1,0:T(1,128)}), f32[32,1,128]{2,1,0:T(1,128)S(1)}, u32[]{:S(2)}, u32[]{:S(2)}) async-start(f32[32,1,128]{2,1,0:T(1,128)} %bitcast.8), calls=%async_computation.2 | async-start | bytes 32768 | tf_op jit(solution)/shard_map/all_to_all | solution.py:655
  65.8 1.6 %turn.1.turned_ref = f32[4,3,64,128]{3,2,1,0:T(8,128)S(1)} custom-call(f32[3,144,128]{2,1,0:T(8,128)S(1)} %get-tuple-element.60.refs_11_.search_ref, f32[3,144,128]{2,1,0:T(8,128)S(1)} %get-tuple-element.50.image_ref.refs_12_.first_ref, f32[3,144,128]{2,1,0:T(8,128)S(1)} %get-tuple-element.62.second_ref, f32[3,144,128]{2,1,0:T(8,128)S(1)} %get-tuple-element.63.image_ref), custom_call_target="tpu_custom_call" | custom-call | tf_op jit(solution)/shard_map/turn/pallas_call | solution.py:608
  67.4 5.5 %all-to-all-done.2 = f32[32,1,128]{2,1,0:T(1,128)S(1)} async-done(((f32[32,1,128]{2,1,0:T(1,128)}), f32[32,1,128]{2,1,0:T(1,128)S(1)}, u32[]{:S(2)}, u32[]{:S(2)}) %all-to-all-start.2) | async-done | bytes 16416 | tf_op jit(solution)/shard_map/all_to_all | solution.py:655
  72.9 0.9 %finish.1 = (f32[3,64,128]{2,1,0:T(8,128)}, f32[3,64,128]{2,1,0:T(8,128)}) custom-call(f32[32,128]{1,0:T(8,128)S(1)} %bitcast.20, f32[3,64,128]{2,1,0:T(8,128)S(1)} %bitcast.16, f32[4,3,64,128]{3,2,1,0:T(8,128)S(1)} %turn.1.turned_ref), custom_call_target="tpu_custom_call" | custom-call | tf_op jit(solution)/shard_map/finish/pallas_call | solution.py:608
  (17 shorter events, 0.0 us)
Async XLA Ops:
  0.6 14.0 %copy-start.2 = (s32[8,8,128]{2,1,0:T(8,128)S(1)}, s32[8,8,128]{2,1,0:T(8,128)}, u32[]{:S(2)}) copy-start(s32[8,8,128]{2,1,0:T(8,128)} %param.8) | copy-start | bytes 98308
  3.3 7.4 %copy-start.6 = (f32[32,128]{1,0:T(8,128)S(1)}, f32[32,128]{1,0:T(8,128)}, u32[]{:S(2)}) copy-start(f32[32,128]{1,0:T(8,128)} %get-tuple-element.36) | copy-start | bytes 49156
  3.4 9.2 %copy-start.5 = (f32[32,128]{1,0:T(8,128)S(1)}, f32[32,128]{1,0:T(8,128)}, u32[]{:S(2)}) copy-start(f32[32,128]{1,0:T(8,128)} %get-tuple-element.37) | copy-start | bytes 49156
  3.4 10.7 %copy-start.4 = (f32[32,128]{1,0:T(8,128)S(1)}, f32[32,128]{1,0:T(8,128)}, u32[]{:S(2)}) copy-start(f32[32,128]{1,0:T(8,128)} %get-tuple-element.38) | copy-start | bytes 49156
  3.4 11.2 %copy-start.3 = (f32[16,64]{1,0:T(8,128)S(1)}, f32[16,64]{1,0:T(8,128)}, u32[]{:S(2)}) copy-start(f32[16,64]{1,0:T(8,128)} %get-tuple-element.34.stiff) | copy-start | bytes 12292
  3.4 11.2 %copy-start = (f32[3,8,8,128]{3,2,1,0:T(8,128)S(1)}, f32[3,8,8,128]{3,2,1,0:T(8,128)}, u32[]{:S(2)}) copy-start(f32[3,8,8,128]{3,2,1,0:T(8,128)} %param.5) | copy-start | bytes 294916
  3.4 15.6 %copy-start.1 = (f32[36,1152]{1,0:T(8,128)S(1)}, f32[36,1152]{1,0:T(8,128)}, u32[]{:S(2)}) copy-start(f32[36,1152]{1,0:T(8,128)} %inverse_ref.1) | copy-start | bytes 497668
  3.4 15.6 %all-to-all-start = ((f32[32,8,128]{2,1,0:T(8,128)}), f32[32,8,128]{2,1,0:T(8,128)S(1)}, u32[]{:S(2)}, u32[]{:S(2)}) async-start(f32[32,8,128]{2,1,0:T(8,128)} %bitcast.22), calls=%async_computation | async-start | bytes 262144 | tf_op jit(solution)/shard_map/all_to_all | solution.py:655
  10.7 4.5 %collective-permute-start = (f32[32,128]{1,0:T(8,128)S(1)}, f32[32,128]{1,0:T(8,128)S(1)}, u32[]{:S(2)}, u32[]{:S(2)}) collective-permute-start(f32[32,128]{1,0:T(8,128)S(1)} %copy-done.6), channel_id=1, source_target_pairs={{0,4},{1,5},{2,6},{3,7},{4,0},{5,1},{6,2},{7,3},{8,12},{9,13},{10,... | collective-permute-start | bytes 49160 | tf_op jit(solution)/shard_map/ppermute | solution.py:641
  12.6 4.0 %collective-permute-start.1 = (f32[32,128]{1,0:T(8,128)S(1)}, f32[32,128]{1,0:T(8,128)S(1)}, u32[]{:S(2)}, u32[]{:S(2)}) collective-permute-start(f32[32,128]{1,0:T(8,128)S(1)} %copy-done.5), channel_id=1, source_target_pairs={{0,16},{1,17},{2,18},{3,19},{4,8},{5,9},{6,10},{7,11},{8,4},{9,5},... | collective-permute-start | bytes 49160 | tf_op jit(solution)/shard_map/ppermute | solution.py:641
  14.0 3.8 %collective-permute-start.2 = (f32[32,128]{1,0:T(8,128)S(1)}, f32[32,128]{1,0:T(8,128)S(1)}, u32[]{:S(2)}, u32[]{:S(2)}) collective-permute-start(f32[32,128]{1,0:T(8,128)S(1)} %copy-done.4), channel_id=1, source_target_pairs={{0,16},{1,17},{2,18},{3,19},{4,20},{5,21},{6,22},{7,23},{8,24},{9,... | collective-permute-start | bytes 49160 | tf_op jit(solution)/shard_map/ppermute | solution.py:641
  23.5 1.3 %collective-permute-start.3 = (f32[24,128]{1,0:T(8,128)S(1)}, f32[24,128]{1,0:T(8,128)S(1)}, u32[]{:S(2)}, u32[]{:S(2)}) collective-permute-start(f32[24,128]{1,0:T(8,128)S(1)} %get-tuple-element.42), channel_id=1, source_target_pairs={{0,1},{1,0},{2,3},{3,2},{4,5},{5,4},{6,7},{7,6},{8,9},{9,8},{10,11... | collective-permute-start | bytes 36872 | tf_op jit(solution)/shard_map/ppermute | solution.py:641
  23.9 3.1 %collective-permute-start.4 = (f32[24,128]{1,0:T(8,128)S(1)}, f32[24,128]{1,0:T(8,128)S(1)}, u32[]{:S(2)}, u32[]{:S(2)}) collective-permute-start(f32[24,128]{1,0:T(8,128)S(1)} %get-tuple-element.43), channel_id=1, source_target_pairs={{0,3},{1,2},{2,1},{3,0},{4,7},{5,6},{6,5},{7,4},{8,11},{9,10},{10,... | collective-permute-start | bytes 36872 | tf_op jit(solution)/shard_map/ppermute | solution.py:641
  27.4 7.5 %collective-permute-start.5 = (f32[144,128]{1,0:T(8,128)S(1)}, f32[144,128]{1,0:T(8,128)S(1)}, u32[]{:S(2)}, u32[]{:S(2)}) collective-permute-start(f32[144,128]{1,0:T(8,128)S(1)} %get-tuple-element.44), channel_id=1, source_target_pairs={{0,4},{1,5},{2,6},{3,7},{4,0},{5,1},{6,2},{7,3},{8,12},{9,13},{10,... | collective-permute-start | bytes 221192 | tf_op jit(solution)/shard_map/ppermute | solution.py:641
  27.5 7.3 %collective-permute-start.6 = (f32[144,128]{1,0:T(8,128)S(1)}, f32[144,128]{1,0:T(8,128)S(1)}, u32[]{:S(2)}, u32[]{:S(2)}) collective-permute-start(f32[144,128]{1,0:T(8,128)S(1)} %get-tuple-element.45), channel_id=1, source_target_pairs={{0,16},{1,17},{2,18},{3,19},{4,8},{5,9},{6,10},{7,11},{8,4},{9,5},... | collective-permute-start | bytes 221192 | tf_op jit(solution)/shard_map/ppermute | solution.py:641
  29.0 5.9 %collective-permute-start.7 = (f32[144,128]{1,0:T(8,128)S(1)}, f32[144,128]{1,0:T(8,128)S(1)}, u32[]{:S(2)}, u32[]{:S(2)}) collective-permute-start(f32[144,128]{1,0:T(8,128)S(1)} %get-tuple-element.46), channel_id=1, source_target_pairs={{0,16},{1,17},{2,18},{3,19},{4,20},{5,21},{6,22},{7,23},{8,24},{9,... | collective-permute-start | bytes 221192 | tf_op jit(solution)/shard_map/ppermute | solution.py:641
  29.6 4.7 %collective-permute-start.8 = (f32[40,128]{1,0:T(8,128)S(1)}, f32[40,128]{1,0:T(8,128)S(1)}, u32[]{:S(2)}, u32[]{:S(2)}) collective-permute-start(f32[40,128]{1,0:T(8,128)S(1)} %get-tuple-element.47), channel_id=1, source_target_pairs={{0,20},{1,21},{2,22},{3,23},{4,16},{5,17},{6,18},{7,19},{8,28},{9,... | collective-permute-start | bytes 61448 | tf_op jit(solution)/shard_map/ppermute | solution.py:641
  31.1 3.8 %collective-permute-start.9 = (f32[40,128]{1,0:T(8,128)S(1)}, f32[40,128]{1,0:T(8,128)S(1)}, u32[]{:S(2)}, u32[]{:S(2)}) collective-permute-start(f32[40,128]{1,0:T(8,128)S(1)} %get-tuple-element.48), channel_id=1, source_target_pairs={{0,16},{1,17},{2,18},{3,19},{4,24},{5,25},{6,26},{7,27},{8,20},{9,... | collective-permute-start | bytes 61448 | tf_op jit(solution)/shard_map/ppermute | solution.py:641
  38.2 10.6 %all-to-all-start.1 = ((f32[32,1,128]{2,1,0:T(1,128)}), f32[32,1,128]{2,1,0:T(1,128)S(1)}, u32[]{:S(2)}, u32[]{:S(2)}) async-start(f32[32,1,128]{2,1,0:T(1,128)} %bitcast.5), calls=%async_computation.1 | async-start | bytes 32768 | tf_op jit(solution)/shard_map/all_to_all | solution.py:655
  49.3 1.2 %collective-permute-start.10 = (f32[24,128]{1,0:T(8,128)S(1)}, f32[24,128]{1,0:T(8,128)S(1)}, u32[]{:S(2)}, u32[]{:S(2)}) collective-permute-start(f32[24,128]{1,0:T(8,128)S(1)} %get-tuple-element.53), channel_id=1, source_target_pairs={{0,1},{1,0},{2,3},{3,2},{4,5},{5,4},{6,7},{7,6},{8,9},{9,8},{10,11... | collective-permute-start | bytes 36872 | tf_op jit(solution)/shard_map/ppermute | solution.py:641
  49.4 3.2 %collective-permute-start.11 = (f32[24,128]{1,0:T(8,128)S(1)}, f32[24,128]{1,0:T(8,128)S(1)}, u32[]{:S(2)}, u32[]{:S(2)}) collective-permute-start(f32[24,128]{1,0:T(8,128)S(1)} %get-tuple-element.54), channel_id=1, source_target_pairs={{0,3},{1,2},{2,1},{3,0},{4,7},{5,6},{6,5},{7,4},{8,11},{9,10},{10,... | collective-permute-start | bytes 36872 | tf_op jit(solution)/shard_map/ppermute | solution.py:641
  53.0 7.3 %collective-permute-start.14 = (f32[144,128]{1,0:T(8,128)S(1)}, f32[144,128]{1,0:T(8,128)S(1)}, u32[]{:S(2)}, u32[]{:S(2)}) collective-permute-start(f32[144,128]{1,0:T(8,128)S(1)} %get-tuple-element.57), channel_id=1, source_target_pairs={{0,16},{1,17},{2,18},{3,19},{4,20},{5,21},{6,22},{7,23},{8,24},{9,... | collective-permute-start | bytes 221192 | tf_op jit(solution)/shard_map/ppermute | solution.py:641
  53.6 6.7 %collective-permute-start.12 = (f32[72,128]{1,0:T(8,128)S(1)}, f32[72,128]{1,0:T(8,128)S(1)}, u32[]{:S(2)}, u32[]{:S(2)}) collective-permute-start(f32[72,128]{1,0:T(8,128)S(1)} %get-tuple-element.55), channel_id=1, source_target_pairs={{0,4},{1,5},{2,6},{3,7},{4,0},{5,1},{6,2},{7,3},{8,12},{9,13},{10,... | collective-permute-start | bytes 110600 | tf_op jit(solution)/shard_map/ppermute | solution.py:641
  54.1 6.2 %collective-permute-start.13 = (f32[72,128]{1,0:T(8,128)S(1)}, f32[72,128]{1,0:T(8,128)S(1)}, u32[]{:S(2)}, u32[]{:S(2)}) collective-permute-start(f32[72,128]{1,0:T(8,128)S(1)} %get-tuple-element.56), channel_id=1, source_target_pairs={{0,16},{1,17},{2,18},{3,19},{4,8},{5,9},{6,10},{7,11},{8,4},{9,5},... | collective-permute-start | bytes 110600 | tf_op jit(solution)/shard_map/ppermute | solution.py:641
  55.6 4.6 %collective-permute-start.15 = (f32[24,128]{1,0:T(8,128)S(1)}, f32[24,128]{1,0:T(8,128)S(1)}, u32[]{:S(2)}, u32[]{:S(2)}) collective-permute-start(f32[24,128]{1,0:T(8,128)S(1)} %get-tuple-element.58), channel_id=1, source_target_pairs={{0,20},{1,21},{2,22},{3,23},{4,16},{5,17},{6,18},{7,19},{8,28},{9,... | collective-permute-start | bytes 36872 | tf_op jit(solution)/shard_map/ppermute | solution.py:641
  56.5 3.8 %collective-permute-start.16 = (f32[24,128]{1,0:T(8,128)S(1)}, f32[24,128]{1,0:T(8,128)S(1)}, u32[]{:S(2)}, u32[]{:S(2)}) collective-permute-start(f32[24,128]{1,0:T(8,128)S(1)} %get-tuple-element.59), channel_id=1, source_target_pairs={{0,16},{1,17},{2,18},{3,19},{4,24},{5,25},{6,26},{7,27},{8,20},{9,... | collective-permute-start | bytes 36872 | tf_op jit(solution)/shard_map/ppermute | solution.py:641
  62.5 10.3 %all-to-all-start.2 = ((f32[32,1,128]{2,1,0:T(1,128)}), f32[32,1,128]{2,1,0:T(1,128)S(1)}, u32[]{:S(2)}, u32[]{:S(2)}) async-start(f32[32,1,128]{2,1,0:T(1,128)} %bitcast.8), calls=%async_computation.2 | async-start | bytes 32768 | tf_op jit(solution)/shard_map/all_to_all | solution.py:655

commit v6 on v5

--- a/solution.py
+++ b/solution.py
@@ -210,7 +210,7 @@
     for ref in refs:
         for f in range(ref.shape[0]):
             ref[f, :EDGE, :] = jnp.zeros((EDGE, LANES), f32)
-            ref[f, sh.tall - EDGE :, :] = jnp.zeros((EDGE, LANES), f32)
+            ref[f, ref.shape[1] - EDGE :, :] = jnp.zeros((EDGE, LANES), f32)
 
 
 def inner(ref, f):
@@ -346,9 +346,17 @@
     return lax.broadcasted_iota(jnp.int32, (sh.rows, LANES), 0) - EDGE
 
 
-def extended_mask(sh):
+def ends_level(sh):
+    row = lax.broadcasted_iota(jnp.int32, (4 * EDGE, LANES), 0)
+    return jnp.where(row < 2 * EDGE, row, row + sh.rows - 4 * EDGE) - EDGE
+
+
+def ends(value):
+    return jnp.concatenate([value[: 2 * EDGE], value[value.shape[0] - 2 * EDGE :]], axis=0)
+
+
+def extended_mask(sh, z):
     lane, _, across = sh.lane_grid(1)
-    z = level(sh)
     return ((lane < sh.used) & (across >= -1) & (across <= sh.y)) & ((z >= -1) & (z <= sh.z))
 
 
@@ -370,27 +378,32 @@
     ref[f, EDGE : ref.shape[1] - EDGE, :] = value
 
 
-def local_solve(sh, residual_ref, springs_ref, v, kv, factor):
+def local_solve(sh, z, residual_ref, springs_ref, v, kv, factor):
     lane, _, _ = sh.lane_grid(1)
-    mask = extended_mask(sh)
+    mask = extended_mask(sh, z)
     for m in range(3):
         factor[m] = pick(mask, relax / jnp.where(mask, springs_ref[m], 1.0))
-        z = residual_ref[m] * factor[m]
-        put(v[0], m, z)
-        put(kv[0], m, springs_ref[6] * z)
+        value = residual_ref[m] * factor[m]
+        put(v[0], m, value)
+        put(kv[0], m, springs_ref[6] * value)
     for sweep in range(SWEEPS - 1):
         old, new = sweep % 2, (sweep + 1) % 2
         image = image_of(sh, lane, v[old], kv[old], None, springs_ref)
         for m in range(3):
-            z = inner(v[old], m) + factor[m] * (residual_ref[m] - image[m])
-            put(v[new], m, z)
-            put(kv[new], m, springs_ref[6] * z)
+            value = inner(v[old], m) + factor[m] * (residual_ref[m] - image[m])
+            put(v[new], m, value)
+            put(kv[new], m, springs_ref[6] * value)
     return (SWEEPS - 1) % 2
 
 
-def coords(sh):
-    lane, along, across = sh.lane_grid(sh.z)
-    z = lax.broadcasted_iota(jnp.int32, (sh.z, LANES), 0)
+def own_level(sh):
+    return lax.broadcasted_iota(jnp.int32, (sh.z, LANES), 0)
+
+
+def coords(sh, z):
+    _, along, across = sh.lane_grid(z.shape[0])
+    along = jnp.where(along < 0, along + sh.x, jnp.where(along < sh.x, along, along - sh.x))
+    across = jnp.where(across < 0, across + sh.y, jnp.where(across < sh.y, across, across - sh.y))
     place = lambda index, size: (2 * index + 1).astype(f32) / size - 1.0
     return place(along, sh.x), place(across, sh.y), place(z, sh.z)
 
@@ -421,17 +434,20 @@
     )
 
 
-def coarse_sums(sh, nodes, field, places, count, sums):
+def coarse_sums(nodes, field, places, count, sums):
     moments = tuple(field) + cross(places, field)
     for node in range(count):
         mask = nodes == node
         for m in range(6):
             sums[node * 6 + m : node * 6 + m + 1, :] = fold_rows(pick(mask, moments[m]))
+
+
+def sums_line(sh, sums, unknowns):
     flat = (sh.here(0) * sh.sizes[1] + sh.here(1)) * sh.sizes[2] + sh.here(2)
-    return pltpu.roll(lane_sums(sums), lax.rem(flat * (6 * count), LANES), 1)[0:1]
-
-
-def coarse_values(sh, nodes, received, inverse_ref, values):
+    return pltpu.roll(lane_sums(sums), lax.rem(flat * unknowns, LANES), 1)[0:1]
+
+
+def coarse_solution(received, inverse_ref, values):
     unknowns, total = inverse_ref.shape
     row = lax.broadcasted_iota(jnp.int32, received.shape, 0)
     part = jnp.zeros((unknowns, LANES), f32)
@@ -442,13 +458,51 @@
     values[0:unknowns, :] = jnp.dot(
         part, jnp.ones((LANES, LANES), f32), precision=highest, preferred_element_type=f32
     )
+
+
+def coarse_shares(sums, inverse_ref, shares):
+    unknowns, total = inverse_ref.shape
+    column = jnp.dot(sums[...], jnp.ones((LANES, LANES), f32), precision=highest, preferred_element_type=f32)
+    for i in range(0, total, LANES):
+        share = inverse_ref[:, i : i + LANES] * column[0:unknowns]
+        shares[i // LANES : i // LANES + 1, :] = jnp.sum(share, axis=0, keepdims=True)
+
+
+def coarse_table(sh, shares_ref, unknowns, flat, table):
+    rows = shares_ref.shape[0] // sh.devices
+    lane = lax.broadcasted_iota(jnp.int32, (1, LANES), 1)
+    for i in range(rows):
+        flat[i : i + 1, :] = jnp.sum(shares_ref[pl.ds(i, sh.devices, stride=rows), :], axis=0, keepdims=True)
+    for device in range(sh.devices):
+        row, place = divmod(device * unknowns, LANES)
+        part = shift(flat[row : row + 1, :], -place)
+        if place + unknowns > LANES:
+            part = jnp.where(lane < LANES - place, part, shift(flat[row + 1 : row + 2, :], -place))
+        table[device : device + 1, :] = pick(lane < unknowns, part)
+
+
+def region_values(sh, table, dz):
+    lane, along, across = sh.lane_grid(1)
+    x = sh.here(0) + jnp.where(along < 0, -1, jnp.where(along < sh.x, 0, 1))
+    y = sh.here(1) + jnp.where(across < 0, -1, jnp.where(across < sh.y, 0, 1))
+    z = sh.here(2) + dz
+    exists = (lane < sh.used) & (x >= 0) & (x < sh.sizes[0]) & (y >= 0) & (y < sh.sizes[1])
+    exists = exists & (z >= 0) & (z < sh.sizes[2])
+    device = jnp.where(exists, (x * sh.sizes[1] + y) * sh.sizes[2] + z, -1)
+    owner = lax.broadcasted_iota(jnp.int32, (sh.devices, LANES), 0) == device
+    return lax.dot_general(
+        table[...], owner.astype(f32), (((0,), (0,)), ((), ())), precision=highest, preferred_element_type=f32
+    )
+
+
+def coarse_cells(nodes, places, values, count):
     cells = []
     for m in range(6):
-        cell = jnp.zeros((sh.z, LANES), f32)
-        for node in range(unknowns // 6):
+        cell = jnp.zeros(nodes.shape, f32)
+        for node in range(count):
             cell = jnp.where(nodes == float(node), values[node * 6 + m : node * 6 + m + 1, :], cell)
         cells.append(cell)
-    turned = cross(cells[3:], coords(sh))
+    turned = cross(cells[3:], places)
     return [cells[m] + turned[m] for m in range(3)]
 
 
@@ -515,7 +569,7 @@
 
 
 def face_shape(sh, label_x, label_y):
-    rows = max(3 * sh.x + label_x, 3 * sh.y + label_y)
+    rows = max(4 * sh.x + label_x, 4 * sh.y + label_y)
     return (-(-rows // 8) * 8, LANES)
 
 
@@ -523,7 +577,7 @@
     even_x, even_y = sh.here(0) % 2 == 0, sh.here(1) % 2 == 0
 
     def face(at, count, stride, label_at, label_count, label_stride):
-        rows = [natural_ref[m, pl.ds(at, count, stride=stride), :] for m in range(3)]
+        rows = [natural_ref[m, pl.ds(at, count, stride=stride), :] for m in range(4)]
         return rows, stiff[pl.ds(label_at, label_count, stride=label_stride), :]
 
     above = face(sh.cells - sh.y, sh.y, 1, (label_x - 1) * label_y, label_y, 1)
@@ -541,14 +595,14 @@
         for i, ref in enumerate(refs):
             ref[...] = jnp.zeros(ref.shape, f32)
             count = above[0][0].shape[0]
-            for m in range(3):
+            for m in range(4):
                 ref[m * count : (m + 1) * count, :] = pair(links, even, above[0][m], below[0][m])[i]
             labels, length = above[1].shape
-            ref[3 * count : 3 * count + labels, 0:length] = pair(links, even, above[1], below[1])[i]
+            ref[4 * count : 4 * count + labels, 0:length] = pair(links, even, above[1], below[1])[i]
 
 
 def merge_start(sh, refs, x_refs, y_refs, received_ref, sizes, cells, labels):
-    residual, stiff, stiff_rim = refs
+    residual, nodes, stiff, stiff_rim = refs
     label_x, label_y, label_z = sizes
     lane, along, across = sh.lane_grid(1)
     inside = lane < sh.used
@@ -561,14 +615,14 @@
     at = label_at = 0
     for axis, face_refs, size, label_size in ((0, x_refs, sh.y, label_y), (1, y_refs, sh.x, label_x)):
         for message in sides(sh, axis, [ref[...] for ref in face_refs]):
-            for m in range(3):
+            for m in range(4):
                 cells[m, at : at + size, :] = message[m * size : (m + 1) * size]
-            labels[label_at : label_at + label_size, :] = message[3 * size : 3 * size + label_size, 0:label_z]
+            labels[label_at : label_at + label_size, :] = message[4 * size : 4 * size + label_size, 0:label_z]
             at, label_at = at + size, label_at + label_size
     for dx, dy in ((-1, -1), (-1, 1), (1, -1), (1, 1)):
         slot = slot_from(sh, received_ref, (dx, dy, 0))
-        for m in range(3):
-            cells[m, at : at + 1, :] = slot[m : m + 1]
+        for m, row in enumerate((0, 1, 2, 5)):
+            cells[m, at : at + 1, :] = slot[row : row + 1]
         labels[label_at : label_at + 1, :] = slot[3:4, 0:label_z]
         at, label_at = at + 1, label_at + 1
     x, y, _, valid = ring(sh.x, sh.y, count)
@@ -577,6 +631,7 @@
     tall_own = slice(2 * EDGE, 2 * EDGE + sh.z)
     for m in range(3):
         residual[m, own, :] += to_lanes(cells[m], place)
+    nodes[own, :] += to_lanes(cells[3], place)
     by_z = lax.dot_general(
         repeat_twice(label_z), labels[...], (((1,), (1,)), ((), ())), precision=highest, preferred_element_type=f32
     )
@@ -598,6 +653,7 @@
         near = EDGE + sh.z if dz > 0 else EDGE - 1
         for m in range(3):
             residual[m, near : near + 1, :] = main[m : m + 1]
+        nodes[near : near + 1, :] = main[5:6]
         for row in (EDGE + near, EDGE + near + dz):
             stiff[0, row : row + 1, :] = main[3:4]
             stiff_rim[0, row : row + 1, :] = edge[3:4]
@@ -714,6 +770,7 @@
     unknowns = coarse_inverse.shape[0]
     node_count = unknowns // 6
     sum_rows = -(-unknowns // 8) * 8
+    share_rows = coarse_inverse.shape[1] // LANES
     own = slice(EDGE, EDGE + sh.z)
     plane = (sh.rows, LANES)
     fields = (3,) + plane
@@ -740,7 +797,7 @@
     def begin(natural_in, labels_in, moduli_in, nodes_in, stiff, slots_ref, *rest):
         x_refs, y_refs = rest[: sh.x_links], rest[sh.x_links : sh.x_links + sh.y_links]
         natural_ref, labels_ref, moduli_ref, nodes_ref, sems, sums, lines = rest[sh.x_links + sh.y_links :]
-        pairs = ((natural_in, natural_ref), (labels_in, labels_ref), (moduli_in, moduli_ref), (nodes_in, nodes_ref))
+        pairs = ((natural_in, natural_ref.at[0:3]), (labels_in, labels_ref), (moduli_in, moduli_ref), (nodes_in, nodes_ref))
         copies = [pltpu.make_async_copy(a, b, sems.at[i]) for i, (a, b) in enumerate(pairs)]
         for copy in copies:
             copy.start()
@@ -754,8 +811,10 @@
             for phase in range(sh.phases):
                 moduli = jnp.where(labels == phase, moduli_ref[phase], moduli)
             stiff[i * label_y : (i + 1) * label_y, :] = moduli
+        natural_ref[3] = nodes_ref[...].astype(f32) + 1.0
         cells = [natural_ref[m] for m in range(3)]
-        line = coarse_sums(sh, nodes_ref[...], cells, cell_coords(sh), node_count, sums)
+        coarse_sums(nodes_ref[...], cells, cell_coords(sh), node_count, sums)
+        line = sums_line(sh, sums, unknowns)
         for i, (cell, block) in enumerate(
             (
                 (0, 0),
@@ -767,11 +826,12 @@
             for m in range(3):
                 lines[8 * i + m : 8 * i + m + 1, :] = natural_ref[m, cell : cell + 1, :]
             lines[8 * i + 3 : 8 * i + 4, 0:label_z] = stiff[block : block + 1, :]
+            lines[8 * i + 5 : 8 * i + 6, :] = natural_ref[3, cell : cell + 1, :]
         select = selection(sh)
-        layers = [end_layers(cells[m], select) for m in range(3)] + [end_layers(stiff[...], block_places())]
+        layers = [end_layers(natural_ref[m], select) for m in range(4)] + [end_layers(stiff[...], block_places())]
         for i in range(2):
-            for f in range(4):
-                lines[8 * (4 + i) + f : 8 * (4 + i) + f + 1, :] = layers[f][i : i + 1]
+            for layer, row in zip(layers, (0, 1, 2, 5, 3)):
+                lines[8 * (4 + i) + row : 8 * (4 + i) + row + 1, :] = layer[i : i + 1]
         for i in range(6):
             lines[8 * i + 4 : 8 * i + 5, :] = line
         send_lines(sh, lines, slots_ref)
@@ -784,7 +844,7 @@
         + [face_shape(sh, label_x, label_y)] * (sh.x_links + sh.y_links),
         [natural, phase_labels, phase_moduli, nodes_natural],
         [
-            natural.shape,
+            (4, sh.cells, sh.z),
             pltpu.VMEM(phase_labels.shape, jnp.int32),
             pltpu.SMEM(phase_moduli.shape, f32),
             pltpu.VMEM(nodes_natural.shape, jnp.int32),
@@ -812,59 +872,104 @@
     from_y, from_x = send_faces(sh, messages[: sh.x_links], messages[sh.x_links :])
     lines = to_all(lines)
 
-    def add_coarse(nodes_ref, coarse, inverse_ref, values, solution_ref, z_refs, ex):
-        added = coarse_values(sh, nodes_ref[...], coarse, inverse_ref, values)
-        valid = nodes_ref[...] >= 0.0
-        for m in range(3):
-            solution_ref[m, own, :] += pick(valid, added[m])
-        pack_z(sh, ex, lambda f, start, count: solution_ref[f, start : start + count, :], z_refs)
-
-    def first_solve(*refs):
+    short = (3, 6 * EDGE, LANES)
+    short_fields = (3, 4 * EDGE, LANES)
+    solve_scratch = [tall] * 4 + [fields]
+    short_scratch = [short] * 4 + [short_fields]
+
+    def end_rows(ref):
+        def rows(f, start, count):
+            place = start + EDGE if start < 2 * EDGE else start - sh.rows + 5 * EDGE
+            return ref[f, place : place + count, :]
+
+        return rows
+
+    def first_ends(*refs):
         take = Taker(refs)
         field_ref = take.one()
         y_refs, x_refs = take(sh.y_links), take(sh.x_links)
         nodes_ref, lines_ref, inverse_ref = take(3)
-        solution_ref, springs_ref = take(2)
+        residual, wide_nodes, stiffness_ref, values = take(4)
         z_refs = take(sh.z_links)
-        residual, stiff, stiff_rim, v0, v1, kv0, kv1, factor, values, cells, labels = take(11)
-        clear_guards(sh, (stiff, stiff_rim, v0, v1, kv0, kv1))
+        stiff, stiff_rim, cells, labels, short_stiff, short_rim, some_residual, springs = take(8)
+        v0, v1, kv0, kv1, factor = take(5)
+        clear_guards(sh, (stiff, stiff_rim, short_stiff, short_rim, v0, v1, kv0, kv1))
         residual[...] = field_ref[0:3]
         put(stiff, 0, field_ref[3])
         put(stiff_rim, 0, jnp.zeros(plane, f32))
         sizes = phase_labels.shape
-        merge_start(sh, (residual, stiff, stiff_rim), x_refs, y_refs, lines_ref, sizes, cells, labels)
-        springs_ref[6] = inner(stiff, 0)
-        springs_ref[7] = inner(stiff_rim, 0)
+        wide_nodes[...] = jnp.zeros(plane, f32)
+        wide_nodes[own, :] = nodes_ref[...] + 1.0
+        merge_start(sh, (residual, wide_nodes, stiff, stiff_rim), x_refs, y_refs, lines_ref, sizes, cells, labels)
+        wide_nodes[...] = wide_nodes[...] - 1.0
+        stiffness_ref[0] = inner(stiff, 0)
+        stiffness_ref[1] = inner(stiff_rim, 0)
+        coarse_solution(lines_ref[pl.ds(4, sh.devices, stride=8), :], inverse_ref, values)
+        lane, _, _ = sh.lane_grid(1)
+        put(short_stiff, 0, ends(stiffness_ref[0]))
+        put(short_rim, 0, ends(stiffness_ref[1]))
+        for f, entry in enumerate(own_block(sh, lane, (short_stiff, short_rim))):
+            springs[f] = entry
+        springs[6] = inner(short_stiff, 0)
+        for m in range(3):
+            some_residual[m] = ends(residual[m])
+        index = local_solve(sh, ends_level(sh), some_residual, springs, (v0, v1), (kv0, kv1), factor)
+        solution = (v0, v1)[index]
+        z = lax.broadcasted_iota(jnp.int32, (2 * EDGE, LANES), 0)
+        z = jnp.where(z < EDGE, z, z + sh.z - 2 * EDGE)
+        some_nodes = jnp.concatenate([nodes_ref[0:EDGE, :], nodes_ref[sh.z - EDGE : sh.z, :]], axis=0)
+        added = coarse_cells(some_nodes, coords(sh, z), values, node_count)
+        for m in range(3):
+            solution[m, 2 * EDGE : 4 * EDGE, :] += pick(some_nodes >= 0.0, added[m])
+        pack_z(sh, DEEP, end_rows(solution), z_refs)
+
+    residual, wide_nodes, stiffness, values, *z_messages = call(
+        first_ends,
+        "first_ends",
+        [fields, plane, (2,) + plane, (sum_rows, LANES)] + z_shape(DEEP),
+        [start_field, *from_y, *from_x, nodes, lines, coarse_inverse],
+        [(1, sh.tall, LANES)] * 2
+        + [
+            (4, 8 * -(-(2 * sh.x + 2 * sh.y + 4) // 8), LANES),
+            (8 * -(-(2 * label_x + 2 * label_y + 4) // 8), label_z),
+        ]
+        + [(1, 6 * EDGE, LANES)] * 2
+        + [short_fields, (7, 4 * EDGE, LANES)]
+        + short_scratch,
+    )
+
+    def first_solve(residual_ref, stiffness_ref, values, nodes_ref, solution_ref, springs_ref, *rest):
+        stiff, stiff_rim, v0, v1, kv0, kv1, factor = rest
+        clear_guards(sh, (stiff, stiff_rim, v0, v1, kv0, kv1))
+        put(stiff, 0, stiffness_ref[0])
+        put(stiff_rim, 0, stiffness_ref[1])
+        springs_ref[6] = stiffness_ref[0]
+        springs_ref[7] = stiffness_ref[1]
         lane, _, _ = sh.lane_grid(1)
         for f, entry in enumerate(own_block(sh, lane, (stiff, stiff_rim))):
             springs_ref[f] = entry
-        index = local_solve(sh, residual, springs_ref, (v0, v1), (kv0, kv1), factor)
-        coarse = lines_ref[pl.ds(4, sh.devices, stride=8), :]
+        index = local_solve(sh, level(sh), residual_ref, springs_ref, (v0, v1), (kv0, kv1), factor)
         for m in range(3):
             solution_ref[m] = inner((v0, v1)[index], m)
-        add_coarse(nodes_ref, coarse, inverse_ref, values, solution_ref, z_refs, DEEP)
-
-    solved, springs, *z_messages = call(
+        added = coarse_cells(nodes_ref[...], coords(sh, own_level(sh)), values, node_count)
+        for m in range(3):
+            solution_ref[m, own, :] += pick(nodes_ref[...] >= 0.0, added[m])
+
+    solved, springs = call(
         first_solve,
         "first_solve",
-        [fields, (8,) + plane] + z_shape(DEEP),
-        [start_field, *from_y, *from_x, nodes, lines, coarse_inverse],
-        [fields, (1, sh.tall, LANES), (1, sh.tall, LANES)]
-        + [tall] * 4
-        + [fields, (LANES, LANES)]
-        + [
-            (3, 8 * -(-(2 * sh.x + 2 * sh.y + 4) // 8), LANES),
-            (8 * -(-(2 * label_x + 2 * label_y + 4) // 8), label_z),
-        ],
+        [fields, (8,) + plane],
+        [residual, stiffness, values, nodes],
+        [(1, sh.tall, LANES)] * 2 + solve_scratch,
     )
     from_z, from_y, from_x = exchange(sh, DEEP, "deep", solved, z_messages)
 
     def first_image(*refs):
         take = Taker(refs)
         merging = take(1 + sh.z_links + sh.y_links + sh.x_links * (1 + sh.y_links))
-        nodes_ref, springs_ref = take(2)
+        nodes_ref, springs_ref, inverse_ref = take(3)
         search_ref, image_ref, slots_ref = take(3)
-        v, rim, kv, k_rim, sums = take(5)
+        v, rim, kv, k_rim, sums, shares = take(6)
         clear_guards(sh, (v, rim, kv, k_rim))
         merge_all(sh, DEEP, Taker(merging), v, rim, EDGE)
         lane, _, _ = sh.lane_grid(1)
@@ -879,58 +984,75 @@
             put(rim, m, value)
             put(k_rim, m, springs_ref[7] * value)
         image = image_of(sh, lane, v, kv, (rim, k_rim), springs_ref)
-        keep = in_grid & extended_mask(sh)
+        keep = in_grid & extended_mask(sh, level(sh))
         for m in range(3):
             image_ref[m] = pick(keep, image[m])
         sums[...] = jnp.zeros(sums.shape, f32)
-        line = coarse_sums(sh, nodes_ref[...], [image_ref[m, own, :] for m in range(3)], coords(sh), node_count, sums)
-        slots_ref[...] = jnp.broadcast_to(line, slots_ref.shape)
-
-    search, image, sums = call(
+        field = [image_ref[m, own, :] for m in range(3)]
+        coarse_sums(nodes_ref[...], field, coords(sh, own_level(sh)), node_count, sums)
+        coarse_shares(sums, inverse_ref, shares)
+        for device in range(sh.devices):
+            slots_ref[device * share_rows : (device + 1) * share_rows, :] = shares[0:share_rows, :]
+
+    search, image, shares = call(
         first_image,
         "first_image",
-        [fields, fields, slots],
-        [solved, *from_z, *from_y, *from_x, nodes, springs],
-        [tall] * 4 + [(LANES, LANES)],
-    )
-    coarse = to_all(sums)
+        [fields, fields, (sh.devices * share_rows, LANES)],
+        [solved, *from_z, *from_y, *from_x, nodes, springs, coarse_inverse],
+        [tall] * 4 + [(LANES, LANES), (8 * -(-share_rows // 8), LANES)],
+    )
+    shares = to_all(shares.reshape(sh.devices, 1, share_rows * LANES)).reshape(shares.shape)
 
     def second_solve(image_ref, springs_ref, local_ref, v0, v1, kv0, kv1, factor):
         clear_guards(sh, (v0, v1, kv0, kv1))
-        index = local_solve(sh, image_ref, springs_ref, (v0, v1), (kv0, kv1), factor)
+        index = local_solve(sh, level(sh), image_ref, springs_ref, (v0, v1), (kv0, kv1), factor)
         for m in range(3):
             local_ref[m] = inner((v0, v1)[index], m)
 
-    (local,) = call(second_solve, "second_solve", [fields], [image, springs], [tall] * 4 + [fields])
-
-    def second_add(local_ref, nodes_ref, coarse_ref, inverse_ref, *rest):
-        solution_ref, z_refs, values = rest[0], rest[1:-1], rest[-1]
-        solution_ref[...] = local_ref[...]
-        add_coarse(nodes_ref, coarse_ref[...], inverse_ref, values, solution_ref, z_refs, NEAR)
-
-    solved, *z_messages = call(
-        second_add,
-        "second_add",
-        [fields] + z_shape(NEAR),
-        [local, nodes, coarse, coarse_inverse],
-        [(LANES, LANES)],
-    )
+    def second_ends(image_ref, springs_ref, *refs):
+        take = Taker(refs)
+        z_refs = take(sh.z_links)
+        some_residual, springs, v0, v1, kv0, kv1, factor = take(7)
+        clear_guards(sh, (v0, v1, kv0, kv1))
+        for m in range(3):
+            some_residual[m] = ends(image_ref[m])
+        for f in range(7):
+            springs[f] = ends(springs_ref[f])
+        index = local_solve(sh, ends_level(sh), some_residual, springs, (v0, v1), (kv0, kv1), factor)
+        pack_z(sh, NEAR, end_rows((v0, v1)[index]), z_refs)
+
+    z_messages = call(
+        second_ends,
+        "second_ends",
+        z_shape(NEAR),
+        [image, springs],
+        [short_fields, (7, 4 * EDGE, LANES)] + short_scratch,
+    )
+    (solved,) = call(second_solve, "second_solve", [fields], [image, springs], solve_scratch)
     from_z, from_y, from_x = exchange(sh, NEAR, "near", solved, z_messages)
 
     def second_image(*refs):
         take = Taker(refs)
         merging = take(1 + sh.z_links + sh.y_links + sh.x_links * (1 + sh.y_links))
-        nodes_ref, springs_ref, start_ref, search_ref, first_ref = take(5)
+        nodes_ref, springs_ref, start_ref, search_ref, first_ref, wide_nodes, shares_ref = take(7)
         second_ref, image_ref, slots_ref = take(3)
-        v, kv, sums = take(3)
+        v, kv, sums, flat, table, values = take(6)
         clear_guards(sh, (v, kv))
         merge_all(sh, NEAR, Taker(merging), v, None, EDGE)
         lane, _, _ = sh.lane_grid(1)
-
         in_grid, _ = grid_masks(sh)
         for m in range(3):
-            value = pick(in_grid, inner(v, m))
-            put(v, m, value)
+            put(v, m, pick(in_grid, inner(v, m)))
+        coarse_table(sh, shares_ref, unknowns, flat, table)
+        last = lax.broadcasted_iota(jnp.int32, (1, LANES), 0) + sh.z - 1
+        for dz, first, z in ((0, EDGE, own_level(sh)), (-1, EDGE - 1, last), (1, EDGE + sh.z, last - sh.z + 1)):
+            values[...] = region_values(sh, table, dz)
+            rows = slice(first, first + z.shape[0])
+            added = coarse_cells(wide_nodes[rows, :], coords(sh, z), values, node_count)
+            for m in range(3):
+                v[m, EDGE + rows.start : EDGE + rows.stop, :] += added[m]
+        for m in range(3):
+            value = inner(v, m)
             second_ref[m] = value
             put(kv, m, springs_ref[6] * value)
         image = image_of(sh, lane, v, kv, None, springs_ref)
@@ -950,8 +1072,9 @@
         second_image,
         "second_image",
         [fields, fields, slots],
-        [solved, *from_z, *from_y, *from_x, nodes, springs, start_field, search, image],
-        [tall] * 2 + [(LANES, LANES)],
+        [solved, *from_z, *from_y, *from_x, nodes, springs, start_field, search, image, wide_nodes, shares],
+        [tall] * 2
+        + [(LANES, LANES), (8 * -(-share_rows // 8) + 8, LANES), (sh.devices, LANES), (LANES, LANES)],
     )
     totals = to_all(sums)
 

time: 74 us -> 72 us (0.973)
  waiting for transfers between devices: 24.6 us -> 14.7 us
  starting transfers between devices: 28.1 us -> 32.7 us
  Pallas kernels: 20.3 us -> 23.4 us
    ppermute x17, waiting for transfers between devices: 14.3 us -> 8.12 us  [send(): return lax.ppermute(value, AXES, permutation(sh.sizes, moves))]
    ppermute x17, starting transfers between devices: 13.8 us -> 19.2 us  [send(): return lax.ppermute(value, AXES, permutation(sh.sizes, moves))]
    all_to_all x3, waiting for transfers between devices: 10.2 us -> 6.58 us  [to_all(): return lax.all_to_all(slots, AXES, 0, 0, tiled=True)]
    pallas_call x11 -> x12, Pallas kernels: 20.3 us -> 23.4 us  [call(): pl.pallas_call(kernel, out_shape=[jax.ShapeDtypeStruct(shape, f32) for sh...]
    all_to_all x3, starting transfers between devices: 14.3 us -> 13.5 us  [to_all(): return lax.all_to_all(slots, AXES, 0, 0, tiled=True)]
  transfers between devices with their start and end apart: 20 -> 20, of which waited for: 13 -> 8; matrix products, arithmetic and copies ran while one was open for 0% -> 0% of each run, Pallas kernels for 7% -> 15%
where the time goes in v6:
time: 72 us; the launch traced here: 71.7 us
  starting transfers between devices  32.7 us (45%)
  Pallas kernels  23.4 us (32%)
  waiting for transfers between devices  14.7 us (20%)
  between operations  0.84 us (1%)
    pallas_call x12, Pallas kernels, call(): pl.pallas_call(kernel, out_shape=[jax.ShapeDtypeStruct(shape, f32) for sh...  23.4 us
    ppermute x17, starting transfers between devices, send(): return lax.ppermute(value, AXES, permutation(sh.sizes, moves))  19.2 us
    all_to_all x3, starting transfers between devices, to_all(): return lax.all_to_all(slots, AXES, 0, 0, tiled=True)  13.5 us
    ppermute x17, waiting for transfers between devices, send(): return lax.ppermute(value, AXES, permutation(sh.sizes, moves))  8.12 us
    all_to_all x3, waiting for transfers between devices, to_all(): return lax.all_to_all(slots, AXES, 0, 0, tiled=True)  6.58 us
  transfers between devices with their start and end apart: 20, of which 8 were waited for; matrix products, arithmetic and copies ran while one was open for 0% of the time, Pallas kernels for 15%

profile of v6, /device:TPU:0, one launch (start us, length us, event | category | flops | bytes accessed | tf_op | source)
XLA Modules:
  0.0 71.7 jit_solution(8556163197058881514)
XLA Ops:
  0.6 2.9 %begin.1 = (f32[16,64]{1,0:T(8,128)}, f32[256,128]{1,0:T(8,128)}, f32[40,128]{1,0:T(8,128)}, f32[40,128]{1,0:T(8,128)}, f32[40,128]{1,0:T(8,128)}) custom-call(f32[3,64,128]{2,1,0:T(8,128)} %bitcast.12, s32[4,4,64]{2,1,0:T(4,128)} %labels_in.1, f32[8]{0:T(128)} %moduli_in.1, s32[64,128]{1,0:T(8,128)} %bitcast.17), custom_call_target="tpu_custom_call" | custom-call | tf_op jit(solution)/shard_map/begin/pallas_call | solution.py:664
  3.6 0.0 copy-start.6
  3.6 0.0 copy-start.4
  3.6 0.0 copy-start
  3.6 0.0 copy-start.1
  3.7 7.3 %all-to-all-start = ((f32[32,8,128]{2,1,0:T(8,128)}), f32[32,8,128]{2,1,0:T(8,128)S(1)}, u32[]{:S(2)}, u32[]{:S(2)}) async-start(f32[32,8,128]{2,1,0:T(8,128)} %bitcast.20), calls=%async_computation | async-start | bytes 262144 | tf_op jit(solution)/shard_map/all_to_all | solution.py:711
  11.0 1.8 %collective-permute-start = (f32[40,128]{1,0:T(8,128)S(1)}, f32[40,128]{1,0:T(8,128)S(1)}, u32[]{:S(2)}, u32[]{:S(2)}) collective-permute-start(f32[40,128]{1,0:T(8,128)S(1)} %copy-done.6), channel_id=1, source_target_pairs={{0,4},{1,5},{2,6},{3,7},{4,0},{5,1},{6,2},{7,3},{8,12},{9,13},{10,... | collective-permute-start | bytes 61448 | tf_op jit(solution)/shard_map/ppermute | solution.py:697
  12.8 1.5 %collective-permute-start.1 = (f32[40,128]{1,0:T(8,128)S(1)}, f32[40,128]{1,0:T(8,128)S(1)}, u32[]{:S(2)}, u32[]{:S(2)}) collective-permute-start(f32[40,128]{1,0:T(8,128)S(1)} %copy-done.5), channel_id=1, source_target_pairs={{0,16},{1,17},{2,18},{3,19},{4,8},{5,9},{6,10},{7,11},{8,4},{9,5},... | collective-permute-start | bytes 61448 | tf_op jit(solution)/shard_map/ppermute | solution.py:697
  14.3 0.6 collective-permute-start.2
  14.9 0.6 spread.1
  15.5 1.5 %collective-permute-done.1.refs_2_ = f32[40,128]{1,0:T(8,128)S(1)} collective-permute-done((f32[40,128]{1,0:T(8,128)S(1)}, f32[40,128]{1,0:T(8,128)S(1)}, u32[]{:S(2)}, u32[]{:S(2)}) %collective-permute-start.1) | collective-permute-done | bytes 20512 | tf_op jit(solution)/shard_map/ppermute | solution.py:697
  17.0 1.2 %collective-permute-done.2.refs_3_ = f32[40,128]{1,0:T(8,128)S(1)} collective-permute-done((f32[40,128]{1,0:T(8,128)S(1)}, f32[40,128]{1,0:T(8,128)S(1)}, u32[]{:S(2)}, u32[]{:S(2)}) %collective-permute-start.2) | collective-permute-done | bytes 20512 | tf_op jit(solution)/shard_map/ppermute | solution.py:697
  18.1 1.1 %all-to-all-done = f32[32,8,128]{2,1,0:T(8,128)S(1)} async-done(((f32[32,8,128]{2,1,0:T(8,128)}), f32[32,8,128]{2,1,0:T(8,128)S(1)}, u32[]{:S(2)}, u32[]{:S(2)}) %all-to-all-start) | async-done | bytes 131104 | tf_op jit(solution)/shard_map/all_to_all | solution.py:711
  19.2 1.9 %first_ends.1 = (f32[3,144,128]{2,1,0:T(8,128)S(1)}, f32[144,128]{1,0:T(8,128)S(1)}, f32[2,144,128]{2,1,0:T(8,128)S(1)}, f32[40,128]{1,0:T(8,128)S(1)}, f32[24,128]{1,0:T(8,128)S(1)}, /*index=5*/f32[24,128]{1,0:T(8,128)S(1)}) custom-call(f32[4,144,128]{2,1,0:T(8,128)S(1)} %get-tuple-element.38.refs_0_.refs_10_, f32[40,128]{1,0:T(8,128)S(1)} %collective-permute-done.refs_1_, ...), custom_call_target="tpu_custom_call" | custom-call | tf_op jit(solution)/shard_map/first_ends/pallas_call | solution.py:664
  21.2 0.5 collective-permute-start.3
  21.7 0.3 collective-permute-start.4
  22.0 4.1 %first_solve.1 = (f32[3,144,128]{2,1,0:T(8,128)S(1)}, f32[8,144,128]{2,1,0:T(8,128)S(1)}) custom-call(f32[3,144,128]{2,1,0:T(8,128)S(1)} %get-tuple-element.44.residual_ref, f32[2,144,128]{2,1,0:T(8,128)S(1)} %get-tuple-element.45.stiffness_ref, f32[40,128]{1,0:T(8,128)S(1)} %get-tuple-element.46.values, ...), custom_call_target="tpu_custom_call" | custom-call | tf_op jit(solution)/shard_map/first_solve/pallas_call | solution.py:664
  26.1 0.0 collective-permute-done.3.refs_1_
  26.1 0.3 deep.1
  26.4 1.3 %collective-permute-start.5 = (f32[144,128]{1,0:T(8,128)S(1)}, f32[144,128]{1,0:T(8,128)S(1)}, u32[]{:S(2)}, u32[]{:S(2)}) collective-permute-start(f32[144,128]{1,0:T(8,128)S(1)} %get-tuple-element.50), channel_id=1, source_target_pairs={{0,4},{1,5},{2,6},{3,7},{4,0},{5,1},{6,2},{7,3},{8,12},{9,13},{10,... | collective-permute-start | bytes 221192 | tf_op jit(solution)/shard_map/ppermute | solution.py:697
  27.7 1.5 %collective-permute-start.6 = (f32[144,128]{1,0:T(8,128)S(1)}, f32[144,128]{1,0:T(8,128)S(1)}, u32[]{:S(2)}, u32[]{:S(2)}) collective-permute-start(f32[144,128]{1,0:T(8,128)S(1)} %get-tuple-element.51), channel_id=1, source_target_pairs={{0,16},{1,17},{2,18},{3,19},{4,8},{5,9},{6,10},{7,11},{8,4},{9,5},... | collective-permute-start | bytes 221192 | tf_op jit(solution)/shard_map/ppermute | solution.py:697
  29.2 0.6 collective-permute-start.7
  29.7 1.4 %collective-permute-start.8 = (f32[40,128]{1,0:T(8,128)S(1)}, f32[40,128]{1,0:T(8,128)S(1)}, u32[]{:S(2)}, u32[]{:S(2)}) collective-permute-start(f32[40,128]{1,0:T(8,128)S(1)} %get-tuple-element.53), channel_id=1, source_target_pairs={{0,20},{1,21},{2,22},{3,23},{4,16},{5,17},{6,18},{7,19},{8,28},{9,... | collective-permute-start | bytes 61448 | tf_op jit(solution)/shard_map/ppermute | solution.py:697
  31.1 0.5 collective-permute-start.9
  31.7 2.8 %collective-permute-done.8.refs_6_ = f32[40,128]{1,0:T(8,128)S(1)} collective-permute-done((f32[40,128]{1,0:T(8,128)S(1)}, f32[40,128]{1,0:T(8,128)S(1)}, u32[]{:S(2)}, u32[]{:S(2)}) %collective-permute-start.8) | collective-permute-done | bytes 20512 | tf_op jit(solution)/shard_map/ppermute | solution.py:697
  34.4 0.5 collective-permute-done.9.refs_7_
  34.9 0.0 collective-permute-done.6.refs_4_
  34.9 0.0 collective-permute-done.7.refs_5_
  34.9 3.4 %first_image.1 = (f32[3,144,128]{2,1,0:T(8,128)S(1)}, f32[3,144,128]{2,1,0:T(8,128)S(1)}, f32[288,128]{1,0:T(8,128)}) custom-call(f32[3,144,128]{2,1,0:T(8,128)S(1)} %get-tuple-element.47.refs_0_, f32[24,128]{1,0:T(8,128)S(1)} %collective-permute-done.3.refs_1_, f32[24,128]{1,0:T(8,128)S(1)} %collective-permute-done.4.refs_2_, ...), custom_call_target="tpu_custom_call" | custom-call | tf_op jit(solution)/shard_map/first_image/pallas_call | solution.py:664
  38.3 3.5 %all-to-all-start.1 = ((f32[32,1,1152]{2,1,0:T(1,128)}), f32[32,1,1152]{2,1,0:T(1,128)S(1)}, u32[]{:S(2)}, u32[]{:S(2)}) async-start(f32[32,1,1152]{2,1,0:T(1,128)} %bitcast.4), calls=%async_computation.1 | async-start | bytes 294912 | tf_op jit(solution)/shard_map/all_to_all | solution.py:711
  41.9 1.0 %second_ends.1 = (f32[24,128]{1,0:T(8,128)S(1)}, f32[24,128]{1,0:T(8,128)S(1)}) custom-call(f32[3,144,128]{2,1,0:T(8,128)S(1)} %get-tuple-element.56.image_ref.refs_12_.first_ref, f32[8,144,128]{2,1,0:T(8,128)S(1)} %get-tuple-element.55.refs_9_.springs_ref), custom_call_target="tpu_custom_call" | custom-call | tf_op jit(solution)/shard_map/second_ends/pallas_call | solution.py:664
  42.9 0.1 collective-permute-start.10
  43.0 1.6 %collective-permute-start.11 = (f32[24,128]{1,0:T(8,128)S(1)}, f32[24,128]{1,0:T(8,128)S(1)}, u32[]{:S(2)}, u32[]{:S(2)}) collective-permute-start(f32[24,128]{1,0:T(8,128)S(1)} %get-tuple-element.58), channel_id=1, source_target_pairs={{0,3},{1,2},{2,1},{3,0},{4,7},{5,6},{6,5},{7,4},{8,11},{9,10},{10,... | collective-permute-start | bytes 36872 | tf_op jit(solution)/shard_map/ppermute | solution.py:697
  44.6 3.4 %second_solve.1.refs_0_ = f32[3,144,128]{2,1,0:T(8,128)S(1)} custom-call(f32[3,144,128]{2,1,0:T(8,128)S(1)} %get-tuple-element.56.image_ref.refs_12_.first_ref, f32[8,144,128]{2,1,0:T(8,128)S(1)} %get-tuple-element.55.refs_9_.springs_ref), custom_call_target="tpu_custom_call" | custom-call | tf_op jit(solution)/shard_map/second_solve/pallas_call | solution.py:664
  48.1 0.0 collective-permute-done.10.refs_1_
  48.1 0.4 near.1
  48.5 1.5 %collective-permute-start.14 = (f32[144,128]{1,0:T(8,128)S(1)}, f32[144,128]{1,0:T(8,128)S(1)}, u32[]{:S(2)}, u32[]{:S(2)}) collective-permute-start(f32[144,128]{1,0:T(8,128)S(1)} %get-tuple-element.61), channel_id=1, source_target_pairs={{0,16},{1,17},{2,18},{3,19},{4,20},{5,21},{6,22},{7,23},{8,24},{9,... | collective-permute-start | bytes 221192 | tf_op jit(solution)/shard_map/ppermute | solution.py:697
  50.0 1.5 %collective-permute-start.12 = (f32[72,128]{1,0:T(8,128)S(1)}, f32[72,128]{1,0:T(8,128)S(1)}, u32[]{:S(2)}, u32[]{:S(2)}) collective-permute-start(f32[72,128]{1,0:T(8,128)S(1)} %get-tuple-element.59), channel_id=1, source_target_pairs={{0,4},{1,5},{2,6},{3,7},{4,0},{5,1},{6,2},{7,3},{8,12},{9,13},{10,... | collective-permute-start | bytes 110600 | tf_op jit(solution)/shard_map/ppermute | solution.py:697
  51.5 0.6 collective-permute-start.13
  52.0 2.4 %collective-permute-start.15 = (f32[24,128]{1,0:T(8,128)S(1)}, f32[24,128]{1,0:T(8,128)S(1)}, u32[]{:S(2)}, u32[]{:S(2)}) collective-permute-start(f32[24,128]{1,0:T(8,128)S(1)} %get-tuple-element.62), channel_id=1, source_target_pairs={{0,20},{1,21},{2,22},{3,23},{4,16},{5,17},{6,18},{7,19},{8,28},{9,... | collective-permute-start | bytes 36872 | tf_op jit(solution)/shard_map/ppermute | solution.py:697
  54.5 1.5 %collective-permute-start.16 = (f32[24,128]{1,0:T(8,128)S(1)}, f32[24,128]{1,0:T(8,128)S(1)}, u32[]{:S(2)}, u32[]{:S(2)}) collective-permute-start(f32[24,128]{1,0:T(8,128)S(1)} %get-tuple-element.63), channel_id=1, source_target_pairs={{0,16},{1,17},{2,18},{3,19},{4,24},{5,25},{6,26},{7,27},{8,20},{9,... | collective-permute-start | bytes 36872 | tf_op jit(solution)/shard_map/ppermute | solution.py:697
  56.0 0.7 collective-permute-done.15.refs_6_
  56.6 1.5 %collective-permute-done.16.refs_7_ = f32[24,128]{1,0:T(8,128)S(1)} collective-permute-done((f32[24,128]{1,0:T(8,128)S(1)}, f32[24,128]{1,0:T(8,128)S(1)}, u32[]{:S(2)}, u32[]{:S(2)}) %collective-permute-start.16) | collective-permute-done | bytes 12320 | tf_op jit(solution)/shard_map/ppermute | solution.py:697
  58.2 2.8 %second_image.1 = (f32[3,144,128]{2,1,0:T(8,128)S(1)}, f32[3,144,128]{2,1,0:T(8,128)S(1)}, f32[32,128]{1,0:T(8,128)}) custom-call(f32[3,144,128]{2,1,0:T(8,128)S(1)} %second_solve.1.refs_0_, f32[24,128]{1,0:T(8,128)S(1)} %collective-permute-done.10.refs_1_, f32[24,128]{1,0:T(8,128)S(1)} %collective-permute-done.11.refs_2_, ...), custom_call_target="tpu_custom_call" | custom-call | tf_op jit(solution)/shard_map/second_image/pallas_call | solution.py:664
  61.0 2.7 %all-to-all-start.2 = ((f32[32,1,128]{2,1,0:T(1,128)}), f32[32,1,128]{2,1,0:T(1,128)S(1)}, u32[]{:S(2)}, u32[]{:S(2)}) async-start(f32[32,1,128]{2,1,0:T(1,128)} %bitcast.7), calls=%async_computation.2 | async-start | bytes 32768 | tf_op jit(solution)/shard_map/all_to_all | solution.py:711
  63.7 1.6 %turn.1.turned_ref = f32[4,3,64,128]{3,2,1,0:T(8,128)S(1)} custom-call(f32[3,144,128]{2,1,0:T(8,128)S(1)} %get-tuple-element.64.refs_11_.search_ref, f32[3,144,128]{2,1,0:T(8,128)S(1)} %get-tuple-element.56.image_ref.refs_12_.first_ref, f32[3,144,128]{2,1,0:T(8,128)S(1)} %get-tuple-element.68.second_ref, f32[3,144,128]{2,1,0:T(8,128)S(1)} %get-tuple-element.69.image_ref), custom_call_target="tpu_custom_call" | custom-call | tf_op jit(solution)/shard_map/turn/pallas_call | solution.py:664
  65.3 5.5 %all-to-all-done.2 = f32[32,1,128]{2,1,0:T(1,128)S(1)} async-done(((f32[32,1,128]{2,1,0:T(1,128)}), f32[32,1,128]{2,1,0:T(1,128)S(1)}, u32[]{:S(2)}, u32[]{:S(2)}) %all-to-all-start.2) | async-done | bytes 16416 | tf_op jit(solution)/shard_map/all_to_all | solution.py:711
  70.8 0.9 %finish.1 = (f32[3,64,128]{2,1,0:T(8,128)}, f32[3,64,128]{2,1,0:T(8,128)}) custom-call(f32[32,128]{1,0:T(8,128)S(1)} %bitcast.19, f32[3,64,128]{2,1,0:T(8,128)S(1)} %bitcast.14, f32[4,3,64,128]{3,2,1,0:T(8,128)S(1)} %turn.1.turned_ref), custom_call_target="tpu_custom_call" | custom-call | tf_op jit(solution)/shard_map/finish/pallas_call | solution.py:664
  (18 shorter events, 0.0 us)
Async XLA Ops:
  0.6 14.2 %copy-start.2 = (s32[8,8,128]{2,1,0:T(8,128)S(1)}, s32[8,8,128]{2,1,0:T(8,128)}, u32[]{:S(2)}) copy-start(s32[8,8,128]{2,1,0:T(8,128)} %param.8) | copy-start | bytes 98308
  3.6 7.4 %copy-start.6 = (f32[40,128]{1,0:T(8,128)S(1)}, f32[40,128]{1,0:T(8,128)}, u32[]{:S(2)}) copy-start(f32[40,128]{1,0:T(8,128)} %get-tuple-element.39) | copy-start | bytes 61444
  3.6 9.2 %copy-start.5 = (f32[40,128]{1,0:T(8,128)S(1)}, f32[40,128]{1,0:T(8,128)}, u32[]{:S(2)}) copy-start(f32[40,128]{1,0:T(8,128)} %get-tuple-element.40) | copy-start | bytes 61444
  3.6 10.7 %copy-start.4 = (f32[40,128]{1,0:T(8,128)S(1)}, f32[40,128]{1,0:T(8,128)}, u32[]{:S(2)}) copy-start(f32[40,128]{1,0:T(8,128)} %get-tuple-element.41) | copy-start | bytes 61444
  3.6 11.2 %copy-start.3 = (f32[16,64]{1,0:T(8,128)S(1)}, f32[16,64]{1,0:T(8,128)}, u32[]{:S(2)}) copy-start(f32[16,64]{1,0:T(8,128)} %get-tuple-element.37.stiff) | copy-start | bytes 12292
  3.6 11.2 %copy-start = (f32[3,8,8,128]{3,2,1,0:T(8,128)S(1)}, f32[3,8,8,128]{3,2,1,0:T(8,128)}, u32[]{:S(2)}) copy-start(f32[3,8,8,128]{3,2,1,0:T(8,128)} %param.5) | copy-start | bytes 294916
  3.6 15.6 %copy-start.1 = (f32[36,1152]{1,0:T(8,128)S(1)}, f32[36,1152]{1,0:T(8,128)}, u32[]{:S(2)}) copy-start(f32[36,1152]{1,0:T(8,128)} %refs_10_.1) | copy-start | bytes 497668
  3.7 15.6 %all-to-all-start = ((f32[32,8,128]{2,1,0:T(8,128)}), f32[32,8,128]{2,1,0:T(8,128)S(1)}, u32[]{:S(2)}, u32[]{:S(2)}) async-start(f32[32,8,128]{2,1,0:T(8,128)} %bitcast.20), calls=%async_computation | async-start | bytes 262144 | tf_op jit(solution)/shard_map/all_to_all | solution.py:711
  11.0 4.5 %collective-permute-start = (f32[40,128]{1,0:T(8,128)S(1)}, f32[40,128]{1,0:T(8,128)S(1)}, u32[]{:S(2)}, u32[]{:S(2)}) collective-permute-start(f32[40,128]{1,0:T(8,128)S(1)} %copy-done.6), channel_id=1, source_target_pairs={{0,4},{1,5},{2,6},{3,7},{4,0},{5,1},{6,2},{7,3},{8,12},{9,13},{10,... | collective-permute-start | bytes 61448 | tf_op jit(solution)/shard_map/ppermute | solution.py:697
  12.8 4.1 %collective-permute-start.1 = (f32[40,128]{1,0:T(8,128)S(1)}, f32[40,128]{1,0:T(8,128)S(1)}, u32[]{:S(2)}, u32[]{:S(2)}) collective-permute-start(f32[40,128]{1,0:T(8,128)S(1)} %copy-done.5), channel_id=1, source_target_pairs={{0,16},{1,17},{2,18},{3,19},{4,8},{5,9},{6,10},{7,11},{8,4},{9,5},... | collective-permute-start | bytes 61448 | tf_op jit(solution)/shard_map/ppermute | solution.py:697
  14.3 3.9 %collective-permute-start.2 = (f32[40,128]{1,0:T(8,128)S(1)}, f32[40,128]{1,0:T(8,128)S(1)}, u32[]{:S(2)}, u32[]{:S(2)}) collective-permute-start(f32[40,128]{1,0:T(8,128)S(1)} %copy-done.4), channel_id=1, source_target_pairs={{0,16},{1,17},{2,18},{3,19},{4,20},{5,21},{6,22},{7,23},{8,24},{9,... | collective-permute-start | bytes 61448 | tf_op jit(solution)/shard_map/ppermute | solution.py:697
  21.2 4.9 %collective-permute-start.3 = (f32[24,128]{1,0:T(8,128)S(1)}, f32[24,128]{1,0:T(8,128)S(1)}, u32[]{:S(2)}, u32[]{:S(2)}) collective-permute-start(f32[24,128]{1,0:T(8,128)S(1)} %get-tuple-element.48), channel_id=1, source_target_pairs={{0,1},{1,0},{2,3},{3,2},{4,5},{5,4},{6,7},{7,6},{8,9},{9,8},{10,11... | collective-permute-start | bytes 36872 | tf_op jit(solution)/shard_map/ppermute | solution.py:697
  21.7 4.4 %collective-permute-start.4 = (f32[24,128]{1,0:T(8,128)S(1)}, f32[24,128]{1,0:T(8,128)S(1)}, u32[]{:S(2)}, u32[]{:S(2)}) collective-permute-start(f32[24,128]{1,0:T(8,128)S(1)} %get-tuple-element.49), channel_id=1, source_target_pairs={{0,3},{1,2},{2,1},{3,0},{4,7},{5,6},{6,5},{7,4},{8,11},{9,10},{10,... | collective-permute-start | bytes 36872 | tf_op jit(solution)/shard_map/ppermute | solution.py:697
  26.4 8.5 %collective-permute-start.5 = (f32[144,128]{1,0:T(8,128)S(1)}, f32[144,128]{1,0:T(8,128)S(1)}, u32[]{:S(2)}, u32[]{:S(2)}) collective-permute-start(f32[144,128]{1,0:T(8,128)S(1)} %get-tuple-element.50), channel_id=1, source_target_pairs={{0,4},{1,5},{2,6},{3,7},{4,0},{5,1},{6,2},{7,3},{8,12},{9,13},{10,... | collective-permute-start | bytes 221192 | tf_op jit(solution)/shard_map/ppermute | solution.py:697
  27.7 7.2 %collective-permute-start.6 = (f32[144,128]{1,0:T(8,128)S(1)}, f32[144,128]{1,0:T(8,128)S(1)}, u32[]{:S(2)}, u32[]{:S(2)}) collective-permute-start(f32[144,128]{1,0:T(8,128)S(1)} %get-tuple-element.51), channel_id=1, source_target_pairs={{0,16},{1,17},{2,18},{3,19},{4,8},{5,9},{6,10},{7,11},{8,4},{9,5},... | collective-permute-start | bytes 221192 | tf_op jit(solution)/shard_map/ppermute | solution.py:697
  29.2 5.8 %collective-permute-start.7 = (f32[144,128]{1,0:T(8,128)S(1)}, f32[144,128]{1,0:T(8,128)S(1)}, u32[]{:S(2)}, u32[]{:S(2)}) collective-permute-start(f32[144,128]{1,0:T(8,128)S(1)} %get-tuple-element.52), channel_id=1, source_target_pairs={{0,16},{1,17},{2,18},{3,19},{4,20},{5,21},{6,22},{7,23},{8,24},{9,... | collective-permute-start | bytes 221192 | tf_op jit(solution)/shard_map/ppermute | solution.py:697
  29.7 4.7 %collective-permute-start.8 = (f32[40,128]{1,0:T(8,128)S(1)}, f32[40,128]{1,0:T(8,128)S(1)}, u32[]{:S(2)}, u32[]{:S(2)}) collective-permute-start(f32[40,128]{1,0:T(8,128)S(1)} %get-tuple-element.53), channel_id=1, source_target_pairs={{0,20},{1,21},{2,22},{3,23},{4,16},{5,17},{6,18},{7,19},{8,28},{9,... | collective-permute-start | bytes 61448 | tf_op jit(solution)/shard_map/ppermute | solution.py:697
  31.1 3.8 %collective-permute-start.9 = (f32[40,128]{1,0:T(8,128)S(1)}, f32[40,128]{1,0:T(8,128)S(1)}, u32[]{:S(2)}, u32[]{:S(2)}) collective-permute-start(f32[40,128]{1,0:T(8,128)S(1)} %get-tuple-element.54), channel_id=1, source_target_pairs={{0,16},{1,17},{2,18},{3,19},{4,24},{5,25},{6,26},{7,27},{8,20},{9,... | collective-permute-start | bytes 61448 | tf_op jit(solution)/shard_map/ppermute | solution.py:697
  38.3 19.8 %all-to-all-start.1 = ((f32[32,1,1152]{2,1,0:T(1,128)}), f32[32,1,1152]{2,1,0:T(1,128)S(1)}, u32[]{:S(2)}, u32[]{:S(2)}) async-start(f32[32,1,1152]{2,1,0:T(1,128)} %bitcast.4), calls=%async_computation.1 | async-start | bytes 294912 | tf_op jit(solution)/shard_map/all_to_all | solution.py:711
  42.9 5.2 %collective-permute-start.10 = (f32[24,128]{1,0:T(8,128)S(1)}, f32[24,128]{1,0:T(8,128)S(1)}, u32[]{:S(2)}, u32[]{:S(2)}) collective-permute-start(f32[24,128]{1,0:T(8,128)S(1)} %get-tuple-element.57), channel_id=1, source_target_pairs={{0,1},{1,0},{2,3},{3,2},{4,5},{5,4},{6,7},{7,6},{8,9},{9,8},{10,11... | collective-permute-start | bytes 36872 | tf_op jit(solution)/shard_map/ppermute | solution.py:697
  43.0 5.1 %collective-permute-start.11 = (f32[24,128]{1,0:T(8,128)S(1)}, f32[24,128]{1,0:T(8,128)S(1)}, u32[]{:S(2)}, u32[]{:S(2)}) collective-permute-start(f32[24,128]{1,0:T(8,128)S(1)} %get-tuple-element.58), channel_id=1, source_target_pairs={{0,3},{1,2},{2,1},{3,0},{4,7},{5,6},{6,5},{7,4},{8,11},{9,10},{10,... | collective-permute-start | bytes 36872 | tf_op jit(solution)/shard_map/ppermute | solution.py:697
  48.5 9.7 %collective-permute-start.14 = (f32[144,128]{1,0:T(8,128)S(1)}, f32[144,128]{1,0:T(8,128)S(1)}, u32[]{:S(2)}, u32[]{:S(2)}) collective-permute-start(f32[144,128]{1,0:T(8,128)S(1)} %get-tuple-element.61), channel_id=1, source_target_pairs={{0,16},{1,17},{2,18},{3,19},{4,20},{5,21},{6,22},{7,23},{8,24},{9,... | collective-permute-start | bytes 221192 | tf_op jit(solution)/shard_map/ppermute | solution.py:697
  50.0 8.2 %collective-permute-start.12 = (f32[72,128]{1,0:T(8,128)S(1)}, f32[72,128]{1,0:T(8,128)S(1)}, u32[]{:S(2)}, u32[]{:S(2)}) collective-permute-start(f32[72,128]{1,0:T(8,128)S(1)} %get-tuple-element.59), channel_id=1, source_target_pairs={{0,4},{1,5},{2,6},{3,7},{4,0},{5,1},{6,2},{7,3},{8,12},{9,13},{10,... | collective-permute-start | bytes 110600 | tf_op jit(solution)/shard_map/ppermute | solution.py:697
  51.5 6.7 %collective-permute-start.13 = (f32[72,128]{1,0:T(8,128)S(1)}, f32[72,128]{1,0:T(8,128)S(1)}, u32[]{:S(2)}, u32[]{:S(2)}) collective-permute-start(f32[72,128]{1,0:T(8,128)S(1)} %get-tuple-element.60), channel_id=1, source_target_pairs={{0,16},{1,17},{2,18},{3,19},{4,8},{5,9},{6,10},{7,11},{8,4},{9,5},... | collective-permute-start | bytes 110600 | tf_op jit(solution)/shard_map/ppermute | solution.py:697
  52.0 4.6 %collective-permute-start.15 = (f32[24,128]{1,0:T(8,128)S(1)}, f32[24,128]{1,0:T(8,128)S(1)}, u32[]{:S(2)}, u32[]{:S(2)}) collective-permute-start(f32[24,128]{1,0:T(8,128)S(1)} %get-tuple-element.62), channel_id=1, source_target_pairs={{0,20},{1,21},{2,22},{3,23},{4,16},{5,17},{6,18},{7,19},{8,28},{9,... | collective-permute-start | bytes 36872 | tf_op jit(solution)/shard_map/ppermute | solution.py:697
  54.5 3.7 %collective-permute-start.16 = (f32[24,128]{1,0:T(8,128)S(1)}, f32[24,128]{1,0:T(8,128)S(1)}, u32[]{:S(2)}, u32[]{:S(2)}) collective-permute-start(f32[24,128]{1,0:T(8,128)S(1)} %get-tuple-element.63), channel_id=1, source_target_pairs={{0,16},{1,17},{2,18},{3,19},{4,24},{5,25},{6,26},{7,27},{8,20},{9,... | collective-permute-start | bytes 36872 | tf_op jit(solution)/shard_map/ppermute | solution.py:697
  61.0 9.8 %all-to-all-start.2 = ((f32[32,1,128]{2,1,0:T(1,128)}), f32[32,1,128]{2,1,0:T(1,128)S(1)}, u32[]{:S(2)}, u32[]{:S(2)}) async-start(f32[32,1,128]{2,1,0:T(1,128)} %bitcast.7), calls=%async_computation.2 | async-start | bytes 32768 | tf_op jit(solution)/shard_map/all_to_all | solution.py:711

commit v7 on v6

--- a/solution.py
+++ b/solution.py
@@ -1031,18 +1031,10 @@
     (solved,) = call(second_solve, "second_solve", [fields], [image, springs], solve_scratch)
     from_z, from_y, from_x = exchange(sh, NEAR, "near", solved, z_messages)
 
-    def second_image(*refs):
-        take = Taker(refs)
-        merging = take(1 + sh.z_links + sh.y_links + sh.x_links * (1 + sh.y_links))
-        nodes_ref, springs_ref, start_ref, search_ref, first_ref, wide_nodes, shares_ref = take(7)
-        second_ref, image_ref, slots_ref = take(3)
-        v, kv, sums, flat, table, values = take(6)
-        clear_guards(sh, (v, kv))
-        merge_all(sh, NEAR, Taker(merging), v, None, EDGE)
-        lane, _, _ = sh.lane_grid(1)
-        in_grid, _ = grid_masks(sh)
-        for m in range(3):
-            put(v, m, pick(in_grid, inner(v, m)))
+    def between(shares_ref, wide_nodes, nodes_ref, start_ref, search_ref, first_ref, coarse_ref, sums, *scratch):
+        flat, table, values = scratch
+        coarse_ref[...] = jnp.zeros(coarse_ref.shape, f32)
+        sums[...] = jnp.zeros(sums.shape, f32)
         coarse_table(sh, shares_ref, unknowns, flat, table)
         last = lax.broadcasted_iota(jnp.int32, (1, LANES), 0) + sh.z - 1
         for dz, first, z in ((0, EDGE, own_level(sh)), (-1, EDGE - 1, last), (1, EDGE + sh.z, last - sh.z + 1)):
@@ -1050,21 +1042,43 @@
             rows = slice(first, first + z.shape[0])
             added = coarse_cells(wide_nodes[rows, :], coords(sh, z), values, node_count)
             for m in range(3):
-                v[m, EDGE + rows.start : EDGE + rows.stop, :] += added[m]
-        for m in range(3):
-            value = inner(v, m)
+                coarse_ref[m, rows, :] = added[m]
+        valid = nodes_ref[...] >= 0.0
+        for i, other in enumerate((start_ref, first_ref)):
+            product = sum(search_ref[m, own, :] * other[m, own, :] for m in range(3))
+            sums[i : i + 1, :] = fold_rows(pick(valid, product))
+
+    coarse_field, sums = call(
+        between,
+        "between",
+        [fields, (8, LANES)],
+        [shares, wide_nodes, nodes, start_field, search, image],
+        [(8 * -(-share_rows // 8) + 8, LANES), (sh.devices, LANES), (LANES, LANES)],
+    )
+
+    def second_image(*refs):
+        take = Taker(refs)
+        merging = take(1 + sh.z_links + sh.y_links + sh.x_links * (1 + sh.y_links))
+        nodes_ref, springs_ref, first_ref, coarse_ref, early_ref = take(5)
+        second_ref, image_ref, slots_ref = take(3)
+        v, kv, sums = take(3)
+        clear_guards(sh, (v, kv))
+        merge_all(sh, NEAR, Taker(merging), v, None, EDGE)
+        lane, _, _ = sh.lane_grid(1)
+        in_grid, _ = grid_masks(sh)
+        for m in range(3):
+            value = pick(in_grid, inner(v, m)) + coarse_ref[m]
+            put(v, m, value)
             second_ref[m] = value
             put(kv, m, springs_ref[6] * value)
         image = image_of(sh, lane, v, kv, None, springs_ref)
         for m in range(3):
             image_ref[m] = image[m]
         valid = nodes_ref[...] >= 0.0
-        names = ("r", "z", "w", "q", "v")
-        sources = (start_ref, search_ref, first_ref, second_ref, image_ref)
-        get = {name: [source[m, own, :] for m in range(3)] for name, source in zip(names, sources)}
         sums[...] = jnp.zeros(sums.shape, f32)
-        for i, (a, b) in enumerate(("rz", "zw", "rq", "wq", "zv", "qv")):
-            product = sum(get[a][m] * get[b][m] for m in range(3))
+        sums[0:8, :] = early_ref[...]
+        for i, other in ((2, first_ref), (3, image_ref)):
+            product = sum(second_ref[m, own, :] * other[m, own, :] for m in range(3))
             sums[i : i + 1, :] = fold_rows(pick(valid, product))
         slots_ref[...] = jnp.broadcast_to(lane_sums(sums)[0:1], slots_ref.shape)
 
@@ -1072,9 +1086,8 @@
         second_image,
         "second_image",
         [fields, fields, slots],
-        [solved, *from_z, *from_y, *from_x, nodes, springs, start_field, search, image, wide_nodes, shares],
-        [tall] * 2
-        + [(LANES, LANES), (8 * -(-share_rows // 8) + 8, LANES), (sh.devices, LANES), (LANES, LANES)],
+        [solved, *from_z, *from_y, *from_x, nodes, springs, image, coarse_field, sums],
+        [tall] * 2 + [(LANES, LANES)],
     )
     totals = to_all(sums)
 
@@ -1088,11 +1101,11 @@
 
     def finish(totals_ref, natural_ref, turned_ref, field_ref, residual_ref):
         total = jnp.sum(totals_ref[...], axis=0, keepdims=True)
-        rz, zw, rq, wq, zv, qv = [total[:, i : i + 1] for i in range(6)]
+        rz, zw, wq, qv = [total[:, i : i + 1] for i in range(4)]
         step0 = rz / zw
-        rho = rz - step0 * zw - step0 * rq + step0 * step0 * wq
+        rho = step0 * step0 * wq - step0 * zw
         grow = 1.0 + rho / rz
-        curvature = grow * grow * zw - grow * step0 * (zv + wq) + step0 * step0 * qv
+        curvature = grow * grow * zw - 2.0 * grow * step0 * wq + step0 * step0 * qv
         step1 = rho / curvature
         first = step0 + step1 * grow
         second = step0 * step1

time: 72 us -> 70.9 us (0.985)
    pallas_call x12 -> x13, Pallas kernels: 23.4 us -> 23 us  [call(): pl.pallas_call(kernel, out_shape=[jax.ShapeDtypeStruct(shape, f32) for sh...]
  transfers between devices with their start and end apart: 20 -> 20, of which waited for: 8 -> 7; matrix products, arithmetic and copies ran while one was open for 0% -> 0% of each run, Pallas kernels for 15% -> 16%
where the time goes in v7:
time: 70.9 us; the launch traced here: 70.6 us
  starting transfers between devices  32.7 us (46%)
  Pallas kernels  23 us (32%)
  waiting for transfers between devices  14 us (20%)
  between operations  0.83 us (1%)
    pallas_call x13, Pallas kernels, call(): pl.pallas_call(kernel, out_shape=[jax.ShapeDtypeStruct(shape, f32) for sh...  23 us
    ppermute x17, starting transfers between devices, send(): return lax.ppermute(value, AXES, permutation(sh.sizes, moves))  19.2 us
    all_to_all x3, starting transfers between devices, to_all(): return lax.all_to_all(slots, AXES, 0, 0, tiled=True)  13.5 us
    ppermute x17, waiting for transfers between devices, send(): return lax.ppermute(value, AXES, permutation(sh.sizes, moves))  7.46 us
    all_to_all x3, waiting for transfers between devices, to_all(): return lax.all_to_all(slots, AXES, 0, 0, tiled=True)  6.58 us
  transfers between devices with their start and end apart: 20, of which 7 were waited for; matrix products, arithmetic and copies ran while one was open for 0% of the time, Pallas kernels for 16%

profile of v7, /device:TPU:0, one launch (start us, length us, event | category | flops | bytes accessed | tf_op | source)
XLA Modules:
  0.0 70.6 jit_solution(653960377464163231)
XLA Ops:
  0.6 2.9 %begin.1 = (f32[16,64]{1,0:T(8,128)}, f32[256,128]{1,0:T(8,128)}, f32[40,128]{1,0:T(8,128)}, f32[40,128]{1,0:T(8,128)}, f32[40,128]{1,0:T(8,128)}) custom-call(f32[3,64,128]{2,1,0:T(8,128)} %bitcast.12, s32[4,4,64]{2,1,0:T(4,128)} %labels_in.1, f32[8]{0:T(128)} %moduli_in.1, s32[64,128]{1,0:T(8,128)} %bitcast.17), custom_call_target="tpu_custom_call" | custom-call | tf_op jit(solution)/shard_map/begin/pallas_call | solution.py:664
  3.6 0.0 copy-start.6
  3.6 0.0 copy-start.4
  3.6 0.0 copy-start
  3.6 0.0 copy-start.1
  3.7 7.3 %all-to-all-start = ((f32[32,8,128]{2,1,0:T(8,128)}), f32[32,8,128]{2,1,0:T(8,128)S(1)}, u32[]{:S(2)}, u32[]{:S(2)}) async-start(f32[32,8,128]{2,1,0:T(8,128)} %bitcast.20), calls=%async_computation | async-start | bytes 262144 | tf_op jit(solution)/shard_map/all_to_all | solution.py:711
  11.0 1.8 %collective-permute-start = (f32[40,128]{1,0:T(8,128)S(1)}, f32[40,128]{1,0:T(8,128)S(1)}, u32[]{:S(2)}, u32[]{:S(2)}) collective-permute-start(f32[40,128]{1,0:T(8,128)S(1)} %copy-done.6), channel_id=1, source_target_pairs={{0,4},{1,5},{2,6},{3,7},{4,0},{5,1},{6,2},{7,3},{8,12},{9,13},{10,... | collective-permute-start | bytes 61448 | tf_op jit(solution)/shard_map/ppermute | solution.py:697
  12.8 1.5 %collective-permute-start.1 = (f32[40,128]{1,0:T(8,128)S(1)}, f32[40,128]{1,0:T(8,128)S(1)}, u32[]{:S(2)}, u32[]{:S(2)}) collective-permute-start(f32[40,128]{1,0:T(8,128)S(1)} %copy-done.5), channel_id=1, source_target_pairs={{0,16},{1,17},{2,18},{3,19},{4,8},{5,9},{6,10},{7,11},{8,4},{9,5},... | collective-permute-start | bytes 61448 | tf_op jit(solution)/shard_map/ppermute | solution.py:697
  14.3 0.6 collective-permute-start.2
  14.9 0.6 spread.1
  15.5 0.0 collective-permute-done.refs_1_
  15.5 1.5 %collective-permute-done.1.refs_2_ = f32[40,128]{1,0:T(8,128)S(1)} collective-permute-done((f32[40,128]{1,0:T(8,128)S(1)}, f32[40,128]{1,0:T(8,128)S(1)}, u32[]{:S(2)}, u32[]{:S(2)}) %collective-permute-start.1) | collective-permute-done | bytes 20512 | tf_op jit(solution)/shard_map/ppermute | solution.py:697
  17.0 1.2 %collective-permute-done.2.refs_3_ = f32[40,128]{1,0:T(8,128)S(1)} collective-permute-done((f32[40,128]{1,0:T(8,128)S(1)}, f32[40,128]{1,0:T(8,128)S(1)}, u32[]{:S(2)}, u32[]{:S(2)}) %collective-permute-start.2) | collective-permute-done | bytes 20512 | tf_op jit(solution)/shard_map/ppermute | solution.py:697
  18.1 1.1 %all-to-all-done = f32[32,8,128]{2,1,0:T(8,128)S(1)} async-done(((f32[32,8,128]{2,1,0:T(8,128)}), f32[32,8,128]{2,1,0:T(8,128)S(1)}, u32[]{:S(2)}, u32[]{:S(2)}) %all-to-all-start) | async-done | bytes 131104 | tf_op jit(solution)/shard_map/all_to_all | solution.py:711
  19.2 1.9 %first_ends.1 = (f32[3,144,128]{2,1,0:T(8,128)S(1)}, f32[144,128]{1,0:T(8,128)S(1)}, f32[2,144,128]{2,1,0:T(8,128)S(1)}, f32[40,128]{1,0:T(8,128)S(1)}, f32[24,128]{1,0:T(8,128)S(1)}, /*index=5*/f32[24,128]{1,0:T(8,128)S(1)}) custom-call(f32[4,144,128]{2,1,0:T(8,128)S(1)} %get-tuple-element.40.refs_0_.start_ref, f32[40,128]{1,0:T(8,128)S(1)} %collective-permute-done.refs_1_, ...), custom_call_target="tpu_custom_call" | custom-call | tf_op jit(solution)/shard_map/first_ends/pallas_call | solution.py:664
  21.2 0.5 collective-permute-start.3
  21.7 0.3 collective-permute-start.4
  22.0 3.9 %first_solve.1 = (f32[3,144,128]{2,1,0:T(8,128)S(1)}, f32[8,144,128]{2,1,0:T(8,128)S(1)}) custom-call(f32[3,144,128]{2,1,0:T(8,128)S(1)} %get-tuple-element.46.residual_ref, f32[2,144,128]{2,1,0:T(8,128)S(1)} %get-tuple-element.47.stiffness_ref, f32[40,128]{1,0:T(8,128)S(1)} %get-tuple-element.48.values, ...), custom_call_target="tpu_custom_call" | custom-call | tf_op jit(solution)/shard_map/first_solve/pallas_call | solution.py:664
  26.0 0.0 collective-permute-done.4.refs_2_
  26.0 0.3 deep.1
  26.3 1.3 %collective-permute-start.5 = (f32[144,128]{1,0:T(8,128)S(1)}, f32[144,128]{1,0:T(8,128)S(1)}, u32[]{:S(2)}, u32[]{:S(2)}) collective-permute-start(f32[144,128]{1,0:T(8,128)S(1)} %get-tuple-element.52), channel_id=1, source_target_pairs={{0,4},{1,5},{2,6},{3,7},{4,0},{5,1},{6,2},{7,3},{8,12},{9,13},{10,... | collective-permute-start | bytes 221192 | tf_op jit(solution)/shard_map/ppermute | solution.py:697
  27.6 1.4 %collective-permute-start.6 = (f32[144,128]{1,0:T(8,128)S(1)}, f32[144,128]{1,0:T(8,128)S(1)}, u32[]{:S(2)}, u32[]{:S(2)}) collective-permute-start(f32[144,128]{1,0:T(8,128)S(1)} %get-tuple-element.53), channel_id=1, source_target_pairs={{0,16},{1,17},{2,18},{3,19},{4,8},{5,9},{6,10},{7,11},{8,4},{9,5},... | collective-permute-start | bytes 221192 | tf_op jit(solution)/shard_map/ppermute | solution.py:697
  29.0 0.6 collective-permute-start.7
  29.6 1.4 %collective-permute-start.8 = (f32[40,128]{1,0:T(8,128)S(1)}, f32[40,128]{1,0:T(8,128)S(1)}, u32[]{:S(2)}, u32[]{:S(2)}) collective-permute-start(f32[40,128]{1,0:T(8,128)S(1)} %get-tuple-element.55), channel_id=1, source_target_pairs={{0,20},{1,21},{2,22},{3,23},{4,16},{5,17},{6,18},{7,19},{8,28},{9,... | collective-permute-start | bytes 61448 | tf_op jit(solution)/shard_map/ppermute | solution.py:697
  31.0 0.5 collective-permute-start.9
  31.5 2.8 %collective-permute-done.8.refs_6_ = f32[40,128]{1,0:T(8,128)S(1)} collective-permute-done((f32[40,128]{1,0:T(8,128)S(1)}, f32[40,128]{1,0:T(8,128)S(1)}, u32[]{:S(2)}, u32[]{:S(2)}) %collective-permute-start.8) | collective-permute-done | bytes 20512 | tf_op jit(solution)/shard_map/ppermute | solution.py:697
  34.3 0.5 collective-permute-done.9.refs_7_
  34.8 3.4 %first_image.1 = (f32[3,144,128]{2,1,0:T(8,128)S(1)}, f32[3,144,128]{2,1,0:T(8,128)S(1)}, f32[288,128]{1,0:T(8,128)}) custom-call(f32[3,144,128]{2,1,0:T(8,128)S(1)} %get-tuple-element.49.refs_0_, f32[24,128]{1,0:T(8,128)S(1)} %collective-permute-done.3.refs_1_, f32[24,128]{1,0:T(8,128)S(1)} %collective-permute-done.4.refs_2_, ...), custom_call_target="tpu_custom_call" | custom-call | tf_op jit(solution)/shard_map/first_image/pallas_call | solution.py:664
  38.2 3.5 %all-to-all-start.1 = ((f32[32,1,1152]{2,1,0:T(1,128)}), f32[32,1,1152]{2,1,0:T(1,128)S(1)}, u32[]{:S(2)}, u32[]{:S(2)}) async-start(f32[32,1,1152]{2,1,0:T(1,128)} %bitcast.4), calls=%async_computation.1 | async-start | bytes 294912 | tf_op jit(solution)/shard_map/all_to_all | solution.py:711
  41.7 1.0 %second_ends.1 = (f32[24,128]{1,0:T(8,128)S(1)}, f32[24,128]{1,0:T(8,128)S(1)}) custom-call(f32[3,144,128]{2,1,0:T(8,128)S(1)} %get-tuple-element.58.image_ref.first_ref.refs_10_, f32[8,144,128]{2,1,0:T(8,128)S(1)} %get-tuple-element.57.refs_9_.springs_ref), custom_call_target="tpu_custom_call" | custom-call | tf_op jit(solution)/shard_map/second_ends/pallas_call | solution.py:664
  42.7 0.1 collective-permute-start.10
  42.9 1.6 %collective-permute-start.11 = (f32[24,128]{1,0:T(8,128)S(1)}, f32[24,128]{1,0:T(8,128)S(1)}, u32[]{:S(2)}, u32[]{:S(2)}) collective-permute-start(f32[24,128]{1,0:T(8,128)S(1)} %get-tuple-element.60), channel_id=1, source_target_pairs={{0,3},{1,2},{2,1},{3,0},{4,7},{5,6},{6,5},{7,4},{8,11},{9,10},{10,... | collective-permute-start | bytes 36872 | tf_op jit(solution)/shard_map/ppermute | solution.py:697
  44.5 3.3 %second_solve.1.refs_0_ = f32[3,144,128]{2,1,0:T(8,128)S(1)} custom-call(f32[3,144,128]{2,1,0:T(8,128)S(1)} %get-tuple-element.58.image_ref.first_ref.refs_10_, f32[8,144,128]{2,1,0:T(8,128)S(1)} %get-tuple-element.57.refs_9_.springs_ref), custom_call_target="tpu_custom_call" | custom-call | tf_op jit(solution)/shard_map/second_solve/pallas_call | solution.py:664
  47.8 0.0 collective-permute-done.11.refs_2_
  47.8 0.4 near.1
  48.2 1.5 %collective-permute-start.14 = (f32[144,128]{1,0:T(8,128)S(1)}, f32[144,128]{1,0:T(8,128)S(1)}, u32[]{:S(2)}, u32[]{:S(2)}) collective-permute-start(f32[144,128]{1,0:T(8,128)S(1)} %get-tuple-element.63), channel_id=1, source_target_pairs={{0,16},{1,17},{2,18},{3,19},{4,20},{5,21},{6,22},{7,23},{8,24},{9,... | collective-permute-start | bytes 221192 | tf_op jit(solution)/shard_map/ppermute | solution.py:697
  49.7 1.5 %collective-permute-start.12 = (f32[72,128]{1,0:T(8,128)S(1)}, f32[72,128]{1,0:T(8,128)S(1)}, u32[]{:S(2)}, u32[]{:S(2)}) collective-permute-start(f32[72,128]{1,0:T(8,128)S(1)} %get-tuple-element.61), channel_id=1, source_target_pairs={{0,4},{1,5},{2,6},{3,7},{4,0},{5,1},{6,2},{7,3},{8,12},{9,13},{10,... | collective-permute-start | bytes 110600 | tf_op jit(solution)/shard_map/ppermute | solution.py:697
  51.2 0.6 collective-permute-start.13
  51.7 2.4 %collective-permute-start.15 = (f32[24,128]{1,0:T(8,128)S(1)}, f32[24,128]{1,0:T(8,128)S(1)}, u32[]{:S(2)}, u32[]{:S(2)}) collective-permute-start(f32[24,128]{1,0:T(8,128)S(1)} %get-tuple-element.64), channel_id=1, source_target_pairs={{0,20},{1,21},{2,22},{3,23},{4,16},{5,17},{6,18},{7,19},{8,28},{9,... | collective-permute-start | bytes 36872 | tf_op jit(solution)/shard_map/ppermute | solution.py:697
  54.2 1.5 %collective-permute-start.16 = (f32[24,128]{1,0:T(8,128)S(1)}, f32[24,128]{1,0:T(8,128)S(1)}, u32[]{:S(2)}, u32[]{:S(2)}) collective-permute-start(f32[24,128]{1,0:T(8,128)S(1)} %get-tuple-element.65), channel_id=1, source_target_pairs={{0,16},{1,17},{2,18},{3,19},{4,24},{5,25},{6,26},{7,27},{8,20},{9,... | collective-permute-start | bytes 36872 | tf_op jit(solution)/shard_map/ppermute | solution.py:697
  55.7 0.7 between.1
  56.3 0.0 collective-permute-done.15.refs_6_
  56.3 1.5 %collective-permute-done.16.refs_7_ = f32[24,128]{1,0:T(8,128)S(1)} collective-permute-done((f32[24,128]{1,0:T(8,128)S(1)}, f32[24,128]{1,0:T(8,128)S(1)}, u32[]{:S(2)}, u32[]{:S(2)}) %collective-permute-start.16) | collective-permute-done | bytes 12320 | tf_op jit(solution)/shard_map/ppermute | solution.py:697
  57.9 2.2 %second_image.1 = (f32[3,144,128]{2,1,0:T(8,128)S(1)}, f32[3,144,128]{2,1,0:T(8,128)S(1)}, f32[32,128]{1,0:T(8,128)}) custom-call(f32[3,144,128]{2,1,0:T(8,128)S(1)} %second_solve.1.refs_0_, f32[24,128]{1,0:T(8,128)S(1)} %collective-permute-done.10.refs_1_, f32[24,128]{1,0:T(8,128)S(1)} %collective-permute-done.11.refs_2_, ...), custom_call_target="tpu_custom_call" | custom-call | tf_op jit(solution)/shard_map/second_image/pallas_call | solution.py:664
  60.0 2.7 %all-to-all-start.2 = ((f32[32,1,128]{2,1,0:T(1,128)}), f32[32,1,128]{2,1,0:T(1,128)S(1)}, u32[]{:S(2)}, u32[]{:S(2)}) async-start(f32[32,1,128]{2,1,0:T(1,128)} %bitcast.7), calls=%async_computation.2 | async-start | bytes 32768 | tf_op jit(solution)/shard_map/all_to_all | solution.py:711
  62.7 1.6 %turn.1.turned_ref = f32[4,3,64,128]{3,2,1,0:T(8,128)S(1)} custom-call(f32[3,144,128]{2,1,0:T(8,128)S(1)} %get-tuple-element.68.search_ref, f32[3,144,128]{2,1,0:T(8,128)S(1)} %get-tuple-element.58.image_ref.first_ref.refs_10_, f32[3,144,128]{2,1,0:T(8,128)S(1)} %get-tuple-element.72.second_ref, f32[3,144,128]{2,1,0:T(8,128)S(1)} %get-tuple-element.73.image_ref), custom_call_target="tpu_custom_call" | custom-call | tf_op jit(solution)/shard_map/turn/pallas_call | solution.py:664
  64.3 5.5 %all-to-all-done.2 = f32[32,1,128]{2,1,0:T(1,128)S(1)} async-done(((f32[32,1,128]{2,1,0:T(1,128)}), f32[32,1,128]{2,1,0:T(1,128)S(1)}, u32[]{:S(2)}, u32[]{:S(2)}) %all-to-all-start.2) | async-done | bytes 16416 | tf_op jit(solution)/shard_map/all_to_all | solution.py:711
  69.8 0.8 %finish.1 = (f32[3,64,128]{2,1,0:T(8,128)}, f32[3,64,128]{2,1,0:T(8,128)}) custom-call(f32[32,128]{1,0:T(8,128)S(1)} %bitcast.19, f32[3,64,128]{2,1,0:T(8,128)S(1)} %bitcast.14, f32[4,3,64,128]{3,2,1,0:T(8,128)S(1)} %turn.1.turned_ref), custom_call_target="tpu_custom_call" | custom-call | tf_op jit(solution)/shard_map/finish/pallas_call | solution.py:664
  (19 shorter events, 0.0 us)
Async XLA Ops:
  0.6 14.2 %copy-start.2 = (s32[8,8,128]{2,1,0:T(8,128)S(1)}, s32[8,8,128]{2,1,0:T(8,128)}, u32[]{:S(2)}) copy-start(s32[8,8,128]{2,1,0:T(8,128)} %param.8) | copy-start | bytes 98308
  3.6 7.4 %copy-start.6 = (f32[40,128]{1,0:T(8,128)S(1)}, f32[40,128]{1,0:T(8,128)}, u32[]{:S(2)}) copy-start(f32[40,128]{1,0:T(8,128)} %get-tuple-element.41) | copy-start | bytes 61444
  3.6 9.2 %copy-start.5 = (f32[40,128]{1,0:T(8,128)S(1)}, f32[40,128]{1,0:T(8,128)}, u32[]{:S(2)}) copy-start(f32[40,128]{1,0:T(8,128)} %get-tuple-element.42) | copy-start | bytes 61444
  3.6 10.7 %copy-start.4 = (f32[40,128]{1,0:T(8,128)S(1)}, f32[40,128]{1,0:T(8,128)}, u32[]{:S(2)}) copy-start(f32[40,128]{1,0:T(8,128)} %get-tuple-element.43) | copy-start | bytes 61444
  3.6 11.2 %copy-start.3 = (f32[16,64]{1,0:T(8,128)S(1)}, f32[16,64]{1,0:T(8,128)}, u32[]{:S(2)}) copy-start(f32[16,64]{1,0:T(8,128)} %get-tuple-element.39.stiff) | copy-start | bytes 12292
  3.6 11.2 %copy-start = (f32[3,8,8,128]{3,2,1,0:T(8,128)S(1)}, f32[3,8,8,128]{3,2,1,0:T(8,128)}, u32[]{:S(2)}) copy-start(f32[3,8,8,128]{3,2,1,0:T(8,128)} %param.5) | copy-start | bytes 294916
  3.6 15.6 %copy-start.1 = (f32[36,1152]{1,0:T(8,128)S(1)}, f32[36,1152]{1,0:T(8,128)}, u32[]{:S(2)}) copy-start(f32[36,1152]{1,0:T(8,128)} %refs_10_.1) | copy-start | bytes 497668
  3.7 15.6 %all-to-all-start = ((f32[32,8,128]{2,1,0:T(8,128)}), f32[32,8,128]{2,1,0:T(8,128)S(1)}, u32[]{:S(2)}, u32[]{:S(2)}) async-start(f32[32,8,128]{2,1,0:T(8,128)} %bitcast.20), calls=%async_computation | async-start | bytes 262144 | tf_op jit(solution)/shard_map/all_to_all | solution.py:711
  11.0 4.5 %collective-permute-start = (f32[40,128]{1,0:T(8,128)S(1)}, f32[40,128]{1,0:T(8,128)S(1)}, u32[]{:S(2)}, u32[]{:S(2)}) collective-permute-start(f32[40,128]{1,0:T(8,128)S(1)} %copy-done.6), channel_id=1, source_target_pairs={{0,4},{1,5},{2,6},{3,7},{4,0},{5,1},{6,2},{7,3},{8,12},{9,13},{10,... | collective-permute-start | bytes 61448 | tf_op jit(solution)/shard_map/ppermute | solution.py:697
  12.8 4.1 %collective-permute-start.1 = (f32[40,128]{1,0:T(8,128)S(1)}, f32[40,128]{1,0:T(8,128)S(1)}, u32[]{:S(2)}, u32[]{:S(2)}) collective-permute-start(f32[40,128]{1,0:T(8,128)S(1)} %copy-done.5), channel_id=1, source_target_pairs={{0,16},{1,17},{2,18},{3,19},{4,8},{5,9},{6,10},{7,11},{8,4},{9,5},... | collective-permute-start | bytes 61448 | tf_op jit(solution)/shard_map/ppermute | solution.py:697
  14.3 3.9 %collective-permute-start.2 = (f32[40,128]{1,0:T(8,128)S(1)}, f32[40,128]{1,0:T(8,128)S(1)}, u32[]{:S(2)}, u32[]{:S(2)}) collective-permute-start(f32[40,128]{1,0:T(8,128)S(1)} %copy-done.4), channel_id=1, source_target_pairs={{0,16},{1,17},{2,18},{3,19},{4,20},{5,21},{6,22},{7,23},{8,24},{9,... | collective-permute-start | bytes 61448 | tf_op jit(solution)/shard_map/ppermute | solution.py:697
  21.2 4.8 %collective-permute-start.3 = (f32[24,128]{1,0:T(8,128)S(1)}, f32[24,128]{1,0:T(8,128)S(1)}, u32[]{:S(2)}, u32[]{:S(2)}) collective-permute-start(f32[24,128]{1,0:T(8,128)S(1)} %get-tuple-element.50), channel_id=1, source_target_pairs={{0,1},{1,0},{2,3},{3,2},{4,5},{5,4},{6,7},{7,6},{8,9},{9,8},{10,11... | collective-permute-start | bytes 36872 | tf_op jit(solution)/shard_map/ppermute | solution.py:697
  21.7 4.3 %collective-permute-start.4 = (f32[24,128]{1,0:T(8,128)S(1)}, f32[24,128]{1,0:T(8,128)S(1)}, u32[]{:S(2)}, u32[]{:S(2)}) collective-permute-start(f32[24,128]{1,0:T(8,128)S(1)} %get-tuple-element.51), channel_id=1, source_target_pairs={{0,3},{1,2},{2,1},{3,0},{4,7},{5,6},{6,5},{7,4},{8,11},{9,10},{10,... | collective-permute-start | bytes 36872 | tf_op jit(solution)/shard_map/ppermute | solution.py:697
  26.3 8.5 %collective-permute-start.5 = (f32[144,128]{1,0:T(8,128)S(1)}, f32[144,128]{1,0:T(8,128)S(1)}, u32[]{:S(2)}, u32[]{:S(2)}) collective-permute-start(f32[144,128]{1,0:T(8,128)S(1)} %get-tuple-element.52), channel_id=1, source_target_pairs={{0,4},{1,5},{2,6},{3,7},{4,0},{5,1},{6,2},{7,3},{8,12},{9,13},{10,... | collective-permute-start | bytes 221192 | tf_op jit(solution)/shard_map/ppermute | solution.py:697
  27.6 7.2 %collective-permute-start.6 = (f32[144,128]{1,0:T(8,128)S(1)}, f32[144,128]{1,0:T(8,128)S(1)}, u32[]{:S(2)}, u32[]{:S(2)}) collective-permute-start(f32[144,128]{1,0:T(8,128)S(1)} %get-tuple-element.53), channel_id=1, source_target_pairs={{0,16},{1,17},{2,18},{3,19},{4,8},{5,9},{6,10},{7,11},{8,4},{9,5},... | collective-permute-start | bytes 221192 | tf_op jit(solution)/shard_map/ppermute | solution.py:697
  29.0 5.8 %collective-permute-start.7 = (f32[144,128]{1,0:T(8,128)S(1)}, f32[144,128]{1,0:T(8,128)S(1)}, u32[]{:S(2)}, u32[]{:S(2)}) collective-permute-start(f32[144,128]{1,0:T(8,128)S(1)} %get-tuple-element.54), channel_id=1, source_target_pairs={{0,16},{1,17},{2,18},{3,19},{4,20},{5,21},{6,22},{7,23},{8,24},{9,... | collective-permute-start | bytes 221192 | tf_op jit(solution)/shard_map/ppermute | solution.py:697
  29.6 4.7 %collective-permute-start.8 = (f32[40,128]{1,0:T(8,128)S(1)}, f32[40,128]{1,0:T(8,128)S(1)}, u32[]{:S(2)}, u32[]{:S(2)}) collective-permute-start(f32[40,128]{1,0:T(8,128)S(1)} %get-tuple-element.55), channel_id=1, source_target_pairs={{0,20},{1,21},{2,22},{3,23},{4,16},{5,17},{6,18},{7,19},{8,28},{9,... | collective-permute-start | bytes 61448 | tf_op jit(solution)/shard_map/ppermute | solution.py:697
  31.0 3.8 %collective-permute-start.9 = (f32[40,128]{1,0:T(8,128)S(1)}, f32[40,128]{1,0:T(8,128)S(1)}, u32[]{:S(2)}, u32[]{:S(2)}) collective-permute-start(f32[40,128]{1,0:T(8,128)S(1)} %get-tuple-element.56), channel_id=1, source_target_pairs={{0,16},{1,17},{2,18},{3,19},{4,24},{5,25},{6,26},{7,27},{8,20},{9,... | collective-permute-start | bytes 61448 | tf_op jit(solution)/shard_map/ppermute | solution.py:697
  38.2 17.5 %all-to-all-start.1 = ((f32[32,1,1152]{2,1,0:T(1,128)}), f32[32,1,1152]{2,1,0:T(1,128)S(1)}, u32[]{:S(2)}, u32[]{:S(2)}) async-start(f32[32,1,1152]{2,1,0:T(1,128)} %bitcast.4), calls=%async_computation.1 | async-start | bytes 294912 | tf_op jit(solution)/shard_map/all_to_all | solution.py:711
  42.7 5.1 %collective-permute-start.10 = (f32[24,128]{1,0:T(8,128)S(1)}, f32[24,128]{1,0:T(8,128)S(1)}, u32[]{:S(2)}, u32[]{:S(2)}) collective-permute-start(f32[24,128]{1,0:T(8,128)S(1)} %get-tuple-element.59), channel_id=1, source_target_pairs={{0,1},{1,0},{2,3},{3,2},{4,5},{5,4},{6,7},{7,6},{8,9},{9,8},{10,11... | collective-permute-start | bytes 36872 | tf_op jit(solution)/shard_map/ppermute | solution.py:697
  42.9 4.9 %collective-permute-start.11 = (f32[24,128]{1,0:T(8,128)S(1)}, f32[24,128]{1,0:T(8,128)S(1)}, u32[]{:S(2)}, u32[]{:S(2)}) collective-permute-start(f32[24,128]{1,0:T(8,128)S(1)} %get-tuple-element.60), channel_id=1, source_target_pairs={{0,3},{1,2},{2,1},{3,0},{4,7},{5,6},{6,5},{7,4},{8,11},{9,10},{10,... | collective-permute-start | bytes 36872 | tf_op jit(solution)/shard_map/ppermute | solution.py:697
  48.2 9.7 %collective-permute-start.14 = (f32[144,128]{1,0:T(8,128)S(1)}, f32[144,128]{1,0:T(8,128)S(1)}, u32[]{:S(2)}, u32[]{:S(2)}) collective-permute-start(f32[144,128]{1,0:T(8,128)S(1)} %get-tuple-element.63), channel_id=1, source_target_pairs={{0,16},{1,17},{2,18},{3,19},{4,20},{5,21},{6,22},{7,23},{8,24},{9,... | collective-permute-start | bytes 221192 | tf_op jit(solution)/shard_map/ppermute | solution.py:697
  49.7 8.2 %collective-permute-start.12 = (f32[72,128]{1,0:T(8,128)S(1)}, f32[72,128]{1,0:T(8,128)S(1)}, u32[]{:S(2)}, u32[]{:S(2)}) collective-permute-start(f32[72,128]{1,0:T(8,128)S(1)} %get-tuple-element.61), channel_id=1, source_target_pairs={{0,4},{1,5},{2,6},{3,7},{4,0},{5,1},{6,2},{7,3},{8,12},{9,13},{10,... | collective-permute-start | bytes 110600 | tf_op jit(solution)/shard_map/ppermute | solution.py:697
  51.2 6.7 %collective-permute-start.13 = (f32[72,128]{1,0:T(8,128)S(1)}, f32[72,128]{1,0:T(8,128)S(1)}, u32[]{:S(2)}, u32[]{:S(2)}) collective-permute-start(f32[72,128]{1,0:T(8,128)S(1)} %get-tuple-element.62), channel_id=1, source_target_pairs={{0,16},{1,17},{2,18},{3,19},{4,8},{5,9},{6,10},{7,11},{8,4},{9,5},... | collective-permute-start | bytes 110600 | tf_op jit(solution)/shard_map/ppermute | solution.py:697
  51.7 4.6 %collective-permute-start.15 = (f32[24,128]{1,0:T(8,128)S(1)}, f32[24,128]{1,0:T(8,128)S(1)}, u32[]{:S(2)}, u32[]{:S(2)}) collective-permute-start(f32[24,128]{1,0:T(8,128)S(1)} %get-tuple-element.64), channel_id=1, source_target_pairs={{0,20},{1,21},{2,22},{3,23},{4,16},{5,17},{6,18},{7,19},{8,28},{9,... | collective-permute-start | bytes 36872 | tf_op jit(solution)/shard_map/ppermute | solution.py:697
  54.2 3.7 %collective-permute-start.16 = (f32[24,128]{1,0:T(8,128)S(1)}, f32[24,128]{1,0:T(8,128)S(1)}, u32[]{:S(2)}, u32[]{:S(2)}) collective-permute-start(f32[24,128]{1,0:T(8,128)S(1)} %get-tuple-element.65), channel_id=1, source_target_pairs={{0,16},{1,17},{2,18},{3,19},{4,24},{5,25},{6,26},{7,27},{8,20},{9,... | collective-permute-start | bytes 36872 | tf_op jit(solution)/shard_map/ppermute | solution.py:697
  60.0 9.8 %all-to-all-start.2 = ((f32[32,1,128]{2,1,0:T(1,128)}), f32[32,1,128]{2,1,0:T(1,128)S(1)}, u32[]{:S(2)}, u32[]{:S(2)}) async-start(f32[32,1,128]{2,1,0:T(1,128)} %bitcast.7), calls=%async_computation.2 | async-start | bytes 32768 | tf_op jit(solution)/shard_map/all_to_all | solution.py:711

commit v8 on v7

--- a/solution.py
+++ b/solution.py
@@ -9,6 +9,7 @@
 SWEEPS = 4
 relax = 0.6
 highest = lax.Precision.HIGHEST
+small = lax.Precision.DEFAULT
 f32 = jnp.float32
 LANES = 128
 EDGE = 8
@@ -89,13 +90,13 @@
 
 def pack_z(sh, ex, source, out_refs):
     even = sh.here(2) % 2 == 0
-    zero = jnp.zeros((8 - ex.layers, LANES), f32)
+    for ref in out_refs:
+        ref[...] = jnp.zeros(ref.shape, f32)
     for f in range(ex.fields):
         upward = source(f, EDGE + sh.z + ex.up, ex.layers)
         downward = source(f, EDGE + ex.down, ex.layers)
         for ref, message in zip(out_refs, pair(sh.z_links, even, upward, downward)):
             ref[8 * f : 8 * f + ex.layers, :] = message
-            ref[8 * f + ex.layers : 8 * f + 8, :] = zero
 
 
 def merge_z(sh, ex, field_ref, received_refs, scratch, guard):
@@ -491,7 +492,7 @@
     device = jnp.where(exists, (x * sh.sizes[1] + y) * sh.sizes[2] + z, -1)
     owner = lax.broadcasted_iota(jnp.int32, (sh.devices, LANES), 0) == device
     return lax.dot_general(
-        table[...], owner.astype(f32), (((0,), (0,)), ((), ())), precision=highest, preferred_element_type=f32
+        table[0 : sh.devices, :], owner.astype(f32), (((0,), (0,)), ((), ())), precision=highest, preferred_element_type=f32
     )
 
 
@@ -513,9 +514,9 @@
     return (inside & (row == along * sh.y + across)).astype(f32)
 
 
-def to_lanes(value, select):
+def to_lanes(value, select, precision=highest):
     return lax.dot_general(
-        value, select, (((0,), (0,)), ((), ())), precision=highest, preferred_element_type=f32
+        value, select, (((0,), (0,)), ((), ())), precision=precision, preferred_element_type=f32
     )
 
 
@@ -631,7 +632,7 @@
     tall_own = slice(2 * EDGE, 2 * EDGE + sh.z)
     for m in range(3):
         residual[m, own, :] += to_lanes(cells[m], place)
-    nodes[own, :] += to_lanes(cells[3], place)
+    nodes[own, :] += to_lanes(cells[3], place, small)
     by_z = lax.dot_general(
         repeat_twice(label_z), labels[...], (((1,), (1,)), ((), ())), precision=highest, preferred_element_type=f32
     )
@@ -659,13 +660,15 @@
             stiff_rim[0, row : row + 1, :] = edge[3:4]
 
 
-def call(kernel, name, outs, ins, scratch=(), remote_ins=False):
+def call(kernel, name, outs, ins, scratch=(), remote_ins=False, remote_outs=()):
     space = pltpu.HBM if remote_ins else pltpu.VMEM
     return pl.pallas_call(
         kernel,
         out_shape=[jax.ShapeDtypeStruct(shape, f32) for shape in outs],
         in_specs=[pl.BlockSpec(memory_space=space) for _ in ins],
-        out_specs=[pl.BlockSpec(memory_space=pltpu.VMEM) for _ in outs],
+        out_specs=[
+            pl.BlockSpec(memory_space=pltpu.HBM if i in remote_outs else pltpu.VMEM) for i in range(len(outs))
+        ],
         scratch_shapes=[pltpu.VMEM(shape, f32) if isinstance(shape, tuple) else shape for shape in scratch],
         compiler_params=pltpu.CompilerParams(vmem_limit_bytes=(62 if remote_ins else 48) * 1024 * 1024),
         name=name,
@@ -769,7 +772,7 @@
     sh = Shape(size_x, size_y, size_z, phase_moduli.shape[0], sizes)
     unknowns = coarse_inverse.shape[0]
     node_count = unknowns // 6
-    sum_rows = -(-unknowns // 8) * 8
+    sum_rows = -(-unknowns // 8) * 8 + 8
     share_rows = coarse_inverse.shape[1] // LANES
     own = slice(EDGE, EDGE + sh.z)
     plane = (sh.rows, LANES)
@@ -797,7 +800,7 @@
     def begin(natural_in, labels_in, moduli_in, nodes_in, stiff, slots_ref, *rest):
         x_refs, y_refs = rest[: sh.x_links], rest[sh.x_links : sh.x_links + sh.y_links]
         natural_ref, labels_ref, moduli_ref, nodes_ref, sems, sums, lines = rest[sh.x_links + sh.y_links :]
-        pairs = ((natural_in, natural_ref.at[0:3]), (labels_in, labels_ref), (moduli_in, moduli_ref), (nodes_in, nodes_ref))
+        pairs = ((natural_in, natural_ref.at[0:3, 0 : sh.cells, :]), (labels_in, labels_ref.at[0:label_x]), (moduli_in, moduli_ref), (nodes_in, nodes_ref))
         copies = [pltpu.make_async_copy(a, b, sems.at[i]) for i, (a, b) in enumerate(pairs)]
         for copy in copies:
             copy.start()
@@ -811,9 +814,9 @@
             for phase in range(sh.phases):
                 moduli = jnp.where(labels == phase, moduli_ref[phase], moduli)
             stiff[i * label_y : (i + 1) * label_y, :] = moduli
-        natural_ref[3] = nodes_ref[...].astype(f32) + 1.0
-        cells = [natural_ref[m] for m in range(3)]
-        coarse_sums(nodes_ref[...], cells, cell_coords(sh), node_count, sums)
+        natural_ref[3, 0 : sh.cells, :] = nodes_ref[...].astype(f32) + 1.0
+        cells = [natural_ref[m, 0 : sh.cells, :] for m in range(4)]
+        coarse_sums(nodes_ref[...], cells[:3], cell_coords(sh), node_count, sums)
         line = sums_line(sh, sums, unknowns)
         for i, (cell, block) in enumerate(
             (
@@ -828,7 +831,7 @@
             lines[8 * i + 3 : 8 * i + 4, 0:label_z] = stiff[block : block + 1, :]
             lines[8 * i + 5 : 8 * i + 6, :] = natural_ref[3, cell : cell + 1, :]
         select = selection(sh)
-        layers = [end_layers(natural_ref[m], select) for m in range(4)] + [end_layers(stiff[...], block_places())]
+        layers = [end_layers(cells[m], select) for m in range(4)] + [end_layers(stiff[0 : label_x * label_y, :], block_places())]
         for i in range(2):
             for layer, row in zip(layers, (0, 1, 2, 5, 3)):
                 lines[8 * (4 + i) + row : 8 * (4 + i) + row + 1, :] = layer[i : i + 1]
@@ -837,20 +840,21 @@
         send_lines(sh, lines, slots_ref)
         pack_faces(sh, natural_ref, stiff, label_x, label_y, x_refs, y_refs)
 
+    block_rows = (8 * -(-(label_x + 8) * label_y // 8), label_z)
     stiff_blocks, lines, *messages = call(
         begin,
         "begin",
-        [(label_x * label_y, label_z), (8 * sh.devices, LANES)]
+        [block_rows, (8 * sh.devices, LANES)]
         + [face_shape(sh, label_x, label_y)] * (sh.x_links + sh.y_links),
         [natural, phase_labels, phase_moduli, nodes_natural],
         [
-            (4, sh.cells, sh.z),
-            pltpu.VMEM(phase_labels.shape, jnp.int32),
+            (4, sh.cells + 8, sh.z),
+            pltpu.VMEM((label_x + 2, label_y, label_z), jnp.int32),
             pltpu.SMEM(phase_moduli.shape, f32),
             pltpu.VMEM(nodes_natural.shape, jnp.int32),
             pltpu.SemaphoreType.DMA((4,)),
             (LANES, LANES),
-            (48, LANES),
+            (56, LANES),
         ],
         remote_ins=True,
     )
@@ -861,10 +865,14 @@
         for m in range(3):
             field_ref[m, own, :] = to_lanes(natural_ref[m], select)
         by_z = lax.dot_general(
-            repeat_twice(label_z), stiff[...], (((1,), (1,)), ((), ())), precision=highest, preferred_element_type=f32
+            repeat_twice(label_z),
+            stiff[0 : label_x * label_y, :],
+            (((1,), (1,)), ((), ())),
+            precision=highest,
+            preferred_element_type=f32,
         )
         field_ref[3, own, :] = jnp.dot(by_z, block_places(), precision=highest, preferred_element_type=f32)
-        lanes_ref[...] = to_lanes(nodes_ref[...].astype(f32) + 1.0, select) - 1.0
+        lanes_ref[...] = to_lanes(nodes_ref[...].astype(f32) + 1.0, select, small) - 1.0
 
     start_field, nodes = call(
         spread, "spread", [(4,) + plane, (sh.z, LANES)], [natural, nodes_natural, stiff_blocks]
@@ -930,8 +938,8 @@
         [start_field, *from_y, *from_x, nodes, lines, coarse_inverse],
         [(1, sh.tall, LANES)] * 2
         + [
-            (4, 8 * -(-(2 * sh.x + 2 * sh.y + 4) // 8), LANES),
-            (8 * -(-(2 * label_x + 2 * label_y + 4) // 8), label_z),
+            (4, 8 * -(-(2 * sh.x + 2 * sh.y + 4) // 8) + 8, LANES),
+            (8 * -(-(2 * label_x + 2 * label_y + 4) // 8) + 8, label_z),
         ]
         + [(1, 6 * EDGE, LANES)] * 2
         + [short_fields, (7, 4 * EDGE, LANES)]
@@ -968,8 +976,11 @@
         take = Taker(refs)
         merging = take(1 + sh.z_links + sh.y_links + sh.x_links * (1 + sh.y_links))
         nodes_ref, springs_ref, inverse_ref = take(3)
-        search_ref, image_ref, slots_ref = take(3)
-        v, rim, kv, k_rim, sums, shares = take(6)
+        search_ref, image_ref, slots_out = take(3)
+        z_refs = take(sh.z_links)
+        v, rim, kv, k_rim, sums, shares, slots_ref, sem = take(8)
+        some_residual, some_springs, v0, v1, kv0, kv1, factor = take(7)
+        clear_guards(sh, (v0, v1, kv0, kv1))
         clear_guards(sh, (v, rim, kv, k_rim))
         merge_all(sh, DEEP, Taker(merging), v, rim, EDGE)
         lane, _, _ = sh.lane_grid(1)
@@ -993,13 +1004,28 @@
         coarse_shares(sums, inverse_ref, shares)
         for device in range(sh.devices):
             slots_ref[device * share_rows : (device + 1) * share_rows, :] = shares[0:share_rows, :]
-
-    search, image, shares = call(
+        copy = pltpu.make_async_copy(slots_ref.at[0 : slots_out.shape[0], :], slots_out, sem)
+        copy.start()
+        for m in range(3):
+            some_residual[m] = ends(image_ref[m])
+        for f in range(7):
+            some_springs[f] = ends(springs_ref[f])
+        index = local_solve(sh, ends_level(sh), some_residual, some_springs, (v0, v1), (kv0, kv1), factor)
+        pack_z(sh, NEAR, end_rows((v0, v1)[index]), z_refs)
+        copy.wait()
+
+    all_slots = (sh.devices * share_rows, LANES)
+    search, image, shares, *z_messages = call(
         first_image,
         "first_image",
-        [fields, fields, (sh.devices * share_rows, LANES)],
+        [fields, fields, all_slots] + z_shape(NEAR),
         [solved, *from_z, *from_y, *from_x, nodes, springs, coarse_inverse],
-        [tall] * 4 + [(LANES, LANES), (8 * -(-share_rows // 8), LANES)],
+        [tall] * 4
+        + [(LANES, LANES), (8 * -(-share_rows // 8) + 8, LANES)]
+        + [(8 * -(-all_slots[0] // 8) + 8, LANES), pltpu.SemaphoreType.DMA]
+        + [short_fields, (7, 4 * EDGE, LANES)]
+        + short_scratch,
+        remote_outs=(2,),
     )
     shares = to_all(shares.reshape(sh.devices, 1, share_rows * LANES)).reshape(shares.shape)
 
@@ -1009,32 +1035,12 @@
         for m in range(3):
             local_ref[m] = inner((v0, v1)[index], m)
 
-    def second_ends(image_ref, springs_ref, *refs):
-        take = Taker(refs)
-        z_refs = take(sh.z_links)
-        some_residual, springs, v0, v1, kv0, kv1, factor = take(7)
-        clear_guards(sh, (v0, v1, kv0, kv1))
-        for m in range(3):
-            some_residual[m] = ends(image_ref[m])
-        for f in range(7):
-            springs[f] = ends(springs_ref[f])
-        index = local_solve(sh, ends_level(sh), some_residual, springs, (v0, v1), (kv0, kv1), factor)
-        pack_z(sh, NEAR, end_rows((v0, v1)[index]), z_refs)
-
-    z_messages = call(
-        second_ends,
-        "second_ends",
-        z_shape(NEAR),
-        [image, springs],
-        [short_fields, (7, 4 * EDGE, LANES)] + short_scratch,
-    )
     (solved,) = call(second_solve, "second_solve", [fields], [image, springs], solve_scratch)
     from_z, from_y, from_x = exchange(sh, NEAR, "near", solved, z_messages)
 
     def between(shares_ref, wide_nodes, nodes_ref, start_ref, search_ref, first_ref, coarse_ref, sums, *scratch):
         flat, table, values = scratch
         coarse_ref[...] = jnp.zeros(coarse_ref.shape, f32)
-        sums[...] = jnp.zeros(sums.shape, f32)
         coarse_table(sh, shares_ref, unknowns, flat, table)
         last = lax.broadcasted_iota(jnp.int32, (1, LANES), 0) + sh.z - 1
         for dz, first, z in ((0, EDGE, own_level(sh)), (-1, EDGE - 1, last), (1, EDGE + sh.z, last - sh.z + 1)):
@@ -1044,16 +1050,19 @@
             for m in range(3):
                 coarse_ref[m, rows, :] = added[m]
         valid = nodes_ref[...] >= 0.0
+        row = lax.broadcasted_iota(jnp.int32, sums.shape, 0)
+        total = jnp.zeros(sums.shape, f32)
         for i, other in enumerate((start_ref, first_ref)):
             product = sum(search_ref[m, own, :] * other[m, own, :] for m in range(3))
-            sums[i : i + 1, :] = fold_rows(pick(valid, product))
+            total = jnp.where(row == i, fold_rows(pick(valid, product)), total)
+        sums[...] = total
 
     coarse_field, sums = call(
         between,
         "between",
         [fields, (8, LANES)],
         [shares, wide_nodes, nodes, start_field, search, image],
-        [(8 * -(-share_rows // 8) + 8, LANES), (sh.devices, LANES), (LANES, LANES)],
+        [(8 * -(-share_rows // 8) + 8, LANES), (8 * -(-sh.devices // 8) + 8, LANES), (LANES, LANES)],
     )
 
     def second_image(*refs):

time: 70.9 us -> 70.1 us (0.989)
  Pallas kernels: 23 us -> 22.2 us
    pallas_call x13 -> x12, Pallas kernels: 23 us -> 22.2 us  [call(): pl.pallas_call(kernel, out_shape=[jax.ShapeDtypeStruct(shape, f32) for sh...]
  transfers between devices with their start and end apart: 20 -> 20, of which waited for: 7 -> 8; matrix products, arithmetic and copies ran while one was open for 0% -> 0% of each run, Pallas kernels for 16% -> 15%
where the time goes in v8:
time: 70.1 us; the launch traced here: 69.8 us
  starting transfers between devices  32.7 us (47%)
  Pallas kernels  22.2 us (32%)
  waiting for transfers between devices  14 us (20%)
  between operations  0.85 us (1%)
    pallas_call x12, Pallas kernels, call(): pl.pallas_call(kernel, out_shape=[jax.ShapeDtypeStruct(shape, f32) for sh...  22.2 us
    ppermute x17, starting transfers between devices, send(): return lax.ppermute(value, AXES, permutation(sh.sizes, moves))  19.2 us
    all_to_all x3, starting transfers between devices, to_all(): return lax.all_to_all(slots, AXES, 0, 0, tiled=True)  13.5 us
    ppermute x17, waiting for transfers between devices, send(): return lax.ppermute(value, AXES, permutation(sh.sizes, moves))  7.47 us
    all_to_all x3, waiting for transfers between devices, to_all(): return lax.all_to_all(slots, AXES, 0, 0, tiled=True)  6.58 us
  transfers between devices with their start and end apart: 20, of which 8 were waited for; matrix products, arithmetic and copies ran while one was open for 0% of the time, Pallas kernels for 15%

profile of v8, /device:TPU:0, one launch (start us, length us, event | category | flops | bytes accessed | tf_op | source)
XLA Modules:
  0.0 69.8 jit_solution(7228344574199595585)
XLA Ops:
  0.6 3.0 %begin.1 = (f32[48,64]{1,0:T(8,128)}, f32[256,128]{1,0:T(8,128)}, f32[40,128]{1,0:T(8,128)}, f32[40,128]{1,0:T(8,128)}, f32[40,128]{1,0:T(8,128)}) custom-call(f32[3,64,128]{2,1,0:T(8,128)} %bitcast.12, s32[4,4,64]{2,1,0:T(4,128)} %labels_in.1, f32[8]{0:T(128)} %moduli_in.1, s32[64,128]{1,0:T(8,128)} %bitcast.17), custom_call_target="tpu_custom_call" | custom-call | tf_op jit(solution)/shard_map/begin/pallas_call | solution.py:665
  3.6 0.0 copy-start.4
  3.6 0.0 copy-start.3
  3.7 0.0 copy-start
  3.7 0.0 copy-start.1
  3.7 7.3 %all-to-all-start = ((f32[32,8,128]{2,1,0:T(8,128)}), f32[32,8,128]{2,1,0:T(8,128)S(1)}, u32[]{:S(2)}, u32[]{:S(2)}) async-start(f32[32,8,128]{2,1,0:T(8,128)} %bitcast.20), calls=%async_computation | async-start | bytes 262144 | tf_op jit(solution)/shard_map/all_to_all | solution.py:714
  11.0 1.8 %collective-permute-start = (f32[40,128]{1,0:T(8,128)S(1)}, f32[40,128]{1,0:T(8,128)S(1)}, u32[]{:S(2)}, u32[]{:S(2)}) collective-permute-start(f32[40,128]{1,0:T(8,128)S(1)} %copy-done.6), channel_id=1, source_target_pairs={{0,4},{1,5},{2,6},{3,7},{4,0},{5,1},{6,2},{7,3},{8,12},{9,13},{10,... | collective-permute-start | bytes 61448 | tf_op jit(solution)/shard_map/ppermute | solution.py:700
  12.8 1.5 %collective-permute-start.1 = (f32[40,128]{1,0:T(8,128)S(1)}, f32[40,128]{1,0:T(8,128)S(1)}, u32[]{:S(2)}, u32[]{:S(2)}) collective-permute-start(f32[40,128]{1,0:T(8,128)S(1)} %copy-done.5), channel_id=1, source_target_pairs={{0,16},{1,17},{2,18},{3,19},{4,8},{5,9},{6,10},{7,11},{8,4},{9,5},... | collective-permute-start | bytes 61448 | tf_op jit(solution)/shard_map/ppermute | solution.py:700
  14.3 0.6 collective-permute-start.2
  14.9 0.7 spread.1
  15.6 1.4 %collective-permute-done.1.refs_2_ = f32[40,128]{1,0:T(8,128)S(1)} collective-permute-done((f32[40,128]{1,0:T(8,128)S(1)}, f32[40,128]{1,0:T(8,128)S(1)}, u32[]{:S(2)}, u32[]{:S(2)}) %collective-permute-start.1) | collective-permute-done | bytes 20512 | tf_op jit(solution)/shard_map/ppermute | solution.py:700
  17.0 1.2 %collective-permute-done.2.refs_3_ = f32[40,128]{1,0:T(8,128)S(1)} collective-permute-done((f32[40,128]{1,0:T(8,128)S(1)}, f32[40,128]{1,0:T(8,128)S(1)}, u32[]{:S(2)}, u32[]{:S(2)}) %collective-permute-start.2) | collective-permute-done | bytes 20512 | tf_op jit(solution)/shard_map/ppermute | solution.py:700
  18.2 1.1 %all-to-all-done = f32[32,8,128]{2,1,0:T(8,128)S(1)} async-done(((f32[32,8,128]{2,1,0:T(8,128)}), f32[32,8,128]{2,1,0:T(8,128)S(1)}, u32[]{:S(2)}, u32[]{:S(2)}) %all-to-all-start) | async-done | bytes 131104 | tf_op jit(solution)/shard_map/all_to_all | solution.py:714
  19.3 1.9 %first_ends.1 = (f32[3,144,128]{2,1,0:T(8,128)S(1)}, f32[144,128]{1,0:T(8,128)S(1)}, f32[2,144,128]{2,1,0:T(8,128)S(1)}, f32[48,128]{1,0:T(8,128)S(1)}, f32[24,128]{1,0:T(8,128)S(1)}, /*index=5*/f32[24,128]{1,0:T(8,128)S(1)}) custom-call(f32[4,144,128]{2,1,0:T(8,128)S(1)} %get-tuple-element.40.refs_0_.start_ref, f32[40,128]{1,0:T(8,128)S(1)} %collective-permute-done.refs_1_, ...), custom_call_target="tpu_custom_call" | custom-call | tf_op jit(solution)/shard_map/first_ends/pallas_call | solution.py:665
  21.1 0.5 collective-permute-start.3
  21.6 0.3 collective-permute-start.4
  22.0 3.9 %first_solve.1 = (f32[3,144,128]{2,1,0:T(8,128)S(1)}, f32[8,144,128]{2,1,0:T(8,128)S(1)}) custom-call(f32[3,144,128]{2,1,0:T(8,128)S(1)} %get-tuple-element.46.residual_ref, f32[2,144,128]{2,1,0:T(8,128)S(1)} %get-tuple-element.47.stiffness_ref, f32[48,128]{1,0:T(8,128)S(1)} %get-tuple-element.48.values, ...), custom_call_target="tpu_custom_call" | custom-call | tf_op jit(solution)/shard_map/first_solve/pallas_call | solution.py:665
  25.9 0.0 collective-permute-done.4.refs_2_
  25.9 0.3 deep.1
  26.2 1.3 %collective-permute-start.5 = (f32[144,128]{1,0:T(8,128)S(1)}, f32[144,128]{1,0:T(8,128)S(1)}, u32[]{:S(2)}, u32[]{:S(2)}) collective-permute-start(f32[144,128]{1,0:T(8,128)S(1)} %get-tuple-element.52), channel_id=1, source_target_pairs={{0,4},{1,5},{2,6},{3,7},{4,0},{5,1},{6,2},{7,3},{8,12},{9,13},{10,... | collective-permute-start | bytes 221192 | tf_op jit(solution)/shard_map/ppermute | solution.py:700
  27.5 1.5 %collective-permute-start.6 = (f32[144,128]{1,0:T(8,128)S(1)}, f32[144,128]{1,0:T(8,128)S(1)}, u32[]{:S(2)}, u32[]{:S(2)}) collective-permute-start(f32[144,128]{1,0:T(8,128)S(1)} %get-tuple-element.53), channel_id=1, source_target_pairs={{0,16},{1,17},{2,18},{3,19},{4,8},{5,9},{6,10},{7,11},{8,4},{9,5},... | collective-permute-start | bytes 221192 | tf_op jit(solution)/shard_map/ppermute | solution.py:700
  29.0 0.6 collective-permute-start.7
  29.6 1.4 %collective-permute-start.8 = (f32[40,128]{1,0:T(8,128)S(1)}, f32[40,128]{1,0:T(8,128)S(1)}, u32[]{:S(2)}, u32[]{:S(2)}) collective-permute-start(f32[40,128]{1,0:T(8,128)S(1)} %get-tuple-element.55), channel_id=1, source_target_pairs={{0,20},{1,21},{2,22},{3,23},{4,16},{5,17},{6,18},{7,19},{8,28},{9,... | collective-permute-start | bytes 61448 | tf_op jit(solution)/shard_map/ppermute | solution.py:700
  30.9 0.5 collective-permute-start.9
  31.5 2.8 %collective-permute-done.8.refs_6_ = f32[40,128]{1,0:T(8,128)S(1)} collective-permute-done((f32[40,128]{1,0:T(8,128)S(1)}, f32[40,128]{1,0:T(8,128)S(1)}, u32[]{:S(2)}, u32[]{:S(2)}) %collective-permute-start.8) | collective-permute-done | bytes 20512 | tf_op jit(solution)/shard_map/ppermute | solution.py:700
  34.2 0.5 collective-permute-done.9.refs_7_
  34.7 0.0 collective-permute-done.5.refs_3_
  34.7 0.0 collective-permute-done.6.refs_4_
  34.7 0.0 collective-permute-done.7.refs_5_
  34.7 3.6 %first_image.1 = (f32[3,144,128]{2,1,0:T(8,128)S(1)}, f32[3,144,128]{2,1,0:T(8,128)S(1)}, f32[288,128]{1,0:T(8,128)}, f32[24,128]{1,0:T(8,128)S(1)}, f32[24,128]{1,0:T(8,128)S(1)}) custom-call(f32[3,144,128]{2,1,0:T(8,128)S(1)} %get-tuple-element.49.refs_0_, f32[24,128]{1,0:T(8,128)S(1)} %collective-permute-done.3.refs_1_, ...), custom_call_target="tpu_custom_call" | custom-call | tf_op jit(solution)/shard_map/first_image/pallas_call | solution.py:665
  38.3 3.5 %all-to-all-start.1 = ((f32[32,1,1152]{2,1,0:T(1,128)}), f32[32,1,1152]{2,1,0:T(1,128)S(1)}, u32[]{:S(2)}, u32[]{:S(2)}) async-start(f32[32,1,1152]{2,1,0:T(1,128)} %bitcast.4), calls=%async_computation.1 | async-start | bytes 294912 | tf_op jit(solution)/shard_map/all_to_all | solution.py:714
  41.9 0.1 collective-permute-start.10
  42.0 1.6 %collective-permute-start.11 = (f32[24,128]{1,0:T(8,128)S(1)}, f32[24,128]{1,0:T(8,128)S(1)}, u32[]{:S(2)}, u32[]{:S(2)}) collective-permute-start(f32[24,128]{1,0:T(8,128)S(1)} %get-tuple-element.60), channel_id=1, source_target_pairs={{0,3},{1,2},{2,1},{3,0},{4,7},{5,6},{6,5},{7,4},{8,11},{9,10},{10,... | collective-permute-start | bytes 36872 | tf_op jit(solution)/shard_map/ppermute | solution.py:700
  43.7 3.3 %second_solve.1.refs_0_ = f32[3,144,128]{2,1,0:T(8,128)S(1)} custom-call(f32[3,144,128]{2,1,0:T(8,128)S(1)} %get-tuple-element.58.image_ref.first_ref.refs_10_, f32[8,144,128]{2,1,0:T(8,128)S(1)} %get-tuple-element.57.refs_9_.springs_ref), custom_call_target="tpu_custom_call" | custom-call | tf_op jit(solution)/shard_map/second_solve/pallas_call | solution.py:665
  47.0 0.4 near.1
  47.4 1.5 %collective-permute-start.14 = (f32[144,128]{1,0:T(8,128)S(1)}, f32[144,128]{1,0:T(8,128)S(1)}, u32[]{:S(2)}, u32[]{:S(2)}) collective-permute-start(f32[144,128]{1,0:T(8,128)S(1)} %get-tuple-element.63), channel_id=1, source_target_pairs={{0,16},{1,17},{2,18},{3,19},{4,20},{5,21},{6,22},{7,23},{8,24},{9,... | collective-permute-start | bytes 221192 | tf_op jit(solution)/shard_map/ppermute | solution.py:700
  48.9 1.5 %collective-permute-start.12 = (f32[72,128]{1,0:T(8,128)S(1)}, f32[72,128]{1,0:T(8,128)S(1)}, u32[]{:S(2)}, u32[]{:S(2)}) collective-permute-start(f32[72,128]{1,0:T(8,128)S(1)} %get-tuple-element.61), channel_id=1, source_target_pairs={{0,4},{1,5},{2,6},{3,7},{4,0},{5,1},{6,2},{7,3},{8,12},{9,13},{10,... | collective-permute-start | bytes 110600 | tf_op jit(solution)/shard_map/ppermute | solution.py:700
  50.4 0.6 collective-permute-start.13
  50.9 2.4 %collective-permute-start.15 = (f32[24,128]{1,0:T(8,128)S(1)}, f32[24,128]{1,0:T(8,128)S(1)}, u32[]{:S(2)}, u32[]{:S(2)}) collective-permute-start(f32[24,128]{1,0:T(8,128)S(1)} %get-tuple-element.64), channel_id=1, source_target_pairs={{0,20},{1,21},{2,22},{3,23},{4,16},{5,17},{6,18},{7,19},{8,28},{9,... | collective-permute-start | bytes 36872 | tf_op jit(solution)/shard_map/ppermute | solution.py:700
  53.4 1.5 %collective-permute-start.16 = (f32[24,128]{1,0:T(8,128)S(1)}, f32[24,128]{1,0:T(8,128)S(1)}, u32[]{:S(2)}, u32[]{:S(2)}) collective-permute-start(f32[24,128]{1,0:T(8,128)S(1)} %get-tuple-element.65), channel_id=1, source_target_pairs={{0,16},{1,17},{2,18},{3,19},{4,24},{5,25},{6,26},{7,27},{8,20},{9,... | collective-permute-start | bytes 36872 | tf_op jit(solution)/shard_map/ppermute | solution.py:700
  54.9 0.6 between.1
  55.5 0.1 collective-permute-done.15.refs_6_
  55.5 1.5 %collective-permute-done.16.refs_7_ = f32[24,128]{1,0:T(8,128)S(1)} collective-permute-done((f32[24,128]{1,0:T(8,128)S(1)}, f32[24,128]{1,0:T(8,128)S(1)}, u32[]{:S(2)}, u32[]{:S(2)}) %collective-permute-start.16) | collective-permute-done | bytes 12320 | tf_op jit(solution)/shard_map/ppermute | solution.py:700
  57.1 2.2 %second_image.1 = (f32[3,144,128]{2,1,0:T(8,128)S(1)}, f32[3,144,128]{2,1,0:T(8,128)S(1)}, f32[32,128]{1,0:T(8,128)}) custom-call(f32[3,144,128]{2,1,0:T(8,128)S(1)} %second_solve.1.refs_0_, f32[24,128]{1,0:T(8,128)S(1)} %collective-permute-done.10.refs_1_, f32[24,128]{1,0:T(8,128)S(1)} %collective-permute-done.11.refs_2_, ...), custom_call_target="tpu_custom_call" | custom-call | tf_op jit(solution)/shard_map/second_image/pallas_call | solution.py:665
  59.2 2.7 %all-to-all-start.2 = ((f32[32,1,128]{2,1,0:T(1,128)}), f32[32,1,128]{2,1,0:T(1,128)S(1)}, u32[]{:S(2)}, u32[]{:S(2)}) async-start(f32[32,1,128]{2,1,0:T(1,128)} %bitcast.7), calls=%async_computation.2 | async-start | bytes 32768 | tf_op jit(solution)/shard_map/all_to_all | solution.py:714
  61.9 1.6 %turn.1.turned_ref = f32[4,3,64,128]{3,2,1,0:T(8,128)S(1)} custom-call(f32[3,144,128]{2,1,0:T(8,128)S(1)} %get-tuple-element.68.search_ref, f32[3,144,128]{2,1,0:T(8,128)S(1)} %get-tuple-element.58.image_ref.first_ref.refs_10_, f32[3,144,128]{2,1,0:T(8,128)S(1)} %get-tuple-element.72.second_ref, f32[3,144,128]{2,1,0:T(8,128)S(1)} %get-tuple-element.73.image_ref), custom_call_target="tpu_custom_call" | custom-call | tf_op jit(solution)/shard_map/turn/pallas_call | solution.py:665
  63.5 5.5 %all-to-all-done.2 = f32[32,1,128]{2,1,0:T(1,128)S(1)} async-done(((f32[32,1,128]{2,1,0:T(1,128)}), f32[32,1,128]{2,1,0:T(1,128)S(1)}, u32[]{:S(2)}, u32[]{:S(2)}) %all-to-all-start.2) | async-done | bytes 16416 | tf_op jit(solution)/shard_map/all_to_all | solution.py:714
  69.0 0.8 %finish.1 = (f32[3,64,128]{2,1,0:T(8,128)}, f32[3,64,128]{2,1,0:T(8,128)}) custom-call(f32[32,128]{1,0:T(8,128)S(1)} %bitcast.19, f32[3,64,128]{2,1,0:T(8,128)S(1)} %bitcast.14, f32[4,3,64,128]{3,2,1,0:T(8,128)S(1)} %turn.1.turned_ref), custom_call_target="tpu_custom_call" | custom-call | tf_op jit(solution)/shard_map/finish/pallas_call | solution.py:665
  (18 shorter events, 0.0 us)
Async XLA Ops:
  0.6 14.2 %copy-start.2 = (s32[8,8,128]{2,1,0:T(8,128)S(1)}, s32[8,8,128]{2,1,0:T(8,128)}, u32[]{:S(2)}) copy-start(s32[8,8,128]{2,1,0:T(8,128)} %param.8) | copy-start | bytes 98308
  3.6 7.4 %copy-start.6 = (f32[40,128]{1,0:T(8,128)S(1)}, f32[40,128]{1,0:T(8,128)}, u32[]{:S(2)}) copy-start(f32[40,128]{1,0:T(8,128)} %get-tuple-element.41) | copy-start | bytes 61444
  3.6 9.2 %copy-start.5 = (f32[40,128]{1,0:T(8,128)S(1)}, f32[40,128]{1,0:T(8,128)}, u32[]{:S(2)}) copy-start(f32[40,128]{1,0:T(8,128)} %get-tuple-element.42) | copy-start | bytes 61444
  3.6 10.7 %copy-start.4 = (f32[40,128]{1,0:T(8,128)S(1)}, f32[40,128]{1,0:T(8,128)}, u32[]{:S(2)}) copy-start(f32[40,128]{1,0:T(8,128)} %get-tuple-element.43) | copy-start | bytes 61444
  3.6 11.2 %copy-start.3 = (f32[48,64]{1,0:T(8,128)S(1)}, f32[48,64]{1,0:T(8,128)}, u32[]{:S(2)}) copy-start(f32[48,64]{1,0:T(8,128)} %get-tuple-element.39.stiff) | copy-start | bytes 36868
  3.7 11.2 %copy-start = (f32[3,8,8,128]{3,2,1,0:T(8,128)S(1)}, f32[3,8,8,128]{3,2,1,0:T(8,128)}, u32[]{:S(2)}) copy-start(f32[3,8,8,128]{3,2,1,0:T(8,128)} %param.5) | copy-start | bytes 294916
  3.7 15.6 %copy-start.1 = (f32[36,1152]{1,0:T(8,128)S(1)}, f32[36,1152]{1,0:T(8,128)}, u32[]{:S(2)}) copy-start(f32[36,1152]{1,0:T(8,128)} %refs_10_.1) | copy-start | bytes 497668
  3.7 15.6 %all-to-all-start = ((f32[32,8,128]{2,1,0:T(8,128)}), f32[32,8,128]{2,1,0:T(8,128)S(1)}, u32[]{:S(2)}, u32[]{:S(2)}) async-start(f32[32,8,128]{2,1,0:T(8,128)} %bitcast.20), calls=%async_computation | async-start | bytes 262144 | tf_op jit(solution)/shard_map/all_to_all | solution.py:714
  11.0 4.5 %collective-permute-start = (f32[40,128]{1,0:T(8,128)S(1)}, f32[40,128]{1,0:T(8,128)S(1)}, u32[]{:S(2)}, u32[]{:S(2)}) collective-permute-start(f32[40,128]{1,0:T(8,128)S(1)} %copy-done.6), channel_id=1, source_target_pairs={{0,4},{1,5},{2,6},{3,7},{4,0},{5,1},{6,2},{7,3},{8,12},{9,13},{10,... | collective-permute-start | bytes 61448 | tf_op jit(solution)/shard_map/ppermute | solution.py:700
  12.8 4.1 %collective-permute-start.1 = (f32[40,128]{1,0:T(8,128)S(1)}, f32[40,128]{1,0:T(8,128)S(1)}, u32[]{:S(2)}, u32[]{:S(2)}) collective-permute-start(f32[40,128]{1,0:T(8,128)S(1)} %copy-done.5), channel_id=1, source_target_pairs={{0,16},{1,17},{2,18},{3,19},{4,8},{5,9},{6,10},{7,11},{8,4},{9,5},... | collective-permute-start | bytes 61448 | tf_op jit(solution)/shard_map/ppermute | solution.py:700
  14.3 3.9 %collective-permute-start.2 = (f32[40,128]{1,0:T(8,128)S(1)}, f32[40,128]{1,0:T(8,128)S(1)}, u32[]{:S(2)}, u32[]{:S(2)}) collective-permute-start(f32[40,128]{1,0:T(8,128)S(1)} %copy-done.4), channel_id=1, source_target_pairs={{0,16},{1,17},{2,18},{3,19},{4,20},{5,21},{6,22},{7,23},{8,24},{9,... | collective-permute-start | bytes 61448 | tf_op jit(solution)/shard_map/ppermute | solution.py:700
  21.1 4.8 %collective-permute-start.3 = (f32[24,128]{1,0:T(8,128)S(1)}, f32[24,128]{1,0:T(8,128)S(1)}, u32[]{:S(2)}, u32[]{:S(2)}) collective-permute-start(f32[24,128]{1,0:T(8,128)S(1)} %get-tuple-element.50), channel_id=1, source_target_pairs={{0,1},{1,0},{2,3},{3,2},{4,5},{5,4},{6,7},{7,6},{8,9},{9,8},{10,11... | collective-permute-start | bytes 36872 | tf_op jit(solution)/shard_map/ppermute | solution.py:700
  21.6 4.3 %collective-permute-start.4 = (f32[24,128]{1,0:T(8,128)S(1)}, f32[24,128]{1,0:T(8,128)S(1)}, u32[]{:S(2)}, u32[]{:S(2)}) collective-permute-start(f32[24,128]{1,0:T(8,128)S(1)} %get-tuple-element.51), channel_id=1, source_target_pairs={{0,3},{1,2},{2,1},{3,0},{4,7},{5,6},{6,5},{7,4},{8,11},{9,10},{10,... | collective-permute-start | bytes 36872 | tf_op jit(solution)/shard_map/ppermute | solution.py:700
  26.2 8.5 %collective-permute-start.5 = (f32[144,128]{1,0:T(8,128)S(1)}, f32[144,128]{1,0:T(8,128)S(1)}, u32[]{:S(2)}, u32[]{:S(2)}) collective-permute-start(f32[144,128]{1,0:T(8,128)S(1)} %get-tuple-element.52), channel_id=1, source_target_pairs={{0,4},{1,5},{2,6},{3,7},{4,0},{5,1},{6,2},{7,3},{8,12},{9,13},{10,... | collective-permute-start | bytes 221192 | tf_op jit(solution)/shard_map/ppermute | solution.py:700
  27.5 7.2 %collective-permute-start.6 = (f32[144,128]{1,0:T(8,128)S(1)}, f32[144,128]{1,0:T(8,128)S(1)}, u32[]{:S(2)}, u32[]{:S(2)}) collective-permute-start(f32[144,128]{1,0:T(8,128)S(1)} %get-tuple-element.53), channel_id=1, source_target_pairs={{0,16},{1,17},{2,18},{3,19},{4,8},{5,9},{6,10},{7,11},{8,4},{9,5},... | collective-permute-start | bytes 221192 | tf_op jit(solution)/shard_map/ppermute | solution.py:700
  29.0 5.8 %collective-permute-start.7 = (f32[144,128]{1,0:T(8,128)S(1)}, f32[144,128]{1,0:T(8,128)S(1)}, u32[]{:S(2)}, u32[]{:S(2)}) collective-permute-start(f32[144,128]{1,0:T(8,128)S(1)} %get-tuple-element.54), channel_id=1, source_target_pairs={{0,16},{1,17},{2,18},{3,19},{4,20},{5,21},{6,22},{7,23},{8,24},{9,... | collective-permute-start | bytes 221192 | tf_op jit(solution)/shard_map/ppermute | solution.py:700
  29.6 4.7 %collective-permute-start.8 = (f32[40,128]{1,0:T(8,128)S(1)}, f32[40,128]{1,0:T(8,128)S(1)}, u32[]{:S(2)}, u32[]{:S(2)}) collective-permute-start(f32[40,128]{1,0:T(8,128)S(1)} %get-tuple-element.55), channel_id=1, source_target_pairs={{0,20},{1,21},{2,22},{3,23},{4,16},{5,17},{6,18},{7,19},{8,28},{9,... | collective-permute-start | bytes 61448 | tf_op jit(solution)/shard_map/ppermute | solution.py:700
  30.9 3.8 %collective-permute-start.9 = (f32[40,128]{1,0:T(8,128)S(1)}, f32[40,128]{1,0:T(8,128)S(1)}, u32[]{:S(2)}, u32[]{:S(2)}) collective-permute-start(f32[40,128]{1,0:T(8,128)S(1)} %get-tuple-element.56), channel_id=1, source_target_pairs={{0,16},{1,17},{2,18},{3,19},{4,24},{5,25},{6,26},{7,27},{8,20},{9,... | collective-permute-start | bytes 61448 | tf_op jit(solution)/shard_map/ppermute | solution.py:700
  38.3 16.5 %all-to-all-start.1 = ((f32[32,1,1152]{2,1,0:T(1,128)}), f32[32,1,1152]{2,1,0:T(1,128)S(1)}, u32[]{:S(2)}, u32[]{:S(2)}) async-start(f32[32,1,1152]{2,1,0:T(1,128)} %bitcast.4), calls=%async_computation.1 | async-start | bytes 294912 | tf_op jit(solution)/shard_map/all_to_all | solution.py:714
  41.9 5.1 %collective-permute-start.10 = (f32[24,128]{1,0:T(8,128)S(1)}, f32[24,128]{1,0:T(8,128)S(1)}, u32[]{:S(2)}, u32[]{:S(2)}) collective-permute-start(f32[24,128]{1,0:T(8,128)S(1)} %get-tuple-element.59), channel_id=1, source_target_pairs={{0,1},{1,0},{2,3},{3,2},{4,5},{5,4},{6,7},{7,6},{8,9},{9,8},{10,11... | collective-permute-start | bytes 36872 | tf_op jit(solution)/shard_map/ppermute | solution.py:700
  42.0 4.9 %collective-permute-start.11 = (f32[24,128]{1,0:T(8,128)S(1)}, f32[24,128]{1,0:T(8,128)S(1)}, u32[]{:S(2)}, u32[]{:S(2)}) collective-permute-start(f32[24,128]{1,0:T(8,128)S(1)} %get-tuple-element.60), channel_id=1, source_target_pairs={{0,3},{1,2},{2,1},{3,0},{4,7},{5,6},{6,5},{7,4},{8,11},{9,10},{10,... | collective-permute-start | bytes 36872 | tf_op jit(solution)/shard_map/ppermute | solution.py:700
  47.4 9.7 %collective-permute-start.14 = (f32[144,128]{1,0:T(8,128)S(1)}, f32[144,128]{1,0:T(8,128)S(1)}, u32[]{:S(2)}, u32[]{:S(2)}) collective-permute-start(f32[144,128]{1,0:T(8,128)S(1)} %get-tuple-element.63), channel_id=1, source_target_pairs={{0,16},{1,17},{2,18},{3,19},{4,20},{5,21},{6,22},{7,23},{8,24},{9,... | collective-permute-start | bytes 221192 | tf_op jit(solution)/shard_map/ppermute | solution.py:700
  48.9 8.2 %collective-permute-start.12 = (f32[72,128]{1,0:T(8,128)S(1)}, f32[72,128]{1,0:T(8,128)S(1)}, u32[]{:S(2)}, u32[]{:S(2)}) collective-permute-start(f32[72,128]{1,0:T(8,128)S(1)} %get-tuple-element.61), channel_id=1, source_target_pairs={{0,4},{1,5},{2,6},{3,7},{4,0},{5,1},{6,2},{7,3},{8,12},{9,13},{10,... | collective-permute-start | bytes 110600 | tf_op jit(solution)/shard_map/ppermute | solution.py:700
  50.4 6.7 %collective-permute-start.13 = (f32[72,128]{1,0:T(8,128)S(1)}, f32[72,128]{1,0:T(8,128)S(1)}, u32[]{:S(2)}, u32[]{:S(2)}) collective-permute-start(f32[72,128]{1,0:T(8,128)S(1)} %get-tuple-element.62), channel_id=1, source_target_pairs={{0,16},{1,17},{2,18},{3,19},{4,8},{5,9},{6,10},{7,11},{8,4},{9,5},... | collective-permute-start | bytes 110600 | tf_op jit(solution)/shard_map/ppermute | solution.py:700
  50.9 4.6 %collective-permute-start.15 = (f32[24,128]{1,0:T(8,128)S(1)}, f32[24,128]{1,0:T(8,128)S(1)}, u32[]{:S(2)}, u32[]{:S(2)}) collective-permute-start(f32[24,128]{1,0:T(8,128)S(1)} %get-tuple-element.64), channel_id=1, source_target_pairs={{0,20},{1,21},{2,22},{3,23},{4,16},{5,17},{6,18},{7,19},{8,28},{9,... | collective-permute-start | bytes 36872 | tf_op jit(solution)/shard_map/ppermute | solution.py:700
  53.4 3.7 %collective-permute-start.16 = (f32[24,128]{1,0:T(8,128)S(1)}, f32[24,128]{1,0:T(8,128)S(1)}, u32[]{:S(2)}, u32[]{:S(2)}) collective-permute-start(f32[24,128]{1,0:T(8,128)S(1)} %get-tuple-element.65), channel_id=1, source_target_pairs={{0,16},{1,17},{2,18},{3,19},{4,24},{5,25},{6,26},{7,27},{8,20},{9,... | collective-permute-start | bytes 36872 | tf_op jit(solution)/shard_map/ppermute | solution.py:700
  59.2 9.8 %all-to-all-start.2 = ((f32[32,1,128]{2,1,0:T(1,128)}), f32[32,1,128]{2,1,0:T(1,128)S(1)}, u32[]{:S(2)}, u32[]{:S(2)}) async-start(f32[32,1,128]{2,1,0:T(1,128)} %bitcast.7), calls=%async_computation.2 | async-start | bytes 32768 | tf_op jit(solution)/shard_map/all_to_all | solution.py:714

commit v9 on v8

--- a/solution.py
+++ b/solution.py
@@ -230,29 +230,40 @@
     return before + after, after - before
 
 
-def yz_parts(ref):
+COLUMNS = [(dx, dy) for dx in (-1, 0, 1) for dy in (-1, 0, 1) if dx or dy]
+
+
+def column_parts(ref, sign=None):
     a, a_sum, a_dif = z_stage(ref, 0)
     b, b_sum, b_dif = z_stage(ref, 1)
     c, c_sum, c_dif = z_stage(ref, 2)
-    pa, ma = y_stage(a)
-    pas, mas = y_stage(a_sum)
-    pad, _ = y_stage(a_dif)
-    pb, mb = y_stage(b)
-    pbs, mbs = y_stage(b_sum)
-    _, mbd = y_stage(b_dif)
-    pc, _ = y_stage(c)
-    pcs, _ = y_stage(c_sum)
-    pcd, mcd = y_stage(c_dif)
-    own_x = ACROSS1 * (pa + a_sum) + ACROSS2 * pas
-    even_x = ALONG1 * a + ALONG2 * (pa + a_sum) + SAME3 * pas
-    odd_x = MIXED2 * (mb + c_dif) + MIXED3 * (mbs + pcd)
-    own_y = ALONG1 * pb + ACROSS1 * b_sum + ALONG2 * pbs + MIXED2 * mcd
-    even_y = ACROSS1 * b + ALONG2 * pb + ACROSS2 * b_sum + SAME3 * pbs + MIXED3 * mcd
-    odd_y = MIXED2 * ma + MIXED3 * mas
-    own_z = ALONG1 * c_sum + ACROSS1 * pc + ALONG2 * pcs + MIXED2 * mbd
-    even_z = ACROSS1 * c + ACROSS2 * pc + ALONG2 * c_sum + SAME3 * pcs + MIXED3 * mbd
-    odd_z = MIXED2 * a_dif + MIXED3 * pad
-    return (own_x, even_x, odd_x), (own_y, even_y, odd_y), (own_z, even_z, odd_z)
+    parts = {(0, 0): (ACROSS1 * a_sum, ACROSS1 * b_sum, ALONG1 * c_sum)}
+    mixed_x, mixed_y = MIXED2 * b + MIXED3 * b_sum, MIXED2 * a + MIXED3 * a_sum
+    x_c_dif = c_dif
+    if sign is not None:
+        mixed_x, mixed_y, x_c_dif, a_dif = sign * mixed_x, sign * mixed_y, sign * c_dif, sign * a_dif
+    both_z = ACROSS1 * c + ALONG2 * c_sum
+    along, across = ALONG1 * a + ALONG2 * a_sum, ACROSS1 * b + ACROSS2 * b_sum
+    for dx in (-1, 1):
+        parts[dx, 0] = (along + dx * MIXED2 * x_c_dif, across, both_z + dx * MIXED2 * a_dif)
+    along, across = ALONG1 * b + ALONG2 * b_sum, ACROSS1 * a + ACROSS2 * a_sum
+    for dy in (-1, 1):
+        parts[0, dy] = (across, along + dy * MIXED2 * c_dif, both_z + dy * MIXED2 * b_dif)
+    same_x, same_y = ALONG2 * a + SAME3 * a_sum, ALONG2 * b + SAME3 * b_sum
+    same_z = ACROSS2 * c + SAME3 * c_sum
+    for dx in (-1, 1):
+        for dy in (-1, 1):
+            parts[dx, dy] = (
+                (same_x + dx * dy * mixed_x) + dx * MIXED3 * x_c_dif,
+                (same_y + dx * dy * mixed_y) + dy * MIXED3 * c_dif,
+                (same_z + dx * MIXED3 * a_dif) + dy * MIXED3 * b_dif,
+            )
+    return parts
+
+
+def put_columns(sh, springs_ref):
+    for i, (dx, dy) in enumerate(COLUMNS):
+        springs_ref[8 + i] = shift(springs_ref[6], dx * sh.pitch + dy)
 
 
 def x_stage(sh, lane, own, plus, minus, rim_plus, rim_minus):
@@ -261,21 +272,6 @@
     if rim_plus is None:
         return own + pick(lane < last, after) + pick(lane >= sh.pitch, before)
     return own + jnp.where(lane < last, after, rim_plus) + jnp.where(lane >= sh.pitch, before, rim_minus)
-
-
-def stencil(sh, lane, ref, rim):
-    parts = yz_parts(ref)
-    rims = yz_parts(rim) if rim is not None else [None] * 3
-    out = []
-    for (own, even, odd), rim_part in zip(parts, rims):
-        if rim_part is None:
-            out.append(x_stage(sh, lane, own, even + odd, even - odd, None, None))
-        else:
-            _, rim_even, rim_odd = rim_part
-            out.append(
-                x_stage(sh, lane, own, even + odd, even - odd, rim_even + rim_odd, rim_even - rim_odd)
-            )
-    return out
 
 
 def spring_parts(ref):
@@ -323,24 +319,33 @@
 
 def image_of(sh, lane, v, kv, rims, springs_ref):
     k = springs_ref[6]
-    k_before, k_after = shift(k, sh.pitch), shift(k, -sh.pitch)
     last = (sh.x + 1) * sh.pitch
     own = apply_block([springs_ref[f] for f in range(6)], [inner(v, m) for m in range(3)])
-    rim_parts = [yz_parts(rims[0]), yz_parts(rims[1])] if rims else None
-    out = []
-    for m, (plain, scaled) in enumerate(zip(yz_parts(v), yz_parts(kv))):
-        after = shift(k_before * (plain[1] + plain[2]) + (scaled[1] + scaled[2]), -sh.pitch)
-        before = shift(k_after * (plain[1] - plain[2]) + (scaled[1] - scaled[2]), sh.pitch)
-        if rims is None:
-            after, before = pick(lane < last, after), pick(lane >= sh.pitch, before)
-        else:
-            plain_rim, scaled_rim = rim_parts[0][m], rim_parts[1][m]
-            edge = k * (plain_rim[1] + plain_rim[2]) + (scaled_rim[1] + scaled_rim[2])
-            after = jnp.where(lane < last, after, edge)
-            edge = k * (plain_rim[1] - plain_rim[2]) + (scaled_rim[1] - scaled_rim[2])
-            before = jnp.where(lane >= sh.pitch, before, edge)
-        out.append(own[m] - (k * plain[0] + scaled[0] + after + before))
-    return out
+    plain, scaled = column_parts(v), column_parts(kv)
+    total = [k * plain[0, 0][m] + scaled[0, 0][m] for m in range(3)]
+    for dx in (0, -1, 1):
+        for m in range(3):
+            side = None
+            for i, column in enumerate(COLUMNS):
+                if column[0] == dx:
+                    moved = springs_ref[8 + i] * plain[column][m] + scaled[column][m]
+                    moved = shift(moved, -(dx * sh.pitch + column[1]))
+                    side = moved if side is None else side + moved
+            if dx:
+                side = pick(lane < last if dx > 0 else lane >= sh.pitch, side)
+            total[m] = total[m] + side
+    if rims is not None:
+        sign = jnp.where(lane < sh.pitch, -1.0, 1.0)
+        plain, scaled = column_parts(rims[0], sign), column_parts(rims[1], sign)
+        at_rim = (lane < sh.pitch) | (lane >= last)
+        for m in range(3):
+            side = None
+            for dy in (-1, 0, 1):
+                moved = shift(k, dy) * plain[1, dy][m] + scaled[1, dy][m]
+                moved = shift(moved, -dy)
+                side = moved if side is None else side + moved
+            total[m] = total[m] + pick(at_rim, side)
+    return [own[m] - total[m] for m in range(3)]
 
 
 def level(sh):
@@ -670,7 +675,7 @@
             pl.BlockSpec(memory_space=pltpu.HBM if i in remote_outs else pltpu.VMEM) for i in range(len(outs))
         ],
         scratch_shapes=[pltpu.VMEM(shape, f32) if isinstance(shape, tuple) else shape for shape in scratch],
-        compiler_params=pltpu.CompilerParams(vmem_limit_bytes=(62 if remote_ins else 48) * 1024 * 1024),
+        compiler_params=pltpu.CompilerParams(vmem_limit_bytes=(56 if remote_ins else 48) * 1024 * 1024),
         name=name,
     )(*ins)
 
@@ -859,7 +864,8 @@
         remote_ins=True,
     )
 
-    def spread(natural_ref, nodes_ref, stiff, field_ref, lanes_ref):
+    def spread(natural_ref, nodes_ref, stiff, inverse_in, field_ref, lanes_ref, inverse_ref):
+        inverse_ref[...] = inverse_in[...]
         select = selection(sh)
         field_ref[...] = jnp.zeros(field_ref.shape, f32)
         for m in range(3):
@@ -874,8 +880,11 @@
         field_ref[3, own, :] = jnp.dot(by_z, block_places(), precision=highest, preferred_element_type=f32)
         lanes_ref[...] = to_lanes(nodes_ref[...].astype(f32) + 1.0, select, small) - 1.0
 
-    start_field, nodes = call(
-        spread, "spread", [(4,) + plane, (sh.z, LANES)], [natural, nodes_natural, stiff_blocks]
+    start_field, nodes, inverse = call(
+        spread,
+        "spread",
+        [(4,) + plane, (sh.z, LANES), coarse_inverse.shape],
+        [natural, nodes_natural, stiff_blocks, coarse_inverse],
     )
     from_y, from_x = send_faces(sh, messages[: sh.x_links], messages[sh.x_links :])
     lines = to_all(lines)
@@ -919,6 +928,7 @@
         for f, entry in enumerate(own_block(sh, lane, (short_stiff, short_rim))):
             springs[f] = entry
         springs[6] = inner(short_stiff, 0)
+        put_columns(sh, springs)
         for m in range(3):
             some_residual[m] = ends(residual[m])
         index = local_solve(sh, ends_level(sh), some_residual, springs, (v0, v1), (kv0, kv1), factor)
@@ -935,14 +945,14 @@
         first_ends,
         "first_ends",
         [fields, plane, (2,) + plane, (sum_rows, LANES)] + z_shape(DEEP),
-        [start_field, *from_y, *from_x, nodes, lines, coarse_inverse],
+        [start_field, *from_y, *from_x, nodes, lines, inverse],
         [(1, sh.tall, LANES)] * 2
         + [
             (4, 8 * -(-(2 * sh.x + 2 * sh.y + 4) // 8) + 8, LANES),
             (8 * -(-(2 * label_x + 2 * label_y + 4) // 8) + 8, label_z),
         ]
         + [(1, 6 * EDGE, LANES)] * 2
-        + [short_fields, (7, 4 * EDGE, LANES)]
+        + [short_fields, (16, 4 * EDGE, LANES)]
         + short_scratch,
     )
 
@@ -953,6 +963,7 @@
         put(stiff_rim, 0, stiffness_ref[1])
         springs_ref[6] = stiffness_ref[0]
         springs_ref[7] = stiffness_ref[1]
+        put_columns(sh, springs_ref)
         lane, _, _ = sh.lane_grid(1)
         for f, entry in enumerate(own_block(sh, lane, (stiff, stiff_rim))):
             springs_ref[f] = entry
@@ -966,7 +977,7 @@
     solved, springs = call(
         first_solve,
         "first_solve",
-        [fields, (8,) + plane],
+        [fields, (16,) + plane],
         [residual, stiffness, values, nodes],
         [(1, sh.tall, LANES)] * 2 + solve_scratch,
     )
@@ -1008,7 +1019,7 @@
         copy.start()
         for m in range(3):
             some_residual[m] = ends(image_ref[m])
-        for f in range(7):
+        for f in range(16):
             some_springs[f] = ends(springs_ref[f])
         index = local_solve(sh, ends_level(sh), some_residual, some_springs, (v0, v1), (kv0, kv1), factor)
         pack_z(sh, NEAR, end_rows((v0, v1)[index]), z_refs)
@@ -1019,11 +1030,11 @@
         first_image,
         "first_image",
         [fields, fields, all_slots] + z_shape(NEAR),
-        [solved, *from_z, *from_y, *from_x, nodes, springs, coarse_inverse],
+        [solved, *from_z, *from_y, *from_x, nodes, springs, inverse],
         [tall] * 4
         + [(LANES, LANES), (8 * -(-share_rows // 8) + 8, LANES)]
         + [(8 * -(-all_slots[0] // 8) + 8, LANES), pltpu.SemaphoreType.DMA]
-        + [short_fields, (7, 4 * EDGE, LANES)]
+        + [short_fields, (16, 4 * EDGE, LANES)]
         + short_scratch,
         remote_outs=(2,),
     )

time: 70.1 us -> 69.1 us (0.986)
  waiting for transfers between devices: 14 us -> 10.2 us
  local copies, waits for them, and re-layouts: 0.04 us -> 3.31 us
  Pallas kernels: 22.2 us -> 19.9 us
  starting transfers between devices: 32.7 us -> 34.4 us
    unnamed x14 -> x10, local copies, waits for them, and re-layouts: 0.04 us -> 3.31 us
    ppermute x17, waiting for transfers between devices: 7.47 us -> 4.35 us  [send(): return lax.ppermute(value, AXES, permutation(sh.sizes, moves))]
    pallas_call x12, Pallas kernels: 22.2 us -> 19.9 us  [call(): pl.pallas_call(kernel, out_shape=[jax.ShapeDtypeStruct(shape, f32) for sh...]
    ppermute x17, starting transfers between devices: 19.2 us -> 20.9 us  [send(): return lax.ppermute(value, AXES, permutation(sh.sizes, moves))]
    all_to_all x3, waiting for transfers between devices: 6.58 us -> 5.87 us  [to_all(): return lax.all_to_all(slots, AXES, 0, 0, tiled=True)]
  transfers between devices with their start and end apart: 20 -> 20, of which waited for: 8 -> 5; matrix products, arithmetic and copies ran while one was open for 0% -> 0% of each run, Pallas kernels for 15% -> 13%
where the time goes in v9:
time: 69.1 us; the launch traced here: 68.6 us
  starting transfers between devices  34.4 us (50%)
  Pallas kernels  19.9 us (29%)
  waiting for transfers between devices  10.2 us (15%)
  local copies, waits for them, and re-layouts  3.31 us (5%)
  between operations  0.81 us (1%)
    ppermute x17, starting transfers between devices, send(): return lax.ppermute(value, AXES, permutation(sh.sizes, moves))  20.9 us
    pallas_call x12, Pallas kernels, call(): pl.pallas_call(kernel, out_shape=[jax.ShapeDtypeStruct(shape, f32) for sh...  19.9 us
    all_to_all x3, starting transfers between devices, to_all(): return lax.all_to_all(slots, AXES, 0, 0, tiled=True)  13.5 us
    all_to_all x3, waiting for transfers between devices, to_all(): return lax.all_to_all(slots, AXES, 0, 0, tiled=True)  5.87 us
    ppermute x17, waiting for transfers between devices, send(): return lax.ppermute(value, AXES, permutation(sh.sizes, moves))  4.35 us
    unnamed x10, local copies, waits for them, and re-layouts  3.31 us
  transfers between devices with their start and end apart: 20, of which 5 were waited for; matrix products, arithmetic and copies ran while one was open for 0% of the time, Pallas kernels for 13%

profile of v9, /device:TPU:0, one launch (start us, length us, event | category | flops | bytes accessed | tf_op | source)
XLA Modules:
  0.0 68.6 jit_solution(12502730648254713389)
XLA Ops:
  0.6 3.0 %begin.1 = (f32[48,64]{1,0:T(8,128)}, f32[256,128]{1,0:T(8,128)}, f32[40,128]{1,0:T(8,128)}, f32[40,128]{1,0:T(8,128)}, f32[40,128]{1,0:T(8,128)}) custom-call(f32[3,64,128]{2,1,0:T(8,128)} %bitcast.12, s32[4,4,64]{2,1,0:T(4,128)} %labels_in.1, f32[8]{0:T(128)} %moduli_in.1, s32[64,128]{1,0:T(8,128)} %bitcast.17), custom_call_target="tpu_custom_call" | custom-call | tf_op jit(solution)/shard_map/begin/pallas_call | solution.py:670
  3.6 7.3 %all-to-all-start = ((f32[32,8,128]{2,1,0:T(8,128)}), f32[32,8,128]{2,1,0:T(8,128)S(1)}, u32[]{:S(2)}, u32[]{:S(2)}) async-start(f32[32,8,128]{2,1,0:T(8,128)} %bitcast.20), calls=%async_computation | async-start | bytes 262144 | tf_op jit(solution)/shard_map/all_to_all | solution.py:719
  10.9 1.8 %collective-permute-start = (f32[40,128]{1,0:T(8,128)}, f32[40,128]{1,0:T(8,128)S(1)}, u32[]{:S(2)}, u32[]{:S(2)}) collective-permute-start(f32[40,128]{1,0:T(8,128)} %get-tuple-element.42), channel_id=1, source_target_pairs={{0,4},{1,5},{2,6},{3,7},{4,0},{5,1},{6,2},{7,3},{8,12},{9,13},{10,... | collective-permute-start | bytes 61448 | tf_op jit(solution)/shard_map/ppermute | solution.py:705
  12.7 1.5 %collective-permute-start.1 = (f32[40,128]{1,0:T(8,128)}, f32[40,128]{1,0:T(8,128)S(1)}, u32[]{:S(2)}, u32[]{:S(2)}) collective-permute-start(f32[40,128]{1,0:T(8,128)} %get-tuple-element.43), channel_id=1, source_target_pairs={{0,16},{1,17},{2,18},{3,19},{4,8},{5,9},{6,10},{7,11},{8,4},{9,5},... | collective-permute-start | bytes 61448 | tf_op jit(solution)/shard_map/ppermute | solution.py:705
  14.2 0.6 collective-permute-start.2
  14.8 0.9 %copy-done = f32[3,8,8,128]{3,2,1,0:T(8,128)S(1)} copy-done((f32[3,8,8,128]{3,2,1,0:T(8,128)S(1)}, f32[3,8,8,128]{3,2,1,0:T(8,128)}, u32[]{:S(2)}) %copy-start) | copy-done | bytes 98328
  15.7 0.9 %copy-done.2 = f32[36,1152]{1,0:T(8,128)S(1)} copy-done((f32[36,1152]{1,0:T(8,128)S(1)}, f32[36,1152]{1,0:T(8,128)}, u32[]{:S(2)}) %copy-start.2) | copy-done | bytes 165912
  16.6 0.8 %copy-done.3 = s32[8,8,128]{2,1,0:T(8,128)S(1)} copy-done((s32[8,8,128]{2,1,0:T(8,128)S(1)}, s32[8,8,128]{2,1,0:T(8,128)}, u32[]{:S(2)}) %copy-start.3) | copy-done | bytes 32792
  17.3 0.7 %copy-done.4 = f32[48,64]{1,0:T(8,128)S(1)} copy-done((f32[48,64]{1,0:T(8,128)S(1)}, f32[48,64]{1,0:T(8,128)}, u32[]{:S(2)}) %copy-start.4) | copy-done | bytes 12312
  18.1 0.7 spread.1
  18.8 0.0 collective-permute-done.refs_1_
  18.8 0.0 collective-permute-done.2.refs_3_
  18.8 0.4 all-to-all-done
  19.2 1.6 %first_ends.1 = (f32[3,144,128]{2,1,0:T(8,128)S(1)}, f32[144,128]{1,0:T(8,128)S(1)}, f32[2,144,128]{2,1,0:T(8,128)S(1)}, f32[48,128]{1,0:T(8,128)S(1)}, f32[24,128]{1,0:T(8,128)S(1)}, /*index=5*/f32[24,128]{1,0:T(8,128)S(1)}) custom-call(f32[4,144,128]{2,1,0:T(8,128)S(1)} %get-tuple-element.41.refs_0_.start_ref, f32[40,128]{1,0:T(8,128)S(1)} %collective-permute-done.refs_1_, ...), custom_call_target="tpu_custom_call" | custom-call | tf_op jit(solution)/shard_map/first_ends/pallas_call | solution.py:670
  20.8 0.5 collective-permute-start.3
  21.3 0.8 %collective-permute-start.4 = (f32[24,128]{1,0:T(8,128)S(1)}, f32[24,128]{1,0:T(8,128)S(1)}, u32[]{:S(2)}, u32[]{:S(2)}) collective-permute-start(f32[24,128]{1,0:T(8,128)S(1)} %get-tuple-element.53), channel_id=1, source_target_pairs={{0,3},{1,2},{2,1},{3,0},{4,7},{5,6},{6,5},{7,4},{8,11},{9,10},{10,... | collective-permute-start | bytes 36872 | tf_op jit(solution)/shard_map/ppermute | solution.py:705
  22.1 3.3 %first_solve.1 = (f32[3,144,128]{2,1,0:T(8,128)S(1)}, f32[16,144,128]{2,1,0:T(8,128)S(1)}) custom-call(f32[3,144,128]{2,1,0:T(8,128)S(1)} %get-tuple-element.48.residual_ref, f32[2,144,128]{2,1,0:T(8,128)S(1)} %get-tuple-element.49.stiffness_ref, f32[48,128]{1,0:T(8,128)S(1)} %get-tuple-element.50.values, ...), custom_call_target="tpu_custom_call" | custom-call | tf_op jit(solution)/shard_map/first_solve/pallas_call | solution.py:670
  25.4 0.0 collective-permute-done.4.refs_2_
  25.4 0.3 deep.1
  25.8 2.5 %collective-permute-start.5 = (f32[144,128]{1,0:T(8,128)S(1)}, f32[144,128]{1,0:T(8,128)S(1)}, u32[]{:S(2)}, u32[]{:S(2)}) collective-permute-start(f32[144,128]{1,0:T(8,128)S(1)} %get-tuple-element.54), channel_id=1, source_target_pairs={{0,4},{1,5},{2,6},{3,7},{4,0},{5,1},{6,2},{7,3},{8,12},{9,13},{10,... | collective-permute-start | bytes 221192 | tf_op jit(solution)/shard_map/ppermute | solution.py:705
  28.3 0.5 collective-permute-start.6
  28.8 1.5 %collective-permute-start.7 = (f32[144,128]{1,0:T(8,128)S(1)}, f32[144,128]{1,0:T(8,128)S(1)}, u32[]{:S(2)}, u32[]{:S(2)}) collective-permute-start(f32[144,128]{1,0:T(8,128)S(1)} %get-tuple-element.56), channel_id=1, source_target_pairs={{0,16},{1,17},{2,18},{3,19},{4,20},{5,21},{6,22},{7,23},{8,24},{9,... | collective-permute-start | bytes 221192 | tf_op jit(solution)/shard_map/ppermute | solution.py:705
  30.3 0.5 collective-permute-start.8
  30.8 1.5 %collective-permute-start.9 = (f32[40,128]{1,0:T(8,128)S(1)}, f32[40,128]{1,0:T(8,128)S(1)}, u32[]{:S(2)}, u32[]{:S(2)}) collective-permute-start(f32[40,128]{1,0:T(8,128)S(1)} %get-tuple-element.58), channel_id=1, source_target_pairs={{0,16},{1,17},{2,18},{3,19},{4,24},{5,25},{6,26},{7,27},{8,20},{9,... | collective-permute-start | bytes 61448 | tf_op jit(solution)/shard_map/ppermute | solution.py:705
  32.3 2.7 %collective-permute-done.8.refs_6_ = f32[40,128]{1,0:T(8,128)S(1)} collective-permute-done((f32[40,128]{1,0:T(8,128)S(1)}, f32[40,128]{1,0:T(8,128)S(1)}, u32[]{:S(2)}, u32[]{:S(2)}) %collective-permute-start.8) | collective-permute-done | bytes 20512 | tf_op jit(solution)/shard_map/ppermute | solution.py:705
  35.0 0.0 collective-permute-done.7.refs_5_
  35.0 3.1 %first_image.1 = (f32[3,144,128]{2,1,0:T(8,128)S(1)}, f32[3,144,128]{2,1,0:T(8,128)S(1)}, f32[288,128]{1,0:T(8,128)}, f32[24,128]{1,0:T(8,128)S(1)}, f32[24,128]{1,0:T(8,128)S(1)}) custom-call(f32[3,144,128]{2,1,0:T(8,128)S(1)} %get-tuple-element.51.refs_0_, f32[24,128]{1,0:T(8,128)S(1)} %collective-permute-done.3.refs_1_, ...), custom_call_target="tpu_custom_call" | custom-call | tf_op jit(solution)/shard_map/first_image/pallas_call | solution.py:670
  38.1 3.5 %all-to-all-start.1 = ((f32[32,1,1152]{2,1,0:T(1,128)}), f32[32,1,1152]{2,1,0:T(1,128)S(1)}, u32[]{:S(2)}, u32[]{:S(2)}) async-start(f32[32,1,1152]{2,1,0:T(1,128)} %bitcast.4), calls=%async_computation.1 | async-start | bytes 294912 | tf_op jit(solution)/shard_map/all_to_all | solution.py:719
  41.6 0.1 collective-permute-start.10
  41.7 1.6 %collective-permute-start.11 = (f32[24,128]{1,0:T(8,128)S(1)}, f32[24,128]{1,0:T(8,128)S(1)}, u32[]{:S(2)}, u32[]{:S(2)}) collective-permute-start(f32[24,128]{1,0:T(8,128)S(1)} %get-tuple-element.62), channel_id=1, source_target_pairs={{0,3},{1,2},{2,1},{3,0},{4,7},{5,6},{6,5},{7,4},{8,11},{9,10},{10,... | collective-permute-start | bytes 36872 | tf_op jit(solution)/shard_map/ppermute | solution.py:705
  43.4 2.6 %second_solve.1.refs_0_ = f32[3,144,128]{2,1,0:T(8,128)S(1)} custom-call(f32[3,144,128]{2,1,0:T(8,128)S(1)} %get-tuple-element.60.image_ref.first_ref.refs_10_, f32[16,144,128]{2,1,0:T(8,128)S(1)} %get-tuple-element.59.refs_9_.springs_ref), custom_call_target="tpu_custom_call" | custom-call | tf_op jit(solution)/shard_map/second_solve/pallas_call | solution.py:670
  46.0 0.0 collective-permute-done.10.refs_1_
  46.0 0.0 collective-permute-done.11.refs_2_
  46.0 0.4 near.1
  46.4 1.5 %collective-permute-start.14 = (f32[144,128]{1,0:T(8,128)S(1)}, f32[144,128]{1,0:T(8,128)S(1)}, u32[]{:S(2)}, u32[]{:S(2)}) collective-permute-start(f32[144,128]{1,0:T(8,128)S(1)} %get-tuple-element.65), channel_id=1, source_target_pairs={{0,16},{1,17},{2,18},{3,19},{4,20},{5,21},{6,22},{7,23},{8,24},{9,... | collective-permute-start | bytes 221192 | tf_op jit(solution)/shard_map/ppermute | solution.py:705
  47.9 1.5 %collective-permute-start.12 = (f32[72,128]{1,0:T(8,128)S(1)}, f32[72,128]{1,0:T(8,128)S(1)}, u32[]{:S(2)}, u32[]{:S(2)}) collective-permute-start(f32[72,128]{1,0:T(8,128)S(1)} %get-tuple-element.63), channel_id=1, source_target_pairs={{0,4},{1,5},{2,6},{3,7},{4,0},{5,1},{6,2},{7,3},{8,12},{9,13},{10,... | collective-permute-start | bytes 110600 | tf_op jit(solution)/shard_map/ppermute | solution.py:705
  49.4 0.6 collective-permute-start.13
  50.0 2.4 %collective-permute-start.15 = (f32[24,128]{1,0:T(8,128)S(1)}, f32[24,128]{1,0:T(8,128)S(1)}, u32[]{:S(2)}, u32[]{:S(2)}) collective-permute-start(f32[24,128]{1,0:T(8,128)S(1)} %get-tuple-element.66), channel_id=1, source_target_pairs={{0,20},{1,21},{2,22},{3,23},{4,16},{5,17},{6,18},{7,19},{8,28},{9,... | collective-permute-start | bytes 36872 | tf_op jit(solution)/shard_map/ppermute | solution.py:705
  52.4 1.5 %collective-permute-start.16 = (f32[24,128]{1,0:T(8,128)S(1)}, f32[24,128]{1,0:T(8,128)S(1)}, u32[]{:S(2)}, u32[]{:S(2)}) collective-permute-start(f32[24,128]{1,0:T(8,128)S(1)} %get-tuple-element.67), channel_id=1, source_target_pairs={{0,16},{1,17},{2,18},{3,19},{4,24},{5,25},{6,26},{7,27},{8,20},{9,... | collective-permute-start | bytes 36872 | tf_op jit(solution)/shard_map/ppermute | solution.py:705
  53.9 0.6 between.1
  54.5 0.1 collective-permute-done.15.refs_6_
  54.6 1.5 %collective-permute-done.16.refs_7_ = f32[24,128]{1,0:T(8,128)S(1)} collective-permute-done((f32[24,128]{1,0:T(8,128)S(1)}, f32[24,128]{1,0:T(8,128)S(1)}, u32[]{:S(2)}, u32[]{:S(2)}) %collective-permute-start.16) | collective-permute-done | bytes 12320 | tf_op jit(solution)/shard_map/ppermute | solution.py:705
  56.1 0.0 collective-permute-done.12.refs_3_
  56.1 1.9 %second_image.1 = (f32[3,144,128]{2,1,0:T(8,128)S(1)}, f32[3,144,128]{2,1,0:T(8,128)S(1)}, f32[32,128]{1,0:T(8,128)}) custom-call(f32[3,144,128]{2,1,0:T(8,128)S(1)} %second_solve.1.refs_0_, f32[24,128]{1,0:T(8,128)S(1)} %collective-permute-done.10.refs_1_, f32[24,128]{1,0:T(8,128)S(1)} %collective-permute-done.11.refs_2_, ...), custom_call_target="tpu_custom_call" | custom-call | tf_op jit(solution)/shard_map/second_image/pallas_call | solution.py:670
  58.0 2.7 %all-to-all-start.2 = ((f32[32,1,128]{2,1,0:T(1,128)}), f32[32,1,128]{2,1,0:T(1,128)S(1)}, u32[]{:S(2)}, u32[]{:S(2)}) async-start(f32[32,1,128]{2,1,0:T(1,128)} %bitcast.7), calls=%async_computation.2 | async-start | bytes 32768 | tf_op jit(solution)/shard_map/all_to_all | solution.py:719
  60.7 1.6 %turn.1.turned_ref = f32[4,3,64,128]{3,2,1,0:T(8,128)S(1)} custom-call(f32[3,144,128]{2,1,0:T(8,128)S(1)} %get-tuple-element.70.search_ref, f32[3,144,128]{2,1,0:T(8,128)S(1)} %get-tuple-element.60.image_ref.first_ref.refs_10_, f32[3,144,128]{2,1,0:T(8,128)S(1)} %get-tuple-element.74.second_ref, f32[3,144,128]{2,1,0:T(8,128)S(1)} %get-tuple-element.75.image_ref), custom_call_target="tpu_custom_call" | custom-call | tf_op jit(solution)/shard_map/turn/pallas_call | solution.py:670
  62.3 5.5 %all-to-all-done.2 = f32[32,1,128]{2,1,0:T(1,128)S(1)} async-done(((f32[32,1,128]{2,1,0:T(1,128)}), f32[32,1,128]{2,1,0:T(1,128)S(1)}, u32[]{:S(2)}, u32[]{:S(2)}) %all-to-all-start.2) | async-done | bytes 16416 | tf_op jit(solution)/shard_map/all_to_all | solution.py:719
  67.8 0.8 %finish.1 = (f32[3,64,128]{2,1,0:T(8,128)}, f32[3,64,128]{2,1,0:T(8,128)}) custom-call(f32[32,128]{1,0:T(8,128)S(1)} %bitcast.19, f32[3,64,128]{2,1,0:T(8,128)S(1)} %bitcast.14, f32[4,3,64,128]{3,2,1,0:T(8,128)S(1)} %turn.1.turned_ref), custom_call_target="tpu_custom_call" | custom-call | tf_op jit(solution)/shard_map/finish/pallas_call | solution.py:670
  (14 shorter events, 0.0 us)
Async XLA Ops:
  3.6 15.6 %all-to-all-start = ((f32[32,8,128]{2,1,0:T(8,128)}), f32[32,8,128]{2,1,0:T(8,128)S(1)}, u32[]{:S(2)}, u32[]{:S(2)}) async-start(f32[32,8,128]{2,1,0:T(8,128)} %bitcast.20), calls=%async_computation | async-start | bytes 262144 | tf_op jit(solution)/shard_map/all_to_all | solution.py:719
  10.9 7.9 %collective-permute-start = (f32[40,128]{1,0:T(8,128)}, f32[40,128]{1,0:T(8,128)S(1)}, u32[]{:S(2)}, u32[]{:S(2)}) collective-permute-start(f32[40,128]{1,0:T(8,128)} %get-tuple-element.42), channel_id=1, source_target_pairs={{0,4},{1,5},{2,6},{3,7},{4,0},{5,1},{6,2},{7,3},{8,12},{9,13},{10,... | collective-permute-start | bytes 61448 | tf_op jit(solution)/shard_map/ppermute | solution.py:705
  12.7 6.0 %collective-permute-start.1 = (f32[40,128]{1,0:T(8,128)}, f32[40,128]{1,0:T(8,128)S(1)}, u32[]{:S(2)}, u32[]{:S(2)}) collective-permute-start(f32[40,128]{1,0:T(8,128)} %get-tuple-element.43), channel_id=1, source_target_pairs={{0,16},{1,17},{2,18},{3,19},{4,8},{5,9},{6,10},{7,11},{8,4},{9,5},... | collective-permute-start | bytes 61448 | tf_op jit(solution)/shard_map/ppermute | solution.py:705
  14.2 4.6 %collective-permute-start.2 = (f32[40,128]{1,0:T(8,128)}, f32[40,128]{1,0:T(8,128)S(1)}, u32[]{:S(2)}, u32[]{:S(2)}) collective-permute-start(f32[40,128]{1,0:T(8,128)} %get-tuple-element.44), channel_id=1, source_target_pairs={{0,16},{1,17},{2,18},{3,19},{4,20},{5,21},{6,22},{7,23},{8,24},{9,... | collective-permute-start | bytes 61448 | tf_op jit(solution)/shard_map/ppermute | solution.py:705
  14.8 0.9 %copy-start = (f32[3,8,8,128]{3,2,1,0:T(8,128)S(1)}, f32[3,8,8,128]{3,2,1,0:T(8,128)}, u32[]{:S(2)}) copy-start(f32[3,8,8,128]{3,2,1,0:T(8,128)} %param.5) | copy-start | bytes 294916
  15.7 0.9 %copy-start.2 = (f32[36,1152]{1,0:T(8,128)S(1)}, f32[36,1152]{1,0:T(8,128)}, u32[]{:S(2)}) copy-start(f32[36,1152]{1,0:T(8,128)} %inverse_in.1) | copy-start | bytes 497668
  16.6 0.8 %copy-start.3 = (s32[8,8,128]{2,1,0:T(8,128)S(1)}, s32[8,8,128]{2,1,0:T(8,128)}, u32[]{:S(2)}) copy-start(s32[8,8,128]{2,1,0:T(8,128)} %param.8) | copy-start | bytes 98308
  17.3 0.7 %copy-start.4 = (f32[48,64]{1,0:T(8,128)S(1)}, f32[48,64]{1,0:T(8,128)}, u32[]{:S(2)}) copy-start(f32[48,64]{1,0:T(8,128)} %get-tuple-element.40.stiff) | copy-start | bytes 36868
  20.8 4.6 %collective-permute-start.3 = (f32[24,128]{1,0:T(8,128)S(1)}, f32[24,128]{1,0:T(8,128)S(1)}, u32[]{:S(2)}, u32[]{:S(2)}) collective-permute-start(f32[24,128]{1,0:T(8,128)S(1)} %get-tuple-element.52), channel_id=1, source_target_pairs={{0,1},{1,0},{2,3},{3,2},{4,5},{5,4},{6,7},{7,6},{8,9},{9,8},{10,11... | collective-permute-start | bytes 36872 | tf_op jit(solution)/shard_map/ppermute | solution.py:705
  21.3 4.1 %collective-permute-start.4 = (f32[24,128]{1,0:T(8,128)S(1)}, f32[24,128]{1,0:T(8,128)S(1)}, u32[]{:S(2)}, u32[]{:S(2)}) collective-permute-start(f32[24,128]{1,0:T(8,128)S(1)} %get-tuple-element.53), channel_id=1, source_target_pairs={{0,3},{1,2},{2,1},{3,0},{4,7},{5,6},{6,5},{7,4},{8,11},{9,10},{10,... | collective-permute-start | bytes 36872 | tf_op jit(solution)/shard_map/ppermute | solution.py:705
  25.8 9.2 %collective-permute-start.5 = (f32[144,128]{1,0:T(8,128)S(1)}, f32[144,128]{1,0:T(8,128)S(1)}, u32[]{:S(2)}, u32[]{:S(2)}) collective-permute-start(f32[144,128]{1,0:T(8,128)S(1)} %get-tuple-element.54), channel_id=1, source_target_pairs={{0,4},{1,5},{2,6},{3,7},{4,0},{5,1},{6,2},{7,3},{8,12},{9,13},{10,... | collective-permute-start | bytes 221192 | tf_op jit(solution)/shard_map/ppermute | solution.py:705
  28.3 6.7 %collective-permute-start.6 = (f32[144,128]{1,0:T(8,128)S(1)}, f32[144,128]{1,0:T(8,128)S(1)}, u32[]{:S(2)}, u32[]{:S(2)}) collective-permute-start(f32[144,128]{1,0:T(8,128)S(1)} %get-tuple-element.55), channel_id=1, source_target_pairs={{0,16},{1,17},{2,18},{3,19},{4,8},{5,9},{6,10},{7,11},{8,4},{9,5},... | collective-permute-start | bytes 221192 | tf_op jit(solution)/shard_map/ppermute | solution.py:705
  28.8 6.2 %collective-permute-start.7 = (f32[144,128]{1,0:T(8,128)S(1)}, f32[144,128]{1,0:T(8,128)S(1)}, u32[]{:S(2)}, u32[]{:S(2)}) collective-permute-start(f32[144,128]{1,0:T(8,128)S(1)} %get-tuple-element.56), channel_id=1, source_target_pairs={{0,16},{1,17},{2,18},{3,19},{4,20},{5,21},{6,22},{7,23},{8,24},{9,... | collective-permute-start | bytes 221192 | tf_op jit(solution)/shard_map/ppermute | solution.py:705
  30.3 4.7 %collective-permute-start.8 = (f32[40,128]{1,0:T(8,128)S(1)}, f32[40,128]{1,0:T(8,128)S(1)}, u32[]{:S(2)}, u32[]{:S(2)}) collective-permute-start(f32[40,128]{1,0:T(8,128)S(1)} %get-tuple-element.57), channel_id=1, source_target_pairs={{0,20},{1,21},{2,22},{3,23},{4,16},{5,17},{6,18},{7,19},{8,28},{9,... | collective-permute-start | bytes 61448 | tf_op jit(solution)/shard_map/ppermute | solution.py:705
  30.8 4.2 %collective-permute-start.9 = (f32[40,128]{1,0:T(8,128)S(1)}, f32[40,128]{1,0:T(8,128)S(1)}, u32[]{:S(2)}, u32[]{:S(2)}) collective-permute-start(f32[40,128]{1,0:T(8,128)S(1)} %get-tuple-element.58), channel_id=1, source_target_pairs={{0,16},{1,17},{2,18},{3,19},{4,24},{5,25},{6,26},{7,27},{8,20},{9,... | collective-permute-start | bytes 61448 | tf_op jit(solution)/shard_map/ppermute | solution.py:705
  38.1 15.8 %all-to-all-start.1 = ((f32[32,1,1152]{2,1,0:T(1,128)}), f32[32,1,1152]{2,1,0:T(1,128)S(1)}, u32[]{:S(2)}, u32[]{:S(2)}) async-start(f32[32,1,1152]{2,1,0:T(1,128)} %bitcast.4), calls=%async_computation.1 | async-start | bytes 294912 | tf_op jit(solution)/shard_map/all_to_all | solution.py:719
  41.6 4.4 %collective-permute-start.10 = (f32[24,128]{1,0:T(8,128)S(1)}, f32[24,128]{1,0:T(8,128)S(1)}, u32[]{:S(2)}, u32[]{:S(2)}) collective-permute-start(f32[24,128]{1,0:T(8,128)S(1)} %get-tuple-element.61), channel_id=1, source_target_pairs={{0,1},{1,0},{2,3},{3,2},{4,5},{5,4},{6,7},{7,6},{8,9},{9,8},{10,11... | collective-permute-start | bytes 36872 | tf_op jit(solution)/shard_map/ppermute | solution.py:705
  41.7 4.3 %collective-permute-start.11 = (f32[24,128]{1,0:T(8,128)S(1)}, f32[24,128]{1,0:T(8,128)S(1)}, u32[]{:S(2)}, u32[]{:S(2)}) collective-permute-start(f32[24,128]{1,0:T(8,128)S(1)} %get-tuple-element.62), channel_id=1, source_target_pairs={{0,3},{1,2},{2,1},{3,0},{4,7},{5,6},{6,5},{7,4},{8,11},{9,10},{10,... | collective-permute-start | bytes 36872 | tf_op jit(solution)/shard_map/ppermute | solution.py:705
  46.4 9.7 %collective-permute-start.14 = (f32[144,128]{1,0:T(8,128)S(1)}, f32[144,128]{1,0:T(8,128)S(1)}, u32[]{:S(2)}, u32[]{:S(2)}) collective-permute-start(f32[144,128]{1,0:T(8,128)S(1)} %get-tuple-element.65), channel_id=1, source_target_pairs={{0,16},{1,17},{2,18},{3,19},{4,20},{5,21},{6,22},{7,23},{8,24},{9,... | collective-permute-start | bytes 221192 | tf_op jit(solution)/shard_map/ppermute | solution.py:705
  47.9 8.2 %collective-permute-start.12 = (f32[72,128]{1,0:T(8,128)S(1)}, f32[72,128]{1,0:T(8,128)S(1)}, u32[]{:S(2)}, u32[]{:S(2)}) collective-permute-start(f32[72,128]{1,0:T(8,128)S(1)} %get-tuple-element.63), channel_id=1, source_target_pairs={{0,4},{1,5},{2,6},{3,7},{4,0},{5,1},{6,2},{7,3},{8,12},{9,13},{10,... | collective-permute-start | bytes 110600 | tf_op jit(solution)/shard_map/ppermute | solution.py:705
  49.4 6.7 %collective-permute-start.13 = (f32[72,128]{1,0:T(8,128)S(1)}, f32[72,128]{1,0:T(8,128)S(1)}, u32[]{:S(2)}, u32[]{:S(2)}) collective-permute-start(f32[72,128]{1,0:T(8,128)S(1)} %get-tuple-element.64), channel_id=1, source_target_pairs={{0,16},{1,17},{2,18},{3,19},{4,8},{5,9},{6,10},{7,11},{8,4},{9,5},... | collective-permute-start | bytes 110600 | tf_op jit(solution)/shard_map/ppermute | solution.py:705
  50.0 4.6 %collective-permute-start.15 = (f32[24,128]{1,0:T(8,128)S(1)}, f32[24,128]{1,0:T(8,128)S(1)}, u32[]{:S(2)}, u32[]{:S(2)}) collective-permute-start(f32[24,128]{1,0:T(8,128)S(1)} %get-tuple-element.66), channel_id=1, source_target_pairs={{0,20},{1,21},{2,22},{3,23},{4,16},{5,17},{6,18},{7,19},{8,28},{9,... | collective-permute-start | bytes 36872 | tf_op jit(solution)/shard_map/ppermute | solution.py:705
  52.4 3.7 %collective-permute-start.16 = (f32[24,128]{1,0:T(8,128)S(1)}, f32[24,128]{1,0:T(8,128)S(1)}, u32[]{:S(2)}, u32[]{:S(2)}) collective-permute-start(f32[24,128]{1,0:T(8,128)S(1)} %get-tuple-element.67), channel_id=1, source_target_pairs={{0,16},{1,17},{2,18},{3,19},{4,24},{5,25},{6,26},{7,27},{8,20},{9,... | collective-permute-start | bytes 36872 | tf_op jit(solution)/shard_map/ppermute | solution.py:705
  58.0 9.8 %copy-start.1 = (f32[3,8,8,128]{3,2,1,0:T(8,128)S(1)}, f32[3,8,8,128]{3,2,1,0:T(8,128)}, u32[]{:S(2)}) copy-start(f32[3,8,8,128]{3,2,1,0:T(8,128)} %param.5) | copy-start | bytes 294916
  58.0 9.8 %all-to-all-start.2 = ((f32[32,1,128]{2,1,0:T(1,128)}), f32[32,1,128]{2,1,0:T(1,128)S(1)}, u32[]{:S(2)}, u32[]{:S(2)}) async-start(f32[32,1,128]{2,1,0:T(1,128)} %bitcast.7), calls=%async_computation.2 | async-start | bytes 32768 | tf_op jit(solution)/shard_map/all_to_all | solution.py:719

commit v10 on v9

--- a/solution.py
+++ b/solution.py
@@ -261,9 +261,9 @@
     return parts
 
 
-def put_columns(sh, springs_ref):
+def put_columns(sh, springs_ref, columns):
     for i, (dx, dy) in enumerate(COLUMNS):
-        springs_ref[8 + i] = shift(springs_ref[6], dx * sh.pitch + dy)
+        columns[i] = shift(springs_ref[6], dx * sh.pitch + dy)
 
 
 def x_stage(sh, lane, own, plus, minus, rim_plus, rim_minus):
@@ -317,7 +317,7 @@
     )
 
 
-def image_of(sh, lane, v, kv, rims, springs_ref):
+def image_of(sh, lane, v, kv, rims, springs_ref, columns):
     k = springs_ref[6]
     last = (sh.x + 1) * sh.pitch
     own = apply_block([springs_ref[f] for f in range(6)], [inner(v, m) for m in range(3)])
@@ -328,7 +328,7 @@
             side = None
             for i, column in enumerate(COLUMNS):
                 if column[0] == dx:
-                    moved = springs_ref[8 + i] * plain[column][m] + scaled[column][m]
+                    moved = columns[i] * plain[column][m] + scaled[column][m]
                     moved = shift(moved, -(dx * sh.pitch + column[1]))
                     side = moved if side is None else side + moved
             if dx:
@@ -384,9 +384,10 @@
     ref[f, EDGE : ref.shape[1] - EDGE, :] = value
 
 
-def local_solve(sh, z, residual_ref, springs_ref, v, kv, factor):
+def local_solve(sh, z, residual_ref, springs_ref, columns, v, kv, factor):
     lane, _, _ = sh.lane_grid(1)
     mask = extended_mask(sh, z)
+    put_columns(sh, springs_ref, columns)
     for m in range(3):
         factor[m] = pick(mask, relax / jnp.where(mask, springs_ref[m], 1.0))
         value = residual_ref[m] * factor[m]
@@ -394,7 +395,7 @@
         put(kv[0], m, springs_ref[6] * value)
     for sweep in range(SWEEPS - 1):
         old, new = sweep % 2, (sweep + 1) % 2
-        image = image_of(sh, lane, v[old], kv[old], None, springs_ref)
+        image = image_of(sh, lane, v[old], kv[old], None, springs_ref, columns)
         for m in range(3):
             value = inner(v[old], m) + factor[m] * (residual_ref[m] - image[m])
             put(v[new], m, value)
@@ -694,8 +695,8 @@
             for z in range(sizes[2]):
                 place = [x, y, z]
                 goal = [partner(a, moves[a], place[a]) if a in moves else place[a] for a in range(3)]
-                if goal == place and 0 not in moves and sizes[0] % 2 == 0:
-                    goal[0] = partner(0, 0, x)
+                if any(goal[a] == place[a] for a in moves) and sizes[2] % 2 == 0:
+                    goal = [x, y, partner(2, 0, z)]
                 flat = [(p[0] * sizes[1] + p[1]) * sizes[2] + p[2] for p in (place, goal)]
                 pairs.append(tuple(flat))
     return pairs
@@ -710,8 +711,8 @@
 
 
 def send_faces(sh, x_messages, y_messages):
+    from_x = [send(sh, message, {0: link}) for link, message in enumerate(x_messages)]
     from_y = [send(sh, message, {1: link}) for link, message in enumerate(y_messages)]
-    from_x = [send(sh, message, {0: link}) for link, message in enumerate(x_messages)]
     return from_y, from_x
 
 
@@ -891,8 +892,8 @@
 
     short = (3, 6 * EDGE, LANES)
     short_fields = (3, 4 * EDGE, LANES)
-    solve_scratch = [tall] * 4 + [fields]
-    short_scratch = [short] * 4 + [short_fields]
+    solve_scratch = [tall] * 4 + [fields, (8,) + plane]
+    short_scratch = [short] * 4 + [short_fields, (8, 4 * EDGE, LANES)]
 
     def end_rows(ref):
         def rows(f, start, count):
@@ -909,7 +910,7 @@
         residual, wide_nodes, stiffness_ref, values = take(4)
         z_refs = take(sh.z_links)
         stiff, stiff_rim, cells, labels, short_stiff, short_rim, some_residual, springs = take(8)
-        v0, v1, kv0, kv1, factor = take(5)
+        v0, v1, kv0, kv1, factor, columns = take(6)
         clear_guards(sh, (stiff, stiff_rim, short_stiff, short_rim, v0, v1, kv0, kv1))
         residual[...] = field_ref[0:3]
         put(stiff, 0, field_ref[3])
@@ -928,10 +929,9 @@
         for f, entry in enumerate(own_block(sh, lane, (short_stiff, short_rim))):
             springs[f] = entry
         springs[6] = inner(short_stiff, 0)
-        put_columns(sh, springs)
         for m in range(3):
             some_residual[m] = ends(residual[m])
-        index = local_solve(sh, ends_level(sh), some_residual, springs, (v0, v1), (kv0, kv1), factor)
+        index = local_solve(sh, ends_level(sh), some_residual, springs, columns, (v0, v1), (kv0, kv1), factor)
         solution = (v0, v1)[index]
         z = lax.broadcasted_iota(jnp.int32, (2 * EDGE, LANES), 0)
         z = jnp.where(z < EDGE, z, z + sh.z - 2 * EDGE)
@@ -952,22 +952,21 @@
             (8 * -(-(2 * label_x + 2 * label_y + 4) // 8) + 8, label_z),
         ]
         + [(1, 6 * EDGE, LANES)] * 2
-        + [short_fields, (16, 4 * EDGE, LANES)]
+        + [short_fields, (7, 4 * EDGE, LANES)]
         + short_scratch,
     )
 
     def first_solve(residual_ref, stiffness_ref, values, nodes_ref, solution_ref, springs_ref, *rest):
-        stiff, stiff_rim, v0, v1, kv0, kv1, factor = rest
+        stiff, stiff_rim, v0, v1, kv0, kv1, factor, columns = rest
         clear_guards(sh, (stiff, stiff_rim, v0, v1, kv0, kv1))
         put(stiff, 0, stiffness_ref[0])
         put(stiff_rim, 0, stiffness_ref[1])
         springs_ref[6] = stiffness_ref[0]
         springs_ref[7] = stiffness_ref[1]
-        put_columns(sh, springs_ref)
         lane, _, _ = sh.lane_grid(1)
         for f, entry in enumerate(own_block(sh, lane, (stiff, stiff_rim))):
             springs_ref[f] = entry
-        index = local_solve(sh, level(sh), residual_ref, springs_ref, (v0, v1), (kv0, kv1), factor)
+        index = local_solve(sh, level(sh), residual_ref, springs_ref, columns, (v0, v1), (kv0, kv1), factor)
         for m in range(3):
             solution_ref[m] = inner((v0, v1)[index], m)
         added = coarse_cells(nodes_ref[...], coords(sh, own_level(sh)), values, node_count)
@@ -977,7 +976,7 @@
     solved, springs = call(
         first_solve,
         "first_solve",
-        [fields, (16,) + plane],
+        [fields, (8,) + plane],
         [residual, stiffness, values, nodes],
         [(1, sh.tall, LANES)] * 2 + solve_scratch,
     )
@@ -990,7 +989,7 @@
         search_ref, image_ref, slots_out = take(3)
         z_refs = take(sh.z_links)
         v, rim, kv, k_rim, sums, shares, slots_ref, sem = take(8)
-        some_residual, some_springs, v0, v1, kv0, kv1, factor = take(7)
+        some_residual, some_springs, v0, v1, kv0, kv1, factor, some_columns, columns = take(9)
         clear_guards(sh, (v0, v1, kv0, kv1))
         clear_guards(sh, (v, rim, kv, k_rim))
         merge_all(sh, DEEP, Taker(merging), v, rim, EDGE)
@@ -1005,7 +1004,8 @@
             value = pick(in_rim, inner(rim, m))
             put(rim, m, value)
             put(k_rim, m, springs_ref[7] * value)
-        image = image_of(sh, lane, v, kv, (rim, k_rim), springs_ref)
+        put_columns(sh, springs_ref, columns)
+        image = image_of(sh, lane, v, kv, (rim, k_rim), springs_ref, columns)
         keep = in_grid & extended_mask(sh, level(sh))
         for m in range(3):
             image_ref[m] = pick(keep, image[m])
@@ -1019,9 +1019,9 @@
         copy.start()
         for m in range(3):
             some_residual[m] = ends(image_ref[m])
-        for f in range(16):
+        for f in range(7):
             some_springs[f] = ends(springs_ref[f])
-        index = local_solve(sh, ends_level(sh), some_residual, some_springs, (v0, v1), (kv0, kv1), factor)
+        index = local_solve(sh, ends_level(sh), some_residual, some_springs, some_columns, (v0, v1), (kv0, kv1), factor)
         pack_z(sh, NEAR, end_rows((v0, v1)[index]), z_refs)
         copy.wait()
 
@@ -1034,15 +1034,16 @@
         [tall] * 4
         + [(LANES, LANES), (8 * -(-share_rows // 8) + 8, LANES)]
         + [(8 * -(-all_slots[0] // 8) + 8, LANES), pltpu.SemaphoreType.DMA]
-        + [short_fields, (16, 4 * EDGE, LANES)]
-        + short_scratch,
+        + [short_fields, (7, 4 * EDGE, LANES)]
+        + short_scratch
+        + [(8,) + plane],
         remote_outs=(2,),
     )
     shares = to_all(shares.reshape(sh.devices, 1, share_rows * LANES)).reshape(shares.shape)
 
-    def second_solve(image_ref, springs_ref, local_ref, v0, v1, kv0, kv1, factor):
+    def second_solve(image_ref, springs_ref, local_ref, v0, v1, kv0, kv1, factor, columns):
         clear_guards(sh, (v0, v1, kv0, kv1))
-        index = local_solve(sh, level(sh), image_ref, springs_ref, (v0, v1), (kv0, kv1), factor)
+        index = local_solve(sh, level(sh), image_ref, springs_ref, columns, (v0, v1), (kv0, kv1), factor)
         for m in range(3):
             local_ref[m] = inner((v0, v1)[index], m)
 
@@ -1081,8 +1082,9 @@
         merging = take(1 + sh.z_links + sh.y_links + sh.x_links * (1 + sh.y_links))
         nodes_ref, springs_ref, first_ref, coarse_ref, early_ref = take(5)
         second_ref, image_ref, slots_ref = take(3)
-        v, kv, sums = take(3)
+        v, kv, sums, columns = take(4)
         clear_guards(sh, (v, kv))
+        put_columns(sh, springs_ref, columns)
         merge_all(sh, NEAR, Taker(merging), v, None, EDGE)
         lane, _, _ = sh.lane_grid(1)
         in_grid, _ = grid_masks(sh)
@@ -1091,7 +1093,7 @@
             put(v, m, value)
             second_ref[m] = value
             put(kv, m, springs_ref[6] * value)
-        image = image_of(sh, lane, v, kv, None, springs_ref)
+        image = image_of(sh, lane, v, kv, None, springs_ref, columns)
         for m in range(3):
             image_ref[m] = image[m]
         valid = nodes_ref[...] >= 0.0
@@ -1107,7 +1109,7 @@
         "second_image",
         [fields, fields, slots],
         [solved, *from_z, *from_y, *from_x, nodes, springs, image, coarse_field, sums],
-        [tall] * 2 + [(LANES, LANES)],
+        [tall] * 2 + [(LANES, LANES), (8,) + plane],
     )
     totals = to_all(sums)
 

time: 69.1 us -> 67.1 us (0.971)
  waiting for transfers between devices: 10.2 us -> 14.1 us
  local copies, waits for them, and re-layouts: 3.31 us -> 0.04 us
  starting transfers between devices: 34.4 us -> 31.4 us
    ppermute x17, starting transfers between devices: 20.9 us -> 16.1 us  [send(): return lax.ppermute(value, AXES, permutation(sh.sizes, moves))]
    unnamed x10 -> x14, local copies, waits for them, and re-layouts: 3.31 us -> 0.04 us
    all_to_all x3, waiting for transfers between devices: 5.87 us -> 7.9 us  [to_all(): return lax.all_to_all(slots, AXES, 0, 0, tiled=True)]
    all_to_all x3, starting transfers between devices: 13.5 us -> 15.3 us  [to_all(): return lax.all_to_all(slots, AXES, 0, 0, tiled=True)]
    ppermute x17, waiting for transfers between devices: 4.35 us -> 6.16 us  [send(): return lax.ppermute(value, AXES, permutation(sh.sizes, moves))]
  transfers between devices with their start and end apart: 20 -> 20, of which waited for: 5 -> 5; matrix products, arithmetic and copies ran while one was open for 0% -> 0% of each run, Pallas kernels for 13% -> 14%
where the time goes in v10:
time: 67.1 us; the launch traced here: 66.8 us
  starting transfers between devices  31.4 us (47%)
  Pallas kernels  20.4 us (30%)
  waiting for transfers between devices  14.1 us (21%)
  between operations  0.86 us (1%)
    pallas_call x12, Pallas kernels, call(): pl.pallas_call(kernel, out_shape=[jax.ShapeDtypeStruct(shape, f32) for sh...  20.4 us
    ppermute x17, starting transfers between devices, send(): return lax.ppermute(value, AXES, permutation(sh.sizes, moves))  16.1 us
    all_to_all x3, starting transfers between devices, to_all(): return lax.all_to_all(slots, AXES, 0, 0, tiled=True)  15.3 us
    all_to_all x3, waiting for transfers between devices, to_all(): return lax.all_to_all(slots, AXES, 0, 0, tiled=True)  7.9 us
    ppermute x17, waiting for transfers between devices, send(): return lax.ppermute(value, AXES, permutation(sh.sizes, moves))  6.16 us
  transfers between devices with their start and end apart: 20, of which 5 were waited for; matrix products, arithmetic and copies ran while one was open for 0% of the time, Pallas kernels for 14%

profile of v10, /device:TPU:0, one launch (start us, length us, event | category | flops | bytes accessed | tf_op | source)
XLA Modules:
  0.0 66.8 jit_solution(15241010755726588462)
XLA Ops:
  0.6 3.0 %begin.1 = (f32[48,64]{1,0:T(8,128)}, f32[256,128]{1,0:T(8,128)}, f32[40,128]{1,0:T(8,128)}, f32[40,128]{1,0:T(8,128)}, f32[40,128]{1,0:T(8,128)}) custom-call(f32[3,64,128]{2,1,0:T(8,128)} %bitcast.12, s32[4,4,64]{2,1,0:T(4,128)} %labels_in.1, f32[8]{0:T(128)} %moduli_in.1, s32[64,128]{1,0:T(8,128)} %bitcast.17), custom_call_target="tpu_custom_call" | custom-call | tf_op jit(solution)/shard_map/begin/pallas_call | solution.py:671
  3.7 0.0 copy-start.4
  3.7 0.0 copy-start
  3.7 0.0 copy-start.2
  3.7 0.0 copy-start.3
  3.7 7.3 %all-to-all-start = ((f32[32,8,128]{2,1,0:T(8,128)}), f32[32,8,128]{2,1,0:T(8,128)S(1)}, u32[]{:S(2)}, u32[]{:S(2)}) async-start(f32[32,8,128]{2,1,0:T(8,128)} %bitcast.20), calls=%async_computation | async-start | bytes 262144 | tf_op jit(solution)/shard_map/all_to_all | solution.py:720
  11.0 1.8 %collective-permute-start = (f32[40,128]{1,0:T(8,128)S(1)}, f32[40,128]{1,0:T(8,128)S(1)}, u32[]{:S(2)}, u32[]{:S(2)}) collective-permute-start(f32[40,128]{1,0:T(8,128)S(1)} %copy-done.6), channel_id=1, source_target_pairs={{0,4},{1,5},{2,6},{3,7},{4,0},{5,1},{6,2},{7,3},{8,12},{9,13},{10,... | collective-permute-start | bytes 61448 | tf_op jit(solution)/shard_map/ppermute | solution.py:706
  12.9 1.5 %collective-permute-start.2 = (f32[40,128]{1,0:T(8,128)S(1)}, f32[40,128]{1,0:T(8,128)S(1)}, u32[]{:S(2)}, u32[]{:S(2)}) collective-permute-start(f32[40,128]{1,0:T(8,128)S(1)} %copy-done.4), channel_id=1, source_target_pairs={{0,16},{1,17},{2,18},{3,19},{4,20},{5,21},{6,22},{7,23},{8,24},{9,... | collective-permute-start | bytes 61448 | tf_op jit(solution)/shard_map/ppermute | solution.py:706
  14.4 0.7 %spread.1 = (f32[4,144,128]{2,1,0:T(8,128)S(1)}, f32[128,128]{1,0:T(8,128)S(1)}, f32[36,1152]{1,0:T(8,128)S(1)}) custom-call(f32[3,64,128]{2,1,0:T(8,128)S(1)} %bitcast.13, s32[64,128]{1,0:T(8,128)S(1)} %bitcast.18, f32[48,64]{1,0:T(8,128)S(1)} %copy-done.3, f32[36,1152]{1,0:T(8,128)S(1)} %copy-done.1), custom_call_target="tpu_custom_call" | custom-call | tf_op jit(solution)/shard_map/spread/pallas_call | solution.py:671
  15.1 0.0 collective-permute-done.refs_1_
  15.1 1.8 %collective-permute-done.2.refs_3_ = f32[40,128]{1,0:T(8,128)S(1)} collective-permute-done((f32[40,128]{1,0:T(8,128)S(1)}, f32[40,128]{1,0:T(8,128)S(1)}, u32[]{:S(2)}, u32[]{:S(2)}) %collective-permute-start.2) | collective-permute-done | bytes 20512 | tf_op jit(solution)/shard_map/ppermute | solution.py:706
  16.9 2.4 %all-to-all-done = f32[32,8,128]{2,1,0:T(8,128)S(1)} async-done(((f32[32,8,128]{2,1,0:T(8,128)}), f32[32,8,128]{2,1,0:T(8,128)S(1)}, u32[]{:S(2)}, u32[]{:S(2)}) %all-to-all-start) | async-done | bytes 131104 | tf_op jit(solution)/shard_map/all_to_all | solution.py:720
  19.3 1.6 %first_ends.1 = (f32[3,144,128]{2,1,0:T(8,128)S(1)}, f32[144,128]{1,0:T(8,128)S(1)}, f32[2,144,128]{2,1,0:T(8,128)S(1)}, f32[48,128]{1,0:T(8,128)S(1)}, f32[24,128]{1,0:T(8,128)S(1)}, /*index=5*/f32[24,128]{1,0:T(8,128)S(1)}) custom-call(f32[4,144,128]{2,1,0:T(8,128)S(1)} %get-tuple-element.41.refs_0_.start_ref, f32[40,128]{1,0:T(8,128)S(1)} %collective-permute-done.refs_1_, ...), custom_call_target="tpu_custom_call" | custom-call | tf_op jit(solution)/shard_map/first_ends/pallas_call | solution.py:671
  20.9 0.5 collective-permute-start.3
  21.4 0.3 collective-permute-start.4
  21.7 3.3 %first_solve.1 = (f32[3,144,128]{2,1,0:T(8,128)S(1)}, f32[8,144,128]{2,1,0:T(8,128)S(1)}) custom-call(f32[3,144,128]{2,1,0:T(8,128)S(1)} %get-tuple-element.48.residual_ref, f32[2,144,128]{2,1,0:T(8,128)S(1)} %get-tuple-element.49.stiffness_ref, f32[48,128]{1,0:T(8,128)S(1)} %get-tuple-element.50.values, ...), custom_call_target="tpu_custom_call" | custom-call | tf_op jit(solution)/shard_map/first_solve/pallas_call | solution.py:671
  25.1 0.0 collective-permute-done.3.refs_1_
  25.1 0.3 deep.1
  25.5 1.3 %collective-permute-start.5 = (f32[144,128]{1,0:T(8,128)S(1)}, f32[144,128]{1,0:T(8,128)S(1)}, u32[]{:S(2)}, u32[]{:S(2)}) collective-permute-start(f32[144,128]{1,0:T(8,128)S(1)} %get-tuple-element.54), channel_id=1, source_target_pairs={{0,4},{1,5},{2,6},{3,7},{4,0},{5,1},{6,2},{7,3},{8,12},{9,13},{10,... | collective-permute-start | bytes 221192 | tf_op jit(solution)/shard_map/ppermute | solution.py:706
  26.7 0.0 collective-permute-start.6
  26.7 1.5 %collective-permute-start.7 = (f32[144,128]{1,0:T(8,128)S(1)}, f32[144,128]{1,0:T(8,128)S(1)}, u32[]{:S(2)}, u32[]{:S(2)}) collective-permute-start(f32[144,128]{1,0:T(8,128)S(1)} %get-tuple-element.56), channel_id=1, source_target_pairs={{0,16},{1,17},{2,18},{3,19},{4,20},{5,21},{6,22},{7,23},{8,24},{9,... | collective-permute-start | bytes 221192 | tf_op jit(solution)/shard_map/ppermute | solution.py:706
  28.2 1.4 %collective-permute-start.8 = (f32[40,128]{1,0:T(8,128)S(1)}, f32[40,128]{1,0:T(8,128)S(1)}, u32[]{:S(2)}, u32[]{:S(2)}) collective-permute-start(f32[40,128]{1,0:T(8,128)S(1)} %get-tuple-element.57), channel_id=1, source_target_pairs={{0,20},{1,21},{2,22},{3,23},{4,16},{5,17},{6,18},{7,19},{8,28},{9,... | collective-permute-start | bytes 61448 | tf_op jit(solution)/shard_map/ppermute | solution.py:706
  29.6 0.0 collective-permute-start.9
  29.6 3.3 %collective-permute-done.8.refs_6_ = f32[40,128]{1,0:T(8,128)S(1)} collective-permute-done((f32[40,128]{1,0:T(8,128)S(1)}, f32[40,128]{1,0:T(8,128)S(1)}, u32[]{:S(2)}, u32[]{:S(2)}) %collective-permute-start.8) | collective-permute-done | bytes 20512 | tf_op jit(solution)/shard_map/ppermute | solution.py:706
  32.9 0.0 collective-permute-done.9.refs_7_
  32.9 0.0 collective-permute-done.5.refs_3_
  32.9 0.0 collective-permute-done.6.refs_4_
  32.9 3.3 %first_image.1 = (f32[3,144,128]{2,1,0:T(8,128)S(1)}, f32[3,144,128]{2,1,0:T(8,128)S(1)}, f32[288,128]{1,0:T(8,128)}, f32[24,128]{1,0:T(8,128)S(1)}, f32[24,128]{1,0:T(8,128)S(1)}) custom-call(f32[3,144,128]{2,1,0:T(8,128)S(1)} %get-tuple-element.51.refs_0_, f32[24,128]{1,0:T(8,128)S(1)} %collective-permute-done.3.refs_1_, ...), custom_call_target="tpu_custom_call" | custom-call | tf_op jit(solution)/shard_map/first_image/pallas_call | solution.py:671
  36.3 3.8 %all-to-all-start.1 = ((f32[32,1,1152]{2,1,0:T(1,128)}), f32[32,1,1152]{2,1,0:T(1,128)S(1)}, u32[]{:S(2)}, u32[]{:S(2)}) async-start(f32[32,1,1152]{2,1,0:T(1,128)} %bitcast.4), calls=%async_computation.1 | async-start | bytes 294912 | tf_op jit(solution)/shard_map/all_to_all | solution.py:720
  40.1 0.1 collective-permute-start.10
  40.2 1.6 %collective-permute-start.11 = (f32[24,128]{1,0:T(8,128)S(1)}, f32[24,128]{1,0:T(8,128)S(1)}, u32[]{:S(2)}, u32[]{:S(2)}) collective-permute-start(f32[24,128]{1,0:T(8,128)S(1)} %get-tuple-element.62), channel_id=1, source_target_pairs={{0,3},{1,2},{2,1},{3,0},{4,7},{5,6},{6,5},{7,4},{8,11},{9,10},{10,... | collective-permute-start | bytes 36872 | tf_op jit(solution)/shard_map/ppermute | solution.py:706
  41.9 2.7 %second_solve.1.refs_0_ = f32[3,144,128]{2,1,0:T(8,128)S(1)} custom-call(f32[3,144,128]{2,1,0:T(8,128)S(1)} %get-tuple-element.60.image_ref.first_ref.refs_10_, f32[8,144,128]{2,1,0:T(8,128)S(1)} %get-tuple-element.59.refs_9_.springs_ref), custom_call_target="tpu_custom_call" | custom-call | tf_op jit(solution)/shard_map/second_solve/pallas_call | solution.py:671
  44.6 0.0 collective-permute-done.11.refs_2_
  44.6 0.4 near.1
  45.0 1.5 %collective-permute-start.14 = (f32[144,128]{1,0:T(8,128)S(1)}, f32[144,128]{1,0:T(8,128)S(1)}, u32[]{:S(2)}, u32[]{:S(2)}) collective-permute-start(f32[144,128]{1,0:T(8,128)S(1)} %get-tuple-element.65), channel_id=1, source_target_pairs={{0,16},{1,17},{2,18},{3,19},{4,20},{5,21},{6,22},{7,23},{8,24},{9,... | collective-permute-start | bytes 221192 | tf_op jit(solution)/shard_map/ppermute | solution.py:706
  46.5 1.5 %collective-permute-start.12 = (f32[72,128]{1,0:T(8,128)S(1)}, f32[72,128]{1,0:T(8,128)S(1)}, u32[]{:S(2)}, u32[]{:S(2)}) collective-permute-start(f32[72,128]{1,0:T(8,128)S(1)} %get-tuple-element.63), channel_id=1, source_target_pairs={{0,4},{1,5},{2,6},{3,7},{4,0},{5,1},{6,2},{7,3},{8,12},{9,13},{10,... | collective-permute-start | bytes 110600 | tf_op jit(solution)/shard_map/ppermute | solution.py:706
  48.0 3.0 %collective-permute-start.15 = (f32[24,128]{1,0:T(8,128)S(1)}, f32[24,128]{1,0:T(8,128)S(1)}, u32[]{:S(2)}, u32[]{:S(2)}) collective-permute-start(f32[24,128]{1,0:T(8,128)S(1)} %get-tuple-element.66), channel_id=1, source_target_pairs={{0,20},{1,21},{2,22},{3,23},{4,16},{5,17},{6,18},{7,19},{8,28},{9,... | collective-permute-start | bytes 36872 | tf_op jit(solution)/shard_map/ppermute | solution.py:706
  51.0 0.0 collective-permute-start.16
  51.0 0.0 all-to-all-done.1
  51.0 0.6 between.1
  51.6 1.1 %collective-permute-done.15.refs_6_ = f32[24,128]{1,0:T(8,128)S(1)} collective-permute-done((f32[24,128]{1,0:T(8,128)S(1)}, f32[24,128]{1,0:T(8,128)S(1)}, u32[]{:S(2)}, u32[]{:S(2)}) %collective-permute-start.15) | collective-permute-done | bytes 12320 | tf_op jit(solution)/shard_map/ppermute | solution.py:706
  52.6 0.0 collective-permute-done.16.refs_7_
  52.6 0.0 collective-permute-done.12.refs_3_
  52.7 2.0 %second_image.1 = (f32[3,144,128]{2,1,0:T(8,128)S(1)}, f32[3,144,128]{2,1,0:T(8,128)S(1)}, f32[32,128]{1,0:T(8,128)}) custom-call(f32[3,144,128]{2,1,0:T(8,128)S(1)} %second_solve.1.refs_0_, f32[24,128]{1,0:T(8,128)S(1)} %collective-permute-done.10.refs_1_, f32[24,128]{1,0:T(8,128)S(1)} %collective-permute-done.11.refs_2_, ...), custom_call_target="tpu_custom_call" | custom-call | tf_op jit(solution)/shard_map/second_image/pallas_call | solution.py:671
  54.7 4.2 %all-to-all-start.2 = ((f32[32,1,128]{2,1,0:T(1,128)}), f32[32,1,128]{2,1,0:T(1,128)S(1)}, u32[]{:S(2)}, u32[]{:S(2)}) async-start(f32[32,1,128]{2,1,0:T(1,128)} %bitcast.7), calls=%async_computation.2 | async-start | bytes 32768 | tf_op jit(solution)/shard_map/all_to_all | solution.py:720
  58.9 1.6 %turn.1.turned_ref = f32[4,3,64,128]{3,2,1,0:T(8,128)S(1)} custom-call(f32[3,144,128]{2,1,0:T(8,128)S(1)} %get-tuple-element.70.search_ref, f32[3,144,128]{2,1,0:T(8,128)S(1)} %get-tuple-element.60.image_ref.first_ref.refs_10_, f32[3,144,128]{2,1,0:T(8,128)S(1)} %get-tuple-element.74.second_ref, f32[3,144,128]{2,1,0:T(8,128)S(1)} %get-tuple-element.75.image_ref), custom_call_target="tpu_custom_call" | custom-call | tf_op jit(solution)/shard_map/turn/pallas_call | solution.py:671
  60.5 5.5 %all-to-all-done.2 = f32[32,1,128]{2,1,0:T(1,128)S(1)} async-done(((f32[32,1,128]{2,1,0:T(1,128)}), f32[32,1,128]{2,1,0:T(1,128)S(1)}, u32[]{:S(2)}, u32[]{:S(2)}) %all-to-all-start.2) | async-done | bytes 16416 | tf_op jit(solution)/shard_map/all_to_all | solution.py:720
  66.0 0.8 %finish.1 = (f32[3,64,128]{2,1,0:T(8,128)}, f32[3,64,128]{2,1,0:T(8,128)}) custom-call(f32[32,128]{1,0:T(8,128)S(1)} %bitcast.19, f32[3,64,128]{2,1,0:T(8,128)S(1)} %bitcast.14, f32[4,3,64,128]{3,2,1,0:T(8,128)S(1)} %turn.1.turned_ref), custom_call_target="tpu_custom_call" | custom-call | tf_op jit(solution)/shard_map/finish/pallas_call | solution.py:671
  (18 shorter events, 0.0 us)
Async XLA Ops:
  0.6 13.8 %copy-start.1 = (f32[36,1152]{1,0:T(8,128)S(1)}, f32[36,1152]{1,0:T(8,128)}, u32[]{:S(2)}) copy-start(f32[36,1152]{1,0:T(8,128)} %inverse_in.1) | copy-start | bytes 497668
  3.6 7.4 %copy-start.6 = (f32[40,128]{1,0:T(8,128)S(1)}, f32[40,128]{1,0:T(8,128)}, u32[]{:S(2)}) copy-start(f32[40,128]{1,0:T(8,128)} %get-tuple-element.42) | copy-start | bytes 61444
  3.7 9.2 %copy-start.5 = (f32[40,128]{1,0:T(8,128)S(1)}, f32[40,128]{1,0:T(8,128)}, u32[]{:S(2)}) copy-start(f32[40,128]{1,0:T(8,128)} %get-tuple-element.43) | copy-start | bytes 61444
  3.7 9.2 %copy-start.4 = (f32[40,128]{1,0:T(8,128)S(1)}, f32[40,128]{1,0:T(8,128)}, u32[]{:S(2)}) copy-start(f32[40,128]{1,0:T(8,128)} %get-tuple-element.44) | copy-start | bytes 61444
  3.7 10.7 %copy-start = (f32[3,8,8,128]{3,2,1,0:T(8,128)S(1)}, f32[3,8,8,128]{3,2,1,0:T(8,128)}, u32[]{:S(2)}) copy-start(f32[3,8,8,128]{3,2,1,0:T(8,128)} %param.5) | copy-start | bytes 294916
  3.7 10.7 %copy-start.2 = (s32[8,8,128]{2,1,0:T(8,128)S(1)}, s32[8,8,128]{2,1,0:T(8,128)}, u32[]{:S(2)}) copy-start(s32[8,8,128]{2,1,0:T(8,128)} %param.8) | copy-start | bytes 98308
  3.7 10.7 %copy-start.3 = (f32[48,64]{1,0:T(8,128)S(1)}, f32[48,64]{1,0:T(8,128)}, u32[]{:S(2)}) copy-start(f32[48,64]{1,0:T(8,128)} %get-tuple-element.40.stiff) | copy-start | bytes 36868
  3.7 15.6 %all-to-all-start = ((f32[32,8,128]{2,1,0:T(8,128)}), f32[32,8,128]{2,1,0:T(8,128)S(1)}, u32[]{:S(2)}, u32[]{:S(2)}) async-start(f32[32,8,128]{2,1,0:T(8,128)} %bitcast.20), calls=%async_computation | async-start | bytes 262144 | tf_op jit(solution)/shard_map/all_to_all | solution.py:720
  11.0 4.1 %collective-permute-start = (f32[40,128]{1,0:T(8,128)S(1)}, f32[40,128]{1,0:T(8,128)S(1)}, u32[]{:S(2)}, u32[]{:S(2)}) collective-permute-start(f32[40,128]{1,0:T(8,128)S(1)} %copy-done.6), channel_id=1, source_target_pairs={{0,4},{1,5},{2,6},{3,7},{4,0},{5,1},{6,2},{7,3},{8,12},{9,13},{10,... | collective-permute-start | bytes 61448 | tf_op jit(solution)/shard_map/ppermute | solution.py:706
  12.9 2.2 %collective-permute-start.1 = (f32[40,128]{1,0:T(8,128)S(1)}, f32[40,128]{1,0:T(8,128)S(1)}, u32[]{:S(2)}, u32[]{:S(2)}) collective-permute-start(f32[40,128]{1,0:T(8,128)S(1)} %copy-done.5), channel_id=1, source_target_pairs={{0,1},{1,0},{2,3},{3,2},{4,8},{5,9},{6,10},{7,11},{8,4},{9,5},{10,... | collective-permute-start | bytes 61448 | tf_op jit(solution)/shard_map/ppermute | solution.py:706
  12.9 4.0 %collective-permute-start.2 = (f32[40,128]{1,0:T(8,128)S(1)}, f32[40,128]{1,0:T(8,128)S(1)}, u32[]{:S(2)}, u32[]{:S(2)}) collective-permute-start(f32[40,128]{1,0:T(8,128)S(1)} %copy-done.4), channel_id=1, source_target_pairs={{0,16},{1,17},{2,18},{3,19},{4,20},{5,21},{6,22},{7,23},{8,24},{9,... | collective-permute-start | bytes 61448 | tf_op jit(solution)/shard_map/ppermute | solution.py:706
  20.9 4.2 %collective-permute-start.3 = (f32[24,128]{1,0:T(8,128)S(1)}, f32[24,128]{1,0:T(8,128)S(1)}, u32[]{:S(2)}, u32[]{:S(2)}) collective-permute-start(f32[24,128]{1,0:T(8,128)S(1)} %get-tuple-element.52), channel_id=1, source_target_pairs={{0,1},{1,0},{2,3},{3,2},{4,5},{5,4},{6,7},{7,6},{8,9},{9,8},{10,11... | collective-permute-start | bytes 36872 | tf_op jit(solution)/shard_map/ppermute | solution.py:706
  21.4 3.7 %collective-permute-start.4 = (f32[24,128]{1,0:T(8,128)S(1)}, f32[24,128]{1,0:T(8,128)S(1)}, u32[]{:S(2)}, u32[]{:S(2)}) collective-permute-start(f32[24,128]{1,0:T(8,128)S(1)} %get-tuple-element.53), channel_id=1, source_target_pairs={{0,3},{1,2},{2,1},{3,0},{4,7},{5,6},{6,5},{7,4},{8,11},{9,10},{10,... | collective-permute-start | bytes 36872 | tf_op jit(solution)/shard_map/ppermute | solution.py:706
  25.5 7.4 %collective-permute-start.5 = (f32[144,128]{1,0:T(8,128)S(1)}, f32[144,128]{1,0:T(8,128)S(1)}, u32[]{:S(2)}, u32[]{:S(2)}) collective-permute-start(f32[144,128]{1,0:T(8,128)S(1)} %get-tuple-element.54), channel_id=1, source_target_pairs={{0,4},{1,5},{2,6},{3,7},{4,0},{5,1},{6,2},{7,3},{8,12},{9,13},{10,... | collective-permute-start | bytes 221192 | tf_op jit(solution)/shard_map/ppermute | solution.py:706
  26.7 6.1 %collective-permute-start.6 = (f32[144,128]{1,0:T(8,128)S(1)}, f32[144,128]{1,0:T(8,128)S(1)}, u32[]{:S(2)}, u32[]{:S(2)}) collective-permute-start(f32[144,128]{1,0:T(8,128)S(1)} %get-tuple-element.55), channel_id=1, source_target_pairs={{0,1},{1,0},{2,3},{3,2},{4,8},{5,9},{6,10},{7,11},{8,4},{9,5},{10,... | collective-permute-start | bytes 221192 | tf_op jit(solution)/shard_map/ppermute | solution.py:706
  26.7 6.2 %collective-permute-start.7 = (f32[144,128]{1,0:T(8,128)S(1)}, f32[144,128]{1,0:T(8,128)S(1)}, u32[]{:S(2)}, u32[]{:S(2)}) collective-permute-start(f32[144,128]{1,0:T(8,128)S(1)} %get-tuple-element.56), channel_id=1, source_target_pairs={{0,16},{1,17},{2,18},{3,19},{4,20},{5,21},{6,22},{7,23},{8,24},{9,... | collective-permute-start | bytes 221192 | tf_op jit(solution)/shard_map/ppermute | solution.py:706
  28.2 4.7 %collective-permute-start.8 = (f32[40,128]{1,0:T(8,128)S(1)}, f32[40,128]{1,0:T(8,128)S(1)}, u32[]{:S(2)}, u32[]{:S(2)}) collective-permute-start(f32[40,128]{1,0:T(8,128)S(1)} %get-tuple-element.57), channel_id=1, source_target_pairs={{0,20},{1,21},{2,22},{3,23},{4,16},{5,17},{6,18},{7,19},{8,28},{9,... | collective-permute-start | bytes 61448 | tf_op jit(solution)/shard_map/ppermute | solution.py:706
  29.6 3.3 %collective-permute-start.9 = (f32[40,128]{1,0:T(8,128)S(1)}, f32[40,128]{1,0:T(8,128)S(1)}, u32[]{:S(2)}, u32[]{:S(2)}) collective-permute-start(f32[40,128]{1,0:T(8,128)S(1)} %get-tuple-element.58), channel_id=1, source_target_pairs={{0,1},{1,0},{2,3},{3,2},{4,24},{5,25},{6,26},{7,27},{8,20},{9,21},... | collective-permute-start | bytes 61448 | tf_op jit(solution)/shard_map/ppermute | solution.py:706
  36.3 14.7 %all-to-all-start.1 = ((f32[32,1,1152]{2,1,0:T(1,128)}), f32[32,1,1152]{2,1,0:T(1,128)S(1)}, u32[]{:S(2)}, u32[]{:S(2)}) async-start(f32[32,1,1152]{2,1,0:T(1,128)} %bitcast.4), calls=%async_computation.1 | async-start | bytes 294912 | tf_op jit(solution)/shard_map/all_to_all | solution.py:720
  40.1 4.5 %collective-permute-start.10 = (f32[24,128]{1,0:T(8,128)S(1)}, f32[24,128]{1,0:T(8,128)S(1)}, u32[]{:S(2)}, u32[]{:S(2)}) collective-permute-start(f32[24,128]{1,0:T(8,128)S(1)} %get-tuple-element.61), channel_id=1, source_target_pairs={{0,1},{1,0},{2,3},{3,2},{4,5},{5,4},{6,7},{7,6},{8,9},{9,8},{10,11... | collective-permute-start | bytes 36872 | tf_op jit(solution)/shard_map/ppermute | solution.py:706
  40.2 4.3 %collective-permute-start.11 = (f32[24,128]{1,0:T(8,128)S(1)}, f32[24,128]{1,0:T(8,128)S(1)}, u32[]{:S(2)}, u32[]{:S(2)}) collective-permute-start(f32[24,128]{1,0:T(8,128)S(1)} %get-tuple-element.62), channel_id=1, source_target_pairs={{0,3},{1,2},{2,1},{3,0},{4,7},{5,6},{6,5},{7,4},{8,11},{9,10},{10,... | collective-permute-start | bytes 36872 | tf_op jit(solution)/shard_map/ppermute | solution.py:706
  45.0 7.7 %collective-permute-start.14 = (f32[144,128]{1,0:T(8,128)S(1)}, f32[144,128]{1,0:T(8,128)S(1)}, u32[]{:S(2)}, u32[]{:S(2)}) collective-permute-start(f32[144,128]{1,0:T(8,128)S(1)} %get-tuple-element.65), channel_id=1, source_target_pairs={{0,16},{1,17},{2,18},{3,19},{4,20},{5,21},{6,22},{7,23},{8,24},{9,... | collective-permute-start | bytes 221192 | tf_op jit(solution)/shard_map/ppermute | solution.py:706
  46.5 6.1 %collective-permute-start.12 = (f32[72,128]{1,0:T(8,128)S(1)}, f32[72,128]{1,0:T(8,128)S(1)}, u32[]{:S(2)}, u32[]{:S(2)}) collective-permute-start(f32[72,128]{1,0:T(8,128)S(1)} %get-tuple-element.63), channel_id=1, source_target_pairs={{0,4},{1,5},{2,6},{3,7},{4,0},{5,1},{6,2},{7,3},{8,12},{9,13},{10,... | collective-permute-start | bytes 110600 | tf_op jit(solution)/shard_map/ppermute | solution.py:706
  48.0 4.7 %collective-permute-start.13 = (f32[72,128]{1,0:T(8,128)S(1)}, f32[72,128]{1,0:T(8,128)S(1)}, u32[]{:S(2)}, u32[]{:S(2)}) collective-permute-start(f32[72,128]{1,0:T(8,128)S(1)} %get-tuple-element.64), channel_id=1, source_target_pairs={{0,1},{1,0},{2,3},{3,2},{4,8},{5,9},{6,10},{7,11},{8,4},{9,5},{10,... | collective-permute-start | bytes 110600 | tf_op jit(solution)/shard_map/ppermute | solution.py:706
  48.0 4.7 %collective-permute-start.15 = (f32[24,128]{1,0:T(8,128)S(1)}, f32[24,128]{1,0:T(8,128)S(1)}, u32[]{:S(2)}, u32[]{:S(2)}) collective-permute-start(f32[24,128]{1,0:T(8,128)S(1)} %get-tuple-element.66), channel_id=1, source_target_pairs={{0,20},{1,21},{2,22},{3,23},{4,16},{5,17},{6,18},{7,19},{8,28},{9,... | collective-permute-start | bytes 36872 | tf_op jit(solution)/shard_map/ppermute | solution.py:706
  51.0 1.7 %collective-permute-start.16 = (f32[24,128]{1,0:T(8,128)S(1)}, f32[24,128]{1,0:T(8,128)S(1)}, u32[]{:S(2)}, u32[]{:S(2)}) collective-permute-start(f32[24,128]{1,0:T(8,128)S(1)} %get-tuple-element.67), channel_id=1, source_target_pairs={{0,1},{1,0},{2,3},{3,2},{4,24},{5,25},{6,26},{7,27},{8,20},{9,21},... | collective-permute-start | bytes 36872 | tf_op jit(solution)/shard_map/ppermute | solution.py:706
  54.7 11.3 %all-to-all-start.2 = ((f32[32,1,128]{2,1,0:T(1,128)}), f32[32,1,128]{2,1,0:T(1,128)S(1)}, u32[]{:S(2)}, u32[]{:S(2)}) async-start(f32[32,1,128]{2,1,0:T(1,128)} %bitcast.7), calls=%async_computation.2 | async-start | bytes 32768 | tf_op jit(solution)/shard_map/all_to_all | solution.py:720

commit v11 on v10

--- a/solution.py
+++ b/solution.py
@@ -14,9 +14,10 @@
 LANES = 128
 EDGE = 8
 
-ALONG1, ACROSS1 = 0.75, 0.5
-ALONG2, ACROSS2, MIXED2 = 0.3125, 0.25, 0.0625
-SAME3, MIXED3 = 7.0 / 36.0, 1.0 / 36.0
+SCALE = 36.0
+ALONG1, ACROSS1 = 27.0, 18.0
+ALONG2, ACROSS2, MIXED2 = 11.25, 9.0, 2.25
+SAME3 = 7.0
 TOTAL = 2 * ALONG1 + 4 * ACROSS1 + 8 * ALONG2 + 4 * ACROSS2 + 8 * SAME3
 
 
@@ -225,11 +226,6 @@
     return inner(ref, f), before + after, after - before
 
 
-def y_stage(value):
-    after, before = shift(value, -1), shift(value, 1)
-    return before + after, after - before
-
-
 COLUMNS = [(dx, dy) for dx in (-1, 0, 1) for dy in (-1, 0, 1) if dx or dy]
 
 
@@ -237,76 +233,61 @@
     a, a_sum, a_dif = z_stage(ref, 0)
     b, b_sum, b_dif = z_stage(ref, 1)
     c, c_sum, c_dif = z_stage(ref, 2)
-    parts = {(0, 0): (ACROSS1 * a_sum, ACROSS1 * b_sum, ALONG1 * c_sum)}
-    mixed_x, mixed_y = MIXED2 * b + MIXED3 * b_sum, MIXED2 * a + MIXED3 * a_sum
+    mixed_x, mixed_y = MIXED2 * b + b_sum, MIXED2 * a + a_sum
     x_c_dif = c_dif
     if sign is not None:
         mixed_x, mixed_y, x_c_dif, a_dif = sign * mixed_x, sign * mixed_y, sign * c_dif, sign * a_dif
     both_z = ACROSS1 * c + ALONG2 * c_sum
-    along, across = ALONG1 * a + ALONG2 * a_sum, ACROSS1 * b + ACROSS2 * b_sum
-    for dx in (-1, 1):
-        parts[dx, 0] = (along + dx * MIXED2 * x_c_dif, across, both_z + dx * MIXED2 * a_dif)
-    along, across = ALONG1 * b + ALONG2 * b_sum, ACROSS1 * a + ACROSS2 * a_sum
-    for dy in (-1, 1):
-        parts[0, dy] = (across, along + dy * MIXED2 * c_dif, both_z + dy * MIXED2 * b_dif)
+    along_x, across_x = ALONG1 * a + ALONG2 * a_sum, ACROSS1 * a + ACROSS2 * a_sum
+    along_y, across_y = ALONG1 * b + ALONG2 * b_sum, ACROSS1 * b + ACROSS2 * b_sum
+    tilt_a, tilt_b, tilt_c, tilt_x = MIXED2 * a_dif, MIXED2 * b_dif, MIXED2 * c_dif, MIXED2 * x_c_dif
     same_x, same_y = ALONG2 * a + SAME3 * a_sum, ALONG2 * b + SAME3 * b_sum
     same_z = ACROSS2 * c + SAME3 * c_sum
-    for dx in (-1, 1):
-        for dy in (-1, 1):
-            parts[dx, dy] = (
-                (same_x + dx * dy * mixed_x) + dx * MIXED3 * x_c_dif,
-                (same_y + dx * dy * mixed_y) + dy * MIXED3 * c_dif,
-                (same_z + dx * MIXED3 * a_dif) + dy * MIXED3 * b_dif,
-            )
-    return parts
-
-
-def put_columns(sh, springs_ref, columns):
+    plus_x, plus_y, plus_z = same_x + mixed_x, same_y + mixed_y, same_z + a_dif
+    minus_x, minus_y, minus_z = same_x - mixed_x, same_y - mixed_y, same_z - a_dif
+    return {
+        (0, 0): (ACROSS1 * a_sum, ACROSS1 * b_sum, ALONG1 * c_sum),
+        (1, 0): (along_x + tilt_x, across_y, both_z + tilt_a),
+        (-1, 0): (along_x - tilt_x, across_y, both_z - tilt_a),
+        (0, 1): (across_x, along_y + tilt_c, both_z + tilt_b),
+        (0, -1): (across_x, along_y - tilt_c, both_z - tilt_b),
+        (1, 1): (plus_x + x_c_dif, plus_y + c_dif, plus_z + b_dif),
+        (1, -1): (minus_x + x_c_dif, minus_y - c_dif, plus_z - b_dif),
+        (-1, 1): (minus_x - x_c_dif, minus_y + c_dif, minus_z + b_dif),
+        (-1, -1): (plus_x - x_c_dif, plus_y - c_dif, minus_z - b_dif),
+    }
+
+
+def put_columns(sh, k, rim, columns):
+    lane, _, _ = sh.lane_grid(1)
     for i, (dx, dy) in enumerate(COLUMNS):
-        columns[i] = shift(springs_ref[6], dx * sh.pitch + dy)
-
-
-def x_stage(sh, lane, own, plus, minus, rim_plus, rim_minus):
-    after, before = shift(plus, -sh.pitch), shift(minus, sh.pitch)
-    last = (sh.x + 1) * sh.pitch
-    if rim_plus is None:
-        return own + pick(lane < last, after) + pick(lane >= sh.pitch, before)
-    return own + jnp.where(lane < last, after, rim_plus) + jnp.where(lane >= sh.pitch, before, rim_minus)
-
-
-def spring_parts(ref):
-    k, k_sum, k_dif = z_stage(ref, 0)
-    pk, mk = y_stage(k)
-    pks, mks = y_stage(k_sum)
-    pkd, mkd = y_stage(k_dif)
-    zero = jnp.zeros_like(k)
-    xx = (ACROSS1 * (pk + k_sum) + ACROSS2 * pks, ALONG1 * k + ALONG2 * (pk + k_sum) + SAME3 * pks, zero)
-    yy = (
-        ALONG1 * pk + ACROSS1 * k_sum + ALONG2 * pks,
-        ACROSS1 * k + ALONG2 * pk + ACROSS2 * k_sum + SAME3 * pks,
-        zero,
-    )
-    zz = (
-        ALONG1 * k_sum + ACROSS1 * pk + ALONG2 * pks,
-        ACROSS1 * k + ACROSS2 * pk + ALONG2 * k_sum + SAME3 * pks,
-        zero,
-    )
-    xy = (zero, zero, MIXED2 * mk + MIXED3 * mks)
-    xz = (zero, zero, MIXED2 * k_dif + MIXED3 * pkd)
-    yz = (MIXED2 * mkd, MIXED3 * mkd, zero)
-    return xx, yy, zz, xy, xz, yz
-
-
-def own_block(sh, lane, springs):
-    main, rim = springs
-    k = inner(main, 0)
-    out = []
-    for index, ((own, even, odd), (_, rim_even, rim_odd)) in enumerate(
-        zip(spring_parts(main), spring_parts(rim))
-    ):
-        total = x_stage(sh, lane, own, even + odd, even - odd, rim_even + rim_odd, rim_even - rim_odd)
-        out.append(total + TOTAL * k if index < 3 else total)
-    return out
+        value = shift(k, dx * sh.pitch + dy)
+        if dx and rim is not None:
+            edge = lane < sh.pitch if dx > 0 else lane >= (sh.x + 1) * sh.pitch
+            value = jnp.where(edge, shift(rim, dy), value)
+        put(columns, i, value)
+
+
+def own_block(stiff, columns):
+    k, k_sum, _ = z_stage(stiff, 0)
+    at = {(-dx, -dy): z_stage(columns, i) for i, (dx, dy) in enumerate(COLUMNS)}
+    total = lambda j, *places: sum(at[place][j] for place in places)
+    in_x, in_y = ((1, 0), (-1, 0)), ((0, 1), (0, -1))
+    same, other = ((1, 1), (-1, -1)), ((1, -1), (-1, 1))
+    x, x_sum, y, y_sum = total(0, *in_x), total(1, *in_x), total(0, *in_y), total(1, *in_y)
+    same_0, same_1, other_0, other_1 = total(0, *same), total(1, *same), total(0, *other), total(1, *other)
+    corner, corner_sum = same_0 + other_0, SAME3 * (same_1 + other_1)
+    shared = ALONG2 * corner + corner_sum + ACROSS1 * k_sum + TOTAL * k
+    turn_x = at[1, 1][2] - at[-1, -1][2]
+    turn_y = at[1, -1][2] - at[-1, 1][2]
+    return (
+        ALONG1 * x + ALONG2 * x_sum + ACROSS1 * y + ACROSS2 * y_sum + shared,
+        ALONG1 * y + ALONG2 * y_sum + ACROSS1 * x + ACROSS2 * x_sum + shared,
+        ACROSS1 * (x + y) + ALONG2 * (x_sum + y_sum) + ACROSS2 * corner + corner_sum + ALONG1 * k_sum + TOTAL * k,
+        MIXED2 * (same_0 - other_0) + (same_1 - other_1),
+        MIXED2 * (at[1, 0][2] - at[-1, 0][2]) + (turn_x + turn_y),
+        MIXED2 * (at[0, 1][2] - at[0, -1][2]) + (turn_x - turn_y),
+    )
 
 
 def apply_block(d, v):
@@ -328,7 +309,7 @@
             side = None
             for i, column in enumerate(COLUMNS):
                 if column[0] == dx:
-                    moved = columns[i] * plain[column][m] + scaled[column][m]
+                    moved = inner(columns, i) * plain[column][m] + scaled[column][m]
                     moved = shift(moved, -(dx * sh.pitch + column[1]))
                     side = moved if side is None else side + moved
             if dx:
@@ -387,7 +368,6 @@
 def local_solve(sh, z, residual_ref, springs_ref, columns, v, kv, factor):
     lane, _, _ = sh.lane_grid(1)
     mask = extended_mask(sh, z)
-    put_columns(sh, springs_ref, columns)
     for m in range(3):
         factor[m] = pick(mask, relax / jnp.where(mask, springs_ref[m], 1.0))
         value = residual_ref[m] * factor[m]
@@ -819,7 +799,7 @@
             moduli = jnp.zeros(labels.shape, f32)
             for phase in range(sh.phases):
                 moduli = jnp.where(labels == phase, moduli_ref[phase], moduli)
-            stiff[i * label_y : (i + 1) * label_y, :] = moduli
+            stiff[i * label_y : (i + 1) * label_y, :] = moduli * (1.0 / SCALE)
         natural_ref[3, 0 : sh.cells, :] = nodes_ref[...].astype(f32) + 1.0
         cells = [natural_ref[m, 0 : sh.cells, :] for m in range(4)]
         coarse_sums(nodes_ref[...], cells[:3], cell_coords(sh), node_count, sums)
@@ -892,8 +872,9 @@
 
     short = (3, 6 * EDGE, LANES)
     short_fields = (3, 4 * EDGE, LANES)
-    solve_scratch = [tall] * 4 + [fields, (8,) + plane]
-    short_scratch = [short] * 4 + [short_fields, (8, 4 * EDGE, LANES)]
+    tall_columns = (len(COLUMNS), sh.tall, LANES)
+    solve_scratch = [tall] * 4 + [fields, tall_columns]
+    short_scratch = [short] * 4 + [short_fields, (len(COLUMNS), 6 * EDGE, LANES)]
 
     def end_rows(ref):
         def rows(f, start, count):
@@ -909,9 +890,9 @@
         nodes_ref, lines_ref, inverse_ref = take(3)
         residual, wide_nodes, stiffness_ref, values = take(4)
         z_refs = take(sh.z_links)
-        stiff, stiff_rim, cells, labels, short_stiff, short_rim, some_residual, springs = take(8)
+        stiff, stiff_rim, cells, labels, short_stiff, some_residual, springs = take(7)
         v0, v1, kv0, kv1, factor, columns = take(6)
-        clear_guards(sh, (stiff, stiff_rim, short_stiff, short_rim, v0, v1, kv0, kv1))
+        clear_guards(sh, (stiff, stiff_rim, short_stiff, v0, v1, kv0, kv1, columns))
         residual[...] = field_ref[0:3]
         put(stiff, 0, field_ref[3])
         put(stiff_rim, 0, jnp.zeros(plane, f32))
@@ -925,8 +906,8 @@
         coarse_solution(lines_ref[pl.ds(4, sh.devices, stride=8), :], inverse_ref, values)
         lane, _, _ = sh.lane_grid(1)
         put(short_stiff, 0, ends(stiffness_ref[0]))
-        put(short_rim, 0, ends(stiffness_ref[1]))
-        for f, entry in enumerate(own_block(sh, lane, (short_stiff, short_rim))):
+        put_columns(sh, ends(stiffness_ref[0]), ends(stiffness_ref[1]), columns)
+        for f, entry in enumerate(own_block(short_stiff, columns)):
             springs[f] = entry
         springs[6] = inner(short_stiff, 0)
         for m in range(3):
@@ -951,20 +932,20 @@
             (4, 8 * -(-(2 * sh.x + 2 * sh.y + 4) // 8) + 8, LANES),
             (8 * -(-(2 * label_x + 2 * label_y + 4) // 8) + 8, label_z),
         ]
-        + [(1, 6 * EDGE, LANES)] * 2
+        + [(1, 6 * EDGE, LANES)]
         + [short_fields, (7, 4 * EDGE, LANES)]
         + short_scratch,
     )
 
     def first_solve(residual_ref, stiffness_ref, values, nodes_ref, solution_ref, springs_ref, *rest):
-        stiff, stiff_rim, v0, v1, kv0, kv1, factor, columns = rest
-        clear_guards(sh, (stiff, stiff_rim, v0, v1, kv0, kv1))
+        stiff, v0, v1, kv0, kv1, factor, columns = rest
+        clear_guards(sh, (stiff, v0, v1, kv0, kv1, columns))
         put(stiff, 0, stiffness_ref[0])
-        put(stiff_rim, 0, stiffness_ref[1])
+        put_columns(sh, stiffness_ref[0], stiffness_ref[1], columns)
         springs_ref[6] = stiffness_ref[0]
         springs_ref[7] = stiffness_ref[1]
         lane, _, _ = sh.lane_grid(1)
-        for f, entry in enumerate(own_block(sh, lane, (stiff, stiff_rim))):
+        for f, entry in enumerate(own_block(stiff, columns)):
             springs_ref[f] = entry
         index = local_solve(sh, level(sh), residual_ref, springs_ref, columns, (v0, v1), (kv0, kv1), factor)
         for m in range(3):
@@ -978,7 +959,7 @@
         "first_solve",
         [fields, (8,) + plane],
         [residual, stiffness, values, nodes],
-        [(1, sh.tall, LANES)] * 2 + solve_scratch,
+        [(1, sh.tall, LANES)] + solve_scratch,
     )
     from_z, from_y, from_x = exchange(sh, DEEP, "deep", solved, z_messages)
 
@@ -1004,7 +985,7 @@
             value = pick(in_rim, inner(rim, m))
             put(rim, m, value)
             put(k_rim, m, springs_ref[7] * value)
-        put_columns(sh, springs_ref, columns)
+        put_columns(sh, springs_ref[6], None, columns)
         image = image_of(sh, lane, v, kv, (rim, k_rim), springs_ref, columns)
         keep = in_grid & extended_mask(sh, level(sh))
         for m in range(3):
@@ -1021,6 +1002,7 @@
             some_residual[m] = ends(image_ref[m])
         for f in range(7):
             some_springs[f] = ends(springs_ref[f])
+        put_columns(sh, some_springs[6], None, some_columns)
         index = local_solve(sh, ends_level(sh), some_residual, some_springs, some_columns, (v0, v1), (kv0, kv1), factor)
         pack_z(sh, NEAR, end_rows((v0, v1)[index]), z_refs)
         copy.wait()
@@ -1036,13 +1018,14 @@
         + [(8 * -(-all_slots[0] // 8) + 8, LANES), pltpu.SemaphoreType.DMA]
         + [short_fields, (7, 4 * EDGE, LANES)]
         + short_scratch
-        + [(8,) + plane],
+        + [tall_columns],
         remote_outs=(2,),
     )
     shares = to_all(shares.reshape(sh.devices, 1, share_rows * LANES)).reshape(shares.shape)
 
     def second_solve(image_ref, springs_ref, local_ref, v0, v1, kv0, kv1, factor, columns):
         clear_guards(sh, (v0, v1, kv0, kv1))
+        put_columns(sh, springs_ref[6], None, columns)
         index = local_solve(sh, level(sh), image_ref, springs_ref, columns, (v0, v1), (kv0, kv1), factor)
         for m in range(3):
             local_ref[m] = inner((v0, v1)[index], m)
@@ -1084,7 +1067,7 @@
         second_ref, image_ref, slots_ref = take(3)
         v, kv, sums, columns = take(4)
         clear_guards(sh, (v, kv))
-        put_columns(sh, springs_ref, columns)
+        put_columns(sh, springs_ref[6], None, columns)
         merge_all(sh, NEAR, Taker(merging), v, None, EDGE)
         lane, _, _ = sh.lane_grid(1)
         in_grid, _ = grid_masks(sh)
@@ -1109,7 +1092,7 @@
         "second_image",
         [fields, fields, slots],
         [solved, *from_z, *from_y, *from_x, nodes, springs, image, coarse_field, sums],
-        [tall] * 2 + [(LANES, LANES), (8,) + plane],
+        [tall] * 2 + [(LANES, LANES), tall_columns],
     )
     totals = to_all(sums)
 

time: 67.1 us -> 66.4 us (0.990)
  Pallas kernels: 20.4 us -> 19.6 us
    pallas_call x12, Pallas kernels: 20.4 us -> 19.6 us  [call(): pl.pallas_call(kernel, out_shape=[jax.ShapeDtypeStruct(shape, f32) for sh...]
  transfers between devices with their start and end apart: 20 -> 20, of which waited for: 5 -> 5; matrix products, arithmetic and copies ran while one was open for 0% -> 0% of each run, Pallas kernels for 14% -> 13%
where the time goes in v11:
time: 66.4 us; the launch traced here: 66.1 us
  starting transfers between devices  31.6 us (48%)
  Pallas kernels  19.6 us (30%)
  waiting for transfers between devices  14.1 us (21%)
  between operations  0.86 us (1%)
    pallas_call x12, Pallas kernels, call(): pl.pallas_call(kernel, out_shape=[jax.ShapeDtypeStruct(shape, f32) for sh...  19.6 us
    ppermute x17, starting transfers between devices, send(): return lax.ppermute(value, AXES, permutation(sh.sizes, moves))  16.1 us
    all_to_all x3, starting transfers between devices, to_all(): return lax.all_to_all(slots, AXES, 0, 0, tiled=True)  15.5 us
    all_to_all x3, waiting for transfers between devices, to_all(): return lax.all_to_all(slots, AXES, 0, 0, tiled=True)  7.9 us
    ppermute x17, waiting for transfers between devices, send(): return lax.ppermute(value, AXES, permutation(sh.sizes, moves))  6.15 us
  transfers between devices with their start and end apart: 20, of which 5 were waited for; matrix products, arithmetic and copies ran while one was open for 0% of the time, Pallas kernels for 13%

profile of v11, /device:TPU:0, one launch (start us, length us, event | category | flops | bytes accessed | tf_op | source)
XLA Modules:
  0.0 66.1 jit_solution(11681652515573428659)
XLA Ops:
  0.6 3.0 %begin.1 = (f32[48,64]{1,0:T(8,128)}, f32[256,128]{1,0:T(8,128)}, f32[40,128]{1,0:T(8,128)}, f32[40,128]{1,0:T(8,128)}, f32[40,128]{1,0:T(8,128)}) custom-call(f32[3,64,128]{2,1,0:T(8,128)} %bitcast.12, s32[4,4,64]{2,1,0:T(4,128)} %labels_in.1, f32[8]{0:T(128)} %moduli_in.1, s32[64,128]{1,0:T(8,128)} %bitcast.17), custom_call_target="tpu_custom_call" | custom-call | tf_op jit(solution)/shard_map/begin/pallas_call | solution.py:651
  3.7 0.0 copy-start.4
  3.7 0.0 copy-start
  3.7 0.0 copy-start.2
  3.7 0.0 copy-start.3
  3.7 7.3 %all-to-all-start = ((f32[32,8,128]{2,1,0:T(8,128)}), f32[32,8,128]{2,1,0:T(8,128)S(1)}, u32[]{:S(2)}, u32[]{:S(2)}) async-start(f32[32,8,128]{2,1,0:T(8,128)} %bitcast.20), calls=%async_computation | async-start | bytes 262144 | tf_op jit(solution)/shard_map/all_to_all | solution.py:700
  11.0 1.8 %collective-permute-start = (f32[40,128]{1,0:T(8,128)S(1)}, f32[40,128]{1,0:T(8,128)S(1)}, u32[]{:S(2)}, u32[]{:S(2)}) collective-permute-start(f32[40,128]{1,0:T(8,128)S(1)} %copy-done.6), channel_id=1, source_target_pairs={{0,4},{1,5},{2,6},{3,7},{4,0},{5,1},{6,2},{7,3},{8,12},{9,13},{10,... | collective-permute-start | bytes 61448 | tf_op jit(solution)/shard_map/ppermute | solution.py:686
  12.9 0.0 collective-permute-start.1
  12.9 1.5 %collective-permute-start.2 = (f32[40,128]{1,0:T(8,128)S(1)}, f32[40,128]{1,0:T(8,128)S(1)}, u32[]{:S(2)}, u32[]{:S(2)}) collective-permute-start(f32[40,128]{1,0:T(8,128)S(1)} %copy-done.4), channel_id=1, source_target_pairs={{0,16},{1,17},{2,18},{3,19},{4,20},{5,21},{6,22},{7,23},{8,24},{9,... | collective-permute-start | bytes 61448 | tf_op jit(solution)/shard_map/ppermute | solution.py:686
  14.4 0.7 %spread.1 = (f32[4,144,128]{2,1,0:T(8,128)S(1)}, f32[128,128]{1,0:T(8,128)S(1)}, f32[36,1152]{1,0:T(8,128)S(1)}) custom-call(f32[3,64,128]{2,1,0:T(8,128)S(1)} %bitcast.13, s32[64,128]{1,0:T(8,128)S(1)} %bitcast.18, f32[48,64]{1,0:T(8,128)S(1)} %copy-done.3, f32[36,1152]{1,0:T(8,128)S(1)} %copy-done.1), custom_call_target="tpu_custom_call" | custom-call | tf_op jit(solution)/shard_map/spread/pallas_call | solution.py:651
  15.1 0.0 collective-permute-done.refs_1_
  15.1 0.0 collective-permute-done.1.refs_2_
  15.1 1.8 %collective-permute-done.2.refs_3_ = f32[40,128]{1,0:T(8,128)S(1)} collective-permute-done((f32[40,128]{1,0:T(8,128)S(1)}, f32[40,128]{1,0:T(8,128)S(1)}, u32[]{:S(2)}, u32[]{:S(2)}) %collective-permute-start.2) | collective-permute-done | bytes 20512 | tf_op jit(solution)/shard_map/ppermute | solution.py:686
  16.9 2.4 %all-to-all-done = f32[32,8,128]{2,1,0:T(8,128)S(1)} async-done(((f32[32,8,128]{2,1,0:T(8,128)}), f32[32,8,128]{2,1,0:T(8,128)S(1)}, u32[]{:S(2)}, u32[]{:S(2)}) %all-to-all-start) | async-done | bytes 131104 | tf_op jit(solution)/shard_map/all_to_all | solution.py:700
  19.3 1.4 %first_ends.1 = (f32[3,144,128]{2,1,0:T(8,128)S(1)}, f32[144,128]{1,0:T(8,128)S(1)}, f32[2,144,128]{2,1,0:T(8,128)S(1)}, f32[48,128]{1,0:T(8,128)S(1)}, f32[24,128]{1,0:T(8,128)S(1)}, /*index=5*/f32[24,128]{1,0:T(8,128)S(1)}) custom-call(f32[4,144,128]{2,1,0:T(8,128)S(1)} %get-tuple-element.41.refs_0_.start_ref, f32[40,128]{1,0:T(8,128)S(1)} %collective-permute-done.refs_1_, ...), custom_call_target="tpu_custom_call" | custom-call | tf_op jit(solution)/shard_map/first_ends/pallas_call | solution.py:651
  20.7 0.5 collective-permute-start.3
  21.2 0.3 collective-permute-start.4
  21.6 3.0 %first_solve.1 = (f32[3,144,128]{2,1,0:T(8,128)S(1)}, f32[8,144,128]{2,1,0:T(8,128)S(1)}) custom-call(f32[3,144,128]{2,1,0:T(8,128)S(1)} %get-tuple-element.48.residual_ref, f32[2,144,128]{2,1,0:T(8,128)S(1)} %get-tuple-element.49.stiffness_ref, f32[48,128]{1,0:T(8,128)S(1)} %get-tuple-element.50.values, ...), custom_call_target="tpu_custom_call" | custom-call | tf_op jit(solution)/shard_map/first_solve/pallas_call | solution.py:651
  24.6 0.0 collective-permute-done.3.refs_1_
  24.6 0.3 deep.1
  24.9 1.3 %collective-permute-start.5 = (f32[144,128]{1,0:T(8,128)S(1)}, f32[144,128]{1,0:T(8,128)S(1)}, u32[]{:S(2)}, u32[]{:S(2)}) collective-permute-start(f32[144,128]{1,0:T(8,128)S(1)} %get-tuple-element.54), channel_id=1, source_target_pairs={{0,4},{1,5},{2,6},{3,7},{4,0},{5,1},{6,2},{7,3},{8,12},{9,13},{10,... | collective-permute-start | bytes 221192 | tf_op jit(solution)/shard_map/ppermute | solution.py:686
  26.2 0.0 collective-permute-start.6
  26.2 1.5 %collective-permute-start.7 = (f32[144,128]{1,0:T(8,128)S(1)}, f32[144,128]{1,0:T(8,128)S(1)}, u32[]{:S(2)}, u32[]{:S(2)}) collective-permute-start(f32[144,128]{1,0:T(8,128)S(1)} %get-tuple-element.56), channel_id=1, source_target_pairs={{0,16},{1,17},{2,18},{3,19},{4,20},{5,21},{6,22},{7,23},{8,24},{9,... | collective-permute-start | bytes 221192 | tf_op jit(solution)/shard_map/ppermute | solution.py:686
  27.7 1.4 %collective-permute-start.8 = (f32[40,128]{1,0:T(8,128)S(1)}, f32[40,128]{1,0:T(8,128)S(1)}, u32[]{:S(2)}, u32[]{:S(2)}) collective-permute-start(f32[40,128]{1,0:T(8,128)S(1)} %get-tuple-element.57), channel_id=1, source_target_pairs={{0,20},{1,21},{2,22},{3,23},{4,16},{5,17},{6,18},{7,19},{8,28},{9,... | collective-permute-start | bytes 61448 | tf_op jit(solution)/shard_map/ppermute | solution.py:686
  29.1 0.0 collective-permute-start.9
  29.1 3.3 %collective-permute-done.8.refs_6_ = f32[40,128]{1,0:T(8,128)S(1)} collective-permute-done((f32[40,128]{1,0:T(8,128)S(1)}, f32[40,128]{1,0:T(8,128)S(1)}, u32[]{:S(2)}, u32[]{:S(2)}) %collective-permute-start.8) | collective-permute-done | bytes 20512 | tf_op jit(solution)/shard_map/ppermute | solution.py:686
  32.4 0.0 collective-permute-done.7.refs_5_
  32.4 3.2 %first_image.1 = (f32[3,144,128]{2,1,0:T(8,128)S(1)}, f32[3,144,128]{2,1,0:T(8,128)S(1)}, f32[288,128]{1,0:T(8,128)}, f32[24,128]{1,0:T(8,128)S(1)}, f32[24,128]{1,0:T(8,128)S(1)}) custom-call(f32[3,144,128]{2,1,0:T(8,128)S(1)} %get-tuple-element.51.refs_0_, f32[24,128]{1,0:T(8,128)S(1)} %collective-permute-done.3.refs_1_, ...), custom_call_target="tpu_custom_call" | custom-call | tf_op jit(solution)/shard_map/first_image/pallas_call | solution.py:651
  35.6 3.8 %all-to-all-start.1 = ((f32[32,1,1152]{2,1,0:T(1,128)}), f32[32,1,1152]{2,1,0:T(1,128)S(1)}, u32[]{:S(2)}, u32[]{:S(2)}) async-start(f32[32,1,1152]{2,1,0:T(1,128)} %bitcast.4), calls=%async_computation.1 | async-start | bytes 294912 | tf_op jit(solution)/shard_map/all_to_all | solution.py:700
  39.5 0.1 collective-permute-start.10
  39.6 1.6 %collective-permute-start.11 = (f32[24,128]{1,0:T(8,128)S(1)}, f32[24,128]{1,0:T(8,128)S(1)}, u32[]{:S(2)}, u32[]{:S(2)}) collective-permute-start(f32[24,128]{1,0:T(8,128)S(1)} %get-tuple-element.62), channel_id=1, source_target_pairs={{0,3},{1,2},{2,1},{3,0},{4,7},{5,6},{6,5},{7,4},{8,11},{9,10},{10,... | collective-permute-start | bytes 36872 | tf_op jit(solution)/shard_map/ppermute | solution.py:686
  41.3 2.5 %second_solve.1.refs_0_ = f32[3,144,128]{2,1,0:T(8,128)S(1)} custom-call(f32[3,144,128]{2,1,0:T(8,128)S(1)} %get-tuple-element.60.image_ref.first_ref.refs_10_, f32[8,144,128]{2,1,0:T(8,128)S(1)} %get-tuple-element.59.refs_9_.springs_ref), custom_call_target="tpu_custom_call" | custom-call | tf_op jit(solution)/shard_map/second_solve/pallas_call | solution.py:651
  43.8 0.0 collective-permute-done.11.refs_2_
  43.8 0.4 near.1
  44.2 1.5 %collective-permute-start.14 = (f32[144,128]{1,0:T(8,128)S(1)}, f32[144,128]{1,0:T(8,128)S(1)}, u32[]{:S(2)}, u32[]{:S(2)}) collective-permute-start(f32[144,128]{1,0:T(8,128)S(1)} %get-tuple-element.65), channel_id=1, source_target_pairs={{0,16},{1,17},{2,18},{3,19},{4,20},{5,21},{6,22},{7,23},{8,24},{9,... | collective-permute-start | bytes 221192 | tf_op jit(solution)/shard_map/ppermute | solution.py:686
  45.7 1.5 %collective-permute-start.12 = (f32[72,128]{1,0:T(8,128)S(1)}, f32[72,128]{1,0:T(8,128)S(1)}, u32[]{:S(2)}, u32[]{:S(2)}) collective-permute-start(f32[72,128]{1,0:T(8,128)S(1)} %get-tuple-element.63), channel_id=1, source_target_pairs={{0,4},{1,5},{2,6},{3,7},{4,0},{5,1},{6,2},{7,3},{8,12},{9,13},{10,... | collective-permute-start | bytes 110600 | tf_op jit(solution)/shard_map/ppermute | solution.py:686
  47.2 3.0 %collective-permute-start.15 = (f32[24,128]{1,0:T(8,128)S(1)}, f32[24,128]{1,0:T(8,128)S(1)}, u32[]{:S(2)}, u32[]{:S(2)}) collective-permute-start(f32[24,128]{1,0:T(8,128)S(1)} %get-tuple-element.66), channel_id=1, source_target_pairs={{0,20},{1,21},{2,22},{3,23},{4,16},{5,17},{6,18},{7,19},{8,28},{9,... | collective-permute-start | bytes 36872 | tf_op jit(solution)/shard_map/ppermute | solution.py:686
  50.2 0.0 collective-permute-start.16
  50.2 0.6 between.1
  50.8 1.1 %collective-permute-done.15.refs_6_ = f32[24,128]{1,0:T(8,128)S(1)} collective-permute-done((f32[24,128]{1,0:T(8,128)S(1)}, f32[24,128]{1,0:T(8,128)S(1)}, u32[]{:S(2)}, u32[]{:S(2)}) %collective-permute-start.15) | collective-permute-done | bytes 12320 | tf_op jit(solution)/shard_map/ppermute | solution.py:686
  51.9 0.0 collective-permute-done.16.refs_7_
  51.9 0.0 collective-permute-done.12.refs_3_
  51.9 0.0 collective-permute-done.13.refs_4_
  51.9 2.0 %second_image.1 = (f32[3,144,128]{2,1,0:T(8,128)S(1)}, f32[3,144,128]{2,1,0:T(8,128)S(1)}, f32[32,128]{1,0:T(8,128)}) custom-call(f32[3,144,128]{2,1,0:T(8,128)S(1)} %second_solve.1.refs_0_, f32[24,128]{1,0:T(8,128)S(1)} %collective-permute-done.10.refs_1_, f32[24,128]{1,0:T(8,128)S(1)} %collective-permute-done.11.refs_2_, ...), custom_call_target="tpu_custom_call" | custom-call | tf_op jit(solution)/shard_map/second_image/pallas_call | solution.py:651
  53.9 4.3 %all-to-all-start.2 = ((f32[32,1,128]{2,1,0:T(1,128)}), f32[32,1,128]{2,1,0:T(1,128)S(1)}, u32[]{:S(2)}, u32[]{:S(2)}) async-start(f32[32,1,128]{2,1,0:T(1,128)} %bitcast.7), calls=%async_computation.2 | async-start | bytes 32768 | tf_op jit(solution)/shard_map/all_to_all | solution.py:700
  58.2 1.6 %turn.1.turned_ref = f32[4,3,64,128]{3,2,1,0:T(8,128)S(1)} custom-call(f32[3,144,128]{2,1,0:T(8,128)S(1)} %get-tuple-element.70.search_ref, f32[3,144,128]{2,1,0:T(8,128)S(1)} %get-tuple-element.60.image_ref.first_ref.refs_10_, f32[3,144,128]{2,1,0:T(8,128)S(1)} %get-tuple-element.74.second_ref, f32[3,144,128]{2,1,0:T(8,128)S(1)} %get-tuple-element.75.image_ref), custom_call_target="tpu_custom_call" | custom-call | tf_op jit(solution)/shard_map/turn/pallas_call | solution.py:651
  59.8 5.5 %all-to-all-done.2 = f32[32,1,128]{2,1,0:T(1,128)S(1)} async-done(((f32[32,1,128]{2,1,0:T(1,128)}), f32[32,1,128]{2,1,0:T(1,128)S(1)}, u32[]{:S(2)}, u32[]{:S(2)}) %all-to-all-start.2) | async-done | bytes 16416 | tf_op jit(solution)/shard_map/all_to_all | solution.py:700
  65.3 0.8 %finish.1 = (f32[3,64,128]{2,1,0:T(8,128)}, f32[3,64,128]{2,1,0:T(8,128)}) custom-call(f32[32,128]{1,0:T(8,128)S(1)} %bitcast.19, f32[3,64,128]{2,1,0:T(8,128)S(1)} %bitcast.14, f32[4,3,64,128]{3,2,1,0:T(8,128)S(1)} %turn.1.turned_ref), custom_call_target="tpu_custom_call" | custom-call | tf_op jit(solution)/shard_map/finish/pallas_call | solution.py:651
  (18 shorter events, 0.0 us)
Async XLA Ops:
  0.6 13.8 %copy-start.1 = (f32[36,1152]{1,0:T(8,128)S(1)}, f32[36,1152]{1,0:T(8,128)}, u32[]{:S(2)}) copy-start(f32[36,1152]{1,0:T(8,128)} %inverse_in.1) | copy-start | bytes 497668
  3.6 7.4 %copy-start.6 = (f32[40,128]{1,0:T(8,128)S(1)}, f32[40,128]{1,0:T(8,128)}, u32[]{:S(2)}) copy-start(f32[40,128]{1,0:T(8,128)} %get-tuple-element.42) | copy-start | bytes 61444
  3.7 9.2 %copy-start.5 = (f32[40,128]{1,0:T(8,128)S(1)}, f32[40,128]{1,0:T(8,128)}, u32[]{:S(2)}) copy-start(f32[40,128]{1,0:T(8,128)} %get-tuple-element.43) | copy-start | bytes 61444
  3.7 9.2 %copy-start.4 = (f32[40,128]{1,0:T(8,128)S(1)}, f32[40,128]{1,0:T(8,128)}, u32[]{:S(2)}) copy-start(f32[40,128]{1,0:T(8,128)} %get-tuple-element.44) | copy-start | bytes 61444
  3.7 10.7 %copy-start = (f32[3,8,8,128]{3,2,1,0:T(8,128)S(1)}, f32[3,8,8,128]{3,2,1,0:T(8,128)}, u32[]{:S(2)}) copy-start(f32[3,8,8,128]{3,2,1,0:T(8,128)} %param.5) | copy-start | bytes 294916
  3.7 10.7 %copy-start.2 = (s32[8,8,128]{2,1,0:T(8,128)S(1)}, s32[8,8,128]{2,1,0:T(8,128)}, u32[]{:S(2)}) copy-start(s32[8,8,128]{2,1,0:T(8,128)} %param.8) | copy-start | bytes 98308
  3.7 10.7 %copy-start.3 = (f32[48,64]{1,0:T(8,128)S(1)}, f32[48,64]{1,0:T(8,128)}, u32[]{:S(2)}) copy-start(f32[48,64]{1,0:T(8,128)} %get-tuple-element.40.stiff) | copy-start | bytes 36868
  3.7 15.6 %all-to-all-start = ((f32[32,8,128]{2,1,0:T(8,128)}), f32[32,8,128]{2,1,0:T(8,128)S(1)}, u32[]{:S(2)}, u32[]{:S(2)}) async-start(f32[32,8,128]{2,1,0:T(8,128)} %bitcast.20), calls=%async_computation | async-start | bytes 262144 | tf_op jit(solution)/shard_map/all_to_all | solution.py:700
  11.0 4.1 %collective-permute-start = (f32[40,128]{1,0:T(8,128)S(1)}, f32[40,128]{1,0:T(8,128)S(1)}, u32[]{:S(2)}, u32[]{:S(2)}) collective-permute-start(f32[40,128]{1,0:T(8,128)S(1)} %copy-done.6), channel_id=1, source_target_pairs={{0,4},{1,5},{2,6},{3,7},{4,0},{5,1},{6,2},{7,3},{8,12},{9,13},{10,... | collective-permute-start | bytes 61448 | tf_op jit(solution)/shard_map/ppermute | solution.py:686
  12.9 2.2 %collective-permute-start.1 = (f32[40,128]{1,0:T(8,128)S(1)}, f32[40,128]{1,0:T(8,128)S(1)}, u32[]{:S(2)}, u32[]{:S(2)}) collective-permute-start(f32[40,128]{1,0:T(8,128)S(1)} %copy-done.5), channel_id=1, source_target_pairs={{0,1},{1,0},{2,3},{3,2},{4,8},{5,9},{6,10},{7,11},{8,4},{9,5},{10,... | collective-permute-start | bytes 61448 | tf_op jit(solution)/shard_map/ppermute | solution.py:686
  12.9 4.0 %collective-permute-start.2 = (f32[40,128]{1,0:T(8,128)S(1)}, f32[40,128]{1,0:T(8,128)S(1)}, u32[]{:S(2)}, u32[]{:S(2)}) collective-permute-start(f32[40,128]{1,0:T(8,128)S(1)} %copy-done.4), channel_id=1, source_target_pairs={{0,16},{1,17},{2,18},{3,19},{4,20},{5,21},{6,22},{7,23},{8,24},{9,... | collective-permute-start | bytes 61448 | tf_op jit(solution)/shard_map/ppermute | solution.py:686
  20.7 3.9 %collective-permute-start.3 = (f32[24,128]{1,0:T(8,128)S(1)}, f32[24,128]{1,0:T(8,128)S(1)}, u32[]{:S(2)}, u32[]{:S(2)}) collective-permute-start(f32[24,128]{1,0:T(8,128)S(1)} %get-tuple-element.52), channel_id=1, source_target_pairs={{0,1},{1,0},{2,3},{3,2},{4,5},{5,4},{6,7},{7,6},{8,9},{9,8},{10,11... | collective-permute-start | bytes 36872 | tf_op jit(solution)/shard_map/ppermute | solution.py:686
  21.2 3.4 %collective-permute-start.4 = (f32[24,128]{1,0:T(8,128)S(1)}, f32[24,128]{1,0:T(8,128)S(1)}, u32[]{:S(2)}, u32[]{:S(2)}) collective-permute-start(f32[24,128]{1,0:T(8,128)S(1)} %get-tuple-element.53), channel_id=1, source_target_pairs={{0,3},{1,2},{2,1},{3,0},{4,7},{5,6},{6,5},{7,4},{8,11},{9,10},{10,... | collective-permute-start | bytes 36872 | tf_op jit(solution)/shard_map/ppermute | solution.py:686
  24.9 7.4 %collective-permute-start.5 = (f32[144,128]{1,0:T(8,128)S(1)}, f32[144,128]{1,0:T(8,128)S(1)}, u32[]{:S(2)}, u32[]{:S(2)}) collective-permute-start(f32[144,128]{1,0:T(8,128)S(1)} %get-tuple-element.54), channel_id=1, source_target_pairs={{0,4},{1,5},{2,6},{3,7},{4,0},{5,1},{6,2},{7,3},{8,12},{9,13},{10,... | collective-permute-start | bytes 221192 | tf_op jit(solution)/shard_map/ppermute | solution.py:686
  26.2 6.1 %collective-permute-start.6 = (f32[144,128]{1,0:T(8,128)S(1)}, f32[144,128]{1,0:T(8,128)S(1)}, u32[]{:S(2)}, u32[]{:S(2)}) collective-permute-start(f32[144,128]{1,0:T(8,128)S(1)} %get-tuple-element.55), channel_id=1, source_target_pairs={{0,1},{1,0},{2,3},{3,2},{4,8},{5,9},{6,10},{7,11},{8,4},{9,5},{10,... | collective-permute-start | bytes 221192 | tf_op jit(solution)/shard_map/ppermute | solution.py:686
  26.2 6.2 %collective-permute-start.7 = (f32[144,128]{1,0:T(8,128)S(1)}, f32[144,128]{1,0:T(8,128)S(1)}, u32[]{:S(2)}, u32[]{:S(2)}) collective-permute-start(f32[144,128]{1,0:T(8,128)S(1)} %get-tuple-element.56), channel_id=1, source_target_pairs={{0,16},{1,17},{2,18},{3,19},{4,20},{5,21},{6,22},{7,23},{8,24},{9,... | collective-permute-start | bytes 221192 | tf_op jit(solution)/shard_map/ppermute | solution.py:686
  27.7 4.7 %collective-permute-start.8 = (f32[40,128]{1,0:T(8,128)S(1)}, f32[40,128]{1,0:T(8,128)S(1)}, u32[]{:S(2)}, u32[]{:S(2)}) collective-permute-start(f32[40,128]{1,0:T(8,128)S(1)} %get-tuple-element.57), channel_id=1, source_target_pairs={{0,20},{1,21},{2,22},{3,23},{4,16},{5,17},{6,18},{7,19},{8,28},{9,... | collective-permute-start | bytes 61448 | tf_op jit(solution)/shard_map/ppermute | solution.py:686
  29.1 3.3 %collective-permute-start.9 = (f32[40,128]{1,0:T(8,128)S(1)}, f32[40,128]{1,0:T(8,128)S(1)}, u32[]{:S(2)}, u32[]{:S(2)}) collective-permute-start(f32[40,128]{1,0:T(8,128)S(1)} %get-tuple-element.58), channel_id=1, source_target_pairs={{0,1},{1,0},{2,3},{3,2},{4,24},{5,25},{6,26},{7,27},{8,20},{9,21},... | collective-permute-start | bytes 61448 | tf_op jit(solution)/shard_map/ppermute | solution.py:686
  35.6 14.5 %all-to-all-start.1 = ((f32[32,1,1152]{2,1,0:T(1,128)}), f32[32,1,1152]{2,1,0:T(1,128)S(1)}, u32[]{:S(2)}, u32[]{:S(2)}) async-start(f32[32,1,1152]{2,1,0:T(1,128)} %bitcast.4), calls=%async_computation.1 | async-start | bytes 294912 | tf_op jit(solution)/shard_map/all_to_all | solution.py:700
  39.5 4.3 %collective-permute-start.10 = (f32[24,128]{1,0:T(8,128)S(1)}, f32[24,128]{1,0:T(8,128)S(1)}, u32[]{:S(2)}, u32[]{:S(2)}) collective-permute-start(f32[24,128]{1,0:T(8,128)S(1)} %get-tuple-element.61), channel_id=1, source_target_pairs={{0,1},{1,0},{2,3},{3,2},{4,5},{5,4},{6,7},{7,6},{8,9},{9,8},{10,11... | collective-permute-start | bytes 36872 | tf_op jit(solution)/shard_map/ppermute | solution.py:686
  39.6 4.2 %collective-permute-start.11 = (f32[24,128]{1,0:T(8,128)S(1)}, f32[24,128]{1,0:T(8,128)S(1)}, u32[]{:S(2)}, u32[]{:S(2)}) collective-permute-start(f32[24,128]{1,0:T(8,128)S(1)} %get-tuple-element.62), channel_id=1, source_target_pairs={{0,3},{1,2},{2,1},{3,0},{4,7},{5,6},{6,5},{7,4},{8,11},{9,10},{10,... | collective-permute-start | bytes 36872 | tf_op jit(solution)/shard_map/ppermute | solution.py:686
  44.2 7.7 %collective-permute-start.14 = (f32[144,128]{1,0:T(8,128)S(1)}, f32[144,128]{1,0:T(8,128)S(1)}, u32[]{:S(2)}, u32[]{:S(2)}) collective-permute-start(f32[144,128]{1,0:T(8,128)S(1)} %get-tuple-element.65), channel_id=1, source_target_pairs={{0,16},{1,17},{2,18},{3,19},{4,20},{5,21},{6,22},{7,23},{8,24},{9,... | collective-permute-start | bytes 221192 | tf_op jit(solution)/shard_map/ppermute | solution.py:686
  45.7 6.1 %collective-permute-start.12 = (f32[72,128]{1,0:T(8,128)S(1)}, f32[72,128]{1,0:T(8,128)S(1)}, u32[]{:S(2)}, u32[]{:S(2)}) collective-permute-start(f32[72,128]{1,0:T(8,128)S(1)} %get-tuple-element.63), channel_id=1, source_target_pairs={{0,4},{1,5},{2,6},{3,7},{4,0},{5,1},{6,2},{7,3},{8,12},{9,13},{10,... | collective-permute-start | bytes 110600 | tf_op jit(solution)/shard_map/ppermute | solution.py:686
  47.2 4.7 %collective-permute-start.13 = (f32[72,128]{1,0:T(8,128)S(1)}, f32[72,128]{1,0:T(8,128)S(1)}, u32[]{:S(2)}, u32[]{:S(2)}) collective-permute-start(f32[72,128]{1,0:T(8,128)S(1)} %get-tuple-element.64), channel_id=1, source_target_pairs={{0,1},{1,0},{2,3},{3,2},{4,8},{5,9},{6,10},{7,11},{8,4},{9,5},{10,... | collective-permute-start | bytes 110600 | tf_op jit(solution)/shard_map/ppermute | solution.py:686
  47.2 4.7 %collective-permute-start.15 = (f32[24,128]{1,0:T(8,128)S(1)}, f32[24,128]{1,0:T(8,128)S(1)}, u32[]{:S(2)}, u32[]{:S(2)}) collective-permute-start(f32[24,128]{1,0:T(8,128)S(1)} %get-tuple-element.66), channel_id=1, source_target_pairs={{0,20},{1,21},{2,22},{3,23},{4,16},{5,17},{6,18},{7,19},{8,28},{9,... | collective-permute-start | bytes 36872 | tf_op jit(solution)/shard_map/ppermute | solution.py:686
  50.2 1.7 %collective-permute-start.16 = (f32[24,128]{1,0:T(8,128)S(1)}, f32[24,128]{1,0:T(8,128)S(1)}, u32[]{:S(2)}, u32[]{:S(2)}) collective-permute-start(f32[24,128]{1,0:T(8,128)S(1)} %get-tuple-element.67), channel_id=1, source_target_pairs={{0,1},{1,0},{2,3},{3,2},{4,24},{5,25},{6,26},{7,27},{8,20},{9,21},... | collective-permute-start | bytes 36872 | tf_op jit(solution)/shard_map/ppermute | solution.py:686
  53.9 11.4 %all-to-all-start.2 = ((f32[32,1,128]{2,1,0:T(1,128)}), f32[32,1,128]{2,1,0:T(1,128)S(1)}, u32[]{:S(2)}, u32[]{:S(2)}) async-start(f32[32,1,128]{2,1,0:T(1,128)} %bitcast.7), calls=%async_computation.2 | async-start | bytes 32768 | tf_op jit(solution)/shard_map/all_to_all | solution.py:700

commit v12 on v11

--- a/solution.py
+++ b/solution.py
@@ -62,6 +62,10 @@
     return value if amount == 0 else pltpu.roll(value, amount, 1)
 
 
+def shift_either(flag, value, first, second):
+    return pltpu.roll(value, jnp.where(flag, first % LANES, second % LANES), 1)
+
+
 def pick(mask, value):
     return jnp.where(mask, value, 0.0)
 
@@ -151,10 +155,13 @@
     y_above, y_below = sh.y + ex.up, ex.down
     for f in range(ex.fields):
         value = scratch[f]
-        start = (sh.x + ex.up + 1) * sh.pitch
-        x_up = x_up + shift(pick(lane_range(lane, start, span), value), f * span - start)
-        start = (ex.down + 1) * sh.pitch
-        x_down = x_down + shift(pick(lane_range(lane, start, span), value), f * span - start)
+        high, low = (sh.x + ex.up + 1) * sh.pitch, (ex.down + 1) * sh.pitch
+        if sh.x_links == 1:
+            part = pick(lane_range(lane, jnp.where(even_x, high, low), span), value)
+            x_up = x_down = x_up + shift_either(even_x, part, f * span - high, f * span - low)
+        else:
+            x_up = x_up + shift(pick(lane_range(lane, high, span), value), f * span - high)
+            x_down = x_down + shift(pick(lane_range(lane, low, span), value), f * span - low)
         mask = inside & lane_range(across, y_above, ex.layers)
         y_up = y_up + shift(pick(mask, value), f * ex.layers - y_above - 2)
         mask = inside & lane_range(across, y_below, ex.layers)
@@ -163,7 +170,7 @@
     y_up, y_down = fold(sh, y_up, packed), fold(sh, y_down, packed)
     for ref, message in zip(y_refs, pair(sh.y_links, even_y, y_up, y_down)):
         ref[...] = message
-    for i, message in enumerate(pair(sh.x_links, even_x, x_up, x_down)):
+    for i, message in enumerate([x_up] if sh.x_links == 1 else pair(sh.x_links, even_x, x_up, x_down)):
         x_refs[i][...] = message
         upward, downward = fold(sh, message, ex.layers, y_above), fold(sh, message, ex.layers, y_below)
         for j, corner in enumerate(pair(sh.y_links, even_y, upward, downward)):
@@ -186,26 +193,37 @@
         below, above = sides(sh, 1, [ref[...] for ref in diagonal])
         total = total + unfold(sh, below, ex.layers, ex.up)
         sums.append(total + unfold(sh, above, ex.layers, sh.y + ex.down))
-    below_x, above_x = sides(sh, 0, sums)
+    single = sh.x_links == 1
+    even = sh.here(0) % 2 == 0
+    if single:
+        message = scale(jnp.where(even, sh.here(0) < sh.sizes[0] - 1, sh.here(0) > 0), sums[0])
+    else:
+        below_x, above_x = sides(sh, 0, sums)
     first = 1 if ex.up == -2 else 0
     last = ex.layers - 1 if ex.down + ex.layers == 2 else ex.layers
+    low, low_count = (ex.up + first + 1) * sh.pitch, (ex.layers - first) * sh.pitch
+    high, high_count = (sh.x + ex.down + 1) * sh.pitch, last * sh.pitch
+    edge = (sh.x + 1) * sh.pitch
     for f in range(ex.fields):
         addend = pick(low_mask, shift(below_y, ex.up + 2 - ex.layers * f))
         addend = addend + pick(high_mask, shift(above_y, sh.y + ex.down + 2 - ex.layers * f))
-        start = (ex.up + first + 1) * sh.pitch
-        count = (ex.layers - first) * sh.pitch
-        moved = shift(below_x, start - f * span - first * sh.pitch)
-        addend = addend + pick(lane_range(lane, start, count), moved)
-        start = (sh.x + ex.down + 1) * sh.pitch
-        moved = shift(above_x, start - f * span)
-        addend = addend + pick(lane_range(lane, start, last * sh.pitch), moved)
+        from_low, from_high = low - f * span - first * sh.pitch, high - f * span
+        if single:
+            mask = lane_range(lane, jnp.where(even, high, low), jnp.where(even, high_count, low_count))
+            addend = addend + pick(mask, shift_either(even, message, from_high, from_low))
+        else:
+            addend = addend + pick(lane_range(lane, low, low_count), shift(below_x, from_low))
+            addend = addend + pick(lane_range(lane, high, high_count), shift(above_x, from_high))
         scratch[f, guard : guard + sh.rows, :] += addend
         if rim is not None:
-            low = pick(lane_range(lane, 0, sh.pitch), shift(below_x, -f * span))
-            start = (sh.x + 1) * sh.pitch
-            moved = shift(above_x, start - f * span - last * sh.pitch)
-            high = pick(lane_range(lane, start, sh.pitch), moved)
-            rim[f, guard : guard + sh.rows, :] = low + high
+            from_high = edge - f * span - last * sh.pitch
+            if single:
+                mask = lane_range(lane, jnp.where(even, edge, 0), sh.pitch)
+                both = pick(mask, shift_either(even, message, from_high, -f * span))
+            else:
+                both = pick(lane_range(lane, 0, sh.pitch), shift(below_x, -f * span))
+                both = both + pick(lane_range(lane, edge, sh.pitch), shift(above_x, from_high))
+            rim[f, guard : guard + sh.rows, :] = both
 
 
 def clear_guards(sh, refs):

time: 66.4 us -> 66.2 us (level)
  no operation moved by 1% of the time
where the time goes in v12:
time: 66.2 us; the launch traced here: 65.9 us
  starting transfers between devices  31.6 us (48%)
  Pallas kernels  19.4 us (29%)
  waiting for transfers between devices  14.1 us (21%)
  between operations  0.86 us (1%)
    pallas_call x12, Pallas kernels, call(): pl.pallas_call(kernel, out_shape=[jax.ShapeDtypeStruct(shape, f32) for sh...  19.4 us
    ppermute x17, starting transfers between devices, send(): return lax.ppermute(value, AXES, permutation(sh.sizes, moves))  16.1 us
    all_to_all x3, starting transfers between devices, to_all(): return lax.all_to_all(slots, AXES, 0, 0, tiled=True)  15.5 us
    all_to_all x3, waiting for transfers between devices, to_all(): return lax.all_to_all(slots, AXES, 0, 0, tiled=True)  7.9 us
    ppermute x17, waiting for transfers between devices, send(): return lax.ppermute(value, AXES, permutation(sh.sizes, moves))  6.15 us
  transfers between devices with their start and end apart: 20, of which 5 were waited for; matrix products, arithmetic and copies ran while one was open for 0% of the time, Pallas kernels for 13%

profile of v12, /device:TPU:0, one launch (start us, length us, event | category | flops | bytes accessed | tf_op | source)
XLA Modules:
  0.0 65.9 jit_solution(14966354560103196783)
XLA Ops:
  0.6 3.0 %begin.1 = (f32[48,64]{1,0:T(8,128)}, f32[256,128]{1,0:T(8,128)}, f32[40,128]{1,0:T(8,128)}, f32[40,128]{1,0:T(8,128)}, f32[40,128]{1,0:T(8,128)}) custom-call(f32[3,64,128]{2,1,0:T(8,128)} %bitcast.12, s32[4,4,64]{2,1,0:T(4,128)} %labels_in.1, f32[8]{0:T(128)} %moduli_in.1, s32[64,128]{1,0:T(8,128)} %bitcast.17), custom_call_target="tpu_custom_call" | custom-call | tf_op jit(solution)/shard_map/begin/pallas_call | solution.py:669
  3.7 0.0 copy-start.4
  3.7 0.0 copy-start
  3.7 0.0 copy-start.2
  3.7 0.0 copy-start.3
  3.7 7.3 %all-to-all-start = ((f32[32,8,128]{2,1,0:T(8,128)}), f32[32,8,128]{2,1,0:T(8,128)S(1)}, u32[]{:S(2)}, u32[]{:S(2)}) async-start(f32[32,8,128]{2,1,0:T(8,128)} %bitcast.20), calls=%async_computation | async-start | bytes 262144 | tf_op jit(solution)/shard_map/all_to_all | solution.py:718
  11.0 1.8 %collective-permute-start = (f32[40,128]{1,0:T(8,128)S(1)}, f32[40,128]{1,0:T(8,128)S(1)}, u32[]{:S(2)}, u32[]{:S(2)}) collective-permute-start(f32[40,128]{1,0:T(8,128)S(1)} %copy-done.6), channel_id=1, source_target_pairs={{0,4},{1,5},{2,6},{3,7},{4,0},{5,1},{6,2},{7,3},{8,12},{9,13},{10,... | collective-permute-start | bytes 61448 | tf_op jit(solution)/shard_map/ppermute | solution.py:704
  12.9 0.0 collective-permute-start.1
  12.9 1.5 %collective-permute-start.2 = (f32[40,128]{1,0:T(8,128)S(1)}, f32[40,128]{1,0:T(8,128)S(1)}, u32[]{:S(2)}, u32[]{:S(2)}) collective-permute-start(f32[40,128]{1,0:T(8,128)S(1)} %copy-done.4), channel_id=1, source_target_pairs={{0,16},{1,17},{2,18},{3,19},{4,20},{5,21},{6,22},{7,23},{8,24},{9,... | collective-permute-start | bytes 61448 | tf_op jit(solution)/shard_map/ppermute | solution.py:704
  14.4 0.7 %spread.1 = (f32[4,144,128]{2,1,0:T(8,128)S(1)}, f32[128,128]{1,0:T(8,128)S(1)}, f32[36,1152]{1,0:T(8,128)S(1)}) custom-call(f32[3,64,128]{2,1,0:T(8,128)S(1)} %bitcast.13, s32[64,128]{1,0:T(8,128)S(1)} %bitcast.18, f32[48,64]{1,0:T(8,128)S(1)} %copy-done.3, f32[36,1152]{1,0:T(8,128)S(1)} %copy-done.1), custom_call_target="tpu_custom_call" | custom-call | tf_op jit(solution)/shard_map/spread/pallas_call | solution.py:669
  15.1 0.0 collective-permute-done.refs_1_
  15.1 0.0 collective-permute-done.1.refs_2_
  15.1 1.8 %collective-permute-done.2.refs_3_ = f32[40,128]{1,0:T(8,128)S(1)} collective-permute-done((f32[40,128]{1,0:T(8,128)S(1)}, f32[40,128]{1,0:T(8,128)S(1)}, u32[]{:S(2)}, u32[]{:S(2)}) %collective-permute-start.2) | collective-permute-done | bytes 20512 | tf_op jit(solution)/shard_map/ppermute | solution.py:704
  16.9 2.4 %all-to-all-done = f32[32,8,128]{2,1,0:T(8,128)S(1)} async-done(((f32[32,8,128]{2,1,0:T(8,128)}), f32[32,8,128]{2,1,0:T(8,128)S(1)}, u32[]{:S(2)}, u32[]{:S(2)}) %all-to-all-start) | async-done | bytes 131104 | tf_op jit(solution)/shard_map/all_to_all | solution.py:718
  19.3 1.4 %first_ends.1 = (f32[3,144,128]{2,1,0:T(8,128)S(1)}, f32[144,128]{1,0:T(8,128)S(1)}, f32[2,144,128]{2,1,0:T(8,128)S(1)}, f32[48,128]{1,0:T(8,128)S(1)}, f32[24,128]{1,0:T(8,128)S(1)}, /*index=5*/f32[24,128]{1,0:T(8,128)S(1)}) custom-call(f32[4,144,128]{2,1,0:T(8,128)S(1)} %get-tuple-element.41.refs_0_.start_ref, f32[40,128]{1,0:T(8,128)S(1)} %collective-permute-done.refs_1_, ...), custom_call_target="tpu_custom_call" | custom-call | tf_op jit(solution)/shard_map/first_ends/pallas_call | solution.py:669
  20.7 0.5 collective-permute-start.3
  21.2 0.3 collective-permute-start.4
  21.6 3.0 %first_solve.1 = (f32[3,144,128]{2,1,0:T(8,128)S(1)}, f32[8,144,128]{2,1,0:T(8,128)S(1)}) custom-call(f32[3,144,128]{2,1,0:T(8,128)S(1)} %get-tuple-element.48.residual_ref, f32[2,144,128]{2,1,0:T(8,128)S(1)} %get-tuple-element.49.stiffness_ref, f32[48,128]{1,0:T(8,128)S(1)} %get-tuple-element.50.values, ...), custom_call_target="tpu_custom_call" | custom-call | tf_op jit(solution)/shard_map/first_solve/pallas_call | solution.py:669
  24.6 0.0 collective-permute-done.3.refs_1_
  24.6 0.0 collective-permute-done.4.refs_2_
  24.6 0.3 deep.1
  24.9 1.3 %collective-permute-start.5 = (f32[144,128]{1,0:T(8,128)S(1)}, f32[144,128]{1,0:T(8,128)S(1)}, u32[]{:S(2)}, u32[]{:S(2)}) collective-permute-start(f32[144,128]{1,0:T(8,128)S(1)} %get-tuple-element.54), channel_id=1, source_target_pairs={{0,4},{1,5},{2,6},{3,7},{4,0},{5,1},{6,2},{7,3},{8,12},{9,13},{10,... | collective-permute-start | bytes 221192 | tf_op jit(solution)/shard_map/ppermute | solution.py:704
  26.2 0.0 collective-permute-start.6
  26.2 1.5 %collective-permute-start.7 = (f32[144,128]{1,0:T(8,128)S(1)}, f32[144,128]{1,0:T(8,128)S(1)}, u32[]{:S(2)}, u32[]{:S(2)}) collective-permute-start(f32[144,128]{1,0:T(8,128)S(1)} %get-tuple-element.56), channel_id=1, source_target_pairs={{0,16},{1,17},{2,18},{3,19},{4,20},{5,21},{6,22},{7,23},{8,24},{9,... | collective-permute-start | bytes 221192 | tf_op jit(solution)/shard_map/ppermute | solution.py:704
  27.7 1.4 %collective-permute-start.8 = (f32[40,128]{1,0:T(8,128)S(1)}, f32[40,128]{1,0:T(8,128)S(1)}, u32[]{:S(2)}, u32[]{:S(2)}) collective-permute-start(f32[40,128]{1,0:T(8,128)S(1)} %get-tuple-element.57), channel_id=1, source_target_pairs={{0,20},{1,21},{2,22},{3,23},{4,16},{5,17},{6,18},{7,19},{8,28},{9,... | collective-permute-start | bytes 61448 | tf_op jit(solution)/shard_map/ppermute | solution.py:704
  29.0 0.0 collective-permute-start.9
  29.0 3.3 %collective-permute-done.8.refs_6_ = f32[40,128]{1,0:T(8,128)S(1)} collective-permute-done((f32[40,128]{1,0:T(8,128)S(1)}, f32[40,128]{1,0:T(8,128)S(1)}, u32[]{:S(2)}, u32[]{:S(2)}) %collective-permute-start.8) | collective-permute-done | bytes 20512 | tf_op jit(solution)/shard_map/ppermute | solution.py:704
  32.3 0.0 collective-permute-done.9.refs_7_
  32.3 0.0 collective-permute-done.6.refs_4_
  32.3 0.0 collective-permute-done.7.refs_5_
  32.4 3.1 %first_image.1 = (f32[3,144,128]{2,1,0:T(8,128)S(1)}, f32[3,144,128]{2,1,0:T(8,128)S(1)}, f32[288,128]{1,0:T(8,128)}, f32[24,128]{1,0:T(8,128)S(1)}, f32[24,128]{1,0:T(8,128)S(1)}) custom-call(f32[3,144,128]{2,1,0:T(8,128)S(1)} %get-tuple-element.51.refs_0_, f32[24,128]{1,0:T(8,128)S(1)} %collective-permute-done.3.refs_1_, ...), custom_call_target="tpu_custom_call" | custom-call | tf_op jit(solution)/shard_map/first_image/pallas_call | solution.py:669
  35.5 3.8 %all-to-all-start.1 = ((f32[32,1,1152]{2,1,0:T(1,128)}), f32[32,1,1152]{2,1,0:T(1,128)S(1)}, u32[]{:S(2)}, u32[]{:S(2)}) async-start(f32[32,1,1152]{2,1,0:T(1,128)} %bitcast.4), calls=%async_computation.1 | async-start | bytes 294912 | tf_op jit(solution)/shard_map/all_to_all | solution.py:718
  39.4 0.1 collective-permute-start.10
  39.5 1.6 %collective-permute-start.11 = (f32[24,128]{1,0:T(8,128)S(1)}, f32[24,128]{1,0:T(8,128)S(1)}, u32[]{:S(2)}, u32[]{:S(2)}) collective-permute-start(f32[24,128]{1,0:T(8,128)S(1)} %get-tuple-element.62), channel_id=1, source_target_pairs={{0,3},{1,2},{2,1},{3,0},{4,7},{5,6},{6,5},{7,4},{8,11},{9,10},{10,... | collective-permute-start | bytes 36872 | tf_op jit(solution)/shard_map/ppermute | solution.py:704
  41.1 2.5 %second_solve.1.refs_0_ = f32[3,144,128]{2,1,0:T(8,128)S(1)} custom-call(f32[3,144,128]{2,1,0:T(8,128)S(1)} %get-tuple-element.60.image_ref.first_ref.refs_10_, f32[8,144,128]{2,1,0:T(8,128)S(1)} %get-tuple-element.59.refs_9_.springs_ref), custom_call_target="tpu_custom_call" | custom-call | tf_op jit(solution)/shard_map/second_solve/pallas_call | solution.py:669
  43.7 0.4 near.1
  44.0 1.5 %collective-permute-start.14 = (f32[144,128]{1,0:T(8,128)S(1)}, f32[144,128]{1,0:T(8,128)S(1)}, u32[]{:S(2)}, u32[]{:S(2)}) collective-permute-start(f32[144,128]{1,0:T(8,128)S(1)} %get-tuple-element.65), channel_id=1, source_target_pairs={{0,16},{1,17},{2,18},{3,19},{4,20},{5,21},{6,22},{7,23},{8,24},{9,... | collective-permute-start | bytes 221192 | tf_op jit(solution)/shard_map/ppermute | solution.py:704
  45.6 1.5 %collective-permute-start.12 = (f32[72,128]{1,0:T(8,128)S(1)}, f32[72,128]{1,0:T(8,128)S(1)}, u32[]{:S(2)}, u32[]{:S(2)}) collective-permute-start(f32[72,128]{1,0:T(8,128)S(1)} %get-tuple-element.63), channel_id=1, source_target_pairs={{0,4},{1,5},{2,6},{3,7},{4,0},{5,1},{6,2},{7,3},{8,12},{9,13},{10,... | collective-permute-start | bytes 110600 | tf_op jit(solution)/shard_map/ppermute | solution.py:704
  47.0 0.0 collective-permute-start.13
  47.0 3.0 %collective-permute-start.15 = (f32[24,128]{1,0:T(8,128)S(1)}, f32[24,128]{1,0:T(8,128)S(1)}, u32[]{:S(2)}, u32[]{:S(2)}) collective-permute-start(f32[24,128]{1,0:T(8,128)S(1)} %get-tuple-element.66), channel_id=1, source_target_pairs={{0,20},{1,21},{2,22},{3,23},{4,16},{5,17},{6,18},{7,19},{8,28},{9,... | collective-permute-start | bytes 36872 | tf_op jit(solution)/shard_map/ppermute | solution.py:704
  50.0 0.6 between.1
  50.6 1.1 %collective-permute-done.15.refs_6_ = f32[24,128]{1,0:T(8,128)S(1)} collective-permute-done((f32[24,128]{1,0:T(8,128)S(1)}, f32[24,128]{1,0:T(8,128)S(1)}, u32[]{:S(2)}, u32[]{:S(2)}) %collective-permute-start.15) | collective-permute-done | bytes 12320 | tf_op jit(solution)/shard_map/ppermute | solution.py:704
  51.7 0.0 collective-permute-done.16.refs_7_
  51.7 2.0 %second_image.1 = (f32[3,144,128]{2,1,0:T(8,128)S(1)}, f32[3,144,128]{2,1,0:T(8,128)S(1)}, f32[32,128]{1,0:T(8,128)}) custom-call(f32[3,144,128]{2,1,0:T(8,128)S(1)} %second_solve.1.refs_0_, f32[24,128]{1,0:T(8,128)S(1)} %collective-permute-done.10.refs_1_, f32[24,128]{1,0:T(8,128)S(1)} %collective-permute-done.11.refs_2_, ...), custom_call_target="tpu_custom_call" | custom-call | tf_op jit(solution)/shard_map/second_image/pallas_call | solution.py:669
  53.7 4.3 %all-to-all-start.2 = ((f32[32,1,128]{2,1,0:T(1,128)}), f32[32,1,128]{2,1,0:T(1,128)S(1)}, u32[]{:S(2)}, u32[]{:S(2)}) async-start(f32[32,1,128]{2,1,0:T(1,128)} %bitcast.7), calls=%async_computation.2 | async-start | bytes 32768 | tf_op jit(solution)/shard_map/all_to_all | solution.py:718
  58.0 1.6 %turn.1.turned_ref = f32[4,3,64,128]{3,2,1,0:T(8,128)S(1)} custom-call(f32[3,144,128]{2,1,0:T(8,128)S(1)} %get-tuple-element.70.search_ref, f32[3,144,128]{2,1,0:T(8,128)S(1)} %get-tuple-element.60.image_ref.first_ref.refs_10_, f32[3,144,128]{2,1,0:T(8,128)S(1)} %get-tuple-element.74.second_ref, f32[3,144,128]{2,1,0:T(8,128)S(1)} %get-tuple-element.75.image_ref), custom_call_target="tpu_custom_call" | custom-call | tf_op jit(solution)/shard_map/turn/pallas_call | solution.py:669
  59.6 5.5 %all-to-all-done.2 = f32[32,1,128]{2,1,0:T(1,128)S(1)} async-done(((f32[32,1,128]{2,1,0:T(1,128)}), f32[32,1,128]{2,1,0:T(1,128)S(1)}, u32[]{:S(2)}, u32[]{:S(2)}) %all-to-all-start.2) | async-done | bytes 16416 | tf_op jit(solution)/shard_map/all_to_all | solution.py:718
  65.1 0.8 %finish.1 = (f32[3,64,128]{2,1,0:T(8,128)}, f32[3,64,128]{2,1,0:T(8,128)}) custom-call(f32[32,128]{1,0:T(8,128)S(1)} %bitcast.19, f32[3,64,128]{2,1,0:T(8,128)S(1)} %bitcast.14, f32[4,3,64,128]{3,2,1,0:T(8,128)S(1)} %turn.1.turned_ref), custom_call_target="tpu_custom_call" | custom-call | tf_op jit(solution)/shard_map/finish/pallas_call | solution.py:669
  (18 shorter events, 0.0 us)
Async XLA Ops:
  0.6 13.8 %copy-start.1 = (f32[36,1152]{1,0:T(8,128)S(1)}, f32[36,1152]{1,0:T(8,128)}, u32[]{:S(2)}) copy-start(f32[36,1152]{1,0:T(8,128)} %inverse_in.1) | copy-start | bytes 497668
  3.6 7.4 %copy-start.6 = (f32[40,128]{1,0:T(8,128)S(1)}, f32[40,128]{1,0:T(8,128)}, u32[]{:S(2)}) copy-start(f32[40,128]{1,0:T(8,128)} %get-tuple-element.42) | copy-start | bytes 61444
  3.7 9.2 %copy-start.5 = (f32[40,128]{1,0:T(8,128)S(1)}, f32[40,128]{1,0:T(8,128)}, u32[]{:S(2)}) copy-start(f32[40,128]{1,0:T(8,128)} %get-tuple-element.43) | copy-start | bytes 61444
  3.7 9.2 %copy-start.4 = (f32[40,128]{1,0:T(8,128)S(1)}, f32[40,128]{1,0:T(8,128)}, u32[]{:S(2)}) copy-start(f32[40,128]{1,0:T(8,128)} %get-tuple-element.44) | copy-start | bytes 61444
  3.7 10.7 %copy-start = (f32[3,8,8,128]{3,2,1,0:T(8,128)S(1)}, f32[3,8,8,128]{3,2,1,0:T(8,128)}, u32[]{:S(2)}) copy-start(f32[3,8,8,128]{3,2,1,0:T(8,128)} %param.5) | copy-start | bytes 294916
  3.7 10.7 %copy-start.2 = (s32[8,8,128]{2,1,0:T(8,128)S(1)}, s32[8,8,128]{2,1,0:T(8,128)}, u32[]{:S(2)}) copy-start(s32[8,8,128]{2,1,0:T(8,128)} %param.8) | copy-start | bytes 98308
  3.7 10.7 %copy-start.3 = (f32[48,64]{1,0:T(8,128)S(1)}, f32[48,64]{1,0:T(8,128)}, u32[]{:S(2)}) copy-start(f32[48,64]{1,0:T(8,128)} %get-tuple-element.40.stiff) | copy-start | bytes 36868
  3.7 15.6 %all-to-all-start = ((f32[32,8,128]{2,1,0:T(8,128)}), f32[32,8,128]{2,1,0:T(8,128)S(1)}, u32[]{:S(2)}, u32[]{:S(2)}) async-start(f32[32,8,128]{2,1,0:T(8,128)} %bitcast.20), calls=%async_computation | async-start | bytes 262144 | tf_op jit(solution)/shard_map/all_to_all | solution.py:718
  11.0 4.1 %collective-permute-start = (f32[40,128]{1,0:T(8,128)S(1)}, f32[40,128]{1,0:T(8,128)S(1)}, u32[]{:S(2)}, u32[]{:S(2)}) collective-permute-start(f32[40,128]{1,0:T(8,128)S(1)} %copy-done.6), channel_id=1, source_target_pairs={{0,4},{1,5},{2,6},{3,7},{4,0},{5,1},{6,2},{7,3},{8,12},{9,13},{10,... | collective-permute-start | bytes 61448 | tf_op jit(solution)/shard_map/ppermute | solution.py:704
  12.9 2.2 %collective-permute-start.1 = (f32[40,128]{1,0:T(8,128)S(1)}, f32[40,128]{1,0:T(8,128)S(1)}, u32[]{:S(2)}, u32[]{:S(2)}) collective-permute-start(f32[40,128]{1,0:T(8,128)S(1)} %copy-done.5), channel_id=1, source_target_pairs={{0,1},{1,0},{2,3},{3,2},{4,8},{5,9},{6,10},{7,11},{8,4},{9,5},{10,... | collective-permute-start | bytes 61448 | tf_op jit(solution)/shard_map/ppermute | solution.py:704
  12.9 4.0 %collective-permute-start.2 = (f32[40,128]{1,0:T(8,128)S(1)}, f32[40,128]{1,0:T(8,128)S(1)}, u32[]{:S(2)}, u32[]{:S(2)}) collective-permute-start(f32[40,128]{1,0:T(8,128)S(1)} %copy-done.4), channel_id=1, source_target_pairs={{0,16},{1,17},{2,18},{3,19},{4,20},{5,21},{6,22},{7,23},{8,24},{9,... | collective-permute-start | bytes 61448 | tf_op jit(solution)/shard_map/ppermute | solution.py:704
  20.7 3.9 %collective-permute-start.3 = (f32[24,128]{1,0:T(8,128)S(1)}, f32[24,128]{1,0:T(8,128)S(1)}, u32[]{:S(2)}, u32[]{:S(2)}) collective-permute-start(f32[24,128]{1,0:T(8,128)S(1)} %get-tuple-element.52), channel_id=1, source_target_pairs={{0,1},{1,0},{2,3},{3,2},{4,5},{5,4},{6,7},{7,6},{8,9},{9,8},{10,11... | collective-permute-start | bytes 36872 | tf_op jit(solution)/shard_map/ppermute | solution.py:704
  21.2 3.4 %collective-permute-start.4 = (f32[24,128]{1,0:T(8,128)S(1)}, f32[24,128]{1,0:T(8,128)S(1)}, u32[]{:S(2)}, u32[]{:S(2)}) collective-permute-start(f32[24,128]{1,0:T(8,128)S(1)} %get-tuple-element.53), channel_id=1, source_target_pairs={{0,3},{1,2},{2,1},{3,0},{4,7},{5,6},{6,5},{7,4},{8,11},{9,10},{10,... | collective-permute-start | bytes 36872 | tf_op jit(solution)/shard_map/ppermute | solution.py:704
  24.9 7.4 %collective-permute-start.5 = (f32[144,128]{1,0:T(8,128)S(1)}, f32[144,128]{1,0:T(8,128)S(1)}, u32[]{:S(2)}, u32[]{:S(2)}) collective-permute-start(f32[144,128]{1,0:T(8,128)S(1)} %get-tuple-element.54), channel_id=1, source_target_pairs={{0,4},{1,5},{2,6},{3,7},{4,0},{5,1},{6,2},{7,3},{8,12},{9,13},{10,... | collective-permute-start | bytes 221192 | tf_op jit(solution)/shard_map/ppermute | solution.py:704
  26.2 6.1 %collective-permute-start.6 = (f32[144,128]{1,0:T(8,128)S(1)}, f32[144,128]{1,0:T(8,128)S(1)}, u32[]{:S(2)}, u32[]{:S(2)}) collective-permute-start(f32[144,128]{1,0:T(8,128)S(1)} %get-tuple-element.55), channel_id=1, source_target_pairs={{0,1},{1,0},{2,3},{3,2},{4,8},{5,9},{6,10},{7,11},{8,4},{9,5},{10,... | collective-permute-start | bytes 221192 | tf_op jit(solution)/shard_map/ppermute | solution.py:704
  26.2 6.2 %collective-permute-start.7 = (f32[144,128]{1,0:T(8,128)S(1)}, f32[144,128]{1,0:T(8,128)S(1)}, u32[]{:S(2)}, u32[]{:S(2)}) collective-permute-start(f32[144,128]{1,0:T(8,128)S(1)} %get-tuple-element.56), channel_id=1, source_target_pairs={{0,16},{1,17},{2,18},{3,19},{4,20},{5,21},{6,22},{7,23},{8,24},{9,... | collective-permute-start | bytes 221192 | tf_op jit(solution)/shard_map/ppermute | solution.py:704
  27.7 4.7 %collective-permute-start.8 = (f32[40,128]{1,0:T(8,128)S(1)}, f32[40,128]{1,0:T(8,128)S(1)}, u32[]{:S(2)}, u32[]{:S(2)}) collective-permute-start(f32[40,128]{1,0:T(8,128)S(1)} %get-tuple-element.57), channel_id=1, source_target_pairs={{0,20},{1,21},{2,22},{3,23},{4,16},{5,17},{6,18},{7,19},{8,28},{9,... | collective-permute-start | bytes 61448 | tf_op jit(solution)/shard_map/ppermute | solution.py:704
  29.0 3.3 %collective-permute-start.9 = (f32[40,128]{1,0:T(8,128)S(1)}, f32[40,128]{1,0:T(8,128)S(1)}, u32[]{:S(2)}, u32[]{:S(2)}) collective-permute-start(f32[40,128]{1,0:T(8,128)S(1)} %get-tuple-element.58), channel_id=1, source_target_pairs={{0,1},{1,0},{2,3},{3,2},{4,24},{5,25},{6,26},{7,27},{8,20},{9,21},... | collective-permute-start | bytes 61448 | tf_op jit(solution)/shard_map/ppermute | solution.py:704
  35.5 14.5 %all-to-all-start.1 = ((f32[32,1,1152]{2,1,0:T(1,128)}), f32[32,1,1152]{2,1,0:T(1,128)S(1)}, u32[]{:S(2)}, u32[]{:S(2)}) async-start(f32[32,1,1152]{2,1,0:T(1,128)} %bitcast.4), calls=%async_computation.1 | async-start | bytes 294912 | tf_op jit(solution)/shard_map/all_to_all | solution.py:718
  39.4 4.3 %collective-permute-start.10 = (f32[24,128]{1,0:T(8,128)S(1)}, f32[24,128]{1,0:T(8,128)S(1)}, u32[]{:S(2)}, u32[]{:S(2)}) collective-permute-start(f32[24,128]{1,0:T(8,128)S(1)} %get-tuple-element.61), channel_id=1, source_target_pairs={{0,1},{1,0},{2,3},{3,2},{4,5},{5,4},{6,7},{7,6},{8,9},{9,8},{10,11... | collective-permute-start | bytes 36872 | tf_op jit(solution)/shard_map/ppermute | solution.py:704
  39.5 4.2 %collective-permute-start.11 = (f32[24,128]{1,0:T(8,128)S(1)}, f32[24,128]{1,0:T(8,128)S(1)}, u32[]{:S(2)}, u32[]{:S(2)}) collective-permute-start(f32[24,128]{1,0:T(8,128)S(1)} %get-tuple-element.62), channel_id=1, source_target_pairs={{0,3},{1,2},{2,1},{3,0},{4,7},{5,6},{6,5},{7,4},{8,11},{9,10},{10,... | collective-permute-start | bytes 36872 | tf_op jit(solution)/shard_map/ppermute | solution.py:704
  44.0 7.7 %collective-permute-start.14 = (f32[144,128]{1,0:T(8,128)S(1)}, f32[144,128]{1,0:T(8,128)S(1)}, u32[]{:S(2)}, u32[]{:S(2)}) collective-permute-start(f32[144,128]{1,0:T(8,128)S(1)} %get-tuple-element.65), channel_id=1, source_target_pairs={{0,16},{1,17},{2,18},{3,19},{4,20},{5,21},{6,22},{7,23},{8,24},{9,... | collective-permute-start | bytes 221192 | tf_op jit(solution)/shard_map/ppermute | solution.py:704
  45.6 6.1 %collective-permute-start.12 = (f32[72,128]{1,0:T(8,128)S(1)}, f32[72,128]{1,0:T(8,128)S(1)}, u32[]{:S(2)}, u32[]{:S(2)}) collective-permute-start(f32[72,128]{1,0:T(8,128)S(1)} %get-tuple-element.63), channel_id=1, source_target_pairs={{0,4},{1,5},{2,6},{3,7},{4,0},{5,1},{6,2},{7,3},{8,12},{9,13},{10,... | collective-permute-start | bytes 110600 | tf_op jit(solution)/shard_map/ppermute | solution.py:704
  47.0 4.7 %collective-permute-start.13 = (f32[72,128]{1,0:T(8,128)S(1)}, f32[72,128]{1,0:T(8,128)S(1)}, u32[]{:S(2)}, u32[]{:S(2)}) collective-permute-start(f32[72,128]{1,0:T(8,128)S(1)} %get-tuple-element.64), channel_id=1, source_target_pairs={{0,1},{1,0},{2,3},{3,2},{4,8},{5,9},{6,10},{7,11},{8,4},{9,5},{10,... | collective-permute-start | bytes 110600 | tf_op jit(solution)/shard_map/ppermute | solution.py:704
  47.0 4.7 %collective-permute-start.15 = (f32[24,128]{1,0:T(8,128)S(1)}, f32[24,128]{1,0:T(8,128)S(1)}, u32[]{:S(2)}, u32[]{:S(2)}) collective-permute-start(f32[24,128]{1,0:T(8,128)S(1)} %get-tuple-element.66), channel_id=1, source_target_pairs={{0,20},{1,21},{2,22},{3,23},{4,16},{5,17},{6,18},{7,19},{8,28},{9,... | collective-permute-start | bytes 36872 | tf_op jit(solution)/shard_map/ppermute | solution.py:704
  50.0 1.7 %collective-permute-start.16 = (f32[24,128]{1,0:T(8,128)S(1)}, f32[24,128]{1,0:T(8,128)S(1)}, u32[]{:S(2)}, u32[]{:S(2)}) collective-permute-start(f32[24,128]{1,0:T(8,128)S(1)} %get-tuple-element.67), channel_id=1, source_target_pairs={{0,1},{1,0},{2,3},{3,2},{4,24},{5,25},{6,26},{7,27},{8,20},{9,21},... | collective-permute-start | bytes 36872 | tf_op jit(solution)/shard_map/ppermute | solution.py:704
  53.7 11.4 %all-to-all-start.2 = ((f32[32,1,128]{2,1,0:T(1,128)}), f32[32,1,128]{2,1,0:T(1,128)S(1)}, u32[]{:S(2)}, u32[]{:S(2)}) async-start(f32[32,1,128]{2,1,0:T(1,128)} %bitcast.7), calls=%async_computation.2 | async-start | bytes 32768 | tf_op jit(solution)/shard_map/all_to_all | solution.py:718

commit v13 on v12

--- a/solution.py
+++ b/solution.py
@@ -184,7 +184,8 @@
     high_mask = inside & lane_range(across, sh.y + ex.down, ex.layers)
     span = ex.layers * sh.pitch
     packed = ex.fields * ex.layers
-    below_y, above_y = [unfold(sh, value, packed, -2) for value in sides(sh, 1, [ref[...] for ref in y_refs])]
+    whole = lambda value: value if value.shape[0] == sh.rows else unfold(sh, value, packed, -2)
+    below_y, above_y = [whole(value) for value in sides(sh, 1, [ref[...] for ref in y_refs])]
     per_link = 1 + sh.y_links
     sums = []
     for link in range(sh.x_links):
@@ -937,7 +938,7 @@
         some_nodes = jnp.concatenate([nodes_ref[0:EDGE, :], nodes_ref[sh.z - EDGE : sh.z, :]], axis=0)
         added = coarse_cells(some_nodes, coords(sh, z), values, node_count)
         for m in range(3):
-            solution[m, 2 * EDGE : 4 * EDGE, :] += pick(some_nodes >= 0.0, added[m])
+            solution[m, 2 * EDGE : 4 * EDGE, :] += added[m]
         pack_z(sh, DEEP, end_rows(solution), z_refs)
 
     residual, wide_nodes, stiffness, values, *z_messages = call(
@@ -970,7 +971,7 @@
             solution_ref[m] = inner((v0, v1)[index], m)
         added = coarse_cells(nodes_ref[...], coords(sh, own_level(sh)), values, node_count)
         for m in range(3):
-            solution_ref[m, own, :] += pick(nodes_ref[...] >= 0.0, added[m])
+            solution_ref[m, own, :] += added[m]
 
     solved, springs = call(
         first_solve,

time: 66.2 us -> 66.2 us (level)
  no operation moved by 1% of the time
where the time goes in v13:
time: 66.2 us; the launch traced here: 65.9 us
  starting transfers between devices  31.6 us (48%)
  Pallas kernels  19.3 us (29%)
  waiting for transfers between devices  14.1 us (21%)
  between operations  0.86 us (1%)
    pallas_call x12, Pallas kernels, call(): pl.pallas_call(kernel, out_shape=[jax.ShapeDtypeStruct(shape, f32) for sh...  19.3 us
    ppermute x17, starting transfers between devices, send(): return lax.ppermute(value, AXES, permutation(sh.sizes, moves))  16.1 us
    all_to_all x3, starting transfers between devices, to_all(): return lax.all_to_all(slots, AXES, 0, 0, tiled=True)  15.5 us
    all_to_all x3, waiting for transfers between devices, to_all(): return lax.all_to_all(slots, AXES, 0, 0, tiled=True)  7.9 us
    ppermute x17, waiting for transfers between devices, send(): return lax.ppermute(value, AXES, permutation(sh.sizes, moves))  6.15 us
  transfers between devices with their start and end apart: 20, of which 5 were waited for; matrix products, arithmetic and copies ran while one was open for 0% of the time, Pallas kernels for 13%

profile of v13, /device:TPU:0, one launch (start us, length us, event | category | flops | bytes accessed | tf_op | source)
XLA Modules:
  0.0 65.9 jit_solution(2806763281732192788)
XLA Ops:
  0.6 3.0 %begin.1 = (f32[48,64]{1,0:T(8,128)}, f32[256,128]{1,0:T(8,128)}, f32[40,128]{1,0:T(8,128)}, f32[40,128]{1,0:T(8,128)}, f32[40,128]{1,0:T(8,128)}) custom-call(f32[3,64,128]{2,1,0:T(8,128)} %bitcast.12, s32[4,4,64]{2,1,0:T(4,128)} %labels_in.1, f32[8]{0:T(128)} %moduli_in.1, s32[64,128]{1,0:T(8,128)} %bitcast.17), custom_call_target="tpu_custom_call" | custom-call | tf_op jit(solution)/shard_map/begin/pallas_call | solution.py:670
  3.7 0.0 copy-start.4
  3.7 0.0 copy-start
  3.7 0.0 copy-start.2
  3.7 0.0 copy-start.3
  3.7 7.3 %all-to-all-start = ((f32[32,8,128]{2,1,0:T(8,128)}), f32[32,8,128]{2,1,0:T(8,128)S(1)}, u32[]{:S(2)}, u32[]{:S(2)}) async-start(f32[32,8,128]{2,1,0:T(8,128)} %bitcast.20), calls=%async_computation | async-start | bytes 262144 | tf_op jit(solution)/shard_map/all_to_all | solution.py:719
  11.0 1.8 %collective-permute-start = (f32[40,128]{1,0:T(8,128)S(1)}, f32[40,128]{1,0:T(8,128)S(1)}, u32[]{:S(2)}, u32[]{:S(2)}) collective-permute-start(f32[40,128]{1,0:T(8,128)S(1)} %copy-done.6), channel_id=1, source_target_pairs={{0,4},{1,5},{2,6},{3,7},{4,0},{5,1},{6,2},{7,3},{8,12},{9,13},{10,... | collective-permute-start | bytes 61448 | tf_op jit(solution)/shard_map/ppermute | solution.py:705
  12.9 0.0 collective-permute-start.1
  12.9 1.5 %collective-permute-start.2 = (f32[40,128]{1,0:T(8,128)S(1)}, f32[40,128]{1,0:T(8,128)S(1)}, u32[]{:S(2)}, u32[]{:S(2)}) collective-permute-start(f32[40,128]{1,0:T(8,128)S(1)} %copy-done.4), channel_id=1, source_target_pairs={{0,16},{1,17},{2,18},{3,19},{4,20},{5,21},{6,22},{7,23},{8,24},{9,... | collective-permute-start | bytes 61448 | tf_op jit(solution)/shard_map/ppermute | solution.py:705
  14.4 0.7 %spread.1 = (f32[4,144,128]{2,1,0:T(8,128)S(1)}, f32[128,128]{1,0:T(8,128)S(1)}, f32[36,1152]{1,0:T(8,128)S(1)}) custom-call(f32[3,64,128]{2,1,0:T(8,128)S(1)} %bitcast.13, s32[64,128]{1,0:T(8,128)S(1)} %bitcast.18, f32[48,64]{1,0:T(8,128)S(1)} %copy-done.3, f32[36,1152]{1,0:T(8,128)S(1)} %copy-done.1), custom_call_target="tpu_custom_call" | custom-call | tf_op jit(solution)/shard_map/spread/pallas_call | solution.py:670
  15.1 0.0 collective-permute-done.refs_1_
  15.1 0.0 collective-permute-done.1.refs_2_
  15.1 1.8 %collective-permute-done.2.refs_3_ = f32[40,128]{1,0:T(8,128)S(1)} collective-permute-done((f32[40,128]{1,0:T(8,128)S(1)}, f32[40,128]{1,0:T(8,128)S(1)}, u32[]{:S(2)}, u32[]{:S(2)}) %collective-permute-start.2) | collective-permute-done | bytes 20512 | tf_op jit(solution)/shard_map/ppermute | solution.py:705
  16.9 2.4 %all-to-all-done = f32[32,8,128]{2,1,0:T(8,128)S(1)} async-done(((f32[32,8,128]{2,1,0:T(8,128)}), f32[32,8,128]{2,1,0:T(8,128)S(1)}, u32[]{:S(2)}, u32[]{:S(2)}) %all-to-all-start) | async-done | bytes 131104 | tf_op jit(solution)/shard_map/all_to_all | solution.py:719
  19.3 1.4 %first_ends.1 = (f32[3,144,128]{2,1,0:T(8,128)S(1)}, f32[144,128]{1,0:T(8,128)S(1)}, f32[2,144,128]{2,1,0:T(8,128)S(1)}, f32[48,128]{1,0:T(8,128)S(1)}, f32[24,128]{1,0:T(8,128)S(1)}, /*index=5*/f32[24,128]{1,0:T(8,128)S(1)}) custom-call(f32[4,144,128]{2,1,0:T(8,128)S(1)} %get-tuple-element.41.refs_0_.start_ref, f32[40,128]{1,0:T(8,128)S(1)} %collective-permute-done.refs_1_, ...), custom_call_target="tpu_custom_call" | custom-call | tf_op jit(solution)/shard_map/first_ends/pallas_call | solution.py:670
  20.7 0.5 collective-permute-start.3
  21.2 0.3 collective-permute-start.4
  21.6 3.0 %first_solve.1 = (f32[3,144,128]{2,1,0:T(8,128)S(1)}, f32[8,144,128]{2,1,0:T(8,128)S(1)}) custom-call(f32[3,144,128]{2,1,0:T(8,128)S(1)} %get-tuple-element.48.residual_ref, f32[2,144,128]{2,1,0:T(8,128)S(1)} %get-tuple-element.49.stiffness_ref, f32[48,128]{1,0:T(8,128)S(1)} %get-tuple-element.50.values, ...), custom_call_target="tpu_custom_call" | custom-call | tf_op jit(solution)/shard_map/first_solve/pallas_call | solution.py:670
  24.6 0.0 collective-permute-done.3.refs_1_
  24.6 0.0 collective-permute-done.4.refs_2_
  24.6 0.3 deep.1
  24.9 1.3 %collective-permute-start.5 = (f32[144,128]{1,0:T(8,128)S(1)}, f32[144,128]{1,0:T(8,128)S(1)}, u32[]{:S(2)}, u32[]{:S(2)}) collective-permute-start(f32[144,128]{1,0:T(8,128)S(1)} %get-tuple-element.54), channel_id=1, source_target_pairs={{0,4},{1,5},{2,6},{3,7},{4,0},{5,1},{6,2},{7,3},{8,12},{9,13},{10,... | collective-permute-start | bytes 221192 | tf_op jit(solution)/shard_map/ppermute | solution.py:705
  26.2 1.5 %collective-permute-start.7 = (f32[144,128]{1,0:T(8,128)S(1)}, f32[144,128]{1,0:T(8,128)S(1)}, u32[]{:S(2)}, u32[]{:S(2)}) collective-permute-start(f32[144,128]{1,0:T(8,128)S(1)} %get-tuple-element.56), channel_id=1, source_target_pairs={{0,16},{1,17},{2,18},{3,19},{4,20},{5,21},{6,22},{7,23},{8,24},{9,... | collective-permute-start | bytes 221192 | tf_op jit(solution)/shard_map/ppermute | solution.py:705
  27.6 1.4 %collective-permute-start.8 = (f32[40,128]{1,0:T(8,128)S(1)}, f32[40,128]{1,0:T(8,128)S(1)}, u32[]{:S(2)}, u32[]{:S(2)}) collective-permute-start(f32[40,128]{1,0:T(8,128)S(1)} %get-tuple-element.57), channel_id=1, source_target_pairs={{0,20},{1,21},{2,22},{3,23},{4,16},{5,17},{6,18},{7,19},{8,28},{9,... | collective-permute-start | bytes 61448 | tf_op jit(solution)/shard_map/ppermute | solution.py:705
  29.0 3.3 %collective-permute-done.8.refs_6_ = f32[40,128]{1,0:T(8,128)S(1)} collective-permute-done((f32[40,128]{1,0:T(8,128)S(1)}, f32[40,128]{1,0:T(8,128)S(1)}, u32[]{:S(2)}, u32[]{:S(2)}) %collective-permute-start.8) | collective-permute-done | bytes 20512 | tf_op jit(solution)/shard_map/ppermute | solution.py:705
  32.3 0.0 collective-permute-done.9.refs_7_
  32.3 0.0 collective-permute-done.5.refs_3_
  32.3 0.0 collective-permute-done.6.refs_4_
  32.3 0.0 collective-permute-done.7.refs_5_
  32.3 3.1 %first_image.1 = (f32[3,144,128]{2,1,0:T(8,128)S(1)}, f32[3,144,128]{2,1,0:T(8,128)S(1)}, f32[288,128]{1,0:T(8,128)}, f32[24,128]{1,0:T(8,128)S(1)}, f32[24,128]{1,0:T(8,128)S(1)}) custom-call(f32[3,144,128]{2,1,0:T(8,128)S(1)} %get-tuple-element.51.refs_0_, f32[24,128]{1,0:T(8,128)S(1)} %collective-permute-done.3.refs_1_, ...), custom_call_target="tpu_custom_call" | custom-call | tf_op jit(solution)/shard_map/first_image/pallas_call | solution.py:670
  35.5 3.8 %all-to-all-start.1 = ((f32[32,1,1152]{2,1,0:T(1,128)}), f32[32,1,1152]{2,1,0:T(1,128)S(1)}, u32[]{:S(2)}, u32[]{:S(2)}) async-start(f32[32,1,1152]{2,1,0:T(1,128)} %bitcast.4), calls=%async_computation.1 | async-start | bytes 294912 | tf_op jit(solution)/shard_map/all_to_all | solution.py:719
  39.3 0.1 collective-permute-start.10
  39.5 1.6 %collective-permute-start.11 = (f32[24,128]{1,0:T(8,128)S(1)}, f32[24,128]{1,0:T(8,128)S(1)}, u32[]{:S(2)}, u32[]{:S(2)}) collective-permute-start(f32[24,128]{1,0:T(8,128)S(1)} %get-tuple-element.62), channel_id=1, source_target_pairs={{0,3},{1,2},{2,1},{3,0},{4,7},{5,6},{6,5},{7,4},{8,11},{9,10},{10,... | collective-permute-start | bytes 36872 | tf_op jit(solution)/shard_map/ppermute | solution.py:705
  41.1 2.5 %second_solve.1.refs_0_ = f32[3,144,128]{2,1,0:T(8,128)S(1)} custom-call(f32[3,144,128]{2,1,0:T(8,128)S(1)} %get-tuple-element.60.image_ref.first_ref.refs_10_, f32[8,144,128]{2,1,0:T(8,128)S(1)} %get-tuple-element.59.refs_9_.springs_ref), custom_call_target="tpu_custom_call" | custom-call | tf_op jit(solution)/shard_map/second_solve/pallas_call | solution.py:670
  43.6 0.0 collective-permute-done.11.refs_2_
  43.6 0.4 near.1
  44.0 1.5 %collective-permute-start.14 = (f32[144,128]{1,0:T(8,128)S(1)}, f32[144,128]{1,0:T(8,128)S(1)}, u32[]{:S(2)}, u32[]{:S(2)}) collective-permute-start(f32[144,128]{1,0:T(8,128)S(1)} %get-tuple-element.65), channel_id=1, source_target_pairs={{0,16},{1,17},{2,18},{3,19},{4,20},{5,21},{6,22},{7,23},{8,24},{9,... | collective-permute-start | bytes 221192 | tf_op jit(solution)/shard_map/ppermute | solution.py:705
  45.5 1.5 %collective-permute-start.12 = (f32[72,128]{1,0:T(8,128)S(1)}, f32[72,128]{1,0:T(8,128)S(1)}, u32[]{:S(2)}, u32[]{:S(2)}) collective-permute-start(f32[72,128]{1,0:T(8,128)S(1)} %get-tuple-element.63), channel_id=1, source_target_pairs={{0,4},{1,5},{2,6},{3,7},{4,0},{5,1},{6,2},{7,3},{8,12},{9,13},{10,... | collective-permute-start | bytes 110600 | tf_op jit(solution)/shard_map/ppermute | solution.py:705
  47.0 3.0 %collective-permute-start.15 = (f32[24,128]{1,0:T(8,128)S(1)}, f32[24,128]{1,0:T(8,128)S(1)}, u32[]{:S(2)}, u32[]{:S(2)}) collective-permute-start(f32[24,128]{1,0:T(8,128)S(1)} %get-tuple-element.66), channel_id=1, source_target_pairs={{0,20},{1,21},{2,22},{3,23},{4,16},{5,17},{6,18},{7,19},{8,28},{9,... | collective-permute-start | bytes 36872 | tf_op jit(solution)/shard_map/ppermute | solution.py:705
  50.0 0.6 between.1
  50.6 1.1 %collective-permute-done.15.refs_6_ = f32[24,128]{1,0:T(8,128)S(1)} collective-permute-done((f32[24,128]{1,0:T(8,128)S(1)}, f32[24,128]{1,0:T(8,128)S(1)}, u32[]{:S(2)}, u32[]{:S(2)}) %collective-permute-start.15) | collective-permute-done | bytes 12320 | tf_op jit(solution)/shard_map/ppermute | solution.py:705
  51.7 0.0 collective-permute-done.16.refs_7_
  51.7 0.0 collective-permute-done.12.refs_3_
  51.7 2.0 %second_image.1 = (f32[3,144,128]{2,1,0:T(8,128)S(1)}, f32[3,144,128]{2,1,0:T(8,128)S(1)}, f32[32,128]{1,0:T(8,128)}) custom-call(f32[3,144,128]{2,1,0:T(8,128)S(1)} %second_solve.1.refs_0_, f32[24,128]{1,0:T(8,128)S(1)} %collective-permute-done.10.refs_1_, f32[24,128]{1,0:T(8,128)S(1)} %collective-permute-done.11.refs_2_, ...), custom_call_target="tpu_custom_call" | custom-call | tf_op jit(solution)/shard_map/second_image/pallas_call | solution.py:670
  53.6 4.3 %all-to-all-start.2 = ((f32[32,1,128]{2,1,0:T(1,128)}), f32[32,1,128]{2,1,0:T(1,128)S(1)}, u32[]{:S(2)}, u32[]{:S(2)}) async-start(f32[32,1,128]{2,1,0:T(1,128)} %bitcast.7), calls=%async_computation.2 | async-start | bytes 32768 | tf_op jit(solution)/shard_map/all_to_all | solution.py:719
  58.0 1.6 %turn.1.turned_ref = f32[4,3,64,128]{3,2,1,0:T(8,128)S(1)} custom-call(f32[3,144,128]{2,1,0:T(8,128)S(1)} %get-tuple-element.70.search_ref, f32[3,144,128]{2,1,0:T(8,128)S(1)} %get-tuple-element.60.image_ref.first_ref.refs_10_, f32[3,144,128]{2,1,0:T(8,128)S(1)} %get-tuple-element.74.second_ref, f32[3,144,128]{2,1,0:T(8,128)S(1)} %get-tuple-element.75.image_ref), custom_call_target="tpu_custom_call" | custom-call | tf_op jit(solution)/shard_map/turn/pallas_call | solution.py:670
  59.6 5.5 %all-to-all-done.2 = f32[32,1,128]{2,1,0:T(1,128)S(1)} async-done(((f32[32,1,128]{2,1,0:T(1,128)}), f32[32,1,128]{2,1,0:T(1,128)S(1)}, u32[]{:S(2)}, u32[]{:S(2)}) %all-to-all-start.2) | async-done | bytes 16416 | tf_op jit(solution)/shard_map/all_to_all | solution.py:719
  65.1 0.8 %finish.1 = (f32[3,64,128]{2,1,0:T(8,128)}, f32[3,64,128]{2,1,0:T(8,128)}) custom-call(f32[32,128]{1,0:T(8,128)S(1)} %bitcast.19, f32[3,64,128]{2,1,0:T(8,128)S(1)} %bitcast.14, f32[4,3,64,128]{3,2,1,0:T(8,128)S(1)} %turn.1.turned_ref), custom_call_target="tpu_custom_call" | custom-call | tf_op jit(solution)/shard_map/finish/pallas_call | solution.py:670
  (18 shorter events, 0.0 us)
Async XLA Ops:
  0.6 13.8 %copy-start.1 = (f32[36,1152]{1,0:T(8,128)S(1)}, f32[36,1152]{1,0:T(8,128)}, u32[]{:S(2)}) copy-start(f32[36,1152]{1,0:T(8,128)} %inverse_in.1) | copy-start | bytes 497668
  3.6 7.4 %copy-start.6 = (f32[40,128]{1,0:T(8,128)S(1)}, f32[40,128]{1,0:T(8,128)}, u32[]{:S(2)}) copy-start(f32[40,128]{1,0:T(8,128)} %get-tuple-element.42) | copy-start | bytes 61444
  3.7 9.2 %copy-start.5 = (f32[40,128]{1,0:T(8,128)S(1)}, f32[40,128]{1,0:T(8,128)}, u32[]{:S(2)}) copy-start(f32[40,128]{1,0:T(8,128)} %get-tuple-element.43) | copy-start | bytes 61444
  3.7 9.2 %copy-start.4 = (f32[40,128]{1,0:T(8,128)S(1)}, f32[40,128]{1,0:T(8,128)}, u32[]{:S(2)}) copy-start(f32[40,128]{1,0:T(8,128)} %get-tuple-element.44) | copy-start | bytes 61444
  3.7 10.7 %copy-start = (f32[3,8,8,128]{3,2,1,0:T(8,128)S(1)}, f32[3,8,8,128]{3,2,1,0:T(8,128)}, u32[]{:S(2)}) copy-start(f32[3,8,8,128]{3,2,1,0:T(8,128)} %param.5) | copy-start | bytes 294916
  3.7 10.7 %copy-start.2 = (s32[8,8,128]{2,1,0:T(8,128)S(1)}, s32[8,8,128]{2,1,0:T(8,128)}, u32[]{:S(2)}) copy-start(s32[8,8,128]{2,1,0:T(8,128)} %param.8) | copy-start | bytes 98308
  3.7 10.7 %copy-start.3 = (f32[48,64]{1,0:T(8,128)S(1)}, f32[48,64]{1,0:T(8,128)}, u32[]{:S(2)}) copy-start(f32[48,64]{1,0:T(8,128)} %get-tuple-element.40.stiff) | copy-start | bytes 36868
  3.7 15.6 %all-to-all-start = ((f32[32,8,128]{2,1,0:T(8,128)}), f32[32,8,128]{2,1,0:T(8,128)S(1)}, u32[]{:S(2)}, u32[]{:S(2)}) async-start(f32[32,8,128]{2,1,0:T(8,128)} %bitcast.20), calls=%async_computation | async-start | bytes 262144 | tf_op jit(solution)/shard_map/all_to_all | solution.py:719
  11.0 4.1 %collective-permute-start = (f32[40,128]{1,0:T(8,128)S(1)}, f32[40,128]{1,0:T(8,128)S(1)}, u32[]{:S(2)}, u32[]{:S(2)}) collective-permute-start(f32[40,128]{1,0:T(8,128)S(1)} %copy-done.6), channel_id=1, source_target_pairs={{0,4},{1,5},{2,6},{3,7},{4,0},{5,1},{6,2},{7,3},{8,12},{9,13},{10,... | collective-permute-start | bytes 61448 | tf_op jit(solution)/shard_map/ppermute | solution.py:705
  12.9 2.2 %collective-permute-start.1 = (f32[40,128]{1,0:T(8,128)S(1)}, f32[40,128]{1,0:T(8,128)S(1)}, u32[]{:S(2)}, u32[]{:S(2)}) collective-permute-start(f32[40,128]{1,0:T(8,128)S(1)} %copy-done.5), channel_id=1, source_target_pairs={{0,1},{1,0},{2,3},{3,2},{4,8},{5,9},{6,10},{7,11},{8,4},{9,5},{10,... | collective-permute-start | bytes 61448 | tf_op jit(solution)/shard_map/ppermute | solution.py:705
  12.9 4.0 %collective-permute-start.2 = (f32[40,128]{1,0:T(8,128)S(1)}, f32[40,128]{1,0:T(8,128)S(1)}, u32[]{:S(2)}, u32[]{:S(2)}) collective-permute-start(f32[40,128]{1,0:T(8,128)S(1)} %copy-done.4), channel_id=1, source_target_pairs={{0,16},{1,17},{2,18},{3,19},{4,20},{5,21},{6,22},{7,23},{8,24},{9,... | collective-permute-start | bytes 61448 | tf_op jit(solution)/shard_map/ppermute | solution.py:705
  20.7 3.8 %collective-permute-start.3 = (f32[24,128]{1,0:T(8,128)S(1)}, f32[24,128]{1,0:T(8,128)S(1)}, u32[]{:S(2)}, u32[]{:S(2)}) collective-permute-start(f32[24,128]{1,0:T(8,128)S(1)} %get-tuple-element.52), channel_id=1, source_target_pairs={{0,1},{1,0},{2,3},{3,2},{4,5},{5,4},{6,7},{7,6},{8,9},{9,8},{10,11... | collective-permute-start | bytes 36872 | tf_op jit(solution)/shard_map/ppermute | solution.py:705
  21.2 3.3 %collective-permute-start.4 = (f32[24,128]{1,0:T(8,128)S(1)}, f32[24,128]{1,0:T(8,128)S(1)}, u32[]{:S(2)}, u32[]{:S(2)}) collective-permute-start(f32[24,128]{1,0:T(8,128)S(1)} %get-tuple-element.53), channel_id=1, source_target_pairs={{0,3},{1,2},{2,1},{3,0},{4,7},{5,6},{6,5},{7,4},{8,11},{9,10},{10,... | collective-permute-start | bytes 36872 | tf_op jit(solution)/shard_map/ppermute | solution.py:705
  24.9 7.4 %collective-permute-start.5 = (f32[144,128]{1,0:T(8,128)S(1)}, f32[144,128]{1,0:T(8,128)S(1)}, u32[]{:S(2)}, u32[]{:S(2)}) collective-permute-start(f32[144,128]{1,0:T(8,128)S(1)} %get-tuple-element.54), channel_id=1, source_target_pairs={{0,4},{1,5},{2,6},{3,7},{4,0},{5,1},{6,2},{7,3},{8,12},{9,13},{10,... | collective-permute-start | bytes 221192 | tf_op jit(solution)/shard_map/ppermute | solution.py:705
  26.2 6.1 %collective-permute-start.6 = (f32[144,128]{1,0:T(8,128)S(1)}, f32[144,128]{1,0:T(8,128)S(1)}, u32[]{:S(2)}, u32[]{:S(2)}) collective-permute-start(f32[144,128]{1,0:T(8,128)S(1)} %get-tuple-element.55), channel_id=1, source_target_pairs={{0,1},{1,0},{2,3},{3,2},{4,8},{5,9},{6,10},{7,11},{8,4},{9,5},{10,... | collective-permute-start | bytes 221192 | tf_op jit(solution)/shard_map/ppermute | solution.py:705
  26.2 6.2 %collective-permute-start.7 = (f32[144,128]{1,0:T(8,128)S(1)}, f32[144,128]{1,0:T(8,128)S(1)}, u32[]{:S(2)}, u32[]{:S(2)}) collective-permute-start(f32[144,128]{1,0:T(8,128)S(1)} %get-tuple-element.56), channel_id=1, source_target_pairs={{0,16},{1,17},{2,18},{3,19},{4,20},{5,21},{6,22},{7,23},{8,24},{9,... | collective-permute-start | bytes 221192 | tf_op jit(solution)/shard_map/ppermute | solution.py:705
  27.6 4.7 %collective-permute-start.8 = (f32[40,128]{1,0:T(8,128)S(1)}, f32[40,128]{1,0:T(8,128)S(1)}, u32[]{:S(2)}, u32[]{:S(2)}) collective-permute-start(f32[40,128]{1,0:T(8,128)S(1)} %get-tuple-element.57), channel_id=1, source_target_pairs={{0,20},{1,21},{2,22},{3,23},{4,16},{5,17},{6,18},{7,19},{8,28},{9,... | collective-permute-start | bytes 61448 | tf_op jit(solution)/shard_map/ppermute | solution.py:705
  29.0 3.3 %collective-permute-start.9 = (f32[40,128]{1,0:T(8,128)S(1)}, f32[40,128]{1,0:T(8,128)S(1)}, u32[]{:S(2)}, u32[]{:S(2)}) collective-permute-start(f32[40,128]{1,0:T(8,128)S(1)} %get-tuple-element.58), channel_id=1, source_target_pairs={{0,1},{1,0},{2,3},{3,2},{4,24},{5,25},{6,26},{7,27},{8,20},{9,21},... | collective-permute-start | bytes 61448 | tf_op jit(solution)/shard_map/ppermute | solution.py:705
  35.5 14.5 %all-to-all-start.1 = ((f32[32,1,1152]{2,1,0:T(1,128)}), f32[32,1,1152]{2,1,0:T(1,128)S(1)}, u32[]{:S(2)}, u32[]{:S(2)}) async-start(f32[32,1,1152]{2,1,0:T(1,128)} %bitcast.4), calls=%async_computation.1 | async-start | bytes 294912 | tf_op jit(solution)/shard_map/all_to_all | solution.py:719
  39.3 4.3 %collective-permute-start.10 = (f32[24,128]{1,0:T(8,128)S(1)}, f32[24,128]{1,0:T(8,128)S(1)}, u32[]{:S(2)}, u32[]{:S(2)}) collective-permute-start(f32[24,128]{1,0:T(8,128)S(1)} %get-tuple-element.61), channel_id=1, source_target_pairs={{0,1},{1,0},{2,3},{3,2},{4,5},{5,4},{6,7},{7,6},{8,9},{9,8},{10,11... | collective-permute-start | bytes 36872 | tf_op jit(solution)/shard_map/ppermute | solution.py:705
  39.5 4.2 %collective-permute-start.11 = (f32[24,128]{1,0:T(8,128)S(1)}, f32[24,128]{1,0:T(8,128)S(1)}, u32[]{:S(2)}, u32[]{:S(2)}) collective-permute-start(f32[24,128]{1,0:T(8,128)S(1)} %get-tuple-element.62), channel_id=1, source_target_pairs={{0,3},{1,2},{2,1},{3,0},{4,7},{5,6},{6,5},{7,4},{8,11},{9,10},{10,... | collective-permute-start | bytes 36872 | tf_op jit(solution)/shard_map/ppermute | solution.py:705
  44.0 7.7 %collective-permute-start.14 = (f32[144,128]{1,0:T(8,128)S(1)}, f32[144,128]{1,0:T(8,128)S(1)}, u32[]{:S(2)}, u32[]{:S(2)}) collective-permute-start(f32[144,128]{1,0:T(8,128)S(1)} %get-tuple-element.65), channel_id=1, source_target_pairs={{0,16},{1,17},{2,18},{3,19},{4,20},{5,21},{6,22},{7,23},{8,24},{9,... | collective-permute-start | bytes 221192 | tf_op jit(solution)/shard_map/ppermute | solution.py:705
  45.5 6.1 %collective-permute-start.12 = (f32[72,128]{1,0:T(8,128)S(1)}, f32[72,128]{1,0:T(8,128)S(1)}, u32[]{:S(2)}, u32[]{:S(2)}) collective-permute-start(f32[72,128]{1,0:T(8,128)S(1)} %get-tuple-element.63), channel_id=1, source_target_pairs={{0,4},{1,5},{2,6},{3,7},{4,0},{5,1},{6,2},{7,3},{8,12},{9,13},{10,... | collective-permute-start | bytes 110600 | tf_op jit(solution)/shard_map/ppermute | solution.py:705
  47.0 4.7 %collective-permute-start.13 = (f32[72,128]{1,0:T(8,128)S(1)}, f32[72,128]{1,0:T(8,128)S(1)}, u32[]{:S(2)}, u32[]{:S(2)}) collective-permute-start(f32[72,128]{1,0:T(8,128)S(1)} %get-tuple-element.64), channel_id=1, source_target_pairs={{0,1},{1,0},{2,3},{3,2},{4,8},{5,9},{6,10},{7,11},{8,4},{9,5},{10,... | collective-permute-start | bytes 110600 | tf_op jit(solution)/shard_map/ppermute | solution.py:705
  47.0 4.7 %collective-permute-start.15 = (f32[24,128]{1,0:T(8,128)S(1)}, f32[24,128]{1,0:T(8,128)S(1)}, u32[]{:S(2)}, u32[]{:S(2)}) collective-permute-start(f32[24,128]{1,0:T(8,128)S(1)} %get-tuple-element.66), channel_id=1, source_target_pairs={{0,20},{1,21},{2,22},{3,23},{4,16},{5,17},{6,18},{7,19},{8,28},{9,... | collective-permute-start | bytes 36872 | tf_op jit(solution)/shard_map/ppermute | solution.py:705
  50.0 1.7 %collective-permute-start.16 = (f32[24,128]{1,0:T(8,128)S(1)}, f32[24,128]{1,0:T(8,128)S(1)}, u32[]{:S(2)}, u32[]{:S(2)}) collective-permute-start(f32[24,128]{1,0:T(8,128)S(1)} %get-tuple-element.67), channel_id=1, source_target_pairs={{0,1},{1,0},{2,3},{3,2},{4,24},{5,25},{6,26},{7,27},{8,20},{9,21},... | collective-permute-start | bytes 36872 | tf_op jit(solution)/shard_map/ppermute | solution.py:705
  53.6 11.4 %all-to-all-start.2 = ((f32[32,1,128]{2,1,0:T(1,128)}), f32[32,1,128]{2,1,0:T(1,128)S(1)}, u32[]{:S(2)}, u32[]{:S(2)}) async-start(f32[32,1,128]{2,1,0:T(1,128)} %bitcast.7), calls=%async_computation.2 | async-start | bytes 32768 | tf_op jit(solution)/shard_map/all_to_all | solution.py:719
